TPU v7x, 32 devices: a whole 2x2x4 slice. The times are simulated.
32 devices in a mesh: groups: 2 (over x), dev: 16 (over z, y, core).
Axes of the slice: x: 2, y: 2, z: 4, core: 2. Of those that a mesh axis runs over, the one named last changes fastest.
Arguments:
- basis_rows: bfloat16 [2097152, 128], P(('groups', 'dev')), parts along dimension 0, may hold values from -4 to 4
- vector: bfloat16 [2097152], P(('groups', 'dev')), parts along dimension 0, may hold values from -6 to 6
- scores: float32 [2097152], P(('groups', 'dev')), parts along dimension 0, may hold values from -8 to 8
- assign: int32 [2097152], P(('groups', 'dev')), parts along dimension 0, may hold values from 0 to 63, as said below
- slot_of: int32 [128], P('groups'), parts along dimension 0, may hold values from 0 to 63, as said below
- partners: int32 [128, 64], P(('groups', 'dev')), parts along dimension 0, may hold values from 0 to 63
- link_blocks: bfloat16 [128, 64, 128, 128], P(('groups', 'dev')), parts along dimension 0, may hold values from -0.0625 to 0.0625
Outputs:
- product: float32 [2097152], P(('groups', 'dev')), parts along dimension 0
There are 2 independent parts, one for each index of `groups`. A program takes and returns all parts, laid end to end along the dimension named above; each array names one. Nothing has to cross between parts.
Inputs may be any that keep to these rules, and one draw needn't show every extreme that they name: A sample in the block of 65536 samples number d has its slot slot_of[assign[s]] on a device (d + o) mod the number of devices with -2 <= o <= 2; cluster sizes are uneven. slot_of is a permutation of the slots.
All inputs are finite; a program needn't handle non-finite values.
Results may differ from a plain program's by a relative error of at most 0.0075.
Values may be sent and summed in bfloat16 or wider, within the bound.
No kernel may reach another device: no remote copies, remote signals or barrier semaphores. Data moves between devices by JAX's collectives and lax.ppermute only.
A program may use at most 128 MiB of HBM per device.

v0:
```python
import math

import jax
import jax.numpy as jnp
from jax import lax
from jax.sharding import PartitionSpec as P

REACH = 2
CL_DEV = 4
S_DEV = 65536


ridge = 0.5


def from_behind(block, axis, distance):
    devices = range(lax.axis_size(axis))
    route = [((i - distance) % len(devices), i) for i in devices]
    return lax.ppermute(block, axis, route)


def shards(basis_rows, vector, scores, assign, slot_of, partners, link_blocks):
    clusters = slot_of.shape[0]
    devices = lax.axis_size("dev")
    per_dev = clusters // devices
    me_index = lax.axis_index("dev")
    numbers = jnp.arange(clusters, dtype=jnp.int32)
    permuter = (slot_of[:, None] == numbers[None, :]).astype(jnp.bfloat16)
    cluster_hits = (assign[:, None] == numbers[None, :]).astype(jnp.bfloat16)
    onehot = jnp.dot(cluster_hits, permuter, preferred_element_type=jnp.float32).astype(
        jnp.bfloat16
    )
    flat_partners = partners.reshape(-1)
    partner_hits = (flat_partners[:, None] == numbers[None, :]).astype(jnp.bfloat16)
    partner_pick = jnp.dot(partner_hits, permuter, preferred_element_type=jnp.float32).astype(
        jnp.bfloat16
    )
    norm = 1.0 / math.sqrt(S_DEV // CL_DEV)

    def block_at(blocks, offset):
        target = (me_index + offset + devices) % devices
        return lax.dynamic_index_in_dim(blocks, target, 0, keepdims=False)

    def kernel_apply(weights):
        partial_coef = lax.dot_general(
            onehot * weights[:, None],
            basis_rows,
            (((0,), (0,)), ((), ())),
            preferred_element_type=jnp.float32,
        )
        blocks = partial_coef.reshape(devices, per_dev, partial_coef.shape[1])
        owned = blocks[me_index]
        for offset in range(-REACH, REACH + 1):
            if offset != 0:
                owned = owned + from_behind(block_at(blocks, offset), "dev", offset)
        scaled = lax.all_gather((owned * norm).astype(jnp.bfloat16), "dev", axis=0, tiled=True)
        picked = jnp.dot(partner_pick, scaled, preferred_element_type=jnp.float32).astype(
            jnp.bfloat16
        )
        gathered = picked.reshape(partners.shape[0], partners.shape[1], scaled.shape[1])
        mixed = jnp.einsum(
            "kpij,kpj->ki", link_blocks, gathered, preferred_element_type=jnp.float32
        ).astype(jnp.bfloat16)
        table = jnp.zeros((devices, per_dev, mixed.shape[1]), jnp.bfloat16)
        for offset in range(-REACH, REACH + 1):
            source = (me_index + offset + devices) % devices
            if offset == 0:
                got = mixed
            else:
                got = from_behind(mixed, "dev", -offset)
            table = lax.dynamic_update_index_in_dim(table, got, source, 0)
        everywhere = table.reshape(clusters, mixed.shape[1])
        rows = jnp.dot(onehot, everywhere, preferred_element_type=jnp.float32).astype(jnp.bfloat16)
        return jnp.einsum("sr,sr->s", basis_rows, rows, preferred_element_type=jnp.float32)

    first = kernel_apply(vector)
    sig = jax.nn.sigmoid(scores)
    weighted = (sig * (1.0 - sig) * first).astype(jnp.bfloat16)
    second = kernel_apply(weighted)
    return second + ridge * first


def solution(mesh):
    in_specs = (
        P(("groups", "dev"), None),
        P(("groups", "dev")),
        P(("groups", "dev")),
        P(("groups", "dev")),
        P("groups"),
        P(("groups", "dev"), None),
        P(("groups", "dev"), None, None, None),
    )
    out_specs = P(("groups", "dev"))
    return jax.shard_map(shards, mesh=mesh, in_specs=in_specs, out_specs=out_specs, check_vma=False)
```

profile of v0, /device:TPU:0, one launch (start us, length us, event | category | flops | bytes accessed | tf_op | source)
XLA Modules:
  0.0 153.9 jit_solution(15250194388038517372)
XLA Ops:
  0.0 5.4 %convolution_convert_fusion.2 = bf16[65536,64]{0,1:T(8,128)(2,1)S(1)} fusion(s32[65536]{0:T(1024)} %param.10, s32[64]{0:T(128)} %param.11), kind=kOutput, calls=%fused_computation.6 | convolution fusion | flops 545263616 | bytes 8651008 | tf_op jit(solution)/shard_map/dot_general | solution.py:30
  5.5 10.6 %fusion.6 = f32[64,128]{1,0:T(8,128)S(1)} fusion(bf16[65536,128]{1,0:T(8,128)(2,1)} %param.7, bf16[65536,64]{0,1:T(8,128)(2,1)S(1)} %convolution_convert_fusion.2, bf16[65536]{0:T(1024)(128)(2,1)S(1)} %copy-done.1), kind=kOutput, calls=%fused_computation.10 | convolution fusion | flops 1077936128 | bytes 25329664 | tf_op jit(solution)/shard_map/dot_general | solution.py:45
  16.1 6.1 %collective-permute-start = (f32[4,128]{1,0:T(4,128)S(1)}, f32[4,128]{1,0:T(4,128)S(1)}, u32[]{:S(2)}, u32[]{:S(2)}) collective-permute-start(f32[4,128]{1,0:T(4,128)S(1)} %get-tuple-element.9), channel_id=1, source_target_pairs={{2,0},{3,1},{4,2},{5,3},{6,4},{7,5},{8,6},{9,7},{10,8},{11,9},{12,... | collective-permute-start | bytes 6152 | tf_op jit(solution)/shard_map/ppermute | solution.py:19
  22.2 4.5 %collective-permute-start.1 = (f32[4,128]{1,0:T(4,128)S(1)}, f32[4,128]{1,0:T(4,128)S(1)}, u32[]{:S(2)}, u32[]{:S(2)}) collective-permute-start(f32[4,128]{1,0:T(4,128)S(1)} %get-tuple-element.12), channel_id=1, source_target_pairs={{1,0},{2,1},{3,2},{4,3},{5,4},{6,5},{7,6},{8,7},{9,8},{10,9},{11,1... | collective-permute-start | bytes 6152 | tf_op jit(solution)/shard_map/ppermute | solution.py:19
  27.0 1.4 collective-permute-done.3
  28.5 18.6 %all-gather = bf16[16,4,128]{2,1,0:T(4,128)(2,1)S(1)} all-gather(bf16[1,4,128]{2,1,0:T(4,128)(2,1)S(1)} %fusion.45), channel_id=1, replica_groups=mesh['groups'=2,'dev'=16] {'dev'}, dimensions={0}, use_global_device_ids=true | all-gather | bytes 17408 | tf_op jit(solution)/shard_map/all_gather | solution.py:56
  47.2 5.6 %fusion.17 = f32[4,1,128,1]{2,1,3,0:T(1,128)S(1)} fusion(bf16[4,64,128,128]{3,2,1,0:T(8,128)(2,1)} %param.13, bf16[4,64,128,1]{2,1,0,3:T(8,128)(2,1)S(1)} %bitcast.103), kind=kOutput, calls=%fused_computation.26 | convolution fusion | flops 8388608 | bytes 8456192 | tf_op jit(solution)/shard_map/kpij,kpj->ki/dot_general | solution.py:61
  52.9 0.6 collective-permute-start.4
  53.5 3.8 %collective-permute-start.6 = (bf16[4,128]{1,0:T(4,128)(2,1)S(1)}, bf16[4,128]{1,0:T(4,128)(2,1)S(1)}, u32[]{:S(2)}, u32[]{:S(2)}) collective-permute-start(bf16[4,128]{1,0:T(4,128)(2,1)S(1)} %convert_element_type.40), channel_id=1, source_target_pairs={{1,0},{2,1},{3,2},{4,3},{5,4},{6,5},{7,6},{8,7},{9,8},{10,9},{11,1... | collective-permute-start | bytes 3080 | tf_op jit(solution)/shard_map/ppermute | solution.py:19
  57.9 1.3 collective-permute-done.4
  59.2 4.1 %collective-permute-done.5 = bf16[4,128]{1,0:T(4,128)(2,1)S(1)} collective-permute-done((bf16[4,128]{1,0:T(4,128)(2,1)S(1)}, bf16[4,128]{1,0:T(4,128)(2,1)S(1)}, u32[]{:S(2)}, u32[]{:S(2)}) %collective-permute-start.5) | collective-permute-done | bytes 1056 | tf_op jit(solution)/shard_map/ppermute | solution.py:19
  63.4 18.0 %fusion.10 = f32[65536]{0:T(1024)S(1)} fusion(bf16[65536,128]{1,0:T(8,128)(2,1)} %param.7, bf16[65536,64]{0,1:T(8,128)(2,1)} %copy-done, bf16[64,128]{1,0:T(8,128)(2,1)S(1)} %bitcast.115), kind=kOutput, calls=%fused_computation.14 | convolution fusion | flops 1115619328 | bytes 25444352 | tf_op jit(solution)/shard_map/dot_general | solution.py:73
  81.5 11.6 %fusion.4 = f32[64,128]{1,0:T(8,128)S(1)} fusion(bf16[65536,128]{1,0:T(8,128)(2,1)} %param.7, bf16[65536,64]{0,1:T(8,128)(2,1)} %copy-done, bf16[65536]{0:T(1024)(128)(2,1)S(1)} %fusion.14), kind=kOutput, calls=%fused_computation.8 | convolution fusion | flops 1077936128 | bytes 25329664 | tf_op jit(solution)/shard_map/dot_general | solution.py:45
  93.6 1.5 collective-permute-start.11
  95.2 4.4 %collective-permute-start.9 = (f32[4,128]{1,0:T(4,128)S(1)}, f32[4,128]{1,0:T(4,128)S(1)}, u32[]{:S(2)}, u32[]{:S(2)}) collective-permute-start(f32[4,128]{1,0:T(4,128)S(1)} %get-tuple-element.8), channel_id=1, source_target_pairs={{1,0},{2,1},{3,2},{4,3},{5,4},{6,5},{7,6},{8,7},{9,8},{10,9},{11,1... | collective-permute-start | bytes 6152 | tf_op jit(solution)/shard_map/ppermute | solution.py:19
  99.9 0.9 collective-permute-done.10
  100.9 17.9 %all-gather.1 = bf16[16,4,128]{2,1,0:T(4,128)(2,1)S(1)} all-gather(bf16[1,4,128]{2,1,0:T(4,128)(2,1)S(1)} %fusion.44), channel_id=1, replica_groups=mesh['groups'=2,'dev'=16] {'dev'}, dimensions={0}, use_global_device_ids=true | all-gather | bytes 17408 | tf_op jit(solution)/shard_map/all_gather | solution.py:56
  119.1 5.6 %fusion.15 = f32[4,1,128,1]{2,1,3,0:T(1,128)S(1)} fusion(bf16[4,64,128,128]{3,2,1,0:T(8,128)(2,1)} %param.13, bf16[4,64,128,1]{2,1,0,3:T(8,128)(2,1)S(1)} %bitcast.102), kind=kOutput, calls=%fused_computation.24 | convolution fusion | flops 8388608 | bytes 8456192 | tf_op jit(solution)/shard_map/kpij,kpj->ki/dot_general | solution.py:61
  124.7 1.3 collective-permute-start.12
  126.0 3.0 %collective-permute-start.14 = (bf16[4,128]{1,0:T(4,128)(2,1)S(1)}, bf16[4,128]{1,0:T(4,128)(2,1)S(1)}, u32[]{:S(2)}, u32[]{:S(2)}) collective-permute-start(bf16[4,128]{1,0:T(4,128)(2,1)S(1)} %convert_element_type.45), channel_id=1, source_target_pairs={{1,0},{2,1},{3,2},{4,3},{5,4},{6,5},{7,6},{8,7},{9,8},{10,9},{11,1... | collective-permute-start | bytes 3080 | tf_op jit(solution)/shard_map/ppermute | solution.py:19
  129.7 1.3 collective-permute-done.12
  131.0 4.1 %collective-permute-done.13 = bf16[4,128]{1,0:T(4,128)(2,1)S(1)} collective-permute-done((bf16[4,128]{1,0:T(4,128)(2,1)S(1)}, bf16[4,128]{1,0:T(4,128)(2,1)S(1)}, u32[]{:S(2)}, u32[]{:S(2)}) %collective-permute-start.13) | collective-permute-done | bytes 1056 | tf_op jit(solution)/shard_map/ppermute | solution.py:19
  135.2 18.0 %fusion.9 = f32[65536]{0:T(1024)S(1)} fusion(bf16[65536,128]{1,0:T(8,128)(2,1)} %param.7, bf16[65536,64]{0,1:T(8,128)(2,1)} %copy-done, bf16[64,128]{1,0:T(8,128)(2,1)S(1)} %bitcast.114), kind=kOutput, calls=%fused_computation.13 | convolution fusion | flops 1115619328 | bytes 25444352 | tf_op jit(solution)/shard_map/dot_general | solution.py:73
  153.2 0.7 multiply_add_fusion
  (51 shorter events, 3.3 us)
Async XLA Ops:
  0.0 5.4 %copy-start.1 = (bf16[65536]{0:T(1024)(128)(2,1)S(1)}, bf16[65536]{0:T(1024)(128)(2,1)}, u32[]{:S(2)}) copy-start(bf16[65536]{0:T(1024)(128)(2,1)} %param.8) | copy-start | bytes 393220
  5.5 10.6 %copy-start = (bf16[65536,64]{0,1:T(8,128)(2,1)}, bf16[65536,64]{0,1:T(8,128)(2,1)S(1)}, u32[]{:S(2)}) copy-start(bf16[65536,64]{0,1:T(8,128)(2,1)S(1)} %convolution_convert_fusion.2) | copy-start | bytes 25165828
  5.5 21.2 %copy-start.3 = (s32[4,64]{1,0:T(4,128)S(1)}, s32[4,64]{1,0:T(4,128)}, u32[]{:S(2)}) copy-start(s32[4,64]{1,0:T(4,128)} %param.12) | copy-start | bytes 3076
  5.5 21.3 %copy-start.4 = (s32[64]{0:T(128)S(1)}, s32[64]{0:T(128)}, u32[]{:S(2)}) copy-start(s32[64]{0:T(128)} %param.11) | copy-start | bytes 772
  16.1 10.9 %collective-permute-start = (f32[4,128]{1,0:T(4,128)S(1)}, f32[4,128]{1,0:T(4,128)S(1)}, u32[]{:S(2)}, u32[]{:S(2)}) collective-permute-start(f32[4,128]{1,0:T(4,128)S(1)} %get-tuple-element.9), channel_id=1, source_target_pairs={{2,0},{3,1},{4,2},{5,3},{6,4},{7,5},{8,6},{9,7},{10,8},{11,9},{12,... | collective-permute-start | bytes 6152 | tf_op jit(solution)/shard_map/ppermute | solution.py:19
  22.2 6.3 %collective-permute-start.3 = (f32[4,128]{1,0:T(4,128)S(1)}, f32[4,128]{1,0:T(4,128)S(1)}, u32[]{:S(2)}, u32[]{:S(2)}) collective-permute-start(f32[4,128]{1,0:T(4,128)S(1)} %get-tuple-element.10), channel_id=1, source_target_pairs={{14,0},{15,1},{0,2},{1,3},{2,4},{3,5},{4,6},{5,7},{6,8},{7,9},{8,1... | collective-permute-start | bytes 6152 | tf_op jit(solution)/shard_map/ppermute | solution.py:19
  22.2 6.3 %collective-permute-start.2 = (f32[4,128]{1,0:T(4,128)S(1)}, f32[4,128]{1,0:T(4,128)S(1)}, u32[]{:S(2)}, u32[]{:S(2)}) collective-permute-start(f32[4,128]{1,0:T(4,128)S(1)} %get-tuple-element.11), channel_id=1, source_target_pairs={{15,0},{0,1},{1,2},{2,3},{3,4},{4,5},{5,6},{6,7},{7,8},{8,9},{9,10... | collective-permute-start | bytes 6152 | tf_op jit(solution)/shard_map/ppermute | solution.py:19
  22.2 6.3 %collective-permute-start.1 = (f32[4,128]{1,0:T(4,128)S(1)}, f32[4,128]{1,0:T(4,128)S(1)}, u32[]{:S(2)}, u32[]{:S(2)}) collective-permute-start(f32[4,128]{1,0:T(4,128)S(1)} %get-tuple-element.12), channel_id=1, source_target_pairs={{1,0},{2,1},{3,2},{4,3},{5,4},{6,5},{7,6},{8,7},{9,8},{10,9},{11,1... | collective-permute-start | bytes 6152 | tf_op jit(solution)/shard_map/ppermute | solution.py:19
  52.9 6.3 %collective-permute-start.4 = (bf16[4,128]{1,0:T(4,128)(2,1)S(1)}, bf16[4,128]{1,0:T(4,128)(2,1)S(1)}, u32[]{:S(2)}, u32[]{:S(2)}) collective-permute-start(bf16[4,128]{1,0:T(4,128)(2,1)S(1)} %convert_element_type.40), channel_id=1, source_target_pairs={{14,0},{15,1},{0,2},{1,3},{2,4},{3,5},{4,6},{5,7},{6,8},{7,9},{8,1... | collective-permute-start | bytes 3080 | tf_op jit(solution)/shard_map/ppermute | solution.py:19
  53.5 9.9 %collective-permute-start.6 = (bf16[4,128]{1,0:T(4,128)(2,1)S(1)}, bf16[4,128]{1,0:T(4,128)(2,1)S(1)}, u32[]{:S(2)}, u32[]{:S(2)}) collective-permute-start(bf16[4,128]{1,0:T(4,128)(2,1)S(1)} %convert_element_type.40), channel_id=1, source_target_pairs={{1,0},{2,1},{3,2},{4,3},{5,4},{6,5},{7,6},{8,7},{9,8},{10,9},{11,1... | collective-permute-start | bytes 3080 | tf_op jit(solution)/shard_map/ppermute | solution.py:19
  57.3 6.1 %collective-permute-start.7 = (bf16[4,128]{1,0:T(4,128)(2,1)S(1)}, bf16[4,128]{1,0:T(4,128)(2,1)S(1)}, u32[]{:S(2)}, u32[]{:S(2)}) collective-permute-start(bf16[4,128]{1,0:T(4,128)(2,1)S(1)} %convert_element_type.40), channel_id=1, source_target_pairs={{2,0},{3,1},{4,2},{5,3},{6,4},{7,5},{8,6},{9,7},{10,8},{11,9},{12,... | collective-permute-start | bytes 3080 | tf_op jit(solution)/shard_map/ppermute | solution.py:19
  57.6 5.7 %collective-permute-start.5 = (bf16[4,128]{1,0:T(4,128)(2,1)S(1)}, bf16[4,128]{1,0:T(4,128)(2,1)S(1)}, u32[]{:S(2)}, u32[]{:S(2)}) collective-permute-start(bf16[4,128]{1,0:T(4,128)(2,1)S(1)} %convert_element_type.40), channel_id=1, source_target_pairs={{15,0},{0,1},{1,2},{2,3},{3,4},{4,5},{5,6},{6,7},{7,8},{8,9},{9,10... | collective-permute-start | bytes 3080 | tf_op jit(solution)/shard_map/ppermute | solution.py:19
  63.4 18.0 %copy-start.2 = (f32[65536]{0:T(1024)S(1)}, f32[65536]{0:T(1024)}, u32[]{:S(2)}) copy-start(f32[65536]{0:T(1024)} %param.9) | copy-start | bytes 786436
  93.1 6.5 %collective-permute-start.8 = (f32[4,128]{1,0:T(4,128)S(1)}, f32[4,128]{1,0:T(4,128)S(1)}, u32[]{:S(2)}, u32[]{:S(2)}) collective-permute-start(f32[4,128]{1,0:T(4,128)S(1)} %get-tuple-element.5), channel_id=1, source_target_pairs={{2,0},{3,1},{4,2},{5,3},{6,4},{7,5},{8,6},{9,7},{10,8},{11,9},{12,... | collective-permute-start | bytes 6152 | tf_op jit(solution)/shard_map/ppermute | solution.py:19
  93.6 6.3 %collective-permute-start.11 = (f32[4,128]{1,0:T(4,128)S(1)}, f32[4,128]{1,0:T(4,128)S(1)}, u32[]{:S(2)}, u32[]{:S(2)}) collective-permute-start(f32[4,128]{1,0:T(4,128)S(1)} %get-tuple-element.6), channel_id=1, source_target_pairs={{14,0},{15,1},{0,2},{1,3},{2,4},{3,5},{4,6},{5,7},{6,8},{7,9},{8,1... | collective-permute-start | bytes 6152 | tf_op jit(solution)/shard_map/ppermute | solution.py:19
  95.2 5.7 %collective-permute-start.10 = (f32[4,128]{1,0:T(4,128)S(1)}, f32[4,128]{1,0:T(4,128)S(1)}, u32[]{:S(2)}, u32[]{:S(2)}) collective-permute-start(f32[4,128]{1,0:T(4,128)S(1)} %get-tuple-element.7), channel_id=1, source_target_pairs={{15,0},{0,1},{1,2},{2,3},{3,4},{4,5},{5,6},{6,7},{7,8},{8,9},{9,10... | collective-permute-start | bytes 6152 | tf_op jit(solution)/shard_map/ppermute | solution.py:19
  95.2 5.7 %collective-permute-start.9 = (f32[4,128]{1,0:T(4,128)S(1)}, f32[4,128]{1,0:T(4,128)S(1)}, u32[]{:S(2)}, u32[]{:S(2)}) collective-permute-start(f32[4,128]{1,0:T(4,128)S(1)} %get-tuple-element.8), channel_id=1, source_target_pairs={{1,0},{2,1},{3,2},{4,3},{5,4},{6,5},{7,6},{8,7},{9,8},{10,9},{11,1... | collective-permute-start | bytes 6152 | tf_op jit(solution)/shard_map/ppermute | solution.py:19
  124.7 6.3 %collective-permute-start.12 = (bf16[4,128]{1,0:T(4,128)(2,1)S(1)}, bf16[4,128]{1,0:T(4,128)(2,1)S(1)}, u32[]{:S(2)}, u32[]{:S(2)}) collective-permute-start(bf16[4,128]{1,0:T(4,128)(2,1)S(1)} %convert_element_type.45), channel_id=1, source_target_pairs={{14,0},{15,1},{0,2},{1,3},{2,4},{3,5},{4,6},{5,7},{6,8},{7,9},{8,1... | collective-permute-start | bytes 3080 | tf_op jit(solution)/shard_map/ppermute | solution.py:19
  126.0 9.2 %collective-permute-start.14 = (bf16[4,128]{1,0:T(4,128)(2,1)S(1)}, bf16[4,128]{1,0:T(4,128)(2,1)S(1)}, u32[]{:S(2)}, u32[]{:S(2)}) collective-permute-start(bf16[4,128]{1,0:T(4,128)(2,1)S(1)} %convert_element_type.45), channel_id=1, source_target_pairs={{1,0},{2,1},{3,2},{4,3},{5,4},{6,5},{7,6},{8,7},{9,8},{10,9},{11,1... | collective-permute-start | bytes 3080 | tf_op jit(solution)/shard_map/ppermute | solution.py:19
  129.0 6.2 %collective-permute-start.15 = (bf16[4,128]{1,0:T(4,128)(2,1)S(1)}, bf16[4,128]{1,0:T(4,128)(2,1)S(1)}, u32[]{:S(2)}, u32[]{:S(2)}) collective-permute-start(bf16[4,128]{1,0:T(4,128)(2,1)S(1)} %convert_element_type.45), channel_id=1, source_target_pairs={{2,0},{3,1},{4,2},{5,3},{6,4},{7,5},{8,6},{9,7},{10,8},{11,9},{12,... | collective-permute-start | bytes 3080 | tf_op jit(solution)/shard_map/ppermute | solution.py:19
  129.5 5.7 %collective-permute-start.13 = (bf16[4,128]{1,0:T(4,128)(2,1)S(1)}, bf16[4,128]{1,0:T(4,128)(2,1)S(1)}, u32[]{:S(2)}, u32[]{:S(2)}) collective-permute-start(bf16[4,128]{1,0:T(4,128)(2,1)S(1)} %convert_element_type.45), channel_id=1, source_target_pairs={{15,0},{0,1},{1,2},{2,3},{3,4},{4,5},{5,6},{6,7},{7,8},{8,9},{9,10... | collective-permute-start | bytes 3080 | tf_op jit(solution)/shard_map/ppermute | solution.py:19
where the time goes:
time: 154 us
  matrix products  75.4 us (49%)
  blocking collectives  36.5 us (24%)
  starting transfers between devices  27 us (18%)
  waiting for transfers between devices  13.7 us (9%)
    all_gather x2, blocking collectives, kernel_apply(): lax.all_gather((owned * norm).astype(jnp.bfloat16), 'dev', axis=0, tiled=...  36.5 us
    dot_general x2, matrix products, kernel_apply(): jnp.dot(onehot, everywhere, preferred_element_type=jnp.float32)  35.9 us
    ppermute x16, starting transfers between devices, from_behind(): return lax.ppermute(block, axis, route)  27 us
    dot_general x2, matrix products, kernel_apply(): lax.dot_general(onehot * weights[:, None], basis_rows, (((0,), (0,)), (()...  22.1 us
    ppermute x16, waiting for transfers between devices, from_behind(): return lax.ppermute(block, axis, route)  13.7 us
    dot_general x2, matrix products, kernel_apply(): jnp.einsum('kpij,kpj->ki', link_blocks, gathered, preferred_element_type=...  11.3 us
    dot_general x1, matrix products, shards(): jnp.dot(cluster_hits, permuter, preferred_element_type=jnp.float32)  5.44 us
  transfers between devices with their start and end apart: 16, of which 7 were waited for; matrix products, arithmetic and copies ran while one was open for 0% of the time, Pallas kernels for 0%

commit v1 on v0

v1 whole, which is shorter than its diff:
```python
import functools
import math

import jax
import jax.numpy as jnp
from jax import lax
from jax.experimental import pallas as pl
from jax.experimental.pallas import tpu as pltpu
from jax.sharding import PartitionSpec as P

REACH = 2
NEAR = 2 * REACH + 1
CL_DEV = 4
S_DEV = 65536
LANES = 128
ROWS = 32

TILE = 4096
PIECE = 1024
LINKS = 32

ridge = 0.5


def near_clusters(devices, per_dev, slot_of_ref, cl_ref):
    clusters = devices * per_dev
    me = lax.axis_index("dev")
    near = lax.broadcasted_iota(jnp.int32, (ROWS, clusters), 0)
    slots = (me + devices - REACH) * per_dev + near
    slots = lax.rem(slots, clusters)
    number = lax.broadcasted_iota(jnp.int32, (ROWS, clusters), 1)
    hit = (slot_of_ref[...] == slots) & (near < NEAR * per_dev)
    found = jnp.sum(jnp.where(hit, number + 1, 0), axis=1, keepdims=True) - 1
    cl_ref[...] = jnp.broadcast_to(found, cl_ref.shape)


def spread_near(devices, per_dev, sums, out_ref):
    me = lax.axis_index("dev")
    out_ref[...] = jnp.zeros_like(out_ref)
    for g in range(NEAR):
        owner = lax.rem(me + devices + g - REACH, devices)
        out_ref[owner] = sums[g * per_dev : (g + 1) * per_dev]


def near_rows(devices, per_dev, mixed_ref, rows_ref):
    me = lax.axis_index("dev")
    rows_ref[...] = jnp.zeros_like(rows_ref)
    for g in range(NEAR):
        owner = lax.rem(me + devices + g - REACH, devices)
        rows_ref[g * per_dev : (g + 1) * per_dev, :] = mixed_ref[owner].astype(jnp.float32)


def coef_kernel(devices, per_dev, slot_of_ref, assign_ref, x_ref, basis_ref, out_ref, cl_ref, sum_ref, xf_ref):
    step = pl.program_id(0)

    @pl.when(step == 0)
    def _():
        near_clusters(devices, per_dev, slot_of_ref, cl_ref)
        sum_ref[...] = jnp.zeros_like(sum_ref)

    xf_ref[...] = x_ref[...].astype(jnp.float32)
    cl = cl_ref[...]
    total = sum_ref[...]
    for p in range(TILE // PIECE):
        parts = []
        for r in range(p * PIECE // LANES, (p + 1) * PIECE // LANES):
            hit = assign_ref[r : r + 1, :] == cl
            parts.append(jnp.where(hit, xf_ref[r : r + 1, :], 0.0).astype(jnp.bfloat16))
        left = jnp.concatenate(parts, axis=1)
        total += jnp.dot(left, basis_ref[p * PIECE : (p + 1) * PIECE, :], preferred_element_type=jnp.float32)
    sum_ref[...] = total

    @pl.when(step == pl.num_programs(0) - 1)
    def _():
        spread_near(devices, per_dev, sum_ref[...], out_ref)


def link_kernel(norm, slot_of_ref, partners_ref, coef_ref, links_ref, out_ref, scaled_ref, acc_ref, mixed_ref):
    j = pl.program_id(0)
    part = pl.program_id(1)

    @pl.when((j == 0) & (part == 0))
    def _():
        scaled_ref[...] = (coef_ref[...] * norm).astype(jnp.bfloat16).astype(jnp.float32)
        mixed_ref[...] = jnp.zeros_like(mixed_ref)

    @pl.when(part == 0)
    def _():
        acc_ref[...] = jnp.zeros_like(acc_ref)

    def body(k, acc):
        s = slot_of_ref[partners_ref[j, part * LINKS + k]]
        return acc + links_ref[0, k].astype(jnp.float32) * scaled_ref[pl.ds(s, 1), :]

    acc_ref[...] = lax.fori_loop(0, LINKS, body, acc_ref[...], unroll=8)

    @pl.when(part == pl.num_programs(1) - 1)
    def _():
        mixed_ref[pl.ds(j, 1), :] = jnp.sum(acc_ref[...].T, axis=0, keepdims=True)

    @pl.when((part == pl.num_programs(1) - 1) & (j == pl.num_programs(0) - 1))
    def _():
        out_ref[...] = mixed_ref[: out_ref.shape[0], :].astype(jnp.bfloat16)


def rows_times(rows, piece):
    return lax.dot_general(rows, piece, (((1,), (1,)), ((), ())), preferred_element_type=jnp.float32)


def both_kernel(
    devices, per_dev, slot_of_ref, mixed_ref, assign_ref, scores_ref, basis_ref,
    first_ref, out_ref, cl_ref, rows_ref, sum_ref, slope_ref,
):
    step = pl.program_id(0)

    @pl.when(step == 0)
    def _():
        near_clusters(devices, per_dev, slot_of_ref, cl_ref)
        near_rows(devices, per_dev, mixed_ref, rows_ref)
        sum_ref[...] = jnp.zeros_like(sum_ref)

    sig = jax.nn.sigmoid(scores_ref[...])
    slope_ref[...] = sig * (1.0 - sig)
    cl = cl_ref[...]
    rows = rows_ref[...].astype(jnp.bfloat16)
    total = sum_ref[...]
    for p in range(TILE // PIECE):
        piece = basis_ref[p * PIECE : (p + 1) * PIECE, :]
        products = rows_times(rows, piece)
        parts = []
        for i in range(PIECE // LANES):
            r = p * PIECE // LANES + i
            hit = assign_ref[r : r + 1, :] == cl
            first = jnp.sum(jnp.where(hit, products[:, i * LANES : (i + 1) * LANES], 0.0), axis=0, keepdims=True)
            first_ref[r : r + 1, :] = first
            weighted = slope_ref[r : r + 1, :] * first
            parts.append(jnp.where(hit, weighted, 0.0).astype(jnp.bfloat16))
        left = jnp.concatenate(parts, axis=1)
        total += jnp.dot(left, piece, preferred_element_type=jnp.float32)
    sum_ref[...] = total

    @pl.when(step == pl.num_programs(0) - 1)
    def _():
        spread_near(devices, per_dev, sum_ref[...], out_ref)


def last_kernel(
    devices, per_dev, slot_of_ref, mixed_ref, assign_ref, first_ref, basis_ref, out_ref, cl_ref, rows_ref
):
    step = pl.program_id(0)

    @pl.when(step == 0)
    def _():
        near_clusters(devices, per_dev, slot_of_ref, cl_ref)
        near_rows(devices, per_dev, mixed_ref, rows_ref)

    cl = cl_ref[...]
    rows = rows_ref[...].astype(jnp.bfloat16)
    for p in range(TILE // PIECE):
        products = rows_times(rows, basis_ref[p * PIECE : (p + 1) * PIECE, :])
        for i in range(PIECE // LANES):
            r = p * PIECE // LANES + i
            hit = assign_ref[r : r + 1, :] == cl
            second = jnp.sum(jnp.where(hit, products[:, i * LANES : (i + 1) * LANES], 0.0), axis=0, keepdims=True)
            out_ref[r : r + 1, :] = second + ridge * first_ref[r : r + 1, :]


def shards(basis_rows, vector, scores, assign, slot_of, partners, link_blocks):
    devices = lax.axis_size("dev")
    clusters = slot_of.shape[0]
    per_dev, n_links, rank, _ = link_blocks.shape
    samples = assign.shape[0]
    norm = 1.0 / math.sqrt(S_DEV // CL_DEV)
    steps = samples // TILE
    high = TILE // LANES
    f32 = jnp.float32

    vector = vector.reshape(samples // LANES, LANES)
    scores = scores.reshape(samples // LANES, LANES)
    assign = assign.reshape(samples // LANES, LANES)
    slot_row = slot_of.reshape(1, clusters)

    whole = lambda *shape: pl.BlockSpec(shape, lambda i: (0,) * len(shape))
    tile = pl.BlockSpec((high, LANES), lambda i: (i, 0))
    basis_tile = pl.BlockSpec((TILE, rank), lambda i: (i, 0))
    coef_shape = jax.ShapeDtypeStruct((devices, per_dev, rank), f32)
    coef_spec = whole(devices, per_dev, rank)
    row_shape = jax.ShapeDtypeStruct((samples // LANES, LANES), f32)
    params = pltpu.CompilerParams(vmem_limit_bytes=32 * 1024 * 1024)

    coef1 = pl.pallas_call(
        functools.partial(coef_kernel, devices, per_dev),
        grid=(steps,),
        in_specs=[whole(1, clusters), tile, tile, basis_tile],
        out_specs=coef_spec,
        out_shape=coef_shape,
        scratch_shapes=[
            pltpu.VMEM((ROWS, LANES), jnp.int32),
            pltpu.VMEM((ROWS, rank), f32),
            pltpu.VMEM((high, LANES), f32),
        ],
        compiler_params=params,
        name="coef_pass",
    )(slot_row, assign, vector, basis_rows)

    def mix(coef):
        coef = lax.psum(coef, "dev").reshape(clusters, rank)
        mixed = pl.pallas_call(
            functools.partial(link_kernel, norm),
            grid_spec=pltpu.PrefetchScalarGridSpec(
                num_scalar_prefetch=2,
                grid=(per_dev, n_links // LINKS),
                in_specs=[
                    pl.BlockSpec((clusters, rank), lambda j, p, *_: (0, 0)),
                    pl.BlockSpec((1, LINKS, rank, rank), lambda j, p, *_: (j, p, 0, 0)),
                ],
                out_specs=pl.BlockSpec((per_dev, rank), lambda j, p, *_: (0, 0)),
                scratch_shapes=[
                    pltpu.VMEM((clusters, rank), f32),
                    pltpu.VMEM((rank, rank), f32),
                    pltpu.VMEM((8, rank), f32),
                ],
            ),
            out_shape=jax.ShapeDtypeStruct((per_dev, rank), jnp.bfloat16),
            compiler_params=params,
            name="link_product",
        )(slot_of, partners, coef, link_blocks)
        copies = jnp.broadcast_to(mixed[None], (devices, per_dev, rank))
        return lax.all_to_all(copies, "dev", 0, 0, tiled=True)

    first, coef2 = pl.pallas_call(
        functools.partial(both_kernel, devices, per_dev),
        grid=(steps,),
        in_specs=[whole(1, clusters), coef_spec, tile, tile, basis_tile],
        out_specs=[tile, coef_spec],
        out_shape=[row_shape, coef_shape],
        scratch_shapes=[
            pltpu.VMEM((ROWS, LANES), jnp.int32),
            pltpu.VMEM((ROWS, rank), f32),
            pltpu.VMEM((ROWS, rank), f32),
            pltpu.VMEM((high, LANES), f32),
        ],
        compiler_params=params,
        name="first_and_coef_pass",
    )(slot_row, mix(coef1), assign, scores, basis_rows)

    out = pl.pallas_call(
        functools.partial(last_kernel, devices, per_dev),
        grid=(steps,),
        in_specs=[whole(1, clusters), coef_spec, tile, tile, basis_tile],
        out_specs=tile,
        out_shape=row_shape,
        scratch_shapes=[
            pltpu.VMEM((ROWS, LANES), jnp.int32),
            pltpu.VMEM((ROWS, rank), f32),
        ],
        compiler_params=params,
        name="last_pass",
    )(slot_row, mix(coef2), assign, first, basis_rows)
    return out.reshape(samples)


def solution(mesh):
    in_specs = (
        P(("groups", "dev"), None),
        P(("groups", "dev")),
        P(("groups", "dev")),
        P(("groups", "dev")),
        P("groups"),
        P(("groups", "dev"), None),
        P(("groups", "dev"), None, None, None),
    )
    out_specs = P(("groups", "dev"))
    return jax.shard_map(shards, mesh=mesh, in_specs=in_specs, out_specs=out_specs, check_vma=False)
```

time: 154 us -> 202 us (1.31)
  blocking collectives: 36.5 us -> 139 us
  matrix products: 75.4 us -> 0 us
  Pallas kernels: 0 us -> 36.5 us
  starting transfers between devices: 27 us -> 0 us
  local copies, waits for them, and re-layouts: 0.22 us -> 26.6 us
  waiting for transfers between devices: 13.7 us -> 0 us
    psum x0 -> x2, blocking collectives: none -> 121 us  [mix(): coef = lax.psum(coef, 'dev').reshape(clusters, rank)]
    dot_general x10 -> x0, matrix products: 75.4 us -> none  [the longest x2 35.9 us: kernel_apply(): jnp.dot(onehot, everywhere, preferred_element_type=jnp.float32)]
    all_gather x2 -> x0, blocking collectives: 36.5 us -> none  [kernel_apply(): lax.all_gather((owned * norm).astype(jnp.bfloat16), 'dev', axis=0, tiled=...]
    pallas_call x0 -> x5, Pallas kernels: none -> 36.5 us  [the longest x1 16 us: shards(): pl.pallas_call(functools.partial(both_kernel, devices, per_dev), grid=(st...]
    ppermute x16 -> x0, starting transfers between devices: 27 us -> none  [from_behind(): return lax.ppermute(block, axis, route)]
    unnamed x10 -> x24, local copies, waits for them, and re-layouts: 0.03 us -> 26.6 us
    all_to_all x0 -> x2, blocking collectives: none -> 18.1 us  [mix(): return lax.all_to_all(copies, 'dev', 0, 0, tiled=True)]
    ppermute x16 -> x0, waiting for transfers between devices: 13.7 us -> none  [from_behind(): return lax.ppermute(block, axis, route)]
  transfers between devices with their start and end apart: 16 -> 0, of which waited for: 7 -> 0; matrix products, arithmetic and copies ran while one was open for 0% -> 0% of each run, Pallas kernels for 0% -> 0%
where the time goes in v1:
time: 202 us
  blocking collectives  139 us (69%)
  Pallas kernels  36.5 us (18%)
  local copies, waits for them, and re-layouts  26.6 us (13%)
    psum x2, blocking collectives, mix(): coef = lax.psum(coef, 'dev').reshape(clusters, rank)  121 us
    unnamed x24, local copies, waits for them, and re-layouts  26.6 us
    all_to_all x2, blocking collectives, mix(): return lax.all_to_all(copies, 'dev', 0, 0, tiled=True)  18.1 us
    pallas_call x1, Pallas kernels, shards(): pl.pallas_call(functools.partial(both_kernel, devices, per_dev), grid=(st...  16 us
    pallas_call x1, Pallas kernels, shards(): pl.pallas_call(functools.partial(last_kernel, devices, per_dev), grid=(st...  9.19 us
    pallas_call x2, Pallas kernels, mix(): pl.pallas_call(functools.partial(link_kernel, norm), grid_spec=pltpu.Pref...  6.41 us
    pallas_call x1, Pallas kernels, shards(): pl.pallas_call(functools.partial(coef_kernel, devices, per_dev), grid=(st...  4.92 us

profile of v1, /device:TPU:0, one launch (start us, length us, event | category | flops | bytes accessed | tf_op | source)
XLA Modules:
  0.0 201.9 jit_solution(11677533118642954736)
XLA Ops:
  0.0 0.0 copy-start.10
  0.0 0.0 copy-start.11
  0.0 0.0 copy-start
  0.0 5.8 %copy-done = bf16[65536,128]{1,0:T(8,128)(2,1)S(1)} copy-done((bf16[65536,128]{1,0:T(8,128)(2,1)S(1)}, bf16[65536,128]{1,0:T(8,128)(2,1)}, u32[]{:S(2)}) %copy-start) | copy-done | bytes 16777240
  5.8 0.9 copy-done.5
  6.8 0.9 copy-done.8
  7.7 0.7 copy-done.9
  8.3 4.9 %coef_pass.1 = f32[16,4,128]{2,1,0:T(4,128)S(1)} custom-call(s32[1,64]{1,0:T(1,128)S(1)} %bitcast.14, s32[512,128]{1,0:T(8,128)S(1)} %bitcast.7, bf16[512,128]{1,0:T(8,128)(2,1)S(1)} %bitcast.11, bf16[65536,128]{1,0:T(8,128)(2,1)S(1)} %copy-done), custom_call_target="tpu_custom_call" | custom-call | tf_op jit(solution)/shard_map/coef_pass/pallas_call | solution.py:191
  13.2 63.0 %psum.14.coef_ref = f32[64,128]{1,0:T(8,128)S(1)} all-reduce(f32[64,128]{1,0:T(8,128)S(1)} %bitcast.12), channel_id=1, replica_groups=mesh['groups'=2,'dev'=16] {'dev'}, use_global_device_ids=true, to_apply=%region_0.0 | all-reduce | flops 8192 | bytes 65536 | tf_op jit(solution)/shard_map/psum | solution.py:207
  76.2 0.0 copy-done.10
  76.2 0.0 copy-done.11
  76.2 3.4 %copy-done.3 = bf16[4,64,128,128]{3,2,1,0:T(8,128)(2,1)S(1)} copy-done((bf16[4,64,128,128]{3,2,1,0:T(8,128)(2,1)S(1)}, bf16[4,64,128,128]{3,2,1,0:T(8,128)(2,1)}, u32[]{:S(2)}) %copy-start.3) | copy-done | bytes 8388632
  79.6 3.2 %link_product.2 = bf16[4,128]{1,0:T(4,128)(2,1)S(1)} custom-call(s32[64]{0:T(128)S(1)} %copy-done.10, s32[4,64]{1,0:T(4,128)S(1)} %copy-done.11, f32[64,128]{1,0:T(8,128)S(1)} %psum.14.coef_ref, bf16[4,64,128,128]{3,2,1,0:T(8,128)(2,1)S(1)} %copy-done.3), custom_call_target="tpu_custom_call" | custom-call | tf_op jit(solution)/shard_map/link_product/pallas_call | solution.py:208
  82.8 9.1 %all_to_all.10.mixed_ref = bf16[16,4,128]{2,1,0:T(4,128)(2,1)S(1)} all-to-all(bf16[16,4,128]{2,1,0:T(4,128)(2,1)S(1)} %broadcast_in_dim.4), channel_id=1, replica_groups=mesh['groups'=2,'dev'=16] {'dev'}, dimensions={0} | all-to-all | bytes 32768 | tf_op jit(solution)/shard_map/all_to_all | solution.py:229
  91.9 0.0 copy-done.6
  91.9 0.0 copy-done.7
  91.9 5.8 %copy-done.1 = bf16[65536,128]{1,0:T(8,128)(2,1)S(1)} copy-done((bf16[65536,128]{1,0:T(8,128)(2,1)S(1)}, bf16[65536,128]{1,0:T(8,128)(2,1)}, u32[]{:S(2)}) %copy-start.1) | copy-done | bytes 16777240
  97.7 16.0 %first_and_coef_pass.1 = (f32[512,128]{1,0:T(8,128)S(1)}, f32[16,4,128]{2,1,0:T(4,128)S(1)}) custom-call(s32[1,64]{1,0:T(1,128)S(1)} %bitcast.15, bf16[16,4,128]{2,1,0:T(4,128)(2,1)S(1)} %all_to_all.10.mixed_ref, s32[512,128]{1,0:T(8,128)S(1)} %bitcast.8, f32[512,128]{1,0:T(8,128)S(1)} %bitcast.10, bf16[65536,128]{1,0:T(8,128)(2,1)S(1)} %copy-done.1), custom_call_target="tpu_custom_call" | custom-call | tf_op jit(solution)/shard_map/first_and_coef_pass/pallas_call | solution.py:231
  113.6 57.7 %psum.15.coef_ref = f32[64,128]{1,0:T(8,128)S(1)} all-reduce(f32[64,128]{1,0:T(8,128)S(1)} %bitcast.13), channel_id=1, replica_groups=mesh['groups'=2,'dev'=16] {'dev'}, use_global_device_ids=true, to_apply=%region_1.0 | all-reduce | flops 8192 | bytes 65536 | tf_op jit(solution)/shard_map/psum | solution.py:207
  171.3 3.4 %copy-done.4 = bf16[4,64,128,128]{3,2,1,0:T(8,128)(2,1)S(1)} copy-done((bf16[4,64,128,128]{3,2,1,0:T(8,128)(2,1)S(1)}, bf16[4,64,128,128]{3,2,1,0:T(8,128)(2,1)}, u32[]{:S(2)}) %copy-start.4) | copy-done | bytes 8388632
  174.7 3.2 %link_product.3 = bf16[4,128]{1,0:T(4,128)(2,1)S(1)} custom-call(s32[64]{0:T(128)S(1)} %copy-done.10, s32[4,64]{1,0:T(4,128)S(1)} %copy-done.11, f32[64,128]{1,0:T(8,128)S(1)} %psum.15.coef_ref, bf16[4,64,128,128]{3,2,1,0:T(8,128)(2,1)S(1)} %copy-done.4), custom_call_target="tpu_custom_call" | custom-call | tf_op jit(solution)/shard_map/link_product/pallas_call | solution.py:208
  177.9 9.1 %all_to_all.11.mixed_ref = bf16[16,4,128]{2,1,0:T(4,128)(2,1)S(1)} all-to-all(bf16[16,4,128]{2,1,0:T(4,128)(2,1)S(1)} %broadcast_in_dim.5), channel_id=1, replica_groups=mesh['groups'=2,'dev'=16] {'dev'}, dimensions={0} | all-to-all | bytes 32768 | tf_op jit(solution)/shard_map/all_to_all | solution.py:229
  187.0 5.8 %copy-done.2 = bf16[65536,128]{1,0:T(8,128)(2,1)S(1)} copy-done((bf16[65536,128]{1,0:T(8,128)(2,1)S(1)}, bf16[65536,128]{1,0:T(8,128)(2,1)}, u32[]{:S(2)}) %copy-start.2) | copy-done | bytes 16777240
  192.8 9.2 %last_pass.1 = f32[512,128]{1,0:T(8,128)} custom-call(s32[1,64]{1,0:T(1,128)S(1)} %bitcast.16, bf16[16,4,128]{2,1,0:T(4,128)(2,1)S(1)} %all_to_all.11.mixed_ref, s32[512,128]{1,0:T(8,128)S(1)} %bitcast.9, f32[512,128]{1,0:T(8,128)S(1)} %get-tuple-element.8.first_ref, bf16[65536,128]{1,0:T(8,128)(2,1)S(1)} %copy-done.2), custom_call_target="tpu_custom_call" | custom-call | tf_op jit(solution)/shard_map/last_pass/pallas_call | solution.py:247
  (11 shorter events, 0.0 us)
Async XLA Ops:
  0.0 76.2 %copy-start.10 = (s32[64]{0:T(128)S(1)}, s32[64]{0:T(128)}, u32[]{:S(2)}) copy-start(s32[64]{0:T(128)} %slot_of_ref.3) | copy-start | bytes 772
  0.0 76.2 %copy-start.11 = (s32[4,64]{1,0:T(4,128)S(1)}, s32[4,64]{1,0:T(4,128)}, u32[]{:S(2)}) copy-start(s32[4,64]{1,0:T(4,128)} %partners_ref.3) | copy-start | bytes 3076
  0.0 5.8 %copy-start = (bf16[65536,128]{1,0:T(8,128)(2,1)S(1)}, bf16[65536,128]{1,0:T(8,128)(2,1)}, u32[]{:S(2)}) copy-start(bf16[65536,128]{1,0:T(8,128)(2,1)} %basis_ref.5) | copy-start | bytes 50331652
  5.8 0.9 copy-start.5
  6.8 0.9 copy-start.8
  7.7 0.7 copy-start.9
  8.3 83.6 %copy-start.6 = (s32[65536]{0:T(1024)S(1)}, s32[65536]{0:T(1024)}, u32[]{:S(2)}) copy-start(s32[65536]{0:T(1024)} %param.10) | copy-start | bytes 786436
  8.3 83.6 %copy-start.7 = (f32[65536]{0:T(1024)S(1)}, f32[65536]{0:T(1024)}, u32[]{:S(2)}) copy-start(f32[65536]{0:T(1024)} %param.9) | copy-start | bytes 786436
  76.2 3.4 %copy-start.3 = (bf16[4,64,128,128]{3,2,1,0:T(8,128)(2,1)S(1)}, bf16[4,64,128,128]{3,2,1,0:T(8,128)(2,1)}, u32[]{:S(2)}) copy-start(bf16[4,64,128,128]{3,2,1,0:T(8,128)(2,1)} %links_ref.3) | copy-start | bytes 25165828
  91.9 5.8 %copy-start.1 = (bf16[65536,128]{1,0:T(8,128)(2,1)S(1)}, bf16[65536,128]{1,0:T(8,128)(2,1)}, u32[]{:S(2)}) copy-start(bf16[65536,128]{1,0:T(8,128)(2,1)} %basis_ref.5) | copy-start | bytes 50331652
  171.3 3.4 %copy-start.4 = (bf16[4,64,128,128]{3,2,1,0:T(8,128)(2,1)S(1)}, bf16[4,64,128,128]{3,2,1,0:T(8,128)(2,1)}, u32[]{:S(2)}) copy-start(bf16[4,64,128,128]{3,2,1,0:T(8,128)(2,1)} %links_ref.3) | copy-start | bytes 25165828
  187.0 5.8 %copy-start.2 = (bf16[65536,128]{1,0:T(8,128)(2,1)S(1)}, bf16[65536,128]{1,0:T(8,128)(2,1)}, u32[]{:S(2)}) copy-start(bf16[65536,128]{1,0:T(8,128)(2,1)} %basis_ref.5) | copy-start | bytes 50331652

commit v2 on v0

v2 whole, which is shorter than its diff:
```python
import functools
import math

import jax
import jax.numpy as jnp
from jax import lax
from jax.experimental import pallas as pl
from jax.experimental.pallas import tpu as pltpu
from jax.sharding import PartitionSpec as P

REACH = 2
NEAR = 2 * REACH + 1
CL_DEV = 4
S_DEV = 65536
LANES = 128
ROWS = 32

TILE = 4096
PIECE = 1024
SLOTS = 4

ridge = 0.5


def near_clusters(devices, per_dev, slot_of_ref, cl_ref):
    clusters = devices * per_dev
    me = lax.axis_index("dev")
    near = lax.broadcasted_iota(jnp.int32, (ROWS, clusters), 0)
    slots = (me + devices - REACH) * per_dev + near
    slots = lax.rem(slots, clusters)
    number = lax.broadcasted_iota(jnp.int32, (ROWS, clusters), 1)
    hit = (slot_of_ref[...] == slots) & (near < NEAR * per_dev)
    found = jnp.sum(jnp.where(hit, number + 1, 0), axis=1, keepdims=True) - 1
    cl_ref[...] = jnp.broadcast_to(found, cl_ref.shape)


def near_rows(devices, per_dev, mixed_ref, rows_ref):
    me = lax.axis_index("dev")
    rows_ref[...] = jnp.zeros_like(rows_ref)
    for g in range(NEAR):
        owner = lax.rem(me + devices + g - REACH, devices)
        rows_ref[g * per_dev : (g + 1) * per_dev, :] = mixed_ref[owner].astype(jnp.float32)


def tile_copy(basis_hbm, slots_ref, sem, t):
    slot = lax.rem(t, SLOTS)
    rows = pl.ds(pl.multiple_of(t * TILE, TILE), TILE)
    return pltpu.make_async_copy(basis_hbm.at[rows, :], slots_ref.at[slot], sem.at[slot])


def coef_kernel(
    devices, per_dev, slot_of_ref, assign_hbm, vector_hbm, basis_hbm, links_hbm,
    out_ref, turned_ref, assign_ref, links_ref,
    cl_ref, sum_ref, vector_ref, x_ref, slots_ref, small_sem, basis_sem, links_sem,
):
    tiles = basis_hbm.shape[0] // TILE
    high = TILE // LANES

    def basis_copy(t):
        return tile_copy(basis_hbm, slots_ref, basis_sem, t)

    assign_copy = pltpu.make_async_copy(assign_hbm, assign_ref, small_sem.at[0])
    vector_copy = pltpu.make_async_copy(vector_hbm, vector_ref, small_sem.at[1])
    links_copy = pltpu.make_async_copy(links_hbm, links_ref, links_sem)
    assign_copy.start()
    vector_copy.start()
    for t in range(SLOTS):
        basis_copy(t).start()
    near_clusters(devices, per_dev, slot_of_ref, cl_ref)
    sum_ref[...] = jnp.zeros_like(sum_ref)
    assign_copy.wait()
    vector_copy.wait()
    x_ref[...] = vector_ref[...].astype(jnp.float32)
    cl = cl_ref[...]

    @pl.loop(0, tiles)
    def _(t):
        basis_copy(t).wait()
        total = sum_ref[...]
        for p in range(TILE // PIECE):
            parts = []
            for i in range(PIECE // LANES):
                r = pl.ds(t * high + p * (PIECE // LANES) + i, 1)
                hit = assign_ref[r, :] == cl
                parts.append(jnp.where(hit, x_ref[r, :], 0.0).astype(jnp.bfloat16))
            left = jnp.concatenate(parts, axis=1)
            at = pl.ds(pl.multiple_of(t * TILE + p * PIECE, PIECE), PIECE)
            piece = slots_ref[lax.rem(t, SLOTS), p * PIECE : (p + 1) * PIECE, :]
            turned_ref[:, at] = piece.T
            total += jnp.dot(left, piece, preferred_element_type=jnp.float32)
        sum_ref[...] = total

        @pl.when(t + SLOTS < tiles)
        def _():
            basis_copy(t + SLOTS).start()

        @pl.when(t + SLOTS == tiles)
        def _():
            links_copy.start()

    out_ref[...] = sum_ref[: NEAR * per_dev, :]
    links_copy.wait()


def link_kernel(norm, devices, per_dev, slot_of_ref, partners_ref, parts_ref, links_ref, out_ref, scaled_ref, mixed_ref):
    for owner in range(devices):
        coef = parts_ref[(owner + REACH) % devices, :per_dev, :]
        for g in range(1, NEAR):
            coef += parts_ref[(owner + REACH - g) % devices, g * per_dev : (g + 1) * per_dev, :]
        scaled_ref[owner * per_dev : (owner + 1) * per_dev, :] = (coef * norm).astype(jnp.bfloat16).astype(jnp.float32)
    mixed_ref[...] = jnp.zeros_like(mixed_ref)
    n_links = links_ref.shape[1]
    for j in range(per_dev):
        def body(k, acc):
            s = slot_of_ref[partners_ref[j, k]]
            return acc + links_ref[j, k].astype(jnp.float32) * scaled_ref[pl.ds(s, 1), :]

        acc = lax.fori_loop(0, n_links, body, jnp.zeros(links_ref.shape[2:], jnp.float32), unroll=8)
        mixed_ref[j : j + 1, :] = jnp.sum(acc.T, axis=0, keepdims=True)
    out_ref[...] = mixed_ref[:per_dev, :].astype(jnp.bfloat16)


def both_kernel(
    devices, per_dev, slot_of_ref, mixed_ref, assign_ref, scores_ref, turned_ref, basis_hbm,
    first_ref, out_ref, cl_ref, rows_ref, sum_ref, slope_ref, slots_ref, basis_sem,
):
    tiles = basis_hbm.shape[0] // TILE

    def basis_copy(t):
        return tile_copy(basis_hbm, slots_ref, basis_sem, t)

    for t in range(SLOTS):
        basis_copy(t).start()
    near_clusters(devices, per_dev, slot_of_ref, cl_ref)
    near_rows(devices, per_dev, mixed_ref, rows_ref)
    sum_ref[...] = jnp.zeros_like(sum_ref)
    sig = jax.nn.sigmoid(scores_ref[...])
    slope_ref[...] = sig * (1.0 - sig)
    cl = cl_ref[...]
    rows = rows_ref[...].astype(jnp.bfloat16)

    @pl.loop(0, tiles)
    def _(t):
        basis_copy(t).wait()
        total = sum_ref[...]
        for p in range(TILE // PIECE):
            at = pl.ds(pl.multiple_of(t * TILE + p * PIECE, PIECE), PIECE)
            products = jnp.dot(rows, turned_ref[:, at], preferred_element_type=jnp.float32)
            parts = []
            for i in range(PIECE // LANES):
                r = pl.ds((t * TILE + p * PIECE) // LANES + i, 1)
                hit = assign_ref[r, :] == cl
                first = jnp.sum(jnp.where(hit, products[:, i * LANES : (i + 1) * LANES], 0.0), axis=0, keepdims=True)
                first_ref[r, :] = first
                weighted = slope_ref[r, :] * first
                parts.append(jnp.where(hit, weighted, 0.0).astype(jnp.bfloat16))
            left = jnp.concatenate(parts, axis=1)
            piece = slots_ref[lax.rem(t, SLOTS), p * PIECE : (p + 1) * PIECE, :]
            total += jnp.dot(left, piece, preferred_element_type=jnp.float32)
        sum_ref[...] = total

        @pl.when(t + SLOTS < tiles)
        def _():
            basis_copy(t + SLOTS).start()

    out_ref[...] = sum_ref[: NEAR * per_dev, :]


def last_kernel(devices, per_dev, slot_of_ref, mixed_ref, assign_ref, first_ref, turned_ref, out_ref, cl_ref, rows_ref):
    near_clusters(devices, per_dev, slot_of_ref, cl_ref)
    near_rows(devices, per_dev, mixed_ref, rows_ref)
    cl = cl_ref[...]
    rows = rows_ref[...].astype(jnp.bfloat16)

    @pl.loop(0, turned_ref.shape[1] // TILE)
    def _(t):
        for p in range(TILE // PIECE):
            at = pl.ds(pl.multiple_of(t * TILE + p * PIECE, PIECE), PIECE)
            products = jnp.dot(rows, turned_ref[:, at], preferred_element_type=jnp.float32)
            for i in range(PIECE // LANES):
                r = pl.ds((t * TILE + p * PIECE) // LANES + i, 1)
                hit = assign_ref[r, :] == cl
                second = jnp.sum(jnp.where(hit, products[:, i * LANES : (i + 1) * LANES], 0.0), axis=0, keepdims=True)
                out_ref[r, :] = second + ridge * first_ref[r, :]


def shards(basis_rows, vector, scores, assign, slot_of, partners, link_blocks):
    devices = lax.axis_size("dev")
    clusters = slot_of.shape[0]
    per_dev, n_links, rank, _ = link_blocks.shape
    samples = assign.shape[0]
    norm = 1.0 / math.sqrt(S_DEV // CL_DEV)
    high = samples // LANES
    near = NEAR * per_dev
    f32, bf16 = jnp.float32, jnp.bfloat16

    vector = vector.reshape(high, LANES)
    scores = scores.reshape(high, LANES)
    assign = assign.reshape(high, LANES)
    slot_row = slot_of.reshape(1, clusters)

    far = lambda x: pltpu.with_memory_space_constraint(x, pltpu.HBM)
    close = lambda x: pltpu.with_memory_space_constraint(x, pltpu.VMEM)
    vmem = pl.BlockSpec(memory_space=pltpu.VMEM)
    smem = pl.BlockSpec(memory_space=pltpu.SMEM)
    hbm = pl.BlockSpec(memory_space=pltpu.HBM)
    coef_shape = jax.ShapeDtypeStruct((near, rank), f32)
    params = pltpu.CompilerParams(vmem_limit_bytes=8 * 1024 * 1024)

    coef1, turned_v, assign_v, links_v = pl.pallas_call(
        functools.partial(coef_kernel, devices, per_dev),
        in_specs=[vmem, hbm, hbm, hbm, hbm],
        out_specs=[vmem] * 4,
        out_shape=[
            coef_shape,
            pltpu.VMEM((rank, samples), bf16),
            pltpu.VMEM((high, LANES), jnp.int32),
            pltpu.VMEM(link_blocks.shape, bf16),
        ],
        scratch_shapes=[
            pltpu.VMEM((ROWS, LANES), jnp.int32),
            pltpu.VMEM((ROWS, rank), f32),
            pltpu.VMEM((high, LANES), bf16),
            pltpu.VMEM((high, LANES), f32),
            pltpu.VMEM((SLOTS, TILE, rank), bf16),
            pltpu.SemaphoreType.DMA((2,)),
            pltpu.SemaphoreType.DMA((SLOTS,)),
            pltpu.SemaphoreType.DMA,
        ],
        compiler_params=params,
        name="coef_pass",
    )(slot_row, far(assign), far(vector), far(basis_rows), far(link_blocks))

    def to_all(block):
        copies = jnp.broadcast_to(block[None], (devices,) + block.shape)
        return lax.all_to_all(copies, "dev", 0, 0, tiled=True)

    def mix(coef):
        mixed = pl.pallas_call(
            functools.partial(link_kernel, norm, devices, per_dev),
            in_specs=[smem, smem, vmem, vmem],
            out_specs=vmem,
            scratch_shapes=[
                pltpu.VMEM((clusters, rank), f32),
                pltpu.VMEM((8, rank), f32),
            ],
            out_shape=jax.ShapeDtypeStruct((per_dev, rank), bf16),
            compiler_params=params,
            name="link_product",
        )(slot_of, partners, to_all(coef), close(links_v))
        return to_all(mixed)

    first, coef2 = pl.pallas_call(
        functools.partial(both_kernel, devices, per_dev),
        in_specs=[vmem] * 5 + [hbm],
        out_specs=[vmem, vmem],
        out_shape=[pltpu.VMEM((high, LANES), f32), coef_shape],
        scratch_shapes=[
            pltpu.VMEM((ROWS, LANES), jnp.int32),
            pltpu.VMEM((ROWS, rank), f32),
            pltpu.VMEM((ROWS, rank), f32),
            pltpu.VMEM((high, LANES), f32),
            pltpu.VMEM((SLOTS, TILE, rank), bf16),
            pltpu.SemaphoreType.DMA((SLOTS,)),
        ],
        compiler_params=params,
        name="first_and_coef_pass",
    )(slot_row, mix(coef1), close(assign_v), scores, close(turned_v), far(basis_rows))

    out = pl.pallas_call(
        functools.partial(last_kernel, devices, per_dev),
        in_specs=[vmem] * 5,
        out_specs=vmem,
        out_shape=jax.ShapeDtypeStruct((high, LANES), f32),
        scratch_shapes=[
            pltpu.VMEM((ROWS, LANES), jnp.int32),
            pltpu.VMEM((ROWS, rank), f32),
        ],
        compiler_params=params,
        name="last_pass",
    )(slot_row, mix(coef2), close(assign_v), close(first), close(turned_v))
    return out.reshape(samples)


def solution(mesh):
    in_specs = (
        P(("groups", "dev"), None),
        P(("groups", "dev")),
        P(("groups", "dev")),
        P(("groups", "dev")),
        P("groups"),
        P(("groups", "dev"), None),
        P(("groups", "dev"), None, None, None),
    )
    out_specs = P(("groups", "dev"))
    return jax.shard_map(shards, mesh=mesh, in_specs=in_specs, out_specs=out_specs, check_vma=False)
```

time: 154 us -> 84 us (0.55)
  matrix products: 75.4 us -> 0 us
  Pallas kernels: 0 us -> 36.9 us
  starting transfers between devices: 27 us -> 0 us
  waiting for transfers between devices: 13.7 us -> 0 us
  blocking collectives: 36.5 us -> 45.9 us
    dot_general x10 -> x0, matrix products: 75.4 us -> none  [the longest x2 35.9 us: kernel_apply(): jnp.dot(onehot, everywhere, preferred_element_type=jnp.float32)]
    all_to_all x0 -> x4, blocking collectives: none -> 45.9 us  [to_all(): return lax.all_to_all(copies, 'dev', 0, 0, tiled=True)]
    pallas_call x0 -> x5, Pallas kernels: none -> 36.9 us  [the longest x1 15.1 us: shards(): pl.pallas_call(functools.partial(both_kernel, devices, per_dev), in_specs...]
    all_gather x2 -> x0, blocking collectives: 36.5 us -> none  [kernel_apply(): lax.all_gather((owned * norm).astype(jnp.bfloat16), 'dev', axis=0, tiled=...]
    ppermute x16 -> x0, starting transfers between devices: 27 us -> none  [from_behind(): return lax.ppermute(block, axis, route)]
    ppermute x16 -> x0, waiting for transfers between devices: 13.7 us -> none  [from_behind(): return lax.ppermute(block, axis, route)]
  transfers between devices with their start and end apart: 16 -> 0, of which waited for: 7 -> 0; matrix products, arithmetic and copies ran while one was open for 0% -> 0% of each run, Pallas kernels for 0% -> 0%
where the time goes in v2:
time: 84 us; the launch traced here: 83.7 us
  blocking collectives  45.9 us (55%)
  Pallas kernels  36.9 us (44%)
    all_to_all x4, blocking collectives, to_all(): return lax.all_to_all(copies, 'dev', 0, 0, tiled=True)  45.9 us
    pallas_call x1, Pallas kernels, shards(): pl.pallas_call(functools.partial(both_kernel, devices, per_dev), in_specs...  15.1 us
    pallas_call x1, Pallas kernels, shards(): pl.pallas_call(functools.partial(coef_kernel, devices, per_dev), in_specs...  10.7 us
    pallas_call x2, Pallas kernels, mix(): pl.pallas_call(functools.partial(link_kernel, norm, devices, per_dev), in...  5.75 us
    pallas_call x1, Pallas kernels, shards(): pl.pallas_call(functools.partial(last_kernel, devices, per_dev), in_specs...  5.39 us

profile of v2, /device:TPU:0, one launch (start us, length us, event | category | flops | bytes accessed | tf_op | source)
XLA Modules:
  0.0 83.7 jit_solution(7324314841744167529)
XLA Ops:
  0.0 0.0 copy-start.2
  0.0 0.0 copy-start.3
  0.0 0.0 copy-start.1
  0.0 0.7 copy-done.1
  0.7 0.0 copy-start
  0.7 10.7 %coef_pass.1 = (f32[20,128]{1,0:T(8,128)S(1)}, bf16[128,65536]{1,0:T(8,128)(2,1)S(1)}, s32[512,128]{1,0:T(8,128)S(1)}, bf16[4,64,128,128]{3,2,1,0:T(8,128)(2,1)S(1)}) custom-call(s32[1,64]{1,0:T(1,128)S(1)} %bitcast.6, s32[512,128]{1,0:T(8,128)} %bitcast.9, bf16[512,128]{1,0:T(8,128)(2,1)} %bitcast.10, bf16[65536,128]{1,0:T(8,128)(2,1)} %basis_hbm.3, ...), custom_call_target="tpu_custom_call" | custom-call | tf_op jit(solution)/shard_map/coef_pass/pallas_call | solution.py:210
  11.4 16.2 %all_to_all.20.parts_ref = f32[16,20,128]{2,1,0:T(8,128)S(1)} all-to-all(f32[16,20,128]{2,1,0:T(8,128)S(1)} %broadcast_in_dim.8), channel_id=1, replica_groups=mesh['groups'=2,'dev'=16] {'dev'}, dimensions={0} | all-to-all | bytes 327680 | tf_op jit(solution)/shard_map/all_to_all | solution.py:236
  27.6 0.0 copy-done.2
  27.6 0.0 copy-done.3
  27.6 2.9 %link_product.2 = bf16[4,128]{1,0:T(4,128)(2,1)S(1)} custom-call(s32[64]{0:T(128)S(1)} %copy-done.2, s32[4,64]{1,0:T(4,128)S(1)} %copy-done.3, f32[16,20,128]{2,1,0:T(8,128)S(1)} %all_to_all.20.parts_ref, bf16[4,64,128,128]{3,2,1,0:T(8,128)(2,1)S(1)} %get-tuple-element.12.links_ref), custom_call_target="tpu_custom_call" | custom-call | tf_op jit(solution)/shard_map/link_product/pallas_call | solution.py:239
  30.5 9.1 %all_to_all.21.mixed_ref = bf16[16,4,128]{2,1,0:T(4,128)(2,1)S(1)} all-to-all(bf16[16,4,128]{2,1,0:T(4,128)(2,1)S(1)} %broadcast_in_dim.9), channel_id=1, replica_groups=mesh['groups'=2,'dev'=16] {'dev'}, dimensions={0} | all-to-all | bytes 32768 | tf_op jit(solution)/shard_map/all_to_all | solution.py:236
  39.6 0.0 copy-done
  39.6 15.1 %first_and_coef_pass.1 = (f32[512,128]{1,0:T(8,128)S(1)}, f32[20,128]{1,0:T(8,128)S(1)}) custom-call(s32[1,64]{1,0:T(1,128)S(1)} %bitcast.7, bf16[16,4,128]{2,1,0:T(4,128)(2,1)S(1)} %all_to_all.21.mixed_ref, s32[512,128]{1,0:T(8,128)S(1)} %get-tuple-element.13.assign_ref, f32[512,128]{1,0:T(8,128)S(1)} %bitcast.5, ...), custom_call_target="tpu_custom_call" | custom-call | tf_op jit(solution)/shard_map/first_and_coef_pass/pallas_call | solution.py:253
  54.7 11.6 %all_to_all.22.parts_ref = f32[16,20,128]{2,1,0:T(8,128)S(1)} all-to-all(f32[16,20,128]{2,1,0:T(8,128)S(1)} %broadcast_in_dim.10), channel_id=1, replica_groups=mesh['groups'=2,'dev'=16] {'dev'}, dimensions={0} | all-to-all | bytes 327680 | tf_op jit(solution)/shard_map/all_to_all | solution.py:236
  66.3 2.9 %link_product.3 = bf16[4,128]{1,0:T(4,128)(2,1)S(1)} custom-call(s32[64]{0:T(128)S(1)} %copy-done.2, s32[4,64]{1,0:T(4,128)S(1)} %copy-done.3, f32[16,20,128]{2,1,0:T(8,128)S(1)} %all_to_all.22.parts_ref, bf16[4,64,128,128]{3,2,1,0:T(8,128)(2,1)S(1)} %get-tuple-element.12.links_ref), custom_call_target="tpu_custom_call" | custom-call | tf_op jit(solution)/shard_map/link_product/pallas_call | solution.py:239
  69.2 9.1 %all_to_all.23.mixed_ref = bf16[16,4,128]{2,1,0:T(4,128)(2,1)S(1)} all-to-all(bf16[16,4,128]{2,1,0:T(4,128)(2,1)S(1)} %broadcast_in_dim.11), channel_id=1, replica_groups=mesh['groups'=2,'dev'=16] {'dev'}, dimensions={0} | all-to-all | bytes 32768 | tf_op jit(solution)/shard_map/all_to_all | solution.py:236
  78.3 5.4 %last_pass.1 = f32[512,128]{1,0:T(8,128)} custom-call(s32[1,64]{1,0:T(1,128)S(1)} %bitcast.8, bf16[16,4,128]{2,1,0:T(4,128)(2,1)S(1)} %all_to_all.23.mixed_ref, s32[512,128]{1,0:T(8,128)S(1)} %get-tuple-element.13.assign_ref, f32[512,128]{1,0:T(8,128)S(1)} %get-tuple-element.16.first_ref, bf16[128,65536]{1,0:T(8,128)(2,1)S(1)} %get-tuple-element.14.turned_ref), custom_call_target="tpu_custom_call" | custom-call | tf_op jit(solution)/shard_map/last_pass/pallas_call | solution.py:270
  (4 shorter events, 0.0 us)
Async XLA Ops:
  0.0 27.6 %copy-start.2 = (s32[64]{0:T(128)S(1)}, s32[64]{0:T(128)}, u32[]{:S(2)}) copy-start(s32[64]{0:T(128)} %slot_of_ref.3) | copy-start | bytes 772
  0.0 27.6 %copy-start.3 = (s32[4,64]{1,0:T(4,128)S(1)}, s32[4,64]{1,0:T(4,128)}, u32[]{:S(2)}) copy-start(s32[4,64]{1,0:T(4,128)} %partners_ref.3) | copy-start | bytes 3076
  0.0 0.7 copy-start.1
  0.7 38.9 %copy-start = (f32[65536]{0:T(1024)S(1)}, f32[65536]{0:T(1024)}, u32[]{:S(2)}) copy-start(f32[65536]{0:T(1024)} %param.9) | copy-start | bytes 786436

commit v3 on v2

v3 whole, which is shorter than its diff:
```python
import functools
import math

import jax
import jax.numpy as jnp
from jax import lax
from jax.experimental import pallas as pl
from jax.experimental.pallas import tpu as pltpu
from jax.sharding import PartitionSpec as P

REACH = 2
NEAR = 2 * REACH + 1
CL_DEV = 4
S_DEV = 65536
LANES = 128
ROWS = 24

COPY = 4096
TILE = 2048
GROUP = 8

ridge = 0.5


def near_clusters(devices, per_dev, slot_of_ref, cl_ref):
    clusters = devices * per_dev
    me = lax.axis_index("dev")
    near = lax.broadcasted_iota(jnp.int32, (ROWS, clusters), 0)
    slots = (me + devices - REACH) * per_dev + near
    slots = lax.rem(slots, clusters)
    number = lax.broadcasted_iota(jnp.int32, (ROWS, clusters), 1)
    hit = (slot_of_ref[...] == slots) & (near < NEAR * per_dev)
    found = jnp.sum(jnp.where(hit, number + 1, 0), axis=1, keepdims=True) - 1
    cl_ref[...] = jnp.broadcast_to(found, cl_ref.shape)


def near_rows(devices, per_dev, mixed_ref, rows_ref):
    me = lax.axis_index("dev")
    rows_ref[...] = jnp.zeros_like(rows_ref)
    for g in range(NEAR):
        owner = lax.rem(me + devices + g - REACH, devices)
        rows_ref[g * per_dev : (g + 1) * per_dev, :] = mixed_ref[owner].astype(jnp.float32)


def put_sums(per_dev, sum_ref, out_ref):
    for g in range(NEAR):
        out_ref[:, g * LANES : (g + 1) * LANES] = sum_ref[g * per_dev : (g + 1) * per_dev, :]


def times_turned(rows, block):
    return lax.dot_general(rows, block, (((1,), (1,)), ((), ())), preferred_element_type=jnp.float32)


def tile_at(t):
    return pl.ds(pl.multiple_of(t * TILE, TILE), TILE)


def row_at(t, i):
    return pl.ds(t * (TILE // LANES) + i, 1)


def coef_kernel(
    devices, per_dev, slot_of_ref, assign_hbm, vector_hbm, basis_hbm,
    out_ref, basis_ref, assign_ref,
    cl_ref, sum_ref, vector_ref, x_ref, small_sem, basis_sem,
):
    copies = basis_ref.shape[0] // COPY

    def basis_copy(t):
        rows = pl.ds(pl.multiple_of(t * COPY, COPY), COPY)
        return pltpu.make_async_copy(basis_hbm.at[rows, :], basis_ref.at[rows, :], basis_sem.at[t])

    assign_copy = pltpu.make_async_copy(assign_hbm, assign_ref, small_sem.at[0])
    vector_copy = pltpu.make_async_copy(vector_hbm, vector_ref, small_sem.at[1])
    assign_copy.start()
    vector_copy.start()
    for t in range(copies):
        basis_copy(t).start()
    near_clusters(devices, per_dev, slot_of_ref, cl_ref)
    sum_ref[...] = jnp.zeros_like(sum_ref)
    assign_copy.wait()
    vector_copy.wait()
    x_ref[...] = vector_ref[...].astype(jnp.float32)
    cl = cl_ref[...]

    @pl.loop(0, copies)
    def _(c):
        basis_copy(c).wait()
        total = sum_ref[...]
        for p in range(COPY // TILE):
            t = c * (COPY // TILE) + p
            parts = []
            for i in range(TILE // LANES):
                hit = assign_ref[row_at(t, i), :] == cl
                parts.append(jnp.where(hit, x_ref[row_at(t, i), :], 0.0).astype(jnp.bfloat16))
            left = jnp.concatenate(parts, axis=1)
            total += jnp.dot(left, basis_ref[tile_at(t), :], preferred_element_type=jnp.float32)
        sum_ref[...] = total

    put_sums(per_dev, sum_ref, out_ref)


def link_kernel(norm, devices, per_dev, slot_of_ref, partners_ref, parts_ref, links_ref, out_ref, scaled_ref, picked_ref, mixed_ref):
    for owner in range(devices):
        coef = parts_ref[(owner + REACH) % devices, :, :LANES]
        for g in range(1, NEAR):
            coef += parts_ref[(owner + REACH - g) % devices, :, g * LANES : (g + 1) * LANES]
        scaled_ref[owner * per_dev : (owner + 1) * per_dev, :] = (coef * norm).astype(jnp.bfloat16).astype(jnp.float32)
    n_links, rank = links_ref.shape[1:3]
    for j in range(per_dev):
        @pl.loop(0, n_links, unroll=8)
        def _(k):
            s = slot_of_ref[partners_ref[j, k]]
            picked_ref[pl.ds(j * n_links + k, 1), :] = scaled_ref[pl.ds(s, 1), :]

    mixed_ref[...] = jnp.zeros_like(mixed_ref)
    row = lax.broadcasted_iota(jnp.int32, (GROUP, rank), 0)
    for j in range(per_dev):
        acc = jnp.zeros((GROUP, rank), jnp.float32)
        for k in range(0, n_links, GROUP):
            at = j * n_links + k
            picked = picked_ref[at : at + GROUP, :].astype(jnp.bfloat16)
            block = links_ref[j, k : k + GROUP].reshape(GROUP * rank, rank)
            products = times_turned(picked, block)
            for i in range(GROUP):
                acc += jnp.where(row == i, products[:, i * rank : (i + 1) * rank], 0.0)
        mixed_ref[j : j + 1, :] = jnp.sum(acc, axis=0, keepdims=True)
    out_ref[...] = mixed_ref[:per_dev, :].astype(jnp.bfloat16)


def own_product(hit, products):
    return jnp.sum(jnp.where(hit, products, 0.0), axis=0, keepdims=True)


def both_kernel(
    devices, per_dev, slot_of_ref, mixed_ref, assign_ref, scores_ref, basis_ref,
    first_ref, out_ref, cl_ref, rows_ref, sum_ref, slope_ref, even_ref, odd_ref, even_left, odd_left,
):
    tiles = basis_ref.shape[0] // TILE
    near_clusters(devices, per_dev, slot_of_ref, cl_ref)
    near_rows(devices, per_dev, mixed_ref, rows_ref)
    sum_ref[...] = jnp.zeros_like(sum_ref)
    sig = jax.nn.sigmoid(scores_ref[...])
    slope_ref[...] = sig * (1.0 - sig)
    cl = cl_ref[...]
    rows = rows_ref[...].astype(jnp.bfloat16)
    products_of = (even_ref, odd_ref)
    left_of = (even_left, odd_left)

    def multiply(t, side):
        products_of[side][...] = times_turned(rows, basis_ref[tile_at(t), :])

    def select(t, side):
        for i in range(TILE // LANES):
            at = slice(i * LANES, (i + 1) * LANES)
            hit = assign_ref[row_at(t, i), :] == cl
            first = own_product(hit, products_of[side][:, at])
            first_ref[row_at(t, i), :] = first
            weighted = slope_ref[row_at(t, i), :] * first
            left_of[side][:, at] = jnp.where(hit, weighted, 0.0).astype(jnp.bfloat16)

    def add_up(t, side):
        sum_ref[...] += jnp.dot(left_of[side][...], basis_ref[tile_at(t), :], preferred_element_type=jnp.float32)

    multiply(0, 0)
    select(0, 0)
    multiply(1, 1)

    @pl.loop(0, tiles // 2 - 1)
    def _(i):
        t = 2 * i + 2
        add_up(t - 2, 0)
        multiply(t, 0)
        select(t - 1, 1)
        add_up(t - 1, 1)
        multiply(t + 1, 1)
        select(t, 0)

    add_up(tiles - 2, 0)
    select(tiles - 1, 1)
    add_up(tiles - 1, 1)
    put_sums(per_dev, sum_ref, out_ref)


def last_kernel(
    devices, per_dev, slot_of_ref, mixed_ref, assign_ref, first_ref, basis_ref, out_ref, cl_ref, rows_ref, even_ref, odd_ref
):
    tiles = basis_ref.shape[0] // TILE
    near_clusters(devices, per_dev, slot_of_ref, cl_ref)
    near_rows(devices, per_dev, mixed_ref, rows_ref)
    cl = cl_ref[...]
    rows = rows_ref[...].astype(jnp.bfloat16)
    products_of = (even_ref, odd_ref)

    def multiply(t, side):
        products_of[side][...] = times_turned(rows, basis_ref[tile_at(t), :])

    def select(t, side):
        for i in range(TILE // LANES):
            hit = assign_ref[row_at(t, i), :] == cl
            second = own_product(hit, products_of[side][:, i * LANES : (i + 1) * LANES])
            out_ref[row_at(t, i), :] = second + ridge * first_ref[row_at(t, i), :]

    multiply(0, 0)

    @pl.loop(0, tiles // 2 - 1)
    def _(i):
        t = 2 * i + 1
        multiply(t, 1)
        select(t - 1, 0)
        multiply(t + 1, 0)
        select(t, 1)

    multiply(tiles - 1, 1)
    select(tiles - 2, 0)
    select(tiles - 1, 1)


def shards(basis_rows, vector, scores, assign, slot_of, partners, link_blocks):
    devices = lax.axis_size("dev")
    clusters = slot_of.shape[0]
    per_dev, n_links, rank, _ = link_blocks.shape
    samples = assign.shape[0]
    norm = 1.0 / math.sqrt(S_DEV // CL_DEV)
    high = samples // LANES
    f32, bf16 = jnp.float32, jnp.bfloat16

    vector = vector.reshape(high, LANES)
    scores = scores.reshape(high, LANES)
    assign = assign.reshape(high, LANES)
    slot_row = slot_of.reshape(1, clusters)

    far = lambda x: pltpu.with_memory_space_constraint(x, pltpu.HBM)
    close = lambda x: pltpu.with_memory_space_constraint(x, pltpu.VMEM)
    vmem = pl.BlockSpec(memory_space=pltpu.VMEM)
    smem = pl.BlockSpec(memory_space=pltpu.SMEM)
    hbm = pl.BlockSpec(memory_space=pltpu.HBM)
    coef_shape = jax.ShapeDtypeStruct((per_dev, NEAR * rank), f32)
    params = pltpu.CompilerParams(vmem_limit_bytes=8 * 1024 * 1024)

    coef1, basis_v, assign_v = pl.pallas_call(
        functools.partial(coef_kernel, devices, per_dev),
        in_specs=[vmem, hbm, hbm, hbm],
        out_specs=[vmem] * 3,
        out_shape=[
            coef_shape,
            pltpu.VMEM((samples, rank), bf16),
            pltpu.VMEM((high, LANES), jnp.int32),
        ],
        scratch_shapes=[
            pltpu.VMEM((ROWS, LANES), jnp.int32),
            pltpu.VMEM((ROWS, rank), f32),
            pltpu.VMEM((high, LANES), bf16),
            pltpu.VMEM((high, LANES), f32),
            pltpu.SemaphoreType.DMA((2,)),
            pltpu.SemaphoreType.DMA((samples // COPY,)),
        ],
        compiler_params=params,
        name="coef_pass",
    )(slot_row, far(assign), far(vector), far(basis_rows))

    def to_all(block):
        copies = jnp.broadcast_to(block[None], (devices,) + block.shape)
        return lax.all_to_all(copies, "dev", 0, 0, tiled=True)

    def mix(coef):
        mixed = pl.pallas_call(
            functools.partial(link_kernel, norm, devices, per_dev),
            in_specs=[smem, smem, vmem, vmem],
            out_specs=vmem,
            scratch_shapes=[
                pltpu.VMEM((clusters, rank), f32),
                pltpu.VMEM((per_dev * n_links, rank), f32),
                pltpu.VMEM((8, rank), f32),
            ],
            out_shape=jax.ShapeDtypeStruct((per_dev, rank), bf16),
            compiler_params=params,
            name="link_product",
        )(slot_of, partners, to_all(coef), close(link_blocks))
        return to_all(mixed)

    first, coef2 = pl.pallas_call(
        functools.partial(both_kernel, devices, per_dev),
        in_specs=[vmem] * 5,
        out_specs=[vmem, vmem],
        out_shape=[pltpu.VMEM((high, LANES), f32), coef_shape],
        scratch_shapes=[
            pltpu.VMEM((ROWS, LANES), jnp.int32),
            pltpu.VMEM((ROWS, rank), f32),
            pltpu.VMEM((ROWS, rank), f32),
            pltpu.VMEM((high, LANES), f32),
            pltpu.VMEM((ROWS, TILE), f32),
            pltpu.VMEM((ROWS, TILE), f32),
            pltpu.VMEM((ROWS, TILE), bf16),
            pltpu.VMEM((ROWS, TILE), bf16),
        ],
        compiler_params=params,
        name="first_and_coef_pass",
    )(slot_row, mix(coef1), close(assign_v), scores, close(basis_v))

    out = pl.pallas_call(
        functools.partial(last_kernel, devices, per_dev),
        in_specs=[vmem] * 5,
        out_specs=vmem,
        out_shape=jax.ShapeDtypeStruct((high, LANES), f32),
        scratch_shapes=[
            pltpu.VMEM((ROWS, LANES), jnp.int32),
            pltpu.VMEM((ROWS, rank), f32),
            pltpu.VMEM((ROWS, TILE), f32),
            pltpu.VMEM((ROWS, TILE), f32),
        ],
        compiler_params=params,
        name="last_pass",
    )(slot_row, mix(coef2), close(assign_v), close(first), close(basis_v))
    return out.reshape(samples)


def solution(mesh):
    in_specs = (
        P(("groups", "dev"), None),
        P(("groups", "dev")),
        P(("groups", "dev")),
        P(("groups", "dev")),
        P("groups"),
        P(("groups", "dev"), None),
        P(("groups", "dev"), None, None, None),
    )
    out_specs = P(("groups", "dev"))
    return jax.shard_map(shards, mesh=mesh, in_specs=in_specs, out_specs=out_specs, check_vma=False)
```

time: 84 us -> 82.8 us (0.986)
  blocking collectives: 45.9 us -> 44.8 us
    pallas_call x1, Pallas kernels: 15.1 us -> 10.4 us  [shards(): pl.pallas_call(functools.partial(both_kernel, devices, per_dev), in_specs...]
    pallas_call x1, Pallas kernels: 5.39 us -> 8.17 us  [shards(): pl.pallas_call(functools.partial(last_kernel, devices, per_dev), in_specs...]
    pallas_call x2, Pallas kernels: 5.75 us -> 7.22 us  [mix(): pl.pallas_call(functools.partial(link_kernel, norm, devices, per_dev), in...]
    all_to_all x4, blocking collectives: 45.9 us -> 44.8 us  [to_all(): return lax.all_to_all(copies, 'dev', 0, 0, tiled=True)]
where the time goes in v3:
time: 82.8 us; the launch traced here: 82.5 us
  blocking collectives  44.8 us (54%)
  Pallas kernels  36.7 us (44%)
  local copies, waits for them, and re-layouts  0.88 us (1%)
    all_to_all x4, blocking collectives, to_all(): return lax.all_to_all(copies, 'dev', 0, 0, tiled=True)  44.8 us
    pallas_call x1, Pallas kernels, shards(): pl.pallas_call(functools.partial(coef_kernel, devices, per_dev), in_specs...  10.9 us
    pallas_call x1, Pallas kernels, shards(): pl.pallas_call(functools.partial(both_kernel, devices, per_dev), in_specs...  10.4 us
    pallas_call x1, Pallas kernels, shards(): pl.pallas_call(functools.partial(last_kernel, devices, per_dev), in_specs...  8.17 us
    pallas_call x2, Pallas kernels, mix(): pl.pallas_call(functools.partial(link_kernel, norm, devices, per_dev), in...  7.22 us

profile of v3, /device:TPU:0, one launch (start us, length us, event | category | flops | bytes accessed | tf_op | source)
XLA Modules:
  0.0 82.5 jit_solution(15778091951579783071)
XLA Ops:
  0.0 0.0 slice-start
  0.0 0.0 copy-start
  0.0 0.0 copy-start.1
  0.0 0.8 copy-done.1
  0.8 0.0 slice-start.1
  0.8 0.0 copy-start.2
  0.8 0.0 copy-start.3
  0.8 10.9 %coef_pass.1 = (f32[4,640]{1,0:T(4,128)S(1)}, bf16[65536,128]{1,0:T(8,128)(2,1)S(1)}, s32[512,128]{1,0:T(8,128)S(1)}) custom-call(s32[1,64]{1,0:T(1,128)S(1)} %bitcast.8, s32[512,128]{1,0:T(8,128)} %bitcast.11, bf16[512,128]{1,0:T(8,128)(2,1)} %bitcast.12, bf16[65536,128]{1,0:T(8,128)(2,1)} %basis_hbm.1), custom_call_target="tpu_custom_call" | custom-call | tf_op jit(solution)/shard_map/coef_pass/pallas_call | solution.py:241
  11.8 15.7 %all_to_all.20.parts_ref = f32[16,4,640]{2,1,0:T(4,128)S(1)} all-to-all(f32[16,4,640]{2,1,0:T(4,128)S(1)} %broadcast_in_dim.8), channel_id=1, replica_groups=mesh['groups'=2,'dev'=16] {'dev'}, dimensions={0} | all-to-all | bytes 327680 | tf_op jit(solution)/shard_map/all_to_all | solution.py:264
  27.4 0.0 slice-done
  27.4 0.0 slice-done.1
  27.4 0.0 copy-done.2
  27.4 0.0 copy-done.3
  27.5 3.6 %link_product.2 = bf16[4,128]{1,0:T(4,128)(2,1)S(1)} custom-call(s32[64]{0:T(128)S(1)} %copy-done.2, s32[4,64]{1,0:T(4,128)S(1)} %copy-done.3, f32[16,4,640]{2,1,0:T(4,128)S(1)} %all_to_all.20.parts_ref, bf16[4,64,128,128]{3,2,1,0:T(8,128)(2,1)S(1)} %bitcast.6), custom_call_target="tpu_custom_call" | custom-call | tf_op jit(solution)/shard_map/link_product/pallas_call | solution.py:267
  31.1 9.1 %all_to_all.21.mixed_ref = bf16[16,4,128]{2,1,0:T(4,128)(2,1)S(1)} all-to-all(bf16[16,4,128]{2,1,0:T(4,128)(2,1)S(1)} %broadcast_in_dim.9), channel_id=1, replica_groups=mesh['groups'=2,'dev'=16] {'dev'}, dimensions={0} | all-to-all | bytes 32768 | tf_op jit(solution)/shard_map/all_to_all | solution.py:264
  40.2 0.0 copy-done
  40.2 10.4 %first_and_coef_pass.1 = (f32[512,128]{1,0:T(8,128)S(1)}, f32[4,640]{1,0:T(4,128)S(1)}) custom-call(s32[1,64]{1,0:T(1,128)S(1)} %bitcast.9, bf16[16,4,128]{2,1,0:T(4,128)(2,1)S(1)} %all_to_all.21.mixed_ref, s32[512,128]{1,0:T(8,128)S(1)} %get-tuple-element.11.assign_ref, f32[512,128]{1,0:T(8,128)S(1)} %bitcast.7, ...), custom_call_target="tpu_custom_call" | custom-call | tf_op jit(solution)/shard_map/first_and_coef_pass/pallas_call | solution.py:282
  50.6 11.1 %all_to_all.22.parts_ref = f32[16,4,640]{2,1,0:T(4,128)S(1)} all-to-all(f32[16,4,640]{2,1,0:T(4,128)S(1)} %broadcast_in_dim.10), channel_id=1, replica_groups=mesh['groups'=2,'dev'=16] {'dev'}, dimensions={0} | all-to-all | bytes 327680 | tf_op jit(solution)/shard_map/all_to_all | solution.py:264
  61.7 3.6 %link_product.3 = bf16[4,128]{1,0:T(4,128)(2,1)S(1)} custom-call(s32[64]{0:T(128)S(1)} %copy-done.2, s32[4,64]{1,0:T(4,128)S(1)} %copy-done.3, f32[16,4,640]{2,1,0:T(4,128)S(1)} %all_to_all.22.parts_ref, bf16[4,64,128,128]{3,2,1,0:T(8,128)(2,1)S(1)} %bitcast.6), custom_call_target="tpu_custom_call" | custom-call | tf_op jit(solution)/shard_map/link_product/pallas_call | solution.py:267
  65.3 9.1 %all_to_all.23.mixed_ref = bf16[16,4,128]{2,1,0:T(4,128)(2,1)S(1)} all-to-all(bf16[16,4,128]{2,1,0:T(4,128)(2,1)S(1)} %broadcast_in_dim.11), channel_id=1, replica_groups=mesh['groups'=2,'dev'=16] {'dev'}, dimensions={0} | all-to-all | bytes 32768 | tf_op jit(solution)/shard_map/all_to_all | solution.py:264
  74.4 8.2 %last_pass.1 = f32[512,128]{1,0:T(8,128)} custom-call(s32[1,64]{1,0:T(1,128)S(1)} %bitcast.10, bf16[16,4,128]{2,1,0:T(4,128)(2,1)S(1)} %all_to_all.23.mixed_ref, s32[512,128]{1,0:T(8,128)S(1)} %get-tuple-element.11.assign_ref, f32[512,128]{1,0:T(8,128)S(1)} %get-tuple-element.14.first_ref, bf16[65536,128]{1,0:T(8,128)(2,1)S(1)} %get-tuple-element.12.basis_ref), custom_call_target="tpu_custom_call" | custom-call | tf_op jit(solution)/shard_map/last_pass/pallas_call | solution.py:301
  (5 shorter events, 0.1 us)
Async XLA Ops:
  0.0 27.4 %slice-start = ((s8[8388608]{0:T(1024)(128)(4,1)}), s8[4194304]{0:T(1024)(128)(4,1)S(1)}, s32[]{:S(2)}) async-start(s8[8388608]{0:T(1024)(128)(4,1)} %bitcast.5), calls=%async_computation.4 | async-start | bytes 8388608
  0.0 40.2 %copy-start = (f32[65536]{0:T(1024)S(1)}, f32[65536]{0:T(1024)}, u32[]{:S(2)}) copy-start(f32[65536]{0:T(1024)} %param.9) | copy-start | bytes 786436
  0.0 0.8 copy-start.1
  0.8 26.6 %slice-start.1 = ((s8[8388608]{0:T(1024)(128)(4,1)}), s8[4194304]{0:T(1024)(128)(4,1)S(1)}, s32[]{:S(2)}) async-start(s8[8388608]{0:T(1024)(128)(4,1)} %bitcast.5), calls=%async_computation.5 | async-start | bytes 8388608
  0.8 26.6 %copy-start.2 = (s32[64]{0:T(128)S(1)}, s32[64]{0:T(128)}, u32[]{:S(2)}) copy-start(s32[64]{0:T(128)} %slot_of_ref.3) | copy-start | bytes 772
  0.8 26.6 %copy-start.3 = (s32[4,64]{1,0:T(4,128)S(1)}, s32[4,64]{1,0:T(4,128)}, u32[]{:S(2)}) copy-start(s32[4,64]{1,0:T(4,128)} %partners_ref.3) | copy-start | bytes 3076

commit v4 on v3

--- a/solution.py
+++ b/solution.py
@@ -17,7 +17,7 @@
 
 COPY = 4096
 TILE = 2048
-GROUP = 8
+SLOTS = 4
 
 ridge = 0.5
 
@@ -47,8 +47,10 @@
         out_ref[:, g * LANES : (g + 1) * LANES] = sum_ref[g * per_dev : (g + 1) * per_dev, :]
 
 
-def times_turned(rows, block):
-    return lax.dot_general(rows, block, (((1,), (1,)), ((), ())), preferred_element_type=jnp.float32)
+def slot_copy(basis_hbm, slots_ref, sem, c):
+    slot = lax.rem(c, SLOTS)
+    rows = pl.ds(pl.multiple_of(c * COPY, COPY), COPY)
+    return pltpu.make_async_copy(basis_hbm.at[rows, :], slots_ref.at[slot], sem.at[slot])
 
 
 def tile_at(t):
@@ -61,21 +63,20 @@
 
 def coef_kernel(
     devices, per_dev, slot_of_ref, assign_hbm, vector_hbm, basis_hbm,
-    out_ref, basis_ref, assign_ref,
-    cl_ref, sum_ref, vector_ref, x_ref, small_sem, basis_sem,
+    out_ref, turned_ref, assign_ref,
+    cl_ref, sum_ref, vector_ref, x_ref, slots_ref, small_sem, basis_sem,
 ):
-    copies = basis_ref.shape[0] // COPY
-
-    def basis_copy(t):
-        rows = pl.ds(pl.multiple_of(t * COPY, COPY), COPY)
-        return pltpu.make_async_copy(basis_hbm.at[rows, :], basis_ref.at[rows, :], basis_sem.at[t])
+    copies = basis_hbm.shape[0] // COPY
+
+    def basis_copy(c):
+        return slot_copy(basis_hbm, slots_ref, basis_sem, c)
 
     assign_copy = pltpu.make_async_copy(assign_hbm, assign_ref, small_sem.at[0])
     vector_copy = pltpu.make_async_copy(vector_hbm, vector_ref, small_sem.at[1])
     assign_copy.start()
     vector_copy.start()
-    for t in range(copies):
-        basis_copy(t).start()
+    for c in range(SLOTS):
+        basis_copy(c).start()
     near_clusters(devices, per_dev, slot_of_ref, cl_ref)
     sum_ref[...] = jnp.zeros_like(sum_ref)
     assign_copy.wait()
@@ -94,37 +95,51 @@
                 hit = assign_ref[row_at(t, i), :] == cl
                 parts.append(jnp.where(hit, x_ref[row_at(t, i), :], 0.0).astype(jnp.bfloat16))
             left = jnp.concatenate(parts, axis=1)
-            total += jnp.dot(left, basis_ref[tile_at(t), :], preferred_element_type=jnp.float32)
+            block = slots_ref[lax.rem(c, SLOTS), p * TILE : (p + 1) * TILE, :]
+            turned_ref[:, tile_at(t)] = block.T
+            total += jnp.dot(left, block, preferred_element_type=jnp.float32)
         sum_ref[...] = total
 
+        @pl.when(c + SLOTS < copies)
+        def _():
+            basis_copy(c + SLOTS).start()
+
     put_sums(per_dev, sum_ref, out_ref)
 
 
-def link_kernel(norm, devices, per_dev, slot_of_ref, partners_ref, parts_ref, links_ref, out_ref, scaled_ref, picked_ref, mixed_ref):
+def link_kernel(norm, devices, per_dev, first_time, slot_of_ref, partners_ref, parts_ref, *refs):
+    if first_time:
+        links_hbm, out_ref, links_ref, scaled_ref, mixed_ref, links_sem = refs
+    else:
+        links_ref, out_ref, scaled_ref, mixed_ref = refs
+    n_links = links_ref.shape[1]
+    halves = (0, 1)
+
+    def half_copy(j, h):
+        ks = pl.ds(h * (n_links // 2), n_links // 2)
+        return pltpu.make_async_copy(links_hbm.at[j, ks], links_ref.at[j, ks], links_sem.at[2 * j + h])
+
+    if first_time:
+        for j in range(per_dev):
+            for h in halves:
+                half_copy(j, h).start()
     for owner in range(devices):
         coef = parts_ref[(owner + REACH) % devices, :, :LANES]
         for g in range(1, NEAR):
             coef += parts_ref[(owner + REACH - g) % devices, :, g * LANES : (g + 1) * LANES]
         scaled_ref[owner * per_dev : (owner + 1) * per_dev, :] = (coef * norm).astype(jnp.bfloat16).astype(jnp.float32)
-    n_links, rank = links_ref.shape[1:3]
+    mixed_ref[...] = jnp.zeros_like(mixed_ref)
     for j in range(per_dev):
-        @pl.loop(0, n_links, unroll=8)
-        def _(k):
+        def body(k, acc):
             s = slot_of_ref[partners_ref[j, k]]
-            picked_ref[pl.ds(j * n_links + k, 1), :] = scaled_ref[pl.ds(s, 1), :]
-
-    mixed_ref[...] = jnp.zeros_like(mixed_ref)
-    row = lax.broadcasted_iota(jnp.int32, (GROUP, rank), 0)
-    for j in range(per_dev):
-        acc = jnp.zeros((GROUP, rank), jnp.float32)
-        for k in range(0, n_links, GROUP):
-            at = j * n_links + k
-            picked = picked_ref[at : at + GROUP, :].astype(jnp.bfloat16)
-            block = links_ref[j, k : k + GROUP].reshape(GROUP * rank, rank)
-            products = times_turned(picked, block)
-            for i in range(GROUP):
-                acc += jnp.where(row == i, products[:, i * rank : (i + 1) * rank], 0.0)
-        mixed_ref[j : j + 1, :] = jnp.sum(acc, axis=0, keepdims=True)
+            return acc + links_ref[j, k].astype(jnp.float32) * scaled_ref[pl.ds(s, 1), :]
+
+        acc = jnp.zeros(links_ref.shape[2:], jnp.float32)
+        for h in halves:
+            if first_time:
+                half_copy(j, h).wait()
+            acc = lax.fori_loop(h * (n_links // 2), (h + 1) * (n_links // 2), body, acc, unroll=8)
+        mixed_ref[j : j + 1, :] = jnp.sum(acc.T, axis=0, keepdims=True)
     out_ref[...] = mixed_ref[:per_dev, :].astype(jnp.bfloat16)
 
 
@@ -133,10 +148,17 @@
 
 
 def both_kernel(
-    devices, per_dev, slot_of_ref, mixed_ref, assign_ref, scores_ref, basis_ref,
-    first_ref, out_ref, cl_ref, rows_ref, sum_ref, slope_ref, even_ref, odd_ref, even_left, odd_left,
+    devices, per_dev, slot_of_ref, mixed_ref, assign_ref, scores_ref, turned_ref, basis_hbm,
+    first_ref, out_ref, cl_ref, rows_ref, sum_ref, slope_ref, even_ref, odd_ref, even_left, odd_left, slots_ref, basis_sem,
 ):
-    tiles = basis_ref.shape[0] // TILE
+    tiles = turned_ref.shape[1] // TILE
+    copies = tiles // 2
+
+    def basis_copy(c):
+        return slot_copy(basis_hbm, slots_ref, basis_sem, c)
+
+    for c in range(SLOTS):
+        basis_copy(c).start()
     near_clusters(devices, per_dev, slot_of_ref, cl_ref)
     near_rows(devices, per_dev, mixed_ref, rows_ref)
     sum_ref[...] = jnp.zeros_like(sum_ref)
@@ -148,7 +170,7 @@
     left_of = (even_left, odd_left)
 
     def multiply(t, side):
-        products_of[side][...] = times_turned(rows, basis_ref[tile_at(t), :])
+        products_of[side][...] = jnp.dot(rows, turned_ref[:, tile_at(t)], preferred_element_type=jnp.float32)
 
     def select(t, side):
         for i in range(TILE // LANES):
@@ -159,8 +181,9 @@
             weighted = slope_ref[row_at(t, i), :] * first
             left_of[side][:, at] = jnp.where(hit, weighted, 0.0).astype(jnp.bfloat16)
 
-    def add_up(t, side):
-        sum_ref[...] += jnp.dot(left_of[side][...], basis_ref[tile_at(t), :], preferred_element_type=jnp.float32)
+    def add_up(c, side):
+        block = slots_ref[lax.rem(c, SLOTS), side * TILE : (side + 1) * TILE, :]
+        sum_ref[...] += jnp.dot(left_of[side][...], block, preferred_element_type=jnp.float32)
 
     multiply(0, 0)
     select(0, 0)
@@ -169,23 +192,29 @@
     @pl.loop(0, tiles // 2 - 1)
     def _(i):
         t = 2 * i + 2
-        add_up(t - 2, 0)
+        basis_copy(i).wait()
+        add_up(i, 0)
         multiply(t, 0)
         select(t - 1, 1)
-        add_up(t - 1, 1)
+        add_up(i, 1)
         multiply(t + 1, 1)
         select(t, 0)
 
-    add_up(tiles - 2, 0)
+        @pl.when(i + SLOTS < copies)
+        def _():
+            basis_copy(i + SLOTS).start()
+
+    basis_copy(copies - 1).wait()
+    add_up(copies - 1, 0)
     select(tiles - 1, 1)
-    add_up(tiles - 1, 1)
+    add_up(copies - 1, 1)
     put_sums(per_dev, sum_ref, out_ref)
 
 
 def last_kernel(
-    devices, per_dev, slot_of_ref, mixed_ref, assign_ref, first_ref, basis_ref, out_ref, cl_ref, rows_ref, even_ref, odd_ref
+    devices, per_dev, slot_of_ref, mixed_ref, assign_ref, first_ref, turned_ref, out_ref, cl_ref, rows_ref, even_ref, odd_ref
 ):
-    tiles = basis_ref.shape[0] // TILE
+    tiles = turned_ref.shape[1] // TILE
     near_clusters(devices, per_dev, slot_of_ref, cl_ref)
     near_rows(devices, per_dev, mixed_ref, rows_ref)
     cl = cl_ref[...]
@@ -193,7 +222,7 @@
     products_of = (even_ref, odd_ref)
 
     def multiply(t, side):
-        products_of[side][...] = times_turned(rows, basis_ref[tile_at(t), :])
+        products_of[side][...] = jnp.dot(rows, turned_ref[:, tile_at(t)], preferred_element_type=jnp.float32)
 
     def select(t, side):
         for i in range(TILE // LANES):
@@ -238,13 +267,13 @@
     coef_shape = jax.ShapeDtypeStruct((per_dev, NEAR * rank), f32)
     params = pltpu.CompilerParams(vmem_limit_bytes=8 * 1024 * 1024)
 
-    coef1, basis_v, assign_v = pl.pallas_call(
+    coef1, turned_v, assign_v = pl.pallas_call(
         functools.partial(coef_kernel, devices, per_dev),
         in_specs=[vmem, hbm, hbm, hbm],
         out_specs=[vmem] * 3,
         out_shape=[
             coef_shape,
-            pltpu.VMEM((samples, rank), bf16),
+            pltpu.VMEM((rank, samples), bf16),
             pltpu.VMEM((high, LANES), jnp.int32),
         ],
         scratch_shapes=[
@@ -252,8 +281,9 @@
             pltpu.VMEM((ROWS, rank), f32),
             pltpu.VMEM((high, LANES), bf16),
             pltpu.VMEM((high, LANES), f32),
+            pltpu.VMEM((SLOTS, COPY, rank), bf16),
             pltpu.SemaphoreType.DMA((2,)),
-            pltpu.SemaphoreType.DMA((samples // COPY,)),
+            pltpu.SemaphoreType.DMA((SLOTS,)),
         ],
         compiler_params=params,
         name="coef_pass",
@@ -263,25 +293,26 @@
         copies = jnp.broadcast_to(block[None], (devices,) + block.shape)
         return lax.all_to_all(copies, "dev", 0, 0, tiled=True)
 
-    def mix(coef):
-        mixed = pl.pallas_call(
-            functools.partial(link_kernel, norm, devices, per_dev),
-            in_specs=[smem, smem, vmem, vmem],
-            out_specs=vmem,
+    def mix(coef, links, first_time):
+        out = pl.pallas_call(
+            functools.partial(link_kernel, norm, devices, per_dev, first_time),
+            in_specs=[smem, smem, vmem, hbm if first_time else vmem],
+            out_specs=[vmem, vmem] if first_time else [vmem],
+            out_shape=[jax.ShapeDtypeStruct((per_dev, rank), bf16)] + [pltpu.VMEM(links.shape, bf16)] * first_time,
             scratch_shapes=[
                 pltpu.VMEM((clusters, rank), f32),
-                pltpu.VMEM((per_dev * n_links, rank), f32),
                 pltpu.VMEM((8, rank), f32),
-            ],
-            out_shape=jax.ShapeDtypeStruct((per_dev, rank), bf16),
+            ]
+            + [pltpu.SemaphoreType.DMA((2 * per_dev,))] * first_time,
             compiler_params=params,
             name="link_product",
-        )(slot_of, partners, to_all(coef), close(link_blocks))
-        return to_all(mixed)
-
+        )(slot_of, partners, to_all(coef), links)
+        return (to_all(out[0]), *out[1:])
+
+    mixed1, links_v = mix(coef1, far(link_blocks), True)
     first, coef2 = pl.pallas_call(
         functools.partial(both_kernel, devices, per_dev),
-        in_specs=[vmem] * 5,
+        in_specs=[vmem] * 5 + [hbm],
         out_specs=[vmem, vmem],
         out_shape=[pltpu.VMEM((high, LANES), f32), coef_shape],
         scratch_shapes=[
@@ -293,10 +324,13 @@
             pltpu.VMEM((ROWS, TILE), f32),
             pltpu.VMEM((ROWS, TILE), bf16),
             pltpu.VMEM((ROWS, TILE), bf16),
+            pltpu.VMEM((SLOTS, COPY, rank), bf16),
+            pltpu.SemaphoreType.DMA((SLOTS,)),
         ],
         compiler_params=params,
         name="first_and_coef_pass",
-    )(slot_row, mix(coef1), close(assign_v), scores, close(basis_v))
+    )(slot_row, mixed1, close(assign_v), scores, close(turned_v), far(basis_rows))
+    (mixed2,) = mix(coef2, close(links_v), False)
 
     out = pl.pallas_call(
         functools.partial(last_kernel, devices, per_dev),
@@ -311,7 +345,7 @@
         ],
         compiler_params=params,
         name="last_pass",
-    )(slot_row, mix(coef2), close(assign_v), close(first), close(basis_v))
+    )(slot_row, mixed2, close(assign_v), close(first), close(turned_v))
     return out.reshape(samples)
 
 

time: 82.8 us -> 75.3 us (0.909)
  Pallas kernels: 36.7 us -> 29.3 us
    pallas_call x1, Pallas kernels: 8.17 us -> 5.29 us  [shards(): pl.pallas_call(functools.partial(last_kernel, devices, per_dev), in_specs...]
    pallas_call x1, Pallas kernels: 10.9 us -> 8.42 us  [shards(): pl.pallas_call(functools.partial(coef_kernel, devices, per_dev), in_specs...]
    pallas_call x1, Pallas kernels: 10.4 us -> 8.34 us  [shards(): pl.pallas_call(functools.partial(both_kernel, devices, per_dev), in_specs...]
where the time goes in v4:
time: 75.3 us; the launch traced here: 75 us
  blocking collectives  44.8 us (59%)
  Pallas kernels  29.3 us (39%)
  local copies, waits for them, and re-layouts  0.77 us (1%)
    all_to_all x4, blocking collectives, to_all(): return lax.all_to_all(copies, 'dev', 0, 0, tiled=True)  44.8 us
    pallas_call x1, Pallas kernels, shards(): pl.pallas_call(functools.partial(coef_kernel, devices, per_dev), in_specs...  8.42 us
    pallas_call x1, Pallas kernels, shards(): pl.pallas_call(functools.partial(both_kernel, devices, per_dev), in_specs...  8.34 us
    pallas_call x2, Pallas kernels, mix(): pl.pallas_call(functools.partial(link_kernel, norm, devices, per_dev, fir...  7.26 us
    pallas_call x1, Pallas kernels, shards(): pl.pallas_call(functools.partial(last_kernel, devices, per_dev), in_specs...  5.29 us

profile of v4, /device:TPU:0, one launch (start us, length us, event | category | flops | bytes accessed | tf_op | source)
XLA Modules:
  0.0 75.0 jit_solution(8002572534108835327)
XLA Ops:
  0.0 0.0 copy-start
  0.0 0.0 copy-start.1
  0.0 0.7 copy-done.1
  0.7 0.0 copy-start.2
  0.7 0.0 copy-start.3
  0.7 8.4 %coef_pass.1 = (f32[4,640]{1,0:T(4,128)S(1)}, bf16[128,65536]{1,0:T(8,128)(2,1)S(1)}, s32[512,128]{1,0:T(8,128)S(1)}) custom-call(s32[1,64]{1,0:T(1,128)S(1)} %bitcast.6, s32[512,128]{1,0:T(8,128)} %bitcast.9, bf16[512,128]{1,0:T(8,128)(2,1)} %bitcast.10, bf16[65536,128]{1,0:T(8,128)(2,1)} %basis_hbm.3), custom_call_target="tpu_custom_call" | custom-call | tf_op jit(solution)/shard_map/coef_pass/pallas_call | solution.py:270
  9.2 15.6 %all_to_all.20.parts_ref = f32[16,4,640]{2,1,0:T(4,128)S(1)} all-to-all(f32[16,4,640]{2,1,0:T(4,128)S(1)} %broadcast_in_dim.8), channel_id=1, replica_groups=mesh['groups'=2,'dev'=16] {'dev'}, dimensions={0} | all-to-all | bytes 327680 | tf_op jit(solution)/shard_map/all_to_all | solution.py:294
  24.8 0.0 copy-done.2
  24.8 0.0 copy-done.3
  24.8 4.4 %link_product.2 = (bf16[4,128]{1,0:T(4,128)(2,1)S(1)}, bf16[4,64,128,128]{3,2,1,0:T(8,128)(2,1)S(1)}) custom-call(s32[64]{0:T(128)S(1)} %copy-done.2, s32[4,64]{1,0:T(4,128)S(1)} %copy-done.3, f32[16,4,640]{2,1,0:T(4,128)S(1)} %all_to_all.20.parts_ref, bf16[4,64,128,128]{3,2,1,0:T(8,128)(2,1)} %refs_0_.1), custom_call_target="tpu_custom_call" | custom-call | tf_op jit(solution)/shard_map/link_product/pallas_call | solution.py:297
  29.2 9.1 %all_to_all.21.mixed_ref = bf16[16,4,128]{2,1,0:T(4,128)(2,1)S(1)} all-to-all(bf16[16,4,128]{2,1,0:T(4,128)(2,1)S(1)} %broadcast_in_dim.9), channel_id=1, replica_groups=mesh['groups'=2,'dev'=16] {'dev'}, dimensions={0} | all-to-all | bytes 32768 | tf_op jit(solution)/shard_map/all_to_all | solution.py:294
  38.3 0.0 copy-done
  38.3 8.3 %first_and_coef_pass.1 = (f32[512,128]{1,0:T(8,128)S(1)}, f32[4,640]{1,0:T(4,128)S(1)}) custom-call(s32[1,64]{1,0:T(1,128)S(1)} %bitcast.7, bf16[16,4,128]{2,1,0:T(4,128)(2,1)S(1)} %all_to_all.21.mixed_ref, s32[512,128]{1,0:T(8,128)S(1)} %get-tuple-element.14.assign_ref, f32[512,128]{1,0:T(8,128)S(1)} %bitcast.5, ...), custom_call_target="tpu_custom_call" | custom-call | tf_op jit(solution)/shard_map/first_and_coef_pass/pallas_call | solution.py:313
  46.7 11.1 %all_to_all.22.parts_ref = f32[16,4,640]{2,1,0:T(4,128)S(1)} all-to-all(f32[16,4,640]{2,1,0:T(4,128)S(1)} %broadcast_in_dim.10), channel_id=1, replica_groups=mesh['groups'=2,'dev'=16] {'dev'}, dimensions={0} | all-to-all | bytes 327680 | tf_op jit(solution)/shard_map/all_to_all | solution.py:294
  57.7 2.9 %link_product.3 = bf16[4,128]{1,0:T(4,128)(2,1)S(1)} custom-call(s32[64]{0:T(128)S(1)} %copy-done.2, s32[4,64]{1,0:T(4,128)S(1)} %copy-done.3, f32[16,4,640]{2,1,0:T(4,128)S(1)} %all_to_all.22.parts_ref, bf16[4,64,128,128]{3,2,1,0:T(8,128)(2,1)S(1)} %get-tuple-element.17.refs_0_), custom_call_target="tpu_custom_call" | custom-call | tf_op jit(solution)/shard_map/link_product/pallas_call | solution.py:297
  60.6 9.1 %all_to_all.23.mixed_ref = bf16[16,4,128]{2,1,0:T(4,128)(2,1)S(1)} all-to-all(bf16[16,4,128]{2,1,0:T(4,128)(2,1)S(1)} %broadcast_in_dim.11), channel_id=1, replica_groups=mesh['groups'=2,'dev'=16] {'dev'}, dimensions={0} | all-to-all | bytes 32768 | tf_op jit(solution)/shard_map/all_to_all | solution.py:294
  69.7 5.3 %last_pass.1 = f32[512,128]{1,0:T(8,128)} custom-call(s32[1,64]{1,0:T(1,128)S(1)} %bitcast.8, bf16[16,4,128]{2,1,0:T(4,128)(2,1)S(1)} %all_to_all.23.mixed_ref, s32[512,128]{1,0:T(8,128)S(1)} %get-tuple-element.14.assign_ref, f32[512,128]{1,0:T(8,128)S(1)} %get-tuple-element.18.first_ref, bf16[128,65536]{1,0:T(8,128)(2,1)S(1)} %get-tuple-element.15.turned_ref), custom_call_target="tpu_custom_call" | custom-call | tf_op jit(solution)/shard_map/last_pass/pallas_call | solution.py:335
  (4 shorter events, 0.1 us)
Async XLA Ops:
  0.0 38.3 %copy-start = (f32[65536]{0:T(1024)S(1)}, f32[65536]{0:T(1024)}, u32[]{:S(2)}) copy-start(f32[65536]{0:T(1024)} %param.9) | copy-start | bytes 786436
  0.0 0.7 copy-start.1
  0.7 24.1 %copy-start.2 = (s32[64]{0:T(128)S(1)}, s32[64]{0:T(128)}, u32[]{:S(2)}) copy-start(s32[64]{0:T(128)} %slot_of_ref.3) | copy-start | bytes 772
  0.7 24.1 %copy-start.3 = (s32[4,64]{1,0:T(4,128)S(1)}, s32[4,64]{1,0:T(4,128)}, u32[]{:S(2)}) copy-start(s32[4,64]{1,0:T(4,128)} %partners_ref.3) | copy-start | bytes 3076

commit v5 on v4

--- a/solution.py
+++ b/solution.py
@@ -15,9 +15,10 @@
 LANES = 128
 ROWS = 24
 
-COPY = 4096
+COPY = 2048
 TILE = 2048
-SLOTS = 4
+SLOTS = 8
+PIECES = 4
 
 ridge = 0.5
 
@@ -44,7 +45,7 @@
 
 def put_sums(per_dev, sum_ref, out_ref):
     for g in range(NEAR):
-        out_ref[:, g * LANES : (g + 1) * LANES] = sum_ref[g * per_dev : (g + 1) * per_dev, :]
+        out_ref[:, g * LANES : (g + 1) * LANES] = sum_ref[g * per_dev : (g + 1) * per_dev, :].astype(jnp.bfloat16)
 
 
 def slot_copy(basis_hbm, slots_ref, sem, c):
@@ -62,21 +63,24 @@
 
 
 def coef_kernel(
-    devices, per_dev, slot_of_ref, assign_hbm, vector_hbm, basis_hbm,
+    devices, per_dev, slot_of_hbm, assign_hbm, vector_hbm, basis_hbm,
     out_ref, turned_ref, assign_ref,
-    cl_ref, sum_ref, vector_ref, x_ref, slots_ref, small_sem, basis_sem,
+    slot_of_ref, cl_ref, sum_ref, vector_ref, x_ref, slots_ref, small_sem, basis_sem,
 ):
     copies = basis_hbm.shape[0] // COPY
 
     def basis_copy(c):
         return slot_copy(basis_hbm, slots_ref, basis_sem, c)
 
+    slot_of_copy = pltpu.make_async_copy(slot_of_hbm, slot_of_ref, small_sem.at[2])
     assign_copy = pltpu.make_async_copy(assign_hbm, assign_ref, small_sem.at[0])
     vector_copy = pltpu.make_async_copy(vector_hbm, vector_ref, small_sem.at[1])
+    slot_of_copy.start()
     assign_copy.start()
     vector_copy.start()
     for c in range(SLOTS):
         basis_copy(c).start()
+    slot_of_copy.wait()
     near_clusters(devices, per_dev, slot_of_ref, cl_ref)
     sum_ref[...] = jnp.zeros_like(sum_ref)
     assign_copy.wait()
@@ -113,20 +117,20 @@
     else:
         links_ref, out_ref, scaled_ref, mixed_ref = refs
     n_links = links_ref.shape[1]
-    halves = (0, 1)
-
-    def half_copy(j, h):
-        ks = pl.ds(h * (n_links // 2), n_links // 2)
-        return pltpu.make_async_copy(links_hbm.at[j, ks], links_ref.at[j, ks], links_sem.at[2 * j + h])
+    piece = n_links // PIECES
+
+    def piece_copy(j, h):
+        ks = pl.ds(h * piece, piece)
+        return pltpu.make_async_copy(links_hbm.at[j, ks], links_ref.at[j, ks], links_sem.at[PIECES * j + h])
 
     if first_time:
         for j in range(per_dev):
-            for h in halves:
-                half_copy(j, h).start()
+            for h in range(PIECES):
+                piece_copy(j, h).start()
     for owner in range(devices):
-        coef = parts_ref[(owner + REACH) % devices, :, :LANES]
+        coef = parts_ref[(owner + REACH) % devices, :, :LANES].astype(jnp.float32)
         for g in range(1, NEAR):
-            coef += parts_ref[(owner + REACH - g) % devices, :, g * LANES : (g + 1) * LANES]
+            coef += parts_ref[(owner + REACH - g) % devices, :, g * LANES : (g + 1) * LANES].astype(jnp.float32)
         scaled_ref[owner * per_dev : (owner + 1) * per_dev, :] = (coef * norm).astype(jnp.bfloat16).astype(jnp.float32)
     mixed_ref[...] = jnp.zeros_like(mixed_ref)
     for j in range(per_dev):
@@ -135,10 +139,10 @@
             return acc + links_ref[j, k].astype(jnp.float32) * scaled_ref[pl.ds(s, 1), :]
 
         acc = jnp.zeros(links_ref.shape[2:], jnp.float32)
-        for h in halves:
+        for h in range(PIECES):
             if first_time:
-                half_copy(j, h).wait()
-            acc = lax.fori_loop(h * (n_links // 2), (h + 1) * (n_links // 2), body, acc, unroll=8)
+                piece_copy(j, h).wait()
+            acc = lax.fori_loop(h * piece, (h + 1) * piece, body, acc, unroll=8)
         mixed_ref[j : j + 1, :] = jnp.sum(acc.T, axis=0, keepdims=True)
     out_ref[...] = mixed_ref[:per_dev, :].astype(jnp.bfloat16)
 
@@ -152,7 +156,7 @@
     first_ref, out_ref, cl_ref, rows_ref, sum_ref, slope_ref, even_ref, odd_ref, even_left, odd_left, slots_ref, basis_sem,
 ):
     tiles = turned_ref.shape[1] // TILE
-    copies = tiles // 2
+    copies = tiles
 
     def basis_copy(c):
         return slot_copy(basis_hbm, slots_ref, basis_sem, c)
@@ -182,7 +186,8 @@
             left_of[side][:, at] = jnp.where(hit, weighted, 0.0).astype(jnp.bfloat16)
 
     def add_up(c, side):
-        block = slots_ref[lax.rem(c, SLOTS), side * TILE : (side + 1) * TILE, :]
+        basis_copy(c).wait()
+        block = slots_ref[lax.rem(c, SLOTS)]
         sum_ref[...] += jnp.dot(left_of[side][...], block, preferred_element_type=jnp.float32)
 
     multiply(0, 0)
@@ -192,20 +197,19 @@
     @pl.loop(0, tiles // 2 - 1)
     def _(i):
         t = 2 * i + 2
-        basis_copy(i).wait()
-        add_up(i, 0)
+        add_up(t - 2, 0)
         multiply(t, 0)
         select(t - 1, 1)
-        add_up(i, 1)
+        add_up(t - 1, 1)
         multiply(t + 1, 1)
         select(t, 0)
 
-        @pl.when(i + SLOTS < copies)
+        @pl.when(t - 2 + SLOTS < copies)
         def _():
-            basis_copy(i + SLOTS).start()
-
-    basis_copy(copies - 1).wait()
-    add_up(copies - 1, 0)
+            basis_copy(t - 2 + SLOTS).start()
+            basis_copy(t - 1 + SLOTS).start()
+
+    add_up(copies - 2, 0)
     select(tiles - 1, 1)
     add_up(copies - 1, 1)
     put_sums(per_dev, sum_ref, out_ref)
@@ -264,12 +268,12 @@
     vmem = pl.BlockSpec(memory_space=pltpu.VMEM)
     smem = pl.BlockSpec(memory_space=pltpu.SMEM)
     hbm = pl.BlockSpec(memory_space=pltpu.HBM)
-    coef_shape = jax.ShapeDtypeStruct((per_dev, NEAR * rank), f32)
+    coef_shape = jax.ShapeDtypeStruct((per_dev, NEAR * rank), bf16)
     params = pltpu.CompilerParams(vmem_limit_bytes=8 * 1024 * 1024)
 
     coef1, turned_v, assign_v = pl.pallas_call(
         functools.partial(coef_kernel, devices, per_dev),
-        in_specs=[vmem, hbm, hbm, hbm],
+        in_specs=[hbm] * 4,
         out_specs=[vmem] * 3,
         out_shape=[
             coef_shape,
@@ -277,17 +281,18 @@
             pltpu.VMEM((high, LANES), jnp.int32),
         ],
         scratch_shapes=[
+            pltpu.VMEM((1, clusters), jnp.int32),
             pltpu.VMEM((ROWS, LANES), jnp.int32),
             pltpu.VMEM((ROWS, rank), f32),
             pltpu.VMEM((high, LANES), bf16),
             pltpu.VMEM((high, LANES), f32),
             pltpu.VMEM((SLOTS, COPY, rank), bf16),
-            pltpu.SemaphoreType.DMA((2,)),
+            pltpu.SemaphoreType.DMA((3,)),
             pltpu.SemaphoreType.DMA((SLOTS,)),
         ],
         compiler_params=params,
         name="coef_pass",
-    )(slot_row, far(assign), far(vector), far(basis_rows))
+    )(far(slot_row), far(assign), far(vector), far(basis_rows))
 
     def to_all(block):
         copies = jnp.broadcast_to(block[None], (devices,) + block.shape)
@@ -303,7 +308,7 @@
                 pltpu.VMEM((clusters, rank), f32),
                 pltpu.VMEM((8, rank), f32),
             ]
-            + [pltpu.SemaphoreType.DMA((2 * per_dev,))] * first_time,
+            + [pltpu.SemaphoreType.DMA((PIECES * per_dev,))] * first_time,
             compiler_params=params,
             name="link_product",
         )(slot_of, partners, to_all(coef), links)

time: 75.3 us -> 75.7 us (level)
  Pallas kernels: 29.3 us -> 33.1 us
  blocking collectives: 44.8 us -> 42.2 us
    all_to_all x4, blocking collectives: 44.8 us -> 42.2 us  [to_all(): return lax.all_to_all(copies, 'dev', 0, 0, tiled=True)]
    pallas_call x1, Pallas kernels: 8.34 us -> 10.8 us  [shards(): pl.pallas_call(functools.partial(both_kernel, devices, per_dev), in_specs...]
    pallas_call x1, Pallas kernels: 8.42 us -> 9.87 us  [shards(): pl.pallas_call(functools.partial(coef_kernel, devices, per_dev), in_specs...]
where the time goes in v5:
time: 75.7 us; the launch traced here: 75.5 us
  blocking collectives  42.2 us (56%)
  Pallas kernels  33.1 us (44%)
    all_to_all x4, blocking collectives, to_all(): return lax.all_to_all(copies, 'dev', 0, 0, tiled=True)  42.2 us
    pallas_call x1, Pallas kernels, shards(): pl.pallas_call(functools.partial(both_kernel, devices, per_dev), in_specs...  10.8 us
    pallas_call x1, Pallas kernels, shards(): pl.pallas_call(functools.partial(coef_kernel, devices, per_dev), in_specs...  9.87 us
    pallas_call x2, Pallas kernels, mix(): pl.pallas_call(functools.partial(link_kernel, norm, devices, per_dev, fir...  7.19 us
    pallas_call x1, Pallas kernels, shards(): pl.pallas_call(functools.partial(last_kernel, devices, per_dev), in_specs...  5.28 us

profile of v5, /device:TPU:0, one launch (start us, length us, event | category | flops | bytes accessed | tf_op | source)
XLA Modules:
  0.0 75.5 jit_solution(3097539612529869583)
XLA Ops:
  0.0 0.0 copy-start.1
  0.0 0.0 copy-start.2
  0.0 0.0 copy-start
  0.0 9.9 %coef_pass.1 = (bf16[4,640]{1,0:T(4,128)(2,1)S(1)}, bf16[128,65536]{1,0:T(8,128)(2,1)S(1)}, s32[512,128]{1,0:T(8,128)S(1)}) custom-call(s32[1,64]{1,0:T(1,128)} %bitcast.6, s32[512,128]{1,0:T(8,128)} %bitcast.9, bf16[512,128]{1,0:T(8,128)(2,1)} %bitcast.10, bf16[65536,128]{1,0:T(8,128)(2,1)} %basis_hbm.3), custom_call_target="tpu_custom_call" | custom-call | tf_op jit(solution)/shard_map/coef_pass/pallas_call | solution.py:274
  9.9 14.4 %all_to_all.20.parts_ref = bf16[16,4,640]{2,1,0:T(4,128)(2,1)S(1)} all-to-all(bf16[16,4,640]{2,1,0:T(4,128)(2,1)S(1)} %broadcast_in_dim.8), channel_id=1, replica_groups=mesh['groups'=2,'dev'=16] {'dev'}, dimensions={0} | all-to-all | bytes 163840 | tf_op jit(solution)/shard_map/all_to_all | solution.py:299
  24.3 0.0 copy-done.1
  24.3 0.0 copy-done.2
  24.3 4.3 %link_product.2 = (bf16[4,128]{1,0:T(4,128)(2,1)S(1)}, bf16[4,64,128,128]{3,2,1,0:T(8,128)(2,1)S(1)}) custom-call(s32[64]{0:T(128)S(1)} %copy-done.1, s32[4,64]{1,0:T(4,128)S(1)} %copy-done.2, bf16[16,4,640]{2,1,0:T(4,128)(2,1)S(1)} %all_to_all.20.parts_ref, bf16[4,64,128,128]{3,2,1,0:T(8,128)(2,1)} %refs_0_.1), custom_call_target="tpu_custom_call" | custom-call | tf_op jit(solution)/shard_map/link_product/pallas_call | solution.py:302
  28.6 9.1 %all_to_all.21.mixed_ref = bf16[16,4,128]{2,1,0:T(4,128)(2,1)S(1)} all-to-all(bf16[16,4,128]{2,1,0:T(4,128)(2,1)S(1)} %broadcast_in_dim.9), channel_id=1, replica_groups=mesh['groups'=2,'dev'=16] {'dev'}, dimensions={0} | all-to-all | bytes 32768 | tf_op jit(solution)/shard_map/all_to_all | solution.py:299
  37.7 0.0 copy-done
  37.7 10.8 %first_and_coef_pass.1 = (f32[512,128]{1,0:T(8,128)S(1)}, bf16[4,640]{1,0:T(4,128)(2,1)S(1)}) custom-call(s32[1,64]{1,0:T(1,128)S(1)} %bitcast.7, bf16[16,4,128]{2,1,0:T(4,128)(2,1)S(1)} %all_to_all.21.mixed_ref, s32[512,128]{1,0:T(8,128)S(1)} %get-tuple-element.14.assign_ref, f32[512,128]{1,0:T(8,128)S(1)} %bitcast.5, ...), custom_call_target="tpu_custom_call" | custom-call | tf_op jit(solution)/shard_map/first_and_coef_pass/pallas_call | solution.py:318
  48.5 9.7 %all_to_all.22.parts_ref = bf16[16,4,640]{2,1,0:T(4,128)(2,1)S(1)} all-to-all(bf16[16,4,640]{2,1,0:T(4,128)(2,1)S(1)} %broadcast_in_dim.10), channel_id=1, replica_groups=mesh['groups'=2,'dev'=16] {'dev'}, dimensions={0} | all-to-all | bytes 163840 | tf_op jit(solution)/shard_map/all_to_all | solution.py:299
  58.2 2.9 %link_product.3 = bf16[4,128]{1,0:T(4,128)(2,1)S(1)} custom-call(s32[64]{0:T(128)S(1)} %copy-done.1, s32[4,64]{1,0:T(4,128)S(1)} %copy-done.2, bf16[16,4,640]{2,1,0:T(4,128)(2,1)S(1)} %all_to_all.22.parts_ref, bf16[4,64,128,128]{3,2,1,0:T(8,128)(2,1)S(1)} %get-tuple-element.17.refs_0_), custom_call_target="tpu_custom_call" | custom-call | tf_op jit(solution)/shard_map/link_product/pallas_call | solution.py:302
  61.1 9.1 %all_to_all.23.mixed_ref = bf16[16,4,128]{2,1,0:T(4,128)(2,1)S(1)} all-to-all(bf16[16,4,128]{2,1,0:T(4,128)(2,1)S(1)} %broadcast_in_dim.11), channel_id=1, replica_groups=mesh['groups'=2,'dev'=16] {'dev'}, dimensions={0} | all-to-all | bytes 32768 | tf_op jit(solution)/shard_map/all_to_all | solution.py:299
  70.2 5.3 %last_pass.1 = f32[512,128]{1,0:T(8,128)} custom-call(s32[1,64]{1,0:T(1,128)S(1)} %bitcast.8, bf16[16,4,128]{2,1,0:T(4,128)(2,1)S(1)} %all_to_all.23.mixed_ref, s32[512,128]{1,0:T(8,128)S(1)} %get-tuple-element.14.assign_ref, f32[512,128]{1,0:T(8,128)S(1)} %get-tuple-element.18.first_ref, bf16[128,65536]{1,0:T(8,128)(2,1)S(1)} %get-tuple-element.15.turned_ref), custom_call_target="tpu_custom_call" | custom-call | tf_op jit(solution)/shard_map/last_pass/pallas_call | solution.py:340
  (4 shorter events, 0.1 us)
Async XLA Ops:
  0.0 24.3 %copy-start.1 = (s32[64]{0:T(128)S(1)}, s32[64]{0:T(128)}, u32[]{:S(2)}) copy-start(s32[64]{0:T(128)} %slot_of_ref.3) | copy-start | bytes 772
  0.0 24.3 %copy-start.2 = (s32[4,64]{1,0:T(4,128)S(1)}, s32[4,64]{1,0:T(4,128)}, u32[]{:S(2)}) copy-start(s32[4,64]{1,0:T(4,128)} %partners_ref.3) | copy-start | bytes 3076
  0.0 37.7 %copy-start = (f32[65536]{0:T(1024)S(1)}, f32[65536]{0:T(1024)}, u32[]{:S(2)}) copy-start(f32[65536]{0:T(1024)} %param.9) | copy-start | bytes 786436

commit v6 on v5

--- a/solution.py
+++ b/solution.py
@@ -15,9 +15,12 @@
 LANES = 128
 ROWS = 24
 
-COPY = 2048
+COPY = 8192
 TILE = 2048
-SLOTS = 8
+PER_COPY = COPY // TILE
+SLOTS = 3
+INNER = 4
+BODY = 8
 PIECES = 4
 
 ridge = 0.5
@@ -92,8 +95,8 @@
     def _(c):
         basis_copy(c).wait()
         total = sum_ref[...]
-        for p in range(COPY // TILE):
-            t = c * (COPY // TILE) + p
+        for p in range(PER_COPY):
+            t = c * PER_COPY + p
             parts = []
             for i in range(TILE // LANES):
                 hit = assign_ref[row_at(t, i), :] == cl
@@ -156,7 +159,7 @@
     first_ref, out_ref, cl_ref, rows_ref, sum_ref, slope_ref, even_ref, odd_ref, even_left, odd_left, slots_ref, basis_sem,
 ):
     tiles = turned_ref.shape[1] // TILE
-    copies = tiles
+    copies = tiles // PER_COPY
 
     def basis_copy(c):
         return slot_copy(basis_hbm, slots_ref, basis_sem, c)
@@ -185,33 +188,35 @@
             weighted = slope_ref[row_at(t, i), :] * first
             left_of[side][:, at] = jnp.where(hit, weighted, 0.0).astype(jnp.bfloat16)
 
-    def add_up(c, side):
-        basis_copy(c).wait()
-        block = slots_ref[lax.rem(c, SLOTS)]
-        sum_ref[...] += jnp.dot(left_of[side][...], block, preferred_element_type=jnp.float32)
+    def add_up(c, p):
+        block = slots_ref[lax.rem(c, SLOTS), p * TILE : (p + 1) * TILE, :]
+        sum_ref[...] += jnp.dot(left_of[p % 2][...], block, preferred_element_type=jnp.float32)
 
     multiply(0, 0)
     select(0, 0)
     multiply(1, 1)
 
-    @pl.loop(0, tiles // 2 - 1)
-    def _(i):
-        t = 2 * i + 2
-        add_up(t - 2, 0)
-        multiply(t, 0)
-        select(t - 1, 1)
-        add_up(t - 1, 1)
-        multiply(t + 1, 1)
-        select(t, 0)
-
-        @pl.when(t - 2 + SLOTS < copies)
+    @pl.loop(0, copies - 1)
+    def _(c):
+        basis_copy(c).wait()
+        for p in range(PER_COPY):
+            t = c * PER_COPY + p
+            add_up(c, p)
+            multiply(t + 2, p % 2)
+            select(t + 1, (p + 1) % 2)
+
+        @pl.when(c + SLOTS < copies)
         def _():
-            basis_copy(t - 2 + SLOTS).start()
-            basis_copy(t - 1 + SLOTS).start()
-
-    add_up(copies - 2, 0)
-    select(tiles - 1, 1)
-    add_up(copies - 1, 1)
+            basis_copy(c + SLOTS).start()
+
+    basis_copy(copies - 1).wait()
+    for p in range(PER_COPY):
+        t = (copies - 1) * PER_COPY + p
+        add_up(copies - 1, p)
+        if p + 2 < PER_COPY:
+            multiply(t + 2, p % 2)
+        if p + 1 < PER_COPY:
+            select(t + 1, (p + 1) % 2)
     put_sums(per_dev, sum_ref, out_ref)
 
 
@@ -236,17 +241,12 @@
 
     multiply(0, 0)
 
-    @pl.loop(0, tiles // 2 - 1)
-    def _(i):
-        t = 2 * i + 1
-        multiply(t, 1)
-        select(t - 1, 0)
-        multiply(t + 1, 0)
-        select(t, 1)
-
-    multiply(tiles - 1, 1)
-    select(tiles - 2, 0)
-    select(tiles - 1, 1)
+    @pl.loop(0, tiles // BODY)
+    def _(c):
+        for p in range(BODY):
+            t = c * BODY + p
+            multiply(lax.rem(t + 1, tiles), (p + 1) % 2)
+            select(t, p % 2)
 
 
 def shards(basis_rows, vector, scores, assign, slot_of, partners, link_blocks):
@@ -269,7 +269,7 @@
     smem = pl.BlockSpec(memory_space=pltpu.SMEM)
     hbm = pl.BlockSpec(memory_space=pltpu.HBM)
     coef_shape = jax.ShapeDtypeStruct((per_dev, NEAR * rank), bf16)
-    params = pltpu.CompilerParams(vmem_limit_bytes=8 * 1024 * 1024)
+    params = pltpu.CompilerParams(vmem_limit_bytes=10 * 1024 * 1024)
 
     coef1, turned_v, assign_v = pl.pallas_call(
         functools.partial(coef_kernel, devices, per_dev),
@@ -298,7 +298,18 @@
         copies = jnp.broadcast_to(block[None], (devices,) + block.shape)
         return lax.all_to_all(copies, "dev", 0, 0, tiled=True)
 
+    def to_all_by_phases(block):
+        outer = devices // INNER
+        near_by = [[o * INNER + i for i in range(INNER)] for o in range(outer)]
+        across = [[o * INNER + i for o in range(outer)] for i in range(INNER)]
+        copies = jnp.broadcast_to(block[None], (INNER,) + block.shape)
+        block = lax.all_to_all(copies, "dev", 0, 0, axis_index_groups=near_by, tiled=True)
+        copies = jnp.broadcast_to(block[None], (outer,) + block.shape)
+        copies = lax.all_to_all(copies, "dev", 0, 0, axis_index_groups=across, tiled=True)
+        return copies.reshape((devices,) + block.shape[1:])
+
     def mix(coef, links, first_time):
+        send = to_all if first_time else to_all_by_phases
         out = pl.pallas_call(
             functools.partial(link_kernel, norm, devices, per_dev, first_time),
             in_specs=[smem, smem, vmem, hbm if first_time else vmem],
@@ -311,8 +322,8 @@
             + [pltpu.SemaphoreType.DMA((PIECES * per_dev,))] * first_time,
             compiler_params=params,
             name="link_product",
-        )(slot_of, partners, to_all(coef), links)
-        return (to_all(out[0]), *out[1:])
+        )(slot_of, partners, send(coef), links)
+        return (send(out[0]), *out[1:])
 
     mixed1, links_v = mix(coef1, far(link_blocks), True)
     first, coef2 = pl.pallas_call(

time: 75.7 us -> 79.6 us (1.052)
  blocking collectives: 42.2 us -> 51.9 us
  Pallas kernels: 33.1 us -> 27.2 us
    all_to_all x0 -> x4, blocking collectives: none -> 28.5 us  [the longest x2 16.1 us: to_all_by_phases(): lax.all_to_all(copies, 'dev', 0, 0, axis_index_groups=across, tiled=True)]
    all_to_all x4 -> x2, blocking collectives: 42.2 us -> 23.4 us  [to_all(): return lax.all_to_all(copies, 'dev', 0, 0, tiled=True)]
    pallas_call x1, Pallas kernels: 10.8 us -> 7.74 us  [shards(): pl.pallas_call(functools.partial(both_kernel, devices, per_dev), in_specs...]
    pallas_call x1, Pallas kernels: 9.87 us -> 8.21 us  [shards(): pl.pallas_call(functools.partial(coef_kernel, devices, per_dev), in_specs...]
    pallas_call x1, Pallas kernels: 5.28 us -> 4.08 us  [shards(): pl.pallas_call(functools.partial(last_kernel, devices, per_dev), in_specs...]
where the time goes in v6:
time: 79.6 us; the launch traced here: 79.3 us
  blocking collectives  51.9 us (65%)
  Pallas kernels  27.2 us (34%)
    all_to_all x2, blocking collectives, to_all(): return lax.all_to_all(copies, 'dev', 0, 0, tiled=True)  23.4 us
    all_to_all x2, blocking collectives, to_all_by_phases(): lax.all_to_all(copies, 'dev', 0, 0, axis_index_groups=across, tiled=True)  16.1 us
    all_to_all x2, blocking collectives, to_all_by_phases(): lax.all_to_all(copies, 'dev', 0, 0, axis_index_groups=near_by, tiled=True)  12.4 us
    pallas_call x1, Pallas kernels, shards(): pl.pallas_call(functools.partial(coef_kernel, devices, per_dev), in_specs...  8.21 us
    pallas_call x1, Pallas kernels, shards(): pl.pallas_call(functools.partial(both_kernel, devices, per_dev), in_specs...  7.74 us
    pallas_call x2, Pallas kernels, mix(): pl.pallas_call(functools.partial(link_kernel, norm, devices, per_dev, fir...  7.19 us
    pallas_call x1, Pallas kernels, shards(): pl.pallas_call(functools.partial(last_kernel, devices, per_dev), in_specs...  4.08 us

profile of v6, /device:TPU:0, one launch (start us, length us, event | category | flops | bytes accessed | tf_op | source)
XLA Modules:
  0.0 79.3 jit_solution(15495155276064517232)
XLA Ops:
  0.0 0.0 copy-start.1
  0.0 0.0 copy-start.2
  0.0 0.0 copy-start
  0.0 8.2 %coef_pass.1 = (bf16[4,640]{1,0:T(4,128)(2,1)S(1)}, bf16[128,65536]{1,0:T(8,128)(2,1)S(1)}, s32[512,128]{1,0:T(8,128)S(1)}) custom-call(s32[1,64]{1,0:T(1,128)} %bitcast.10, s32[512,128]{1,0:T(8,128)} %bitcast.13, bf16[512,128]{1,0:T(8,128)(2,1)} %bitcast.14, bf16[65536,128]{1,0:T(8,128)(2,1)} %basis_hbm.3), custom_call_target="tpu_custom_call" | custom-call | tf_op jit(solution)/shard_map/coef_pass/pallas_call | solution.py:274
  8.3 14.3 %all_to_all.30.parts_ref = bf16[16,4,640]{2,1,0:T(4,128)(2,1)S(1)} all-to-all(bf16[16,4,640]{2,1,0:T(4,128)(2,1)S(1)} %broadcast_in_dim.12), channel_id=1, replica_groups=mesh['groups'=2,'dev'=16] {'dev'}, dimensions={0} | all-to-all | bytes 163840 | tf_op jit(solution)/shard_map/all_to_all | solution.py:299
  22.6 0.0 copy-done.1
  22.6 0.0 copy-done.2
  22.6 4.3 %link_product.2 = (bf16[4,128]{1,0:T(4,128)(2,1)S(1)}, bf16[4,64,128,128]{3,2,1,0:T(8,128)(2,1)S(1)}) custom-call(s32[64]{0:T(128)S(1)} %copy-done.1, s32[4,64]{1,0:T(4,128)S(1)} %copy-done.2, bf16[16,4,640]{2,1,0:T(4,128)(2,1)S(1)} %all_to_all.30.parts_ref, bf16[4,64,128,128]{3,2,1,0:T(8,128)(2,1)} %refs_0_.1), custom_call_target="tpu_custom_call" | custom-call | tf_op jit(solution)/shard_map/link_product/pallas_call | solution.py:313
  26.9 9.1 %all_to_all.31.mixed_ref = bf16[16,4,128]{2,1,0:T(4,128)(2,1)S(1)} all-to-all(bf16[16,4,128]{2,1,0:T(4,128)(2,1)S(1)} %broadcast_in_dim.13), channel_id=1, replica_groups=mesh['groups'=2,'dev'=16] {'dev'}, dimensions={0} | all-to-all | bytes 32768 | tf_op jit(solution)/shard_map/all_to_all | solution.py:299
  36.0 0.0 copy-done
  36.0 7.7 %first_and_coef_pass.1 = (f32[512,128]{1,0:T(8,128)S(1)}, bf16[4,640]{1,0:T(4,128)(2,1)S(1)}) custom-call(s32[1,64]{1,0:T(1,128)S(1)} %bitcast.11, bf16[16,4,128]{2,1,0:T(4,128)(2,1)S(1)} %all_to_all.31.mixed_ref, s32[512,128]{1,0:T(8,128)S(1)} %get-tuple-element.14.assign_ref, f32[512,128]{1,0:T(8,128)S(1)} %bitcast.8, ...), custom_call_target="tpu_custom_call" | custom-call | tf_op jit(solution)/shard_map/first_and_coef_pass/pallas_call | solution.py:329
  43.8 6.2 %all_to_all.32 = bf16[4,4,640]{2,1,0:T(4,128)(2,1)S(1)} all-to-all(bf16[4,4,640]{2,1,0:T(4,128)(2,1)S(1)} %broadcast_in_dim.14), channel_id=1, replica_groups={{0,1,2,3},{4,5,6,7},{8,9,10,11},{12,13,14,15},{16,17,18,19},{20,21,22,2..., dimensions={0} | all-to-all | bytes 40960 | tf_op jit(solution)/shard_map/all_to_all | solution.py:306
  50.0 8.2 %all_to_all.33 = bf16[4,4,4,640]{3,2,1,0:T(4,128)(2,1)S(1)} all-to-all(bf16[4,4,4,640]{3,2,1,0:T(4,128)(2,1)S(1)} %broadcast_in_dim.15), channel_id=1, replica_groups={{0,4,8,12},{1,5,9,13},{2,6,10,14},{3,7,11,15},{16,20,24,28},{17,21,25,2..., dimensions={0} | all-to-all | bytes 163840 | tf_op jit(solution)/shard_map/all_to_all | solution.py:308
  58.2 2.9 %link_product.3 = bf16[4,128]{1,0:T(4,128)(2,1)S(1)} custom-call(s32[64]{0:T(128)S(1)} %copy-done.1, s32[4,64]{1,0:T(4,128)S(1)} %copy-done.2, bf16[16,4,640]{2,1,0:T(4,128)(2,1)S(1)} %bitcast.7, bf16[4,64,128,128]{3,2,1,0:T(8,128)(2,1)S(1)} %get-tuple-element.17.refs_0_), custom_call_target="tpu_custom_call" | custom-call | tf_op jit(solution)/shard_map/link_product/pallas_call | solution.py:313
  61.1 6.1 %all_to_all.34 = bf16[4,4,128]{2,1,0:T(4,128)(2,1)S(1)} all-to-all(bf16[4,4,128]{2,1,0:T(4,128)(2,1)S(1)} %broadcast_in_dim.16), channel_id=1, replica_groups={{0,1,2,3},{4,5,6,7},{8,9,10,11},{12,13,14,15},{16,17,18,19},{20,21,22,2..., dimensions={0} | all-to-all | bytes 8192 | tf_op jit(solution)/shard_map/all_to_all | solution.py:306
  67.2 8.0 %all_to_all.35 = bf16[4,4,4,128]{3,2,1,0:T(4,128)(2,1)S(1)} all-to-all(bf16[4,4,4,128]{3,2,1,0:T(4,128)(2,1)S(1)} %broadcast_in_dim.17), channel_id=1, replica_groups={{0,4,8,12},{1,5,9,13},{2,6,10,14},{3,7,11,15},{16,20,24,28},{17,21,25,2..., dimensions={0} | all-to-all | bytes 32768 | tf_op jit(solution)/shard_map/all_to_all | solution.py:308
  75.2 4.1 %last_pass.1 = f32[512,128]{1,0:T(8,128)} custom-call(s32[1,64]{1,0:T(1,128)S(1)} %bitcast.12, bf16[16,4,128]{2,1,0:T(4,128)(2,1)S(1)} %bitcast.9, s32[512,128]{1,0:T(8,128)S(1)} %get-tuple-element.14.assign_ref, f32[512,128]{1,0:T(8,128)S(1)} %get-tuple-element.18.first_ref, bf16[128,65536]{1,0:T(8,128)(2,1)S(1)} %get-tuple-element.15.turned_ref), custom_call_target="tpu_custom_call" | custom-call | tf_op jit(solution)/shard_map/last_pass/pallas_call | solution.py:351
  (6 shorter events, 0.1 us)
Async XLA Ops:
  0.0 22.6 %copy-start.1 = (s32[64]{0:T(128)S(1)}, s32[64]{0:T(128)}, u32[]{:S(2)}) copy-start(s32[64]{0:T(128)} %slot_of_ref.3) | copy-start | bytes 772
  0.0 22.6 %copy-start.2 = (s32[4,64]{1,0:T(4,128)S(1)}, s32[4,64]{1,0:T(4,128)}, u32[]{:S(2)}) copy-start(s32[4,64]{1,0:T(4,128)} %partners_ref.3) | copy-start | bytes 3076
  0.0 36.0 %copy-start = (f32[65536]{0:T(1024)S(1)}, f32[65536]{0:T(1024)}, u32[]{:S(2)}) copy-start(f32[65536]{0:T(1024)} %param.9) | copy-start | bytes 786436

commit v7 on v6

--- a/solution.py
+++ b/solution.py
@@ -19,8 +19,7 @@
 TILE = 2048
 PER_COPY = COPY // TILE
 SLOTS = 3
-INNER = 4
-BODY = 8
+BODY = 16
 PIECES = 4
 
 ridge = 0.5
@@ -145,7 +144,7 @@
         for h in range(PIECES):
             if first_time:
                 piece_copy(j, h).wait()
-            acc = lax.fori_loop(h * piece, (h + 1) * piece, body, acc, unroll=8)
+            acc = lax.fori_loop(h * piece, (h + 1) * piece, body, acc, unroll=16)
         mixed_ref[j : j + 1, :] = jnp.sum(acc.T, axis=0, keepdims=True)
     out_ref[...] = mixed_ref[:per_dev, :].astype(jnp.bfloat16)
 
@@ -298,18 +297,7 @@
         copies = jnp.broadcast_to(block[None], (devices,) + block.shape)
         return lax.all_to_all(copies, "dev", 0, 0, tiled=True)
 
-    def to_all_by_phases(block):
-        outer = devices // INNER
-        near_by = [[o * INNER + i for i in range(INNER)] for o in range(outer)]
-        across = [[o * INNER + i for o in range(outer)] for i in range(INNER)]
-        copies = jnp.broadcast_to(block[None], (INNER,) + block.shape)
-        block = lax.all_to_all(copies, "dev", 0, 0, axis_index_groups=near_by, tiled=True)
-        copies = jnp.broadcast_to(block[None], (outer,) + block.shape)
-        copies = lax.all_to_all(copies, "dev", 0, 0, axis_index_groups=across, tiled=True)
-        return copies.reshape((devices,) + block.shape[1:])
-
     def mix(coef, links, first_time):
-        send = to_all if first_time else to_all_by_phases
         out = pl.pallas_call(
             functools.partial(link_kernel, norm, devices, per_dev, first_time),
             in_specs=[smem, smem, vmem, hbm if first_time else vmem],
@@ -322,8 +310,8 @@
             + [pltpu.SemaphoreType.DMA((PIECES * per_dev,))] * first_time,
             compiler_params=params,
             name="link_product",
-        )(slot_of, partners, send(coef), links)
-        return (send(out[0]), *out[1:])
+        )(slot_of, partners, to_all(coef), links)
+        return (to_all(out[0]), *out[1:])
 
     mixed1, links_v = mix(coef1, far(link_blocks), True)
     first, coef2 = pl.pallas_call(

time: 79.6 us -> 70.2 us (0.88)
  blocking collectives: 51.9 us -> 42.2 us
    all_to_all x4 -> x0, blocking collectives: 28.5 us -> none  [the longest x2 16.1 us: to_all_by_phases(): lax.all_to_all(copies, 'dev', 0, 0, axis_index_groups=across, tiled=True)]
    all_to_all x2 -> x4, blocking collectives: 23.4 us -> 42.2 us  [to_all(): return lax.all_to_all(copies, 'dev', 0, 0, tiled=True)]
where the time goes in v7:
time: 70.2 us; the launch traced here: 69.9 us
  blocking collectives  42.2 us (60%)
  Pallas kernels  27.6 us (39%)
    all_to_all x4, blocking collectives, to_all(): return lax.all_to_all(copies, 'dev', 0, 0, tiled=True)  42.2 us
    pallas_call x1, Pallas kernels, shards(): pl.pallas_call(functools.partial(coef_kernel, devices, per_dev), in_specs...  8.21 us
    pallas_call x2, Pallas kernels, mix(): pl.pallas_call(functools.partial(link_kernel, norm, devices, per_dev, fir...  7.91 us
    pallas_call x1, Pallas kernels, shards(): pl.pallas_call(functools.partial(both_kernel, devices, per_dev), in_specs...  7.74 us
    pallas_call x1, Pallas kernels, shards(): pl.pallas_call(functools.partial(last_kernel, devices, per_dev), in_specs...  3.74 us

profile of v7, /device:TPU:0, one launch (start us, length us, event | category | flops | bytes accessed | tf_op | source)
XLA Modules:
  0.0 69.9 jit_solution(6730104266241828330)
XLA Ops:
  0.0 0.0 copy-start.1
  0.0 0.0 copy-start.2
  0.0 0.0 copy-start
  0.0 8.2 %coef_pass.1 = (bf16[4,640]{1,0:T(4,128)(2,1)S(1)}, bf16[128,65536]{1,0:T(8,128)(2,1)S(1)}, s32[512,128]{1,0:T(8,128)S(1)}) custom-call(s32[1,64]{1,0:T(1,128)} %bitcast.6, s32[512,128]{1,0:T(8,128)} %bitcast.9, bf16[512,128]{1,0:T(8,128)(2,1)} %bitcast.10, bf16[65536,128]{1,0:T(8,128)(2,1)} %basis_hbm.3), custom_call_target="tpu_custom_call" | custom-call | tf_op jit(solution)/shard_map/coef_pass/pallas_call | solution.py:273
  8.3 14.3 %all_to_all.20.parts_ref = bf16[16,4,640]{2,1,0:T(4,128)(2,1)S(1)} all-to-all(bf16[16,4,640]{2,1,0:T(4,128)(2,1)S(1)} %broadcast_in_dim.8), channel_id=1, replica_groups=mesh['groups'=2,'dev'=16] {'dev'}, dimensions={0} | all-to-all | bytes 163840 | tf_op jit(solution)/shard_map/all_to_all | solution.py:298
  22.6 0.0 copy-done.1
  22.6 0.0 copy-done.2
  22.6 4.3 %link_product.2 = (bf16[4,128]{1,0:T(4,128)(2,1)S(1)}, bf16[4,64,128,128]{3,2,1,0:T(8,128)(2,1)S(1)}) custom-call(s32[64]{0:T(128)S(1)} %copy-done.1, s32[4,64]{1,0:T(4,128)S(1)} %copy-done.2, bf16[16,4,640]{2,1,0:T(4,128)(2,1)S(1)} %all_to_all.20.parts_ref, bf16[4,64,128,128]{3,2,1,0:T(8,128)(2,1)} %refs_0_.1), custom_call_target="tpu_custom_call" | custom-call | tf_op jit(solution)/shard_map/link_product/pallas_call | solution.py:301
  26.9 9.1 %all_to_all.21.mixed_ref = bf16[16,4,128]{2,1,0:T(4,128)(2,1)S(1)} all-to-all(bf16[16,4,128]{2,1,0:T(4,128)(2,1)S(1)} %broadcast_in_dim.9), channel_id=1, replica_groups=mesh['groups'=2,'dev'=16] {'dev'}, dimensions={0} | all-to-all | bytes 32768 | tf_op jit(solution)/shard_map/all_to_all | solution.py:298
  36.0 0.0 copy-done
  36.0 7.7 %first_and_coef_pass.1 = (f32[512,128]{1,0:T(8,128)S(1)}, bf16[4,640]{1,0:T(4,128)(2,1)S(1)}) custom-call(s32[1,64]{1,0:T(1,128)S(1)} %bitcast.7, bf16[16,4,128]{2,1,0:T(4,128)(2,1)S(1)} %all_to_all.21.mixed_ref, s32[512,128]{1,0:T(8,128)S(1)} %get-tuple-element.14.assign_ref, f32[512,128]{1,0:T(8,128)S(1)} %bitcast.5, ...), custom_call_target="tpu_custom_call" | custom-call | tf_op jit(solution)/shard_map/first_and_coef_pass/pallas_call | solution.py:317
  43.8 9.7 %all_to_all.22.parts_ref = bf16[16,4,640]{2,1,0:T(4,128)(2,1)S(1)} all-to-all(bf16[16,4,640]{2,1,0:T(4,128)(2,1)S(1)} %broadcast_in_dim.10), channel_id=1, replica_groups=mesh['groups'=2,'dev'=16] {'dev'}, dimensions={0} | all-to-all | bytes 163840 | tf_op jit(solution)/shard_map/all_to_all | solution.py:298
  53.5 3.6 %link_product.3 = bf16[4,128]{1,0:T(4,128)(2,1)S(1)} custom-call(s32[64]{0:T(128)S(1)} %copy-done.1, s32[4,64]{1,0:T(4,128)S(1)} %copy-done.2, bf16[16,4,640]{2,1,0:T(4,128)(2,1)S(1)} %all_to_all.22.parts_ref, bf16[4,64,128,128]{3,2,1,0:T(8,128)(2,1)S(1)} %get-tuple-element.17.refs_0_), custom_call_target="tpu_custom_call" | custom-call | tf_op jit(solution)/shard_map/link_product/pallas_call | solution.py:301
  57.1 9.1 %all_to_all.23.mixed_ref = bf16[16,4,128]{2,1,0:T(4,128)(2,1)S(1)} all-to-all(bf16[16,4,128]{2,1,0:T(4,128)(2,1)S(1)} %broadcast_in_dim.11), channel_id=1, replica_groups=mesh['groups'=2,'dev'=16] {'dev'}, dimensions={0} | all-to-all | bytes 32768 | tf_op jit(solution)/shard_map/all_to_all | solution.py:298
  66.2 3.7 %last_pass.1 = f32[512,128]{1,0:T(8,128)} custom-call(s32[1,64]{1,0:T(1,128)S(1)} %bitcast.8, bf16[16,4,128]{2,1,0:T(4,128)(2,1)S(1)} %all_to_all.23.mixed_ref, s32[512,128]{1,0:T(8,128)S(1)} %get-tuple-element.14.assign_ref, f32[512,128]{1,0:T(8,128)S(1)} %get-tuple-element.18.first_ref, bf16[128,65536]{1,0:T(8,128)(2,1)S(1)} %get-tuple-element.15.turned_ref), custom_call_target="tpu_custom_call" | custom-call | tf_op jit(solution)/shard_map/last_pass/pallas_call | solution.py:339
  (4 shorter events, 0.1 us)
Async XLA Ops:
  0.0 22.6 %copy-start.1 = (s32[64]{0:T(128)S(1)}, s32[64]{0:T(128)}, u32[]{:S(2)}) copy-start(s32[64]{0:T(128)} %slot_of_ref.3) | copy-start | bytes 772
  0.0 22.6 %copy-start.2 = (s32[4,64]{1,0:T(4,128)S(1)}, s32[4,64]{1,0:T(4,128)}, u32[]{:S(2)}) copy-start(s32[4,64]{1,0:T(4,128)} %partners_ref.3) | copy-start | bytes 3076
  0.0 36.0 %copy-start = (f32[65536]{0:T(1024)S(1)}, f32[65536]{0:T(1024)}, u32[]{:S(2)}) copy-start(f32[65536]{0:T(1024)} %param.9) | copy-start | bytes 786436

commit v8 on v7

--- a/solution.py
+++ b/solution.py
@@ -20,6 +20,8 @@
 PER_COPY = COPY // TILE
 SLOTS = 3
 BODY = 16
+FOLD = 4
+WIDE = LANES // FOLD
 PIECES = 4
 
 ridge = 0.5
@@ -144,7 +146,7 @@
         for h in range(PIECES):
             if first_time:
                 piece_copy(j, h).wait()
-            acc = lax.fori_loop(h * piece, (h + 1) * piece, body, acc, unroll=16)
+            acc = lax.fori_loop(h * piece, (h + 1) * piece, body, acc, unroll=8)
         mixed_ref[j : j + 1, :] = jnp.sum(acc.T, axis=0, keepdims=True)
     out_ref[...] = mixed_ref[:per_dev, :].astype(jnp.bfloat16)
 
@@ -153,12 +155,20 @@
     return jnp.sum(jnp.where(hit, products, 0.0), axis=0, keepdims=True)
 
 
+def side_by_side(rows_ref, table_ref):
+    rank = rows_ref.shape[1]
+    for q in range(FOLD):
+        pads = [jnp.zeros((q * WIDE, rank), jnp.float32), rows_ref[...], jnp.zeros((LANES - q * WIDE - ROWS, rank), jnp.float32)]
+        tall = jnp.concatenate([p for p in pads if p.shape[0]], axis=0)
+        table_ref[q * rank : (q + 1) * rank, :] = tall.T.astype(jnp.bfloat16)
+
+
 def both_kernel(
-    devices, per_dev, slot_of_ref, mixed_ref, assign_ref, scores_ref, turned_ref, basis_hbm,
-    first_ref, out_ref, cl_ref, rows_ref, sum_ref, slope_ref, even_ref, odd_ref, even_left, odd_left, slots_ref, basis_sem,
+    devices, per_dev, slot_of_ref, mixed_ref, assign_ref, scores_ref, basis_hbm,
+    first_ref, out_ref, cl_ref, rows_ref, sum_ref, slope_ref, table_ref,
+    even_ref, odd_ref, even_left, odd_left, slots_ref, basis_sem,
 ):
-    tiles = turned_ref.shape[1] // TILE
-    copies = tiles // PER_COPY
+    copies = basis_hbm.shape[0] // COPY
 
     def basis_copy(c):
         return slot_copy(basis_hbm, slots_ref, basis_sem, c)
@@ -167,16 +177,28 @@
         basis_copy(c).start()
     near_clusters(devices, per_dev, slot_of_ref, cl_ref)
     near_rows(devices, per_dev, mixed_ref, rows_ref)
+    side_by_side(rows_ref, table_ref)
     sum_ref[...] = jnp.zeros_like(sum_ref)
     sig = jax.nn.sigmoid(scores_ref[...])
     slope_ref[...] = sig * (1.0 - sig)
     cl = cl_ref[...]
-    rows = rows_ref[...].astype(jnp.bfloat16)
     products_of = (even_ref, odd_ref)
     left_of = (even_left, odd_left)
 
-    def multiply(t, side):
-        products_of[side][...] = jnp.dot(rows, turned_ref[:, tile_at(t)], preferred_element_type=jnp.float32)
+    def multiply(c, p):
+        c, p = c + p // PER_COPY, p % PER_COPY
+        slot = lax.rem(c, SLOTS)
+        lefts = []
+        for b in range(TILE // (FOLD * LANES)):
+            at = p * TILE + b * FOLD * LANES
+            blocks = [slots_ref[slot, at + q * LANES : at + (q + 1) * LANES, :] for q in range(FOLD)]
+            lefts.append(jnp.concatenate(blocks, axis=1))
+        out = jnp.dot(jnp.concatenate(lefts, axis=0), table_ref[...], preferred_element_type=jnp.float32)
+        for b in range(TILE // (FOLD * LANES)):
+            turned = out[b * LANES : (b + 1) * LANES, :].T
+            for q in range(FOLD):
+                at = (b * FOLD + q) * LANES
+                products_of[p % 2][:, at : at + LANES] = turned[q * WIDE : q * WIDE + ROWS, :]
 
     def select(t, side):
         for i in range(TILE // LANES):
@@ -191,42 +213,56 @@
         block = slots_ref[lax.rem(c, SLOTS), p * TILE : (p + 1) * TILE, :]
         sum_ref[...] += jnp.dot(left_of[p % 2][...], block, preferred_element_type=jnp.float32)
 
+    basis_copy(0).wait()
     multiply(0, 0)
     select(0, 0)
-    multiply(1, 1)
+    multiply(0, 1)
 
     @pl.loop(0, copies - 1)
     def _(c):
-        basis_copy(c).wait()
+        basis_copy(c + 1).wait()
         for p in range(PER_COPY):
-            t = c * PER_COPY + p
             add_up(c, p)
-            multiply(t + 2, p % 2)
-            select(t + 1, (p + 1) % 2)
+            multiply(c, p + 2)
+            select(c * PER_COPY + p + 1, (p + 1) % 2)
 
         @pl.when(c + SLOTS < copies)
         def _():
             basis_copy(c + SLOTS).start()
 
-    basis_copy(copies - 1).wait()
     for p in range(PER_COPY):
-        t = (copies - 1) * PER_COPY + p
         add_up(copies - 1, p)
         if p + 2 < PER_COPY:
-            multiply(t + 2, p % 2)
+            multiply(copies - 1, p + 2)
         if p + 1 < PER_COPY:
-            select(t + 1, (p + 1) % 2)
+            select((copies - 1) * PER_COPY + p + 1, (p + 1) % 2)
     put_sums(per_dev, sum_ref, out_ref)
 
 
+def chip_clusters(devices, per_dev, slot_of_ref, cl_ref):
+    clusters = devices * per_dev
+    me = lax.axis_index("dev")
+    core = lax.rem(me, 2)
+    row = lax.broadcasted_iota(jnp.int32, (ROWS, clusters), 0)
+    group = row // per_dev
+    there = lax.rem(group, 2)
+    owner = me - core + devices - 2 + (group - there) + jnp.where(there == core, 0, 1)
+    slots = lax.rem(owner, devices) * per_dev + lax.rem(row, per_dev)
+    number = lax.broadcasted_iota(jnp.int32, (ROWS, clusters), 1)
+    hit = slot_of_ref[...] == slots
+    found = jnp.sum(jnp.where(hit, number + 1, 0), axis=1, keepdims=True) - 1
+    cl_ref[...] = jnp.broadcast_to(found, cl_ref.shape)
+
+
 def last_kernel(
-    devices, per_dev, slot_of_ref, mixed_ref, assign_ref, first_ref, turned_ref, out_ref, cl_ref, rows_ref, even_ref, odd_ref
+    devices, per_dev, slot_of_ref, behind_ref, own_ref, ahead_ref, assign_ref, first_ref, turned_ref,
+    out_ref, cl_ref, even_ref, odd_ref,
 ):
     tiles = turned_ref.shape[1] // TILE
-    near_clusters(devices, per_dev, slot_of_ref, cl_ref)
-    near_rows(devices, per_dev, mixed_ref, rows_ref)
+    chip_clusters(devices, per_dev, slot_of_ref, cl_ref)
+    around = [ref[...].astype(jnp.float32) for ref in (behind_ref, own_ref, ahead_ref)]
+    rows = jnp.concatenate(around, axis=0).astype(jnp.bfloat16)
     cl = cl_ref[...]
-    rows = rows_ref[...].astype(jnp.bfloat16)
     products_of = (even_ref, odd_ref)
 
     def multiply(t, side):
@@ -297,6 +333,13 @@
         copies = jnp.broadcast_to(block[None], (devices,) + block.shape)
         return lax.all_to_all(copies, "dev", 0, 0, tiled=True)
 
+    def from_device(block, source):
+        return lax.ppermute(block, "dev", [(source(i) % devices, i) for i in range(devices)])
+
+    def to_chips(mixed):
+        own = jnp.concatenate([mixed, from_device(mixed, lambda i: i ^ 1)], axis=0)
+        return from_device(own, lambda i: i - 2), own, from_device(own, lambda i: i + 2)
+
     def mix(coef, links, first_time):
         out = pl.pallas_call(
             functools.partial(link_kernel, norm, devices, per_dev, first_time),
@@ -311,12 +354,12 @@
             compiler_params=params,
             name="link_product",
         )(slot_of, partners, to_all(coef), links)
-        return (to_all(out[0]), *out[1:])
+        return out
 
     mixed1, links_v = mix(coef1, far(link_blocks), True)
     first, coef2 = pl.pallas_call(
         functools.partial(both_kernel, devices, per_dev),
-        in_specs=[vmem] * 5 + [hbm],
+        in_specs=[vmem] * 4 + [hbm],
         out_specs=[vmem, vmem],
         out_shape=[pltpu.VMEM((high, LANES), f32), coef_shape],
         scratch_shapes=[
@@ -324,6 +367,7 @@
             pltpu.VMEM((ROWS, rank), f32),
             pltpu.VMEM((ROWS, rank), f32),
             pltpu.VMEM((high, LANES), f32),
+            pltpu.VMEM((FOLD * rank, LANES), bf16),
             pltpu.VMEM((ROWS, TILE), f32),
             pltpu.VMEM((ROWS, TILE), f32),
             pltpu.VMEM((ROWS, TILE), bf16),
@@ -333,23 +377,22 @@
         ],
         compiler_params=params,
         name="first_and_coef_pass",
-    )(slot_row, mixed1, close(assign_v), scores, close(turned_v), far(basis_rows))
+    )(slot_row, to_all(mixed1), close(assign_v), scores, far(basis_rows))
     (mixed2,) = mix(coef2, close(links_v), False)
 
     out = pl.pallas_call(
         functools.partial(last_kernel, devices, per_dev),
-        in_specs=[vmem] * 5,
+        in_specs=[vmem] * 7,
         out_specs=vmem,
         out_shape=jax.ShapeDtypeStruct((high, LANES), f32),
         scratch_shapes=[
             pltpu.VMEM((ROWS, LANES), jnp.int32),
-            pltpu.VMEM((ROWS, rank), f32),
             pltpu.VMEM((ROWS, TILE), f32),
             pltpu.VMEM((ROWS, TILE), f32),
         ],
         compiler_params=params,
         name="last_pass",
-    )(slot_row, mixed2, close(assign_v), close(first), close(turned_v))
+    )(slot_row, *to_chips(mixed2), close(assign_v), close(first), close(turned_v))
     return out.reshape(samples)
 
 

time: 70.2 us -> 73.2 us (1.043)
  blocking collectives: 42.2 us -> 33.1 us
  waiting for transfers between devices: 0 us -> 6.05 us
  Pallas kernels: 27.6 us -> 31.4 us
  starting transfers between devices: 0 us -> 2.15 us
    all_to_all x4 -> x3, blocking collectives: 42.2 us -> 33.1 us  [to_all(): return lax.all_to_all(copies, 'dev', 0, 0, tiled=True)]
    ppermute x0 -> x3, waiting for transfers between devices: none -> 6.05 us  [from_device(): lax.ppermute(block, 'dev', [(source(i) % devices, i) for i in range(devic...]
    pallas_call x1, Pallas kernels: 7.74 us -> 12.4 us  [shards(): pl.pallas_call(functools.partial(both_kernel, devices, per_dev), in_specs...]
    ppermute x0 -> x3, starting transfers between devices: none -> 2.15 us  [from_device(): lax.ppermute(block, 'dev', [(source(i) % devices, i) for i in range(devic...]
  transfers between devices with their start and end apart: 0 -> 3, of which waited for: 0 -> 3; matrix products, arithmetic and copies ran while one was open for 0% -> 0% of each run, Pallas kernels for 0% -> 0%
where the time goes in v8:
time: 73.2 us; the launch traced here: 72.9 us
  blocking collectives  33.1 us (45%)
  Pallas kernels  31.4 us (43%)
  waiting for transfers between devices  6.05 us (8%)
  starting transfers between devices  2.15 us (3%)
    all_to_all x3, blocking collectives, to_all(): return lax.all_to_all(copies, 'dev', 0, 0, tiled=True)  33.1 us
    pallas_call x1, Pallas kernels, shards(): pl.pallas_call(functools.partial(both_kernel, devices, per_dev), in_specs...  12.4 us
    pallas_call x1, Pallas kernels, shards(): pl.pallas_call(functools.partial(coef_kernel, devices, per_dev), in_specs...  8.18 us
    pallas_call x2, Pallas kernels, mix(): pl.pallas_call(functools.partial(link_kernel, norm, devices, per_dev, fir...  7.19 us
    ppermute x3, waiting for transfers between devices, from_device(): lax.ppermute(block, 'dev', [(source(i) % devices, i) for i in range(devic...  6.05 us
    pallas_call x1, Pallas kernels, shards(): pl.pallas_call(functools.partial(last_kernel, devices, per_dev), in_specs...  3.63 us
    ppermute x3, starting transfers between devices, from_device(): lax.ppermute(block, 'dev', [(source(i) % devices, i) for i in range(devic...  2.15 us
  transfers between devices with their start and end apart: 3, of which 3 were waited for; matrix products, arithmetic and copies ran while one was open for 0% of the time, Pallas kernels for 0%

profile of v8, /device:TPU:0, one launch (start us, length us, event | category | flops | bytes accessed | tf_op | source)
XLA Modules:
  0.0 72.9 jit_solution(9943393431546126578)
XLA Ops:
  0.0 0.0 copy-start.1
  0.0 0.0 copy-start.2
  0.0 0.0 copy-start
  0.0 8.2 %coef_pass.1 = (bf16[4,640]{1,0:T(4,128)(2,1)S(1)}, bf16[128,65536]{1,0:T(8,128)(2,1)S(1)}, s32[512,128]{1,0:T(8,128)S(1)}) custom-call(s32[1,64]{1,0:T(1,128)} %bitcast.6, s32[512,128]{1,0:T(8,128)} %bitcast.9, bf16[512,128]{1,0:T(8,128)(2,1)} %bitcast.10, bf16[65536,128]{1,0:T(8,128)(2,1)} %basis_hbm.3), custom_call_target="tpu_custom_call" | custom-call | tf_op jit(solution)/shard_map/coef_pass/pallas_call | solution.py:309
  8.2 14.3 %all_to_all.15.parts_ref = bf16[16,4,640]{2,1,0:T(4,128)(2,1)S(1)} all-to-all(bf16[16,4,640]{2,1,0:T(4,128)(2,1)S(1)} %broadcast_in_dim.6), channel_id=1, replica_groups=mesh['groups'=2,'dev'=16] {'dev'}, dimensions={0} | all-to-all | bytes 163840 | tf_op jit(solution)/shard_map/all_to_all | solution.py:334
  22.6 0.0 copy-done.1
  22.6 0.0 copy-done.2
  22.6 4.3 %link_product.2 = (bf16[4,128]{1,0:T(4,128)(2,1)S(1)}, bf16[4,64,128,128]{3,2,1,0:T(8,128)(2,1)S(1)}) custom-call(s32[64]{0:T(128)S(1)} %copy-done.1, s32[4,64]{1,0:T(4,128)S(1)} %copy-done.2, bf16[16,4,640]{2,1,0:T(4,128)(2,1)S(1)} %all_to_all.15.parts_ref, bf16[4,64,128,128]{3,2,1,0:T(8,128)(2,1)} %refs_0_.1), custom_call_target="tpu_custom_call" | custom-call | tf_op jit(solution)/shard_map/link_product/pallas_call | solution.py:344
  26.9 9.1 %all_to_all.16.mixed_ref = bf16[16,4,128]{2,1,0:T(4,128)(2,1)S(1)} all-to-all(bf16[16,4,128]{2,1,0:T(4,128)(2,1)S(1)} %broadcast_in_dim.7), channel_id=1, replica_groups=mesh['groups'=2,'dev'=16] {'dev'}, dimensions={0} | all-to-all | bytes 32768 | tf_op jit(solution)/shard_map/all_to_all | solution.py:334
  36.0 0.0 copy-done
  36.0 12.4 %first_and_coef_pass.1 = (f32[512,128]{1,0:T(8,128)S(1)}, bf16[4,640]{1,0:T(4,128)(2,1)S(1)}) custom-call(s32[1,64]{1,0:T(1,128)S(1)} %bitcast.7, bf16[16,4,128]{2,1,0:T(4,128)(2,1)S(1)} %all_to_all.16.mixed_ref, s32[512,128]{1,0:T(8,128)S(1)} %get-tuple-element.14.assign_ref, f32[512,128]{1,0:T(8,128)S(1)} %bitcast.5, bf16[65536,128]{1,0:T(8,128)(2,1)} %basis_hbm.3), custom_call_target="tpu_custom_call" | custom-call | tf_op jit(solution)/shard_map/first_and_coef_pass/pallas_call | solution.py:360
  48.4 9.7 %all_to_all.17.parts_ref = bf16[16,4,640]{2,1,0:T(4,128)(2,1)S(1)} all-to-all(bf16[16,4,640]{2,1,0:T(4,128)(2,1)S(1)} %broadcast_in_dim.8), channel_id=1, replica_groups=mesh['groups'=2,'dev'=16] {'dev'}, dimensions={0} | all-to-all | bytes 163840 | tf_op jit(solution)/shard_map/all_to_all | solution.py:334
  58.1 2.9 %link_product.3 = bf16[4,128]{1,0:T(4,128)(2,1)S(1)} custom-call(s32[64]{0:T(128)S(1)} %copy-done.1, s32[4,64]{1,0:T(4,128)S(1)} %copy-done.2, bf16[16,4,640]{2,1,0:T(4,128)(2,1)S(1)} %all_to_all.17.parts_ref, bf16[4,64,128,128]{3,2,1,0:T(8,128)(2,1)S(1)} %get-tuple-element.16.refs_0_), custom_call_target="tpu_custom_call" | custom-call | tf_op jit(solution)/shard_map/link_product/pallas_call | solution.py:344
  61.0 0.1 collective-permute-start
  61.1 1.1 %collective-permute-done = bf16[4,128]{1,0:T(4,128)(2,1)S(1)} collective-permute-done((bf16[4,128]{1,0:T(4,128)(2,1)S(1)}, bf16[4,128]{1,0:T(4,128)(2,1)S(1)}, u32[]{:S(2)}, u32[]{:S(2)}) %collective-permute-start) | collective-permute-done | bytes 1056 | tf_op jit(solution)/shard_map/ppermute | solution.py:337
  62.2 0.7 collective-permute-start.2
  63.0 1.4 %collective-permute-start.1 = (bf16[8,128]{1,0:T(8,128)(2,1)S(1)}, bf16[8,128]{1,0:T(8,128)(2,1)S(1)}, u32[]{:S(2)}, u32[]{:S(2)}) collective-permute-start(bf16[8,128]{1,0:T(8,128)(2,1)S(1)} %pad_maximum_fusion.own_ref), channel_id=1, source_target_pairs={{14,0},{15,1},{0,2},{1,3},{2,4},{3,5},{4,6},{5,7},{6,8},{7,9},{8,1... | collective-permute-start | bytes 6152 | tf_op jit(solution)/shard_map/ppermute | solution.py:337
  64.3 1.6 %collective-permute-done.2.ahead_ref = bf16[8,128]{1,0:T(8,128)(2,1)S(1)} collective-permute-done((bf16[8,128]{1,0:T(8,128)(2,1)S(1)}, bf16[8,128]{1,0:T(8,128)(2,1)S(1)}, u32[]{:S(2)}, u32[]{:S(2)}) %collective-permute-start.2) | collective-permute-done | bytes 2080 | tf_op jit(solution)/shard_map/ppermute | solution.py:337
  65.9 3.4 %collective-permute-done.1.behind_ref = bf16[8,128]{1,0:T(8,128)(2,1)S(1)} collective-permute-done((bf16[8,128]{1,0:T(8,128)(2,1)S(1)}, bf16[8,128]{1,0:T(8,128)(2,1)S(1)}, u32[]{:S(2)}, u32[]{:S(2)}) %collective-permute-start.1) | collective-permute-done | bytes 2080 | tf_op jit(solution)/shard_map/ppermute | solution.py:337
  69.2 3.6 %last_pass.1 = f32[512,128]{1,0:T(8,128)} custom-call(s32[1,64]{1,0:T(1,128)S(1)} %bitcast.8, bf16[8,128]{1,0:T(8,128)(2,1)S(1)} %collective-permute-done.1.behind_ref, bf16[8,128]{1,0:T(8,128)(2,1)S(1)} %pad_maximum_fusion.own_ref, bf16[8,128]{1,0:T(8,128)(2,1)S(1)} %collective-permute-done.2.ahead_ref, s32[512,128]{1,0:T(8,128)S(1)} %get-tuple-element.14.assign_ref, ...), custom_call_target="tpu_custom_call" | custom-call | tf_op jit(solution)/shard_map/last_pass/pallas_call | solution.py:383
  (4 shorter events, 0.1 us)
Async XLA Ops:
  0.0 22.6 %copy-start.1 = (s32[64]{0:T(128)S(1)}, s32[64]{0:T(128)}, u32[]{:S(2)}) copy-start(s32[64]{0:T(128)} %slot_of_ref.3) | copy-start | bytes 772
  0.0 22.6 %copy-start.2 = (s32[4,64]{1,0:T(4,128)S(1)}, s32[4,64]{1,0:T(4,128)}, u32[]{:S(2)}) copy-start(s32[4,64]{1,0:T(4,128)} %partners_ref.3) | copy-start | bytes 3076
  0.0 36.0 %copy-start = (f32[65536]{0:T(1024)S(1)}, f32[65536]{0:T(1024)}, u32[]{:S(2)}) copy-start(f32[65536]{0:T(1024)} %param.9) | copy-start | bytes 786436
  61.0 1.2 %collective-permute-start = (bf16[4,128]{1,0:T(4,128)(2,1)S(1)}, bf16[4,128]{1,0:T(4,128)(2,1)S(1)}, u32[]{:S(2)}, u32[]{:S(2)}) collective-permute-start(bf16[4,128]{1,0:T(4,128)(2,1)S(1)} %link_product.3), channel_id=1, source_target_pairs={{1,0},{0,1},{3,2},{2,3},{5,4},{4,5},{7,6},{6,7},{9,8},{8,9},{11,10... | collective-permute-start | bytes 3080 | tf_op jit(solution)/shard_map/ppermute | solution.py:337
  62.2 3.6 %collective-permute-start.2 = (bf16[8,128]{1,0:T(8,128)(2,1)S(1)}, bf16[8,128]{1,0:T(8,128)(2,1)S(1)}, u32[]{:S(2)}, u32[]{:S(2)}) collective-permute-start(bf16[8,128]{1,0:T(8,128)(2,1)S(1)} %pad_maximum_fusion.own_ref), channel_id=1, source_target_pairs={{2,0},{3,1},{4,2},{5,3},{6,4},{7,5},{8,6},{9,7},{10,8},{11,9},{12,... | collective-permute-start | bytes 6152 | tf_op jit(solution)/shard_map/ppermute | solution.py:337
  63.0 6.3 %collective-permute-start.1 = (bf16[8,128]{1,0:T(8,128)(2,1)S(1)}, bf16[8,128]{1,0:T(8,128)(2,1)S(1)}, u32[]{:S(2)}, u32[]{:S(2)}) collective-permute-start(bf16[8,128]{1,0:T(8,128)(2,1)S(1)} %pad_maximum_fusion.own_ref), channel_id=1, source_target_pairs={{14,0},{15,1},{0,2},{1,3},{2,4},{3,5},{4,6},{5,7},{6,8},{7,9},{8,1... | collective-permute-start | bytes 6152 | tf_op jit(solution)/shard_map/ppermute | solution.py:337

commit v9 on v7

--- a/solution.py
+++ b/solution.py
@@ -20,6 +20,8 @@
 PER_COPY = COPY // TILE
 SLOTS = 3
 BODY = 16
+HALF = TILE // 2
+PAIR = 64
 PIECES = 4
 
 ridge = 0.5
@@ -37,12 +39,39 @@
     cl_ref[...] = jnp.broadcast_to(found, cl_ref.shape)
 
 
-def near_rows(devices, per_dev, mixed_ref, rows_ref):
-    me = lax.axis_index("dev")
+def near_rows(per_dev, chips, rows_ref):
+    even_core = lax.rem(lax.axis_index("dev"), 2) == 0
+    chips = [chip[...].astype(jnp.float32) for chip in chips]
+    rank = rows_ref.shape[1] // 2
     rows_ref[...] = jnp.zeros_like(rows_ref)
     for g in range(NEAR):
-        owner = lax.rem(me + devices + g - REACH, devices)
-        rows_ref[g * per_dev : (g + 1) * per_dev, :] = mixed_ref[owner].astype(jnp.float32)
+        if g % 2 == 0:
+            rows = chips[g // 2][:per_dev, :]
+        else:
+            rows = jnp.where(even_core, chips[g // 2][per_dev:, :], chips[g // 2 + 1][per_dev:, :])
+        for h in range(2):
+            at = h * (PAIR // 2) + g * per_dev
+            rows_ref[at : at + per_dev, h * rank : (h + 1) * rank] = rows
+
+
+def first_product(rows, turned_ref, t, out_ref):
+    at = [pl.ds(pl.multiple_of(t * TILE + h * HALF, HALF), HALF) for h in range(2)]
+    both = jnp.concatenate([turned_ref[:, at[0]], turned_ref[:, at[1]]], axis=0)
+    out = jnp.dot(rows, both, preferred_element_type=jnp.float32)
+    for h in range(2):
+        out_ref[:, h * HALF : (h + 1) * HALF] = out[h * (PAIR // 2) : h * (PAIR // 2) + ROWS, :]
+
+
+def second_product(left, block):
+    rank = block.shape[1]
+    both = jnp.concatenate([block[:HALF, :], block[HALF:, :]], axis=1)
+    out = jnp.dot(left, both, preferred_element_type=jnp.float32)
+    return out[:ROWS, :rank] + out[PAIR // 2 : PAIR // 2 + ROWS, rank:]
+
+
+def half_left(hit, x):
+    pad = jnp.zeros((PAIR // 2 - ROWS, LANES), jnp.float32)
+    return jnp.concatenate([jnp.where(hit, x, 0.0), pad], axis=0).astype(jnp.bfloat16)
 
 
 def put_sums(per_dev, sum_ref, out_ref):
@@ -96,14 +125,12 @@
         total = sum_ref[...]
         for p in range(PER_COPY):
             t = c * PER_COPY + p
-            parts = []
-            for i in range(TILE // LANES):
-                hit = assign_ref[row_at(t, i), :] == cl
-                parts.append(jnp.where(hit, x_ref[row_at(t, i), :], 0.0).astype(jnp.bfloat16))
-            left = jnp.concatenate(parts, axis=1)
+            parts = [half_left(assign_ref[row_at(t, i), :] == cl, x_ref[row_at(t, i), :]) for i in range(TILE // LANES)]
+            half = len(parts) // 2
+            left = jnp.concatenate([jnp.concatenate(parts[:half], axis=1), jnp.concatenate(parts[half:], axis=1)], axis=0)
             block = slots_ref[lax.rem(c, SLOTS), p * TILE : (p + 1) * TILE, :]
             turned_ref[:, tile_at(t)] = block.T
-            total += jnp.dot(left, block, preferred_element_type=jnp.float32)
+            total += second_product(left, block)
         sum_ref[...] = total
 
         @pl.when(c + SLOTS < copies)
@@ -144,7 +171,7 @@
         for h in range(PIECES):
             if first_time:
                 piece_copy(j, h).wait()
-            acc = lax.fori_loop(h * piece, (h + 1) * piece, body, acc, unroll=16)
+            acc = lax.fori_loop(h * piece, (h + 1) * piece, body, acc, unroll=8)
         mixed_ref[j : j + 1, :] = jnp.sum(acc.T, axis=0, keepdims=True)
     out_ref[...] = mixed_ref[:per_dev, :].astype(jnp.bfloat16)
 
@@ -154,7 +181,7 @@
 
 
 def both_kernel(
-    devices, per_dev, slot_of_ref, mixed_ref, assign_ref, scores_ref, turned_ref, basis_hbm,
+    devices, per_dev, slot_of_ref, behind_ref, own_ref, ahead_ref, assign_ref, scores_ref, turned_ref, basis_hbm,
     first_ref, out_ref, cl_ref, rows_ref, sum_ref, slope_ref, even_ref, odd_ref, even_left, odd_left, slots_ref, basis_sem,
 ):
     tiles = turned_ref.shape[1] // TILE
@@ -166,7 +193,7 @@
     for c in range(SLOTS):
         basis_copy(c).start()
     near_clusters(devices, per_dev, slot_of_ref, cl_ref)
-    near_rows(devices, per_dev, mixed_ref, rows_ref)
+    near_rows(per_dev, (behind_ref, own_ref, ahead_ref), rows_ref)
     sum_ref[...] = jnp.zeros_like(sum_ref)
     sig = jax.nn.sigmoid(scores_ref[...])
     slope_ref[...] = sig * (1.0 - sig)
@@ -176,7 +203,7 @@
     left_of = (even_left, odd_left)
 
     def multiply(t, side):
-        products_of[side][...] = jnp.dot(rows, turned_ref[:, tile_at(t)], preferred_element_type=jnp.float32)
+        first_product(rows, turned_ref, t, products_of[side])
 
     def select(t, side):
         for i in range(TILE // LANES):
@@ -185,11 +212,12 @@
             first = own_product(hit, products_of[side][:, at])
             first_ref[row_at(t, i), :] = first
             weighted = slope_ref[row_at(t, i), :] * first
-            left_of[side][:, at] = jnp.where(hit, weighted, 0.0).astype(jnp.bfloat16)
+            half, col = divmod(i * LANES, HALF)
+            left_of[side][half * (PAIR // 2) : (half + 1) * (PAIR // 2), col : col + LANES] = half_left(hit, weighted)
 
     def add_up(c, p):
         block = slots_ref[lax.rem(c, SLOTS), p * TILE : (p + 1) * TILE, :]
-        sum_ref[...] += jnp.dot(left_of[p % 2][...], block, preferred_element_type=jnp.float32)
+        sum_ref[...] += second_product(left_of[p % 2][...], block)
 
     multiply(0, 0)
     select(0, 0)
@@ -220,17 +248,17 @@
 
 
 def last_kernel(
-    devices, per_dev, slot_of_ref, mixed_ref, assign_ref, first_ref, turned_ref, out_ref, cl_ref, rows_ref, even_ref, odd_ref
+    devices, per_dev, slot_of_ref, behind_ref, own_ref, ahead_ref, assign_ref, first_ref, turned_ref, out_ref, cl_ref, rows_ref, even_ref, odd_ref
 ):
     tiles = turned_ref.shape[1] // TILE
     near_clusters(devices, per_dev, slot_of_ref, cl_ref)
-    near_rows(devices, per_dev, mixed_ref, rows_ref)
+    near_rows(per_dev, (behind_ref, own_ref, ahead_ref), rows_ref)
     cl = cl_ref[...]
     rows = rows_ref[...].astype(jnp.bfloat16)
     products_of = (even_ref, odd_ref)
 
     def multiply(t, side):
-        products_of[side][...] = jnp.dot(rows, turned_ref[:, tile_at(t)], preferred_element_type=jnp.float32)
+        first_product(rows, turned_ref, t, products_of[side])
 
     def select(t, side):
         for i in range(TILE // LANES):
@@ -297,6 +325,13 @@
         copies = jnp.broadcast_to(block[None], (devices,) + block.shape)
         return lax.all_to_all(copies, "dev", 0, 0, tiled=True)
 
+    def from_device(block, source):
+        return lax.ppermute(block, "dev", [(source(i) % devices, i) for i in range(devices)])
+
+    def to_chips(mixed):
+        own = jnp.concatenate([mixed, from_device(mixed, lambda i: i ^ 1)], axis=0)
+        return from_device(own, lambda i: i - 2), own, from_device(own, lambda i: i + 2)
+
     def mix(coef, links, first_time):
         out = pl.pallas_call(
             functools.partial(link_kernel, norm, devices, per_dev, first_time),
@@ -311,45 +346,45 @@
             compiler_params=params,
             name="link_product",
         )(slot_of, partners, to_all(coef), links)
-        return (to_all(out[0]), *out[1:])
+        return out
 
     mixed1, links_v = mix(coef1, far(link_blocks), True)
     first, coef2 = pl.pallas_call(
         functools.partial(both_kernel, devices, per_dev),
-        in_specs=[vmem] * 5 + [hbm],
+        in_specs=[vmem] * 7 + [hbm],
         out_specs=[vmem, vmem],
         out_shape=[pltpu.VMEM((high, LANES), f32), coef_shape],
         scratch_shapes=[
             pltpu.VMEM((ROWS, LANES), jnp.int32),
-            pltpu.VMEM((ROWS, rank), f32),
+            pltpu.VMEM((PAIR, 2 * rank), f32),
             pltpu.VMEM((ROWS, rank), f32),
             pltpu.VMEM((high, LANES), f32),
             pltpu.VMEM((ROWS, TILE), f32),
             pltpu.VMEM((ROWS, TILE), f32),
-            pltpu.VMEM((ROWS, TILE), bf16),
-            pltpu.VMEM((ROWS, TILE), bf16),
+            pltpu.VMEM((PAIR, HALF), bf16),
+            pltpu.VMEM((PAIR, HALF), bf16),
             pltpu.VMEM((SLOTS, COPY, rank), bf16),
             pltpu.SemaphoreType.DMA((SLOTS,)),
         ],
         compiler_params=params,
         name="first_and_coef_pass",
-    )(slot_row, mixed1, close(assign_v), scores, close(turned_v), far(basis_rows))
+    )(slot_row, *to_chips(mixed1), close(assign_v), scores, close(turned_v), far(basis_rows))
     (mixed2,) = mix(coef2, close(links_v), False)
 
     out = pl.pallas_call(
         functools.partial(last_kernel, devices, per_dev),
-        in_specs=[vmem] * 5,
+        in_specs=[vmem] * 7,
         out_specs=vmem,
         out_shape=jax.ShapeDtypeStruct((high, LANES), f32),
         scratch_shapes=[
             pltpu.VMEM((ROWS, LANES), jnp.int32),
-            pltpu.VMEM((ROWS, rank), f32),
+            pltpu.VMEM((PAIR, 2 * rank), f32),
             pltpu.VMEM((ROWS, TILE), f32),
             pltpu.VMEM((ROWS, TILE), f32),
         ],
         compiler_params=params,
         name="last_pass",
-    )(slot_row, mixed2, close(assign_v), close(first), close(turned_v))
+    )(slot_row, *to_chips(mixed2), close(assign_v), close(first), close(turned_v))
     return out.reshape(samples)
 
 

time: 70.2 us -> 69.4 us (0.989)
  blocking collectives: 42.2 us -> 24.1 us
  waiting for transfers between devices: 0 us -> 12.2 us
  starting transfers between devices: 0 us -> 4.3 us
  Pallas kernels: 27.6 us -> 28.5 us
    all_to_all x4 -> x2, blocking collectives: 42.2 us -> 24.1 us  [to_all(): return lax.all_to_all(copies, 'dev', 0, 0, tiled=True)]
    ppermute x0 -> x6, waiting for transfers between devices: none -> 12.2 us  [from_device(): lax.ppermute(block, 'dev', [(source(i) % devices, i) for i in range(devic...]
    ppermute x0 -> x6, starting transfers between devices: none -> 4.3 us  [from_device(): lax.ppermute(block, 'dev', [(source(i) % devices, i) for i in range(devic...]
    pallas_call x1, Pallas kernels: 7.74 us -> 8.73 us  [shards(): pl.pallas_call(functools.partial(both_kernel, devices, per_dev), in_specs...]
    pallas_call x2, Pallas kernels: 7.91 us -> 7.19 us  [mix(): pl.pallas_call(functools.partial(link_kernel, norm, devices, per_dev, fir...]
  transfers between devices with their start and end apart: 0 -> 6, of which waited for: 0 -> 6; matrix products, arithmetic and copies ran while one was open for 0% -> 0% of each run, Pallas kernels for 0% -> 0%
where the time goes in v9:
time: 69.4 us; the launch traced here: 69.2 us
  Pallas kernels  28.5 us (41%)
  blocking collectives  24.1 us (35%)
  waiting for transfers between devices  12.2 us (18%)
  starting transfers between devices  4.3 us (6%)
    all_to_all x2, blocking collectives, to_all(): return lax.all_to_all(copies, 'dev', 0, 0, tiled=True)  24.1 us
    ppermute x6, waiting for transfers between devices, from_device(): lax.ppermute(block, 'dev', [(source(i) % devices, i) for i in range(devic...  12.2 us
    pallas_call x1, Pallas kernels, shards(): pl.pallas_call(functools.partial(both_kernel, devices, per_dev), in_specs...  8.73 us
    pallas_call x1, Pallas kernels, shards(): pl.pallas_call(functools.partial(coef_kernel, devices, per_dev), in_specs...  8.31 us
    pallas_call x2, Pallas kernels, mix(): pl.pallas_call(functools.partial(link_kernel, norm, devices, per_dev, fir...  7.19 us
    pallas_call x1, Pallas kernels, shards(): pl.pallas_call(functools.partial(last_kernel, devices, per_dev), in_specs...  4.3 us
    ppermute x6, starting transfers between devices, from_device(): lax.ppermute(block, 'dev', [(source(i) % devices, i) for i in range(devic...  4.3 us
  transfers between devices with their start and end apart: 6, of which 6 were waited for; matrix products, arithmetic and copies ran while one was open for 0% of the time, Pallas kernels for 0%

profile of v9, /device:TPU:0, one launch (start us, length us, event | category | flops | bytes accessed | tf_op | source)
XLA Modules:
  0.0 69.2 jit_solution(4772741470371308454)
XLA Ops:
  0.0 0.0 copy-start.1
  0.0 0.0 copy-start.2
  0.0 8.3 %coef_pass.1 = (bf16[4,640]{1,0:T(4,128)(2,1)S(1)}, bf16[128,65536]{1,0:T(8,128)(2,1)S(1)}, s32[512,128]{1,0:T(8,128)S(1)}) custom-call(s32[1,64]{1,0:T(1,128)} %bitcast.6, s32[512,128]{1,0:T(8,128)} %bitcast.9, bf16[512,128]{1,0:T(8,128)(2,1)} %bitcast.10, bf16[65536,128]{1,0:T(8,128)(2,1)} %basis_hbm.3), custom_call_target="tpu_custom_call" | custom-call | tf_op jit(solution)/shard_map/coef_pass/pallas_call | solution.py:301
  8.4 14.3 %all_to_all.10.parts_ref = bf16[16,4,640]{2,1,0:T(4,128)(2,1)S(1)} all-to-all(bf16[16,4,640]{2,1,0:T(4,128)(2,1)S(1)} %broadcast_in_dim.4), channel_id=1, replica_groups=mesh['groups'=2,'dev'=16] {'dev'}, dimensions={0} | all-to-all | bytes 163840 | tf_op jit(solution)/shard_map/all_to_all | solution.py:326
  22.7 0.0 copy-done.1
  22.7 0.0 copy-done.2
  22.7 4.3 %link_product.2 = (bf16[4,128]{1,0:T(4,128)(2,1)S(1)}, bf16[4,64,128,128]{3,2,1,0:T(8,128)(2,1)S(1)}) custom-call(s32[64]{0:T(128)S(1)} %copy-done.1, s32[4,64]{1,0:T(4,128)S(1)} %copy-done.2, bf16[16,4,640]{2,1,0:T(4,128)(2,1)S(1)} %all_to_all.10.parts_ref, bf16[4,64,128,128]{3,2,1,0:T(8,128)(2,1)} %refs_0_.1), custom_call_target="tpu_custom_call" | custom-call | tf_op jit(solution)/shard_map/link_product/pallas_call | solution.py:336
  27.0 0.1 collective-permute-start
  27.1 1.1 %collective-permute-done = bf16[4,128]{1,0:T(4,128)(2,1)S(1)} collective-permute-done((bf16[4,128]{1,0:T(4,128)(2,1)S(1)}, bf16[4,128]{1,0:T(4,128)(2,1)S(1)}, u32[]{:S(2)}, u32[]{:S(2)}) %collective-permute-start) | collective-permute-done | bytes 1056 | tf_op jit(solution)/shard_map/ppermute | solution.py:329
  28.2 0.8 %collective-permute-start.2 = (bf16[8,128]{1,0:T(8,128)(2,1)S(1)}, bf16[8,128]{1,0:T(8,128)(2,1)S(1)}, u32[]{:S(2)}, u32[]{:S(2)}) collective-permute-start(bf16[8,128]{1,0:T(8,128)(2,1)S(1)} %pad_maximum_fusion.own_ref), channel_id=1, source_target_pairs={{2,0},{3,1},{4,2},{5,3},{6,4},{7,5},{8,6},{9,7},{10,8},{11,9},{12,... | collective-permute-start | bytes 6152 | tf_op jit(solution)/shard_map/ppermute | solution.py:329
  29.0 1.3 %collective-permute-start.1 = (bf16[8,128]{1,0:T(8,128)(2,1)S(1)}, bf16[8,128]{1,0:T(8,128)(2,1)S(1)}, u32[]{:S(2)}, u32[]{:S(2)}) collective-permute-start(bf16[8,128]{1,0:T(8,128)(2,1)S(1)} %pad_maximum_fusion.own_ref), channel_id=1, source_target_pairs={{14,0},{15,1},{0,2},{1,3},{2,4},{3,5},{4,6},{5,7},{6,8},{7,9},{8,1... | collective-permute-start | bytes 6152 | tf_op jit(solution)/shard_map/ppermute | solution.py:329
  30.3 1.6 %collective-permute-done.2.ahead_ref = bf16[8,128]{1,0:T(8,128)(2,1)S(1)} collective-permute-done((bf16[8,128]{1,0:T(8,128)(2,1)S(1)}, bf16[8,128]{1,0:T(8,128)(2,1)S(1)}, u32[]{:S(2)}, u32[]{:S(2)}) %collective-permute-start.2) | collective-permute-done | bytes 2080 | tf_op jit(solution)/shard_map/ppermute | solution.py:329
  31.9 3.4 %collective-permute-done.1.behind_ref = bf16[8,128]{1,0:T(8,128)(2,1)S(1)} collective-permute-done((bf16[8,128]{1,0:T(8,128)(2,1)S(1)}, bf16[8,128]{1,0:T(8,128)(2,1)S(1)}, u32[]{:S(2)}, u32[]{:S(2)}) %collective-permute-start.1) | collective-permute-done | bytes 2080 | tf_op jit(solution)/shard_map/ppermute | solution.py:329
  35.3 0.0 copy-done
  35.3 8.7 %first_and_coef_pass.1 = (f32[512,128]{1,0:T(8,128)S(1)}, bf16[4,640]{1,0:T(4,128)(2,1)S(1)}) custom-call(s32[1,64]{1,0:T(1,128)S(1)} %bitcast.7, bf16[8,128]{1,0:T(8,128)(2,1)S(1)} %collective-permute-done.1.behind_ref, bf16[8,128]{1,0:T(8,128)(2,1)S(1)} %pad_maximum_fusion.own_ref, bf16[8,128]{1,0:T(8,128)(2,1)S(1)} %collective-permute-done.2.ahead_ref, ...), custom_call_target="tpu_custom_call" | custom-call | tf_op jit(solution)/shard_map/first_and_coef_pass/pallas_call | solution.py:352
  44.1 9.7 %all_to_all.11.parts_ref = bf16[16,4,640]{2,1,0:T(4,128)(2,1)S(1)} all-to-all(bf16[16,4,640]{2,1,0:T(4,128)(2,1)S(1)} %broadcast_in_dim.5), channel_id=1, replica_groups=mesh['groups'=2,'dev'=16] {'dev'}, dimensions={0} | all-to-all | bytes 163840 | tf_op jit(solution)/shard_map/all_to_all | solution.py:326
  53.8 2.9 %link_product.3 = bf16[4,128]{1,0:T(4,128)(2,1)S(1)} custom-call(s32[64]{0:T(128)S(1)} %copy-done.1, s32[4,64]{1,0:T(4,128)S(1)} %copy-done.2, bf16[16,4,640]{2,1,0:T(4,128)(2,1)S(1)} %all_to_all.11.parts_ref, bf16[4,64,128,128]{3,2,1,0:T(8,128)(2,1)S(1)} %get-tuple-element.17.refs_0_), custom_call_target="tpu_custom_call" | custom-call | tf_op jit(solution)/shard_map/link_product/pallas_call | solution.py:336
  56.7 0.1 collective-permute-start.3
  56.8 1.1 %collective-permute-done.3 = bf16[4,128]{1,0:T(4,128)(2,1)S(1)} collective-permute-done((bf16[4,128]{1,0:T(4,128)(2,1)S(1)}, bf16[4,128]{1,0:T(4,128)(2,1)S(1)}, u32[]{:S(2)}, u32[]{:S(2)}) %collective-permute-start.3) | collective-permute-done | bytes 1056 | tf_op jit(solution)/shard_map/ppermute | solution.py:329
  57.9 0.7 %collective-permute-start.5 = (bf16[8,128]{1,0:T(8,128)(2,1)S(1)}, bf16[8,128]{1,0:T(8,128)(2,1)S(1)}, u32[]{:S(2)}, u32[]{:S(2)}) collective-permute-start(bf16[8,128]{1,0:T(8,128)(2,1)S(1)} %pad_maximum_fusion.1.own_ref), channel_id=1, source_target_pairs={{2,0},{3,1},{4,2},{5,3},{6,4},{7,5},{8,6},{9,7},{10,8},{11,9},{12,... | collective-permute-start | bytes 6152 | tf_op jit(solution)/shard_map/ppermute | solution.py:329
  58.6 1.4 %collective-permute-start.4 = (bf16[8,128]{1,0:T(8,128)(2,1)S(1)}, bf16[8,128]{1,0:T(8,128)(2,1)S(1)}, u32[]{:S(2)}, u32[]{:S(2)}) collective-permute-start(bf16[8,128]{1,0:T(8,128)(2,1)S(1)} %pad_maximum_fusion.1.own_ref), channel_id=1, source_target_pairs={{14,0},{15,1},{0,2},{1,3},{2,4},{3,5},{4,6},{5,7},{6,8},{7,9},{8,1... | collective-permute-start | bytes 6152 | tf_op jit(solution)/shard_map/ppermute | solution.py:329
  60.0 1.6 %collective-permute-done.5.ahead_ref = bf16[8,128]{1,0:T(8,128)(2,1)S(1)} collective-permute-done((bf16[8,128]{1,0:T(8,128)(2,1)S(1)}, bf16[8,128]{1,0:T(8,128)(2,1)S(1)}, u32[]{:S(2)}, u32[]{:S(2)}) %collective-permute-start.5) | collective-permute-done | bytes 2080 | tf_op jit(solution)/shard_map/ppermute | solution.py:329
  61.5 3.4 %collective-permute-done.4.behind_ref = bf16[8,128]{1,0:T(8,128)(2,1)S(1)} collective-permute-done((bf16[8,128]{1,0:T(8,128)(2,1)S(1)}, bf16[8,128]{1,0:T(8,128)(2,1)S(1)}, u32[]{:S(2)}, u32[]{:S(2)}) %collective-permute-start.4) | collective-permute-done | bytes 2080 | tf_op jit(solution)/shard_map/ppermute | solution.py:329
  64.9 4.3 %last_pass.1 = f32[512,128]{1,0:T(8,128)} custom-call(s32[1,64]{1,0:T(1,128)S(1)} %bitcast.8, bf16[8,128]{1,0:T(8,128)(2,1)S(1)} %collective-permute-done.4.behind_ref, bf16[8,128]{1,0:T(8,128)(2,1)S(1)} %pad_maximum_fusion.1.own_ref, bf16[8,128]{1,0:T(8,128)(2,1)S(1)} %collective-permute-done.5.ahead_ref, s32[512,128]{1,0:T(8,128)S(1)} %get-tuple-element.14.assign_ref, ...), custom_call_target="tpu_custom_call" | custom-call | tf_op jit(solution)/shard_map/last_pass/pallas_call | solution.py:374
  (5 shorter events, 0.1 us)
Async XLA Ops:
  0.0 22.7 %copy-start.1 = (s32[64]{0:T(128)S(1)}, s32[64]{0:T(128)}, u32[]{:S(2)}) copy-start(s32[64]{0:T(128)} %slot_of_ref.3) | copy-start | bytes 772
  0.0 22.7 %copy-start.2 = (s32[4,64]{1,0:T(4,128)S(1)}, s32[4,64]{1,0:T(4,128)}, u32[]{:S(2)}) copy-start(s32[4,64]{1,0:T(4,128)} %partners_ref.3) | copy-start | bytes 3076
  0.0 35.3 %copy-start = (f32[65536]{0:T(1024)S(1)}, f32[65536]{0:T(1024)}, u32[]{:S(2)}) copy-start(f32[65536]{0:T(1024)} %param.9) | copy-start | bytes 786436
  27.0 1.2 %collective-permute-start = (bf16[4,128]{1,0:T(4,128)(2,1)S(1)}, bf16[4,128]{1,0:T(4,128)(2,1)S(1)}, u32[]{:S(2)}, u32[]{:S(2)}) collective-permute-start(bf16[4,128]{1,0:T(4,128)(2,1)S(1)} %get-tuple-element.13), channel_id=1, source_target_pairs={{1,0},{0,1},{3,2},{2,3},{5,4},{4,5},{7,6},{6,7},{9,8},{8,9},{11,10... | collective-permute-start | bytes 3080 | tf_op jit(solution)/shard_map/ppermute | solution.py:329
  28.2 3.6 %collective-permute-start.2 = (bf16[8,128]{1,0:T(8,128)(2,1)S(1)}, bf16[8,128]{1,0:T(8,128)(2,1)S(1)}, u32[]{:S(2)}, u32[]{:S(2)}) collective-permute-start(bf16[8,128]{1,0:T(8,128)(2,1)S(1)} %pad_maximum_fusion.own_ref), channel_id=1, source_target_pairs={{2,0},{3,1},{4,2},{5,3},{6,4},{7,5},{8,6},{9,7},{10,8},{11,9},{12,... | collective-permute-start | bytes 6152 | tf_op jit(solution)/shard_map/ppermute | solution.py:329
  29.0 6.3 %collective-permute-start.1 = (bf16[8,128]{1,0:T(8,128)(2,1)S(1)}, bf16[8,128]{1,0:T(8,128)(2,1)S(1)}, u32[]{:S(2)}, u32[]{:S(2)}) collective-permute-start(bf16[8,128]{1,0:T(8,128)(2,1)S(1)} %pad_maximum_fusion.own_ref), channel_id=1, source_target_pairs={{14,0},{15,1},{0,2},{1,3},{2,4},{3,5},{4,6},{5,7},{6,8},{7,9},{8,1... | collective-permute-start | bytes 6152 | tf_op jit(solution)/shard_map/ppermute | solution.py:329
  56.7 1.2 %collective-permute-start.3 = (bf16[4,128]{1,0:T(4,128)(2,1)S(1)}, bf16[4,128]{1,0:T(4,128)(2,1)S(1)}, u32[]{:S(2)}, u32[]{:S(2)}) collective-permute-start(bf16[4,128]{1,0:T(4,128)(2,1)S(1)} %link_product.3), channel_id=1, source_target_pairs={{1,0},{0,1},{3,2},{2,3},{5,4},{4,5},{7,6},{6,7},{9,8},{8,9},{11,10... | collective-permute-start | bytes 3080 | tf_op jit(solution)/shard_map/ppermute | solution.py:329
  57.9 3.6 %collective-permute-start.5 = (bf16[8,128]{1,0:T(8,128)(2,1)S(1)}, bf16[8,128]{1,0:T(8,128)(2,1)S(1)}, u32[]{:S(2)}, u32[]{:S(2)}) collective-permute-start(bf16[8,128]{1,0:T(8,128)(2,1)S(1)} %pad_maximum_fusion.1.own_ref), channel_id=1, source_target_pairs={{2,0},{3,1},{4,2},{5,3},{6,4},{7,5},{8,6},{9,7},{10,8},{11,9},{12,... | collective-permute-start | bytes 6152 | tf_op jit(solution)/shard_map/ppermute | solution.py:329
  58.6 6.3 %collective-permute-start.4 = (bf16[8,128]{1,0:T(8,128)(2,1)S(1)}, bf16[8,128]{1,0:T(8,128)(2,1)S(1)}, u32[]{:S(2)}, u32[]{:S(2)}) collective-permute-start(bf16[8,128]{1,0:T(8,128)(2,1)S(1)} %pad_maximum_fusion.1.own_ref), channel_id=1, source_target_pairs={{14,0},{15,1},{0,2},{1,3},{2,4},{3,5},{4,6},{5,7},{6,8},{7,9},{8,1... | collective-permute-start | bytes 6152 | tf_op jit(solution)/shard_map/ppermute | solution.py:329

commit v10 on v7

--- a/solution.py
+++ b/solution.py
@@ -20,7 +20,8 @@
 PER_COPY = COPY // TILE
 SLOTS = 3
 BODY = 16
-PIECES = 4
+PIECE = 512
+GROUP = 8
 
 ridge = 0.5
 
@@ -37,17 +38,29 @@
     cl_ref[...] = jnp.broadcast_to(found, cl_ref.shape)
 
 
-def near_rows(devices, per_dev, mixed_ref, rows_ref):
-    me = lax.axis_index("dev")
+def near_rows(per_dev, chips, rows_ref):
+    even_core = lax.rem(lax.axis_index("dev"), 2) == 0
+    chips = [chip[...].astype(jnp.float32) for chip in chips]
     rows_ref[...] = jnp.zeros_like(rows_ref)
     for g in range(NEAR):
-        owner = lax.rem(me + devices + g - REACH, devices)
-        rows_ref[g * per_dev : (g + 1) * per_dev, :] = mixed_ref[owner].astype(jnp.float32)
+        if g % 2 == 0:
+            rows = chips[g // 2][:per_dev, :]
+        else:
+            rows = jnp.where(even_core, chips[g // 2][per_dev:, :], chips[g // 2 + 1][per_dev:, :])
+        rows_ref[g * per_dev : (g + 1) * per_dev, :] = rows
 
 
 def put_sums(per_dev, sum_ref, out_ref):
     for g in range(NEAR):
         out_ref[:, g * LANES : (g + 1) * LANES] = sum_ref[g * per_dev : (g + 1) * per_dev, :].astype(jnp.bfloat16)
+
+
+def spread_sums(devices, per_dev, sum_ref, out_ref):
+    me = lax.axis_index("dev")
+    out_ref[...] = jnp.zeros_like(out_ref)
+    for g in range(NEAR):
+        owner = lax.rem(me + devices + g - REACH, devices)
+        out_ref[owner] = sum_ref[g * per_dev : (g + 1) * per_dev, :]
 
 
 def slot_copy(basis_hbm, slots_ref, sem, c):
@@ -113,39 +126,52 @@
     put_sums(per_dev, sum_ref, out_ref)
 
 
-def link_kernel(norm, devices, per_dev, first_time, slot_of_ref, partners_ref, parts_ref, *refs):
+def link_kernel(norm, devices, per_dev, first_time, slot_of_ref, partners_ref, coef_ref, *refs):
     if first_time:
-        links_hbm, out_ref, links_ref, scaled_ref, mixed_ref, links_sem = refs
+        links_hbm, out_ref, links_ref, scaled_ref, picked_ref, mixed_ref, links_sem = refs
     else:
-        links_ref, out_ref, scaled_ref, mixed_ref = refs
-    n_links = links_ref.shape[1]
-    piece = n_links // PIECES
-
-    def piece_copy(j, h):
-        ks = pl.ds(h * piece, piece)
-        return pltpu.make_async_copy(links_hbm.at[j, ks], links_ref.at[j, ks], links_sem.at[PIECES * j + h])
+        links_ref, out_ref, scaled_ref, picked_ref, mixed_ref = refs
+    n_links, rank = links_ref.shape[1:3]
+    step = 2 * GROUP
+
+    def piece_copy(j, k):
+        ks = pl.ds(k, step)
+        return pltpu.make_async_copy(links_hbm.at[j, ks], links_ref.at[j, ks], links_sem.at[(j * n_links + k) // step])
 
     if first_time:
         for j in range(per_dev):
-            for h in range(PIECES):
-                piece_copy(j, h).start()
-    for owner in range(devices):
-        coef = parts_ref[(owner + REACH) % devices, :, :LANES].astype(jnp.float32)
-        for g in range(1, NEAR):
-            coef += parts_ref[(owner + REACH - g) % devices, :, g * LANES : (g + 1) * LANES].astype(jnp.float32)
-        scaled_ref[owner * per_dev : (owner + 1) * per_dev, :] = (coef * norm).astype(jnp.bfloat16).astype(jnp.float32)
+            for k in range(0, n_links, step):
+                piece_copy(j, k).start()
+        for owner in range(devices):
+            coef = coef_ref[(owner + REACH) % devices, :, :LANES].astype(jnp.float32)
+            for g in range(1, NEAR):
+                coef += coef_ref[(owner + REACH - g) % devices, :, g * LANES : (g + 1) * LANES].astype(jnp.float32)
+            scaled_ref[owner * per_dev : (owner + 1) * per_dev, :] = (coef * norm).astype(jnp.bfloat16).astype(jnp.float32)
+    else:
+        scaled_ref[...] = (coef_ref[...] * norm).astype(jnp.bfloat16).astype(jnp.float32)
+
+    def partner(j, k):
+        return scaled_ref[pl.ds(slot_of_ref[partners_ref[j, k]], 1), :]
+
+    row = lax.broadcasted_iota(jnp.int32, (GROUP, rank), 0)
     mixed_ref[...] = jnp.zeros_like(mixed_ref)
     for j in range(per_dev):
-        def body(k, acc):
-            s = slot_of_ref[partners_ref[j, k]]
-            return acc + links_ref[j, k].astype(jnp.float32) * scaled_ref[pl.ds(s, 1), :]
-
-        acc = jnp.zeros(links_ref.shape[2:], jnp.float32)
-        for h in range(PIECES):
+        acc = jnp.zeros((rank, rank), jnp.float32)
+        few = jnp.zeros((GROUP, rank), jnp.float32)
+        for k in range(0, n_links, step):
             if first_time:
-                piece_copy(j, h).wait()
-            acc = lax.fori_loop(h * piece, (h + 1) * piece, body, acc, unroll=16)
-        mixed_ref[j : j + 1, :] = jnp.sum(acc.T, axis=0, keepdims=True)
+                piece_copy(j, k).wait()
+            at = (j * n_links + k) // 2
+            for u in range(GROUP):
+                picked_ref[at + u : at + u + 1, :] = partner(j, k + GROUP + u)
+            blocks = links_ref[j, k + GROUP : k + step].reshape(GROUP * rank, rank)
+            picked = picked_ref[at : at + GROUP, :].astype(jnp.bfloat16)
+            products = lax.dot_general(picked, blocks, (((1,), (1,)), ((), ())), preferred_element_type=jnp.float32)
+            for u in range(GROUP):
+                acc += links_ref[j, k + u].astype(jnp.float32) * partner(j, k + u)
+            for u in range(GROUP):
+                few += jnp.where(row == u, products[:, u * rank : (u + 1) * rank], 0.0)
+        mixed_ref[j : j + 1, :] = jnp.sum(acc.T, axis=0, keepdims=True) + jnp.sum(few, axis=0, keepdims=True)
     out_ref[...] = mixed_ref[:per_dev, :].astype(jnp.bfloat16)
 
 
@@ -154,8 +180,8 @@
 
 
 def both_kernel(
-    devices, per_dev, slot_of_ref, mixed_ref, assign_ref, scores_ref, turned_ref, basis_hbm,
-    first_ref, out_ref, cl_ref, rows_ref, sum_ref, slope_ref, even_ref, odd_ref, even_left, odd_left, slots_ref, basis_sem,
+    devices, per_dev, slot_of_ref, behind_ref, own_ref, ahead_ref, assign_ref, scores_ref, turned_ref, basis_hbm,
+    first_ref, out_ref, cl_ref, rows_ref, sum_ref, slope_ref, even_left, odd_left, slots_ref, basis_sem,
 ):
     tiles = turned_ref.shape[1] // TILE
     copies = tiles // PER_COPY
@@ -166,43 +192,38 @@
     for c in range(SLOTS):
         basis_copy(c).start()
     near_clusters(devices, per_dev, slot_of_ref, cl_ref)
-    near_rows(devices, per_dev, mixed_ref, rows_ref)
+    near_rows(per_dev, (behind_ref, own_ref, ahead_ref), rows_ref)
     sum_ref[...] = jnp.zeros_like(sum_ref)
     sig = jax.nn.sigmoid(scores_ref[...])
     slope_ref[...] = sig * (1.0 - sig)
     cl = cl_ref[...]
     rows = rows_ref[...].astype(jnp.bfloat16)
-    products_of = (even_ref, odd_ref)
     left_of = (even_left, odd_left)
 
-    def multiply(t, side):
-        products_of[side][...] = jnp.dot(rows, turned_ref[:, tile_at(t)], preferred_element_type=jnp.float32)
-
     def select(t, side):
-        for i in range(TILE // LANES):
-            at = slice(i * LANES, (i + 1) * LANES)
-            hit = assign_ref[row_at(t, i), :] == cl
-            first = own_product(hit, products_of[side][:, at])
-            first_ref[row_at(t, i), :] = first
-            weighted = slope_ref[row_at(t, i), :] * first
-            left_of[side][:, at] = jnp.where(hit, weighted, 0.0).astype(jnp.bfloat16)
+        for piece in range(TILE // PIECE):
+            at = pl.ds(pl.multiple_of(t * TILE + piece * PIECE, PIECE), PIECE)
+            products = jnp.dot(rows, turned_ref[:, at], preferred_element_type=jnp.float32)
+            for k in range(PIECE // LANES):
+                i = piece * (PIECE // LANES) + k
+                hit = assign_ref[row_at(t, i), :] == cl
+                first = own_product(hit, products[:, k * LANES : (k + 1) * LANES])
+                first_ref[row_at(t, i), :] = first
+                weighted = slope_ref[row_at(t, i), :] * first
+                left_of[side][:, i * LANES : (i + 1) * LANES] = jnp.where(hit, weighted, 0.0).astype(jnp.bfloat16)
 
     def add_up(c, p):
         block = slots_ref[lax.rem(c, SLOTS), p * TILE : (p + 1) * TILE, :]
         sum_ref[...] += jnp.dot(left_of[p % 2][...], block, preferred_element_type=jnp.float32)
 
-    multiply(0, 0)
     select(0, 0)
-    multiply(1, 1)
 
     @pl.loop(0, copies - 1)
     def _(c):
         basis_copy(c).wait()
         for p in range(PER_COPY):
-            t = c * PER_COPY + p
             add_up(c, p)
-            multiply(t + 2, p % 2)
-            select(t + 1, (p + 1) % 2)
+            select(c * PER_COPY + p + 1, (p + 1) % 2)
 
         @pl.when(c + SLOTS < copies)
         def _():
@@ -210,42 +231,30 @@
 
     basis_copy(copies - 1).wait()
     for p in range(PER_COPY):
-        t = (copies - 1) * PER_COPY + p
         add_up(copies - 1, p)
-        if p + 2 < PER_COPY:
-            multiply(t + 2, p % 2)
         if p + 1 < PER_COPY:
-            select(t + 1, (p + 1) % 2)
-    put_sums(per_dev, sum_ref, out_ref)
+            select((copies - 1) * PER_COPY + p + 1, (p + 1) % 2)
+    spread_sums(devices, per_dev, sum_ref, out_ref)
 
 
 def last_kernel(
-    devices, per_dev, slot_of_ref, mixed_ref, assign_ref, first_ref, turned_ref, out_ref, cl_ref, rows_ref, even_ref, odd_ref
+    devices, per_dev, slot_of_ref, behind_ref, own_ref, ahead_ref, assign_ref, first_ref, turned_ref, out_ref, cl_ref, rows_ref
 ):
-    tiles = turned_ref.shape[1] // TILE
     near_clusters(devices, per_dev, slot_of_ref, cl_ref)
-    near_rows(devices, per_dev, mixed_ref, rows_ref)
+    near_rows(per_dev, (behind_ref, own_ref, ahead_ref), rows_ref)
     cl = cl_ref[...]
     rows = rows_ref[...].astype(jnp.bfloat16)
-    products_of = (even_ref, odd_ref)
-
-    def multiply(t, side):
-        products_of[side][...] = jnp.dot(rows, turned_ref[:, tile_at(t)], preferred_element_type=jnp.float32)
-
-    def select(t, side):
-        for i in range(TILE // LANES):
-            hit = assign_ref[row_at(t, i), :] == cl
-            second = own_product(hit, products_of[side][:, i * LANES : (i + 1) * LANES])
-            out_ref[row_at(t, i), :] = second + ridge * first_ref[row_at(t, i), :]
-
-    multiply(0, 0)
-
-    @pl.loop(0, tiles // BODY)
+
+    @pl.loop(0, turned_ref.shape[1] // (BODY * TILE))
     def _(c):
-        for p in range(BODY):
-            t = c * BODY + p
-            multiply(lax.rem(t + 1, tiles), (p + 1) % 2)
-            select(t, p % 2)
+        for piece in range(BODY * TILE // PIECE):
+            at = pl.ds(pl.multiple_of(c * (BODY * TILE) + piece * PIECE, PIECE), PIECE)
+            products = jnp.dot(rows, turned_ref[:, at], preferred_element_type=jnp.float32)
+            for k in range(PIECE // LANES):
+                row = row_at(c * BODY, piece * (PIECE // LANES) + k)
+                hit = assign_ref[row, :] == cl
+                second = own_product(hit, products[:, k * LANES : (k + 1) * LANES])
+                out_ref[row, :] = second + ridge * first_ref[row, :]
 
 
 def shards(basis_rows, vector, scores, assign, slot_of, partners, link_blocks):
@@ -297,6 +306,20 @@
         copies = jnp.broadcast_to(block[None], (devices,) + block.shape)
         return lax.all_to_all(copies, "dev", 0, 0, tiled=True)
 
+    def from_device(block, source):
+        return lax.ppermute(block, "dev", [(source(i) % devices, i) for i in range(devices)])
+
+    def sum_over_devices(x):
+        distance = 1
+        while distance < devices:
+            x = x + from_device(x, lambda i: i ^ distance)
+            distance *= 2
+        return x
+
+    def to_chips(mixed):
+        own = jnp.concatenate([mixed, from_device(mixed, lambda i: i ^ 1)], axis=0)
+        return from_device(own, lambda i: i - 2), own, from_device(own, lambda i: i + 2)
+
     def mix(coef, links, first_time):
         out = pl.pallas_call(
             functools.partial(link_kernel, norm, devices, per_dev, first_time),
@@ -305,27 +328,26 @@
             out_shape=[jax.ShapeDtypeStruct((per_dev, rank), bf16)] + [pltpu.VMEM(links.shape, bf16)] * first_time,
             scratch_shapes=[
                 pltpu.VMEM((clusters, rank), f32),
+                pltpu.VMEM((per_dev * n_links // 2, rank), f32),
                 pltpu.VMEM((8, rank), f32),
             ]
-            + [pltpu.SemaphoreType.DMA((PIECES * per_dev,))] * first_time,
+            + [pltpu.SemaphoreType.DMA((per_dev * n_links // (2 * GROUP),))] * first_time,
             compiler_params=params,
             name="link_product",
-        )(slot_of, partners, to_all(coef), links)
-        return (to_all(out[0]), *out[1:])
-
-    mixed1, links_v = mix(coef1, far(link_blocks), True)
+        )(slot_of, partners, coef, links)
+        return out
+
+    mixed1, links_v = mix(to_all(coef1), far(link_blocks), True)
     first, coef2 = pl.pallas_call(
         functools.partial(both_kernel, devices, per_dev),
-        in_specs=[vmem] * 5 + [hbm],
+        in_specs=[vmem] * 7 + [hbm],
         out_specs=[vmem, vmem],
-        out_shape=[pltpu.VMEM((high, LANES), f32), coef_shape],
+        out_shape=[pltpu.VMEM((high, LANES), f32), jax.ShapeDtypeStruct((devices, per_dev, rank), f32)],
         scratch_shapes=[
             pltpu.VMEM((ROWS, LANES), jnp.int32),
             pltpu.VMEM((ROWS, rank), f32),
             pltpu.VMEM((ROWS, rank), f32),
             pltpu.VMEM((high, LANES), f32),
-            pltpu.VMEM((ROWS, TILE), f32),
-            pltpu.VMEM((ROWS, TILE), f32),
             pltpu.VMEM((ROWS, TILE), bf16),
             pltpu.VMEM((ROWS, TILE), bf16),
             pltpu.VMEM((SLOTS, COPY, rank), bf16),
@@ -333,23 +355,21 @@
         ],
         compiler_params=params,
         name="first_and_coef_pass",
-    )(slot_row, mixed1, close(assign_v), scores, close(turned_v), far(basis_rows))
-    (mixed2,) = mix(coef2, close(links_v), False)
+    )(slot_row, *to_chips(mixed1), close(assign_v), scores, close(turned_v), far(basis_rows))
+    (mixed2,) = mix(sum_over_devices(coef2).reshape(clusters, rank), close(links_v), False)
 
     out = pl.pallas_call(
         functools.partial(last_kernel, devices, per_dev),
-        in_specs=[vmem] * 5,
+        in_specs=[vmem] * 7,
         out_specs=vmem,
         out_shape=jax.ShapeDtypeStruct((high, LANES), f32),
         scratch_shapes=[
             pltpu.VMEM((ROWS, LANES), jnp.int32),
             pltpu.VMEM((ROWS, rank), f32),
-            pltpu.VMEM((ROWS, TILE), f32),
-            pltpu.VMEM((ROWS, TILE), f32),
         ],
         compiler_params=params,
         name="last_pass",
-    )(slot_row, mixed2, close(assign_v), close(first), close(turned_v))
+    )(slot_row, *to_chips(mixed2), close(assign_v), close(first), close(turned_v))
     return out.reshape(samples)
 
 

time: 70.2 us -> 72.9 us (1.038)
  blocking collectives: 42.2 us -> 14.3 us
  waiting for transfers between devices: 0 us -> 25.3 us
  starting transfers between devices: 0 us -> 4.58 us
    all_to_all x4 -> x1, blocking collectives: 42.2 us -> 14.3 us  [to_all(): return lax.all_to_all(copies, 'dev', 0, 0, tiled=True)]
    ppermute x0 -> x10, waiting for transfers between devices: none -> 25.3 us  [from_device(): lax.ppermute(block, 'dev', [(source(i) % devices, i) for i in range(devic...]
    ppermute x0 -> x10, starting transfers between devices: none -> 4.58 us  [from_device(): lax.ppermute(block, 'dev', [(source(i) % devices, i) for i in range(devic...]
    pallas_call x1, Pallas kernels: 7.74 us -> 9.58 us  [shards(): pl.pallas_call(functools.partial(both_kernel, devices, per_dev), in_specs...]
    pallas_call x2, Pallas kernels: 7.91 us -> 7.16 us  [mix(): pl.pallas_call(functools.partial(link_kernel, norm, devices, per_dev, fir...]
  transfers between devices with their start and end apart: 0 -> 10, of which waited for: 0 -> 10; matrix products, arithmetic and copies ran while one was open for 0% -> 0% of each run, Pallas kernels for 0% -> 0%
where the time goes in v10:
time: 72.9 us; the launch traced here: 72.8 us
  Pallas kernels  28.3 us (39%)
  waiting for transfers between devices  25.3 us (35%)
  blocking collectives  14.3 us (20%)
  starting transfers between devices  4.58 us (6%)
    ppermute x10, waiting for transfers between devices, from_device(): lax.ppermute(block, 'dev', [(source(i) % devices, i) for i in range(devic...  25.3 us
    all_to_all x1, blocking collectives, to_all(): return lax.all_to_all(copies, 'dev', 0, 0, tiled=True)  14.3 us
    pallas_call x1, Pallas kernels, shards(): pl.pallas_call(functools.partial(both_kernel, devices, per_dev), in_specs...  9.58 us
    pallas_call x1, Pallas kernels, shards(): pl.pallas_call(functools.partial(coef_kernel, devices, per_dev), in_specs...  8.21 us
    pallas_call x2, Pallas kernels, mix(): pl.pallas_call(functools.partial(link_kernel, norm, devices, per_dev, fir...  7.16 us
    ppermute x10, starting transfers between devices, from_device(): lax.ppermute(block, 'dev', [(source(i) % devices, i) for i in range(devic...  4.58 us
    pallas_call x1, Pallas kernels, shards(): pl.pallas_call(functools.partial(last_kernel, devices, per_dev), in_specs...  3.35 us
  transfers between devices with their start and end apart: 10, of which 10 were waited for; matrix products, arithmetic and copies ran while one was open for 0% of the time, Pallas kernels for 0%

profile of v10, /device:TPU:0, one launch (start us, length us, event | category | flops | bytes accessed | tf_op | source)
XLA Modules:
  0.0 72.8 jit_solution(13134867733420970488)
XLA Ops:
  0.0 8.2 %coef_pass.1 = (bf16[4,640]{1,0:T(4,128)(2,1)S(1)}, bf16[128,65536]{1,0:T(8,128)(2,1)S(1)}, s32[512,128]{1,0:T(8,128)S(1)}) custom-call(s32[1,64]{1,0:T(1,128)} %bitcast.8, s32[512,128]{1,0:T(8,128)} %bitcast.11, bf16[512,128]{1,0:T(8,128)(2,1)} %bitcast.12, bf16[65536,128]{1,0:T(8,128)(2,1)} %basis_hbm.3), custom_call_target="tpu_custom_call" | custom-call | tf_op jit(solution)/shard_map/coef_pass/pallas_call | solution.py:282
  8.3 14.3 %all_to_all.5.coef_ref = bf16[16,4,640]{2,1,0:T(4,128)(2,1)S(1)} all-to-all(bf16[16,4,640]{2,1,0:T(4,128)(2,1)S(1)} %broadcast_in_dim.2), channel_id=1, replica_groups=mesh['groups'=2,'dev'=16] {'dev'}, dimensions={0} | all-to-all | bytes 163840 | tf_op jit(solution)/shard_map/all_to_all | solution.py:307
  22.6 5.0 %link_product.2 = (bf16[4,128]{1,0:T(4,128)(2,1)S(1)}, bf16[4,64,128,128]{3,2,1,0:T(8,128)(2,1)S(1)}) custom-call(s32[64]{0:T(128)S(1)} %copy-done.1, s32[4,64]{1,0:T(4,128)S(1)} %copy-done.2, bf16[16,4,640]{2,1,0:T(4,128)(2,1)S(1)} %all_to_all.5.coef_ref, bf16[4,64,128,128]{3,2,1,0:T(8,128)(2,1)} %refs_0_.1), custom_call_target="tpu_custom_call" | custom-call | tf_op jit(solution)/shard_map/link_product/pallas_call | solution.py:324
  27.6 0.1 collective-permute-start
  27.7 1.1 %collective-permute-done = bf16[4,128]{1,0:T(4,128)(2,1)S(1)} collective-permute-done((bf16[4,128]{1,0:T(4,128)(2,1)S(1)}, bf16[4,128]{1,0:T(4,128)(2,1)S(1)}, u32[]{:S(2)}, u32[]{:S(2)}) %collective-permute-start) | collective-permute-done | bytes 1056 | tf_op jit(solution)/shard_map/ppermute | solution.py:310
  28.8 0.8 %collective-permute-start.2 = (bf16[8,128]{1,0:T(8,128)(2,1)S(1)}, bf16[8,128]{1,0:T(8,128)(2,1)S(1)}, u32[]{:S(2)}, u32[]{:S(2)}) collective-permute-start(bf16[8,128]{1,0:T(8,128)(2,1)S(1)} %pad_maximum_fusion.own_ref), channel_id=1, source_target_pairs={{2,0},{3,1},{4,2},{5,3},{6,4},{7,5},{8,6},{9,7},{10,8},{11,9},{12,... | collective-permute-start | bytes 6152 | tf_op jit(solution)/shard_map/ppermute | solution.py:310
  29.6 1.3 %collective-permute-start.1 = (bf16[8,128]{1,0:T(8,128)(2,1)S(1)}, bf16[8,128]{1,0:T(8,128)(2,1)S(1)}, u32[]{:S(2)}, u32[]{:S(2)}) collective-permute-start(bf16[8,128]{1,0:T(8,128)(2,1)S(1)} %pad_maximum_fusion.own_ref), channel_id=1, source_target_pairs={{14,0},{15,1},{0,2},{1,3},{2,4},{3,5},{4,6},{5,7},{6,8},{7,9},{8,1... | collective-permute-start | bytes 6152 | tf_op jit(solution)/shard_map/ppermute | solution.py:310
  30.9 1.6 %collective-permute-done.2.ahead_ref = bf16[8,128]{1,0:T(8,128)(2,1)S(1)} collective-permute-done((bf16[8,128]{1,0:T(8,128)(2,1)S(1)}, bf16[8,128]{1,0:T(8,128)(2,1)S(1)}, u32[]{:S(2)}, u32[]{:S(2)}) %collective-permute-start.2) | collective-permute-done | bytes 2080 | tf_op jit(solution)/shard_map/ppermute | solution.py:310
  32.5 3.4 %collective-permute-done.1.behind_ref = bf16[8,128]{1,0:T(8,128)(2,1)S(1)} collective-permute-done((bf16[8,128]{1,0:T(8,128)(2,1)S(1)}, bf16[8,128]{1,0:T(8,128)(2,1)S(1)}, u32[]{:S(2)}, u32[]{:S(2)}) %collective-permute-start.1) | collective-permute-done | bytes 2080 | tf_op jit(solution)/shard_map/ppermute | solution.py:310
  35.9 9.6 %first_and_coef_pass.1 = (f32[512,128]{1,0:T(8,128)S(1)}, f32[16,4,128]{2,1,0:T(4,128)S(1)}) custom-call(s32[1,64]{1,0:T(1,128)S(1)} %bitcast.9, bf16[8,128]{1,0:T(8,128)(2,1)S(1)} %collective-permute-done.1.behind_ref, bf16[8,128]{1,0:T(8,128)(2,1)S(1)} %pad_maximum_fusion.own_ref, bf16[8,128]{1,0:T(8,128)(2,1)S(1)} %collective-permute-done.2.ahead_ref, ...), custom_call_target="tpu_custom_call" | custom-call | tf_op jit(solution)/shard_map/first_and_coef_pass/pallas_call | solution.py:341
  45.5 0.1 collective-permute-start.3
  45.6 1.2 %collective-permute-done.3 = f32[16,4,128]{2,1,0:T(4,128)S(1)} collective-permute-done((f32[16,4,128]{2,1,0:T(4,128)S(1)}, f32[16,4,128]{2,1,0:T(4,128)S(1)}, u32[]{:S(2)}, u32[]{:S(2)}) %collective-permute-start.3) | collective-permute-done | bytes 32800 | tf_op jit(solution)/shard_map/ppermute | solution.py:310
  46.8 0.1 collective-permute-start.4
  46.9 3.9 %collective-permute-done.4 = f32[16,4,128]{2,1,0:T(4,128)S(1)} collective-permute-done((f32[16,4,128]{2,1,0:T(4,128)S(1)}, f32[16,4,128]{2,1,0:T(4,128)S(1)}, u32[]{:S(2)}, u32[]{:S(2)}) %collective-permute-start.4) | collective-permute-done | bytes 32800 | tf_op jit(solution)/shard_map/ppermute | solution.py:310
  50.9 3.9 %collective-permute-done.5 = f32[16,4,128]{2,1,0:T(4,128)S(1)} collective-permute-done((f32[16,4,128]{2,1,0:T(4,128)S(1)}, f32[16,4,128]{2,1,0:T(4,128)S(1)}, u32[]{:S(2)}, u32[]{:S(2)}) %collective-permute-start.5) | collective-permute-done | bytes 32800 | tf_op jit(solution)/shard_map/ppermute | solution.py:310
  54.8 0.1 collective-permute-start.6
  54.8 4.8 %collective-permute-done.6 = f32[16,4,128]{2,1,0:T(4,128)S(1)} collective-permute-done((f32[16,4,128]{2,1,0:T(4,128)S(1)}, f32[16,4,128]{2,1,0:T(4,128)S(1)}, u32[]{:S(2)}, u32[]{:S(2)}) %collective-permute-start.6) | collective-permute-done | bytes 32800 | tf_op jit(solution)/shard_map/ppermute | solution.py:310
  59.7 2.1 %link_product.3 = bf16[4,128]{1,0:T(4,128)(2,1)S(1)} custom-call(s32[64]{0:T(128)S(1)} %copy-done.1, s32[4,64]{1,0:T(4,128)S(1)} %copy-done.2, f32[64,128]{1,0:T(8,128)S(1)} %bitcast.7, bf16[4,64,128,128]{3,2,1,0:T(8,128)(2,1)S(1)} %get-tuple-element.17.refs_0_), custom_call_target="tpu_custom_call" | custom-call | tf_op jit(solution)/shard_map/link_product/pallas_call | solution.py:324
  61.9 1.1 %collective-permute-done.7 = bf16[4,128]{1,0:T(4,128)(2,1)S(1)} collective-permute-done((bf16[4,128]{1,0:T(4,128)(2,1)S(1)}, bf16[4,128]{1,0:T(4,128)(2,1)S(1)}, u32[]{:S(2)}, u32[]{:S(2)}) %collective-permute-start.7) | collective-permute-done | bytes 1056 | tf_op jit(solution)/shard_map/ppermute | solution.py:310
  63.0 0.1 collective-permute-start.9
  63.1 2.0 %collective-permute-start.8 = (bf16[8,128]{1,0:T(8,128)(2,1)S(1)}, bf16[8,128]{1,0:T(8,128)(2,1)S(1)}, u32[]{:S(2)}, u32[]{:S(2)}) collective-permute-start(bf16[8,128]{1,0:T(8,128)(2,1)S(1)} %pad_maximum_fusion.1.own_ref), channel_id=1, source_target_pairs={{14,0},{15,1},{0,2},{1,3},{2,4},{3,5},{4,6},{5,7},{6,8},{7,9},{8,1... | collective-permute-start | bytes 6152 | tf_op jit(solution)/shard_map/ppermute | solution.py:310
  65.1 1.6 %collective-permute-done.9.ahead_ref = bf16[8,128]{1,0:T(8,128)(2,1)S(1)} collective-permute-done((bf16[8,128]{1,0:T(8,128)(2,1)S(1)}, bf16[8,128]{1,0:T(8,128)(2,1)S(1)}, u32[]{:S(2)}, u32[]{:S(2)}) %collective-permute-start.9) | collective-permute-done | bytes 2080 | tf_op jit(solution)/shard_map/ppermute | solution.py:310
  66.6 2.8 %collective-permute-done.8.behind_ref = bf16[8,128]{1,0:T(8,128)(2,1)S(1)} collective-permute-done((bf16[8,128]{1,0:T(8,128)(2,1)S(1)}, bf16[8,128]{1,0:T(8,128)(2,1)S(1)}, u32[]{:S(2)}, u32[]{:S(2)}) %collective-permute-start.8) | collective-permute-done | bytes 2080 | tf_op jit(solution)/shard_map/ppermute | solution.py:310
  69.4 3.3 %last_pass.1 = f32[512,128]{1,0:T(8,128)} custom-call(s32[1,64]{1,0:T(1,128)S(1)} %bitcast.10, bf16[8,128]{1,0:T(8,128)(2,1)S(1)} %collective-permute-done.8.behind_ref, bf16[8,128]{1,0:T(8,128)(2,1)S(1)} %pad_maximum_fusion.1.own_ref, bf16[8,128]{1,0:T(8,128)(2,1)S(1)} %collective-permute-done.9.ahead_ref, s32[512,128]{1,0:T(8,128)S(1)} %get-tuple-element.14.assign_ref, ...), custom_call_target="tpu_custom_call" | custom-call | tf_op jit(solution)/shard_map/last_pass/pallas_call | solution.py:361
  (15 shorter events, 0.2 us)
Async XLA Ops:
  0.0 22.6 %copy-start.1 = (s32[64]{0:T(128)S(1)}, s32[64]{0:T(128)}, u32[]{:S(2)}) copy-start(s32[64]{0:T(128)} %slot_of_ref.3) | copy-start | bytes 772
  0.0 22.6 %copy-start.2 = (s32[4,64]{1,0:T(4,128)S(1)}, s32[4,64]{1,0:T(4,128)}, u32[]{:S(2)}) copy-start(s32[4,64]{1,0:T(4,128)} %partners_ref.3) | copy-start | bytes 3076
  0.0 35.9 %copy-start = (f32[65536]{0:T(1024)S(1)}, f32[65536]{0:T(1024)}, u32[]{:S(2)}) copy-start(f32[65536]{0:T(1024)} %param.9) | copy-start | bytes 786436
  27.6 1.2 %collective-permute-start = (bf16[4,128]{1,0:T(4,128)(2,1)S(1)}, bf16[4,128]{1,0:T(4,128)(2,1)S(1)}, u32[]{:S(2)}, u32[]{:S(2)}) collective-permute-start(bf16[4,128]{1,0:T(4,128)(2,1)S(1)} %get-tuple-element.13), channel_id=1, source_target_pairs={{1,0},{0,1},{3,2},{2,3},{5,4},{4,5},{7,6},{6,7},{9,8},{8,9},{11,10... | collective-permute-start | bytes 3080 | tf_op jit(solution)/shard_map/ppermute | solution.py:310
  28.8 3.6 %collective-permute-start.2 = (bf16[8,128]{1,0:T(8,128)(2,1)S(1)}, bf16[8,128]{1,0:T(8,128)(2,1)S(1)}, u32[]{:S(2)}, u32[]{:S(2)}) collective-permute-start(bf16[8,128]{1,0:T(8,128)(2,1)S(1)} %pad_maximum_fusion.own_ref), channel_id=1, source_target_pairs={{2,0},{3,1},{4,2},{5,3},{6,4},{7,5},{8,6},{9,7},{10,8},{11,9},{12,... | collective-permute-start | bytes 6152 | tf_op jit(solution)/shard_map/ppermute | solution.py:310
  29.6 6.3 %collective-permute-start.1 = (bf16[8,128]{1,0:T(8,128)(2,1)S(1)}, bf16[8,128]{1,0:T(8,128)(2,1)S(1)}, u32[]{:S(2)}, u32[]{:S(2)}) collective-permute-start(bf16[8,128]{1,0:T(8,128)(2,1)S(1)} %pad_maximum_fusion.own_ref), channel_id=1, source_target_pairs={{14,0},{15,1},{0,2},{1,3},{2,4},{3,5},{4,6},{5,7},{6,8},{7,9},{8,1... | collective-permute-start | bytes 6152 | tf_op jit(solution)/shard_map/ppermute | solution.py:310
  45.5 1.3 %collective-permute-start.3 = (f32[16,4,128]{2,1,0:T(4,128)S(1)}, f32[16,4,128]{2,1,0:T(4,128)S(1)}, u32[]{:S(2)}, u32[]{:S(2)}) collective-permute-start(f32[16,4,128]{2,1,0:T(4,128)S(1)} %get-tuple-element.16), channel_id=1, source_target_pairs={{1,0},{0,1},{3,2},{2,3},{5,4},{4,5},{7,6},{6,7},{9,8},{8,9},{11,10... | collective-permute-start | bytes 98312 | tf_op jit(solution)/shard_map/ppermute | solution.py:310
  46.8 4.0 %collective-permute-start.4 = (f32[16,4,128]{2,1,0:T(4,128)S(1)}, f32[16,4,128]{2,1,0:T(4,128)S(1)}, u32[]{:S(2)}, u32[]{:S(2)}) collective-permute-start(f32[16,4,128]{2,1,0:T(4,128)S(1)} %add.12), channel_id=1, source_target_pairs={{2,0},{3,1},{0,2},{1,3},{6,4},{7,5},{4,6},{5,7},{10,8},{11,9},{8,1... | collective-permute-start | bytes 98312 | tf_op jit(solution)/shard_map/ppermute | solution.py:310
  50.8 4.0 %collective-permute-start.5 = (f32[16,4,128]{2,1,0:T(4,128)S(1)}, f32[16,4,128]{2,1,0:T(4,128)S(1)}, u32[]{:S(2)}, u32[]{:S(2)}) collective-permute-start(f32[16,4,128]{2,1,0:T(4,128)S(1)} %add.13), channel_id=1, source_target_pairs={{4,0},{5,1},{6,2},{7,3},{0,4},{1,5},{2,6},{3,7},{12,8},{13,9},{14,... | collective-permute-start | bytes 98312 | tf_op jit(solution)/shard_map/ppermute | solution.py:310
  54.8 4.9 %collective-permute-start.6 = (f32[16,4,128]{2,1,0:T(4,128)S(1)}, f32[16,4,128]{2,1,0:T(4,128)S(1)}, u32[]{:S(2)}, u32[]{:S(2)}) collective-permute-start(f32[16,4,128]{2,1,0:T(4,128)S(1)} %add.14), channel_id=1, source_target_pairs={{8,0},{9,1},{10,2},{11,3},{12,4},{13,5},{14,6},{15,7},{0,8},{1,9},... | collective-permute-start | bytes 98312 | tf_op jit(solution)/shard_map/ppermute | solution.py:310
  61.8 1.2 %collective-permute-start.7 = (bf16[4,128]{1,0:T(4,128)(2,1)S(1)}, bf16[4,128]{1,0:T(4,128)(2,1)S(1)}, u32[]{:S(2)}, u32[]{:S(2)}) collective-permute-start(bf16[4,128]{1,0:T(4,128)(2,1)S(1)} %link_product.3), channel_id=1, source_target_pairs={{1,0},{0,1},{3,2},{2,3},{5,4},{4,5},{7,6},{6,7},{9,8},{8,9},{11,10... | collective-permute-start | bytes 3080 | tf_op jit(solution)/shard_map/ppermute | solution.py:310
  63.0 3.6 %collective-permute-start.9 = (bf16[8,128]{1,0:T(8,128)(2,1)S(1)}, bf16[8,128]{1,0:T(8,128)(2,1)S(1)}, u32[]{:S(2)}, u32[]{:S(2)}) collective-permute-start(bf16[8,128]{1,0:T(8,128)(2,1)S(1)} %pad_maximum_fusion.1.own_ref), channel_id=1, source_target_pairs={{2,0},{3,1},{4,2},{5,3},{6,4},{7,5},{8,6},{9,7},{10,8},{11,9},{12,... | collective-permute-start | bytes 6152 | tf_op jit(solution)/shard_map/ppermute | solution.py:310
  63.1 6.3 %collective-permute-start.8 = (bf16[8,128]{1,0:T(8,128)(2,1)S(1)}, bf16[8,128]{1,0:T(8,128)(2,1)S(1)}, u32[]{:S(2)}, u32[]{:S(2)}) collective-permute-start(bf16[8,128]{1,0:T(8,128)(2,1)S(1)} %pad_maximum_fusion.1.own_ref), channel_id=1, source_target_pairs={{14,0},{15,1},{0,2},{1,3},{2,4},{3,5},{4,6},{5,7},{6,8},{7,9},{8,1... | collective-permute-start | bytes 6152 | tf_op jit(solution)/shard_map/ppermute | solution.py:310

commit v11 on v10

--- a/solution.py
+++ b/solution.py
@@ -22,6 +22,7 @@
 BODY = 16
 PIECE = 512
 GROUP = 8
+LINKS = 32
 
 ridge = 0.5
 
@@ -55,14 +56,6 @@
         out_ref[:, g * LANES : (g + 1) * LANES] = sum_ref[g * per_dev : (g + 1) * per_dev, :].astype(jnp.bfloat16)
 
 
-def spread_sums(devices, per_dev, sum_ref, out_ref):
-    me = lax.axis_index("dev")
-    out_ref[...] = jnp.zeros_like(out_ref)
-    for g in range(NEAR):
-        owner = lax.rem(me + devices + g - REACH, devices)
-        out_ref[owner] = sum_ref[g * per_dev : (g + 1) * per_dev, :]
-
-
 def slot_copy(basis_hbm, slots_ref, sem, c):
     slot = lax.rem(c, SLOTS)
     rows = pl.ds(pl.multiple_of(c * COPY, COPY), COPY)
@@ -79,7 +72,7 @@
 
 def coef_kernel(
     devices, per_dev, slot_of_hbm, assign_hbm, vector_hbm, basis_hbm,
-    out_ref, turned_ref, assign_ref,
+    out_ref, assign_ref,
     slot_of_ref, cl_ref, sum_ref, vector_ref, x_ref, slots_ref, small_sem, basis_sem,
 ):
     copies = basis_hbm.shape[0] // COPY
@@ -115,7 +108,6 @@
                 parts.append(jnp.where(hit, x_ref[row_at(t, i), :], 0.0).astype(jnp.bfloat16))
             left = jnp.concatenate(parts, axis=1)
             block = slots_ref[lax.rem(c, SLOTS), p * TILE : (p + 1) * TILE, :]
-            turned_ref[:, tile_at(t)] = block.T
             total += jnp.dot(left, block, preferred_element_type=jnp.float32)
         sum_ref[...] = total
 
@@ -126,7 +118,27 @@
     put_sums(per_dev, sum_ref, out_ref)
 
 
-def link_kernel(norm, devices, per_dev, first_time, slot_of_ref, partners_ref, coef_ref, *refs):
+def turn_kernel(after_ref, basis_hbm, turned_ref, slots_ref, basis_sem):
+    copies = basis_hbm.shape[0] // COPY
+
+    def basis_copy(c):
+        return slot_copy(basis_hbm, slots_ref, basis_sem, c)
+
+    for c in range(SLOTS):
+        basis_copy(c).start()
+
+    @pl.loop(0, copies)
+    def _(c):
+        basis_copy(c).wait()
+        for p in range(PER_COPY):
+            turned_ref[:, tile_at(c * PER_COPY + p)] = slots_ref[lax.rem(c, SLOTS), p * TILE : (p + 1) * TILE, :].T
+
+        @pl.when(c + SLOTS < copies)
+        def _():
+            basis_copy(c + SLOTS).start()
+
+
+def link_kernel(norm, devices, per_dev, first_time, slot_of_ref, partners_ref, parts_ref, *refs):
     if first_time:
         links_hbm, out_ref, links_ref, scaled_ref, picked_ref, mixed_ref, links_sem = refs
     else:
@@ -135,20 +147,18 @@
     step = 2 * GROUP
 
     def piece_copy(j, k):
-        ks = pl.ds(k, step)
-        return pltpu.make_async_copy(links_hbm.at[j, ks], links_ref.at[j, ks], links_sem.at[(j * n_links + k) // step])
+        ks = pl.ds(k, LINKS)
+        return pltpu.make_async_copy(links_hbm.at[j, ks], links_ref.at[j, ks], links_sem.at[(j * n_links + k) // LINKS])
 
     if first_time:
         for j in range(per_dev):
-            for k in range(0, n_links, step):
+            for k in range(0, n_links, LINKS):
                 piece_copy(j, k).start()
-        for owner in range(devices):
-            coef = coef_ref[(owner + REACH) % devices, :, :LANES].astype(jnp.float32)
-            for g in range(1, NEAR):
-                coef += coef_ref[(owner + REACH - g) % devices, :, g * LANES : (g + 1) * LANES].astype(jnp.float32)
-            scaled_ref[owner * per_dev : (owner + 1) * per_dev, :] = (coef * norm).astype(jnp.bfloat16).astype(jnp.float32)
-    else:
-        scaled_ref[...] = (coef_ref[...] * norm).astype(jnp.bfloat16).astype(jnp.float32)
+    for owner in range(devices):
+        coef = parts_ref[(owner + REACH) % devices, :, :LANES].astype(jnp.float32)
+        for g in range(1, NEAR):
+            coef += parts_ref[(owner + REACH - g) % devices, :, g * LANES : (g + 1) * LANES].astype(jnp.float32)
+        scaled_ref[owner * per_dev : (owner + 1) * per_dev, :] = (coef * norm).astype(jnp.bfloat16).astype(jnp.float32)
 
     def partner(j, k):
         return scaled_ref[pl.ds(slot_of_ref[partners_ref[j, k]], 1), :]
@@ -159,7 +169,7 @@
         acc = jnp.zeros((rank, rank), jnp.float32)
         few = jnp.zeros((GROUP, rank), jnp.float32)
         for k in range(0, n_links, step):
-            if first_time:
+            if first_time and k % LINKS == 0:
                 piece_copy(j, k).wait()
             at = (j * n_links + k) // 2
             for u in range(GROUP):
@@ -181,7 +191,7 @@
 
 def both_kernel(
     devices, per_dev, slot_of_ref, behind_ref, own_ref, ahead_ref, assign_ref, scores_ref, turned_ref, basis_hbm,
-    first_ref, out_ref, cl_ref, rows_ref, sum_ref, slope_ref, even_left, odd_left, slots_ref, basis_sem,
+    first_ref, out_ref, cl_ref, rows_ref, sum_ref, slope_ref, even_ref, odd_ref, even_left, odd_left, slots_ref, basis_sem,
 ):
     tiles = turned_ref.shape[1] // TILE
     copies = tiles // PER_COPY
@@ -198,32 +208,37 @@
     slope_ref[...] = sig * (1.0 - sig)
     cl = cl_ref[...]
     rows = rows_ref[...].astype(jnp.bfloat16)
+    products_of = (even_ref, odd_ref)
     left_of = (even_left, odd_left)
 
+    def multiply(t, side):
+        products_of[side][...] = jnp.dot(rows, turned_ref[:, tile_at(t)], preferred_element_type=jnp.float32)
+
     def select(t, side):
-        for piece in range(TILE // PIECE):
-            at = pl.ds(pl.multiple_of(t * TILE + piece * PIECE, PIECE), PIECE)
-            products = jnp.dot(rows, turned_ref[:, at], preferred_element_type=jnp.float32)
-            for k in range(PIECE // LANES):
-                i = piece * (PIECE // LANES) + k
-                hit = assign_ref[row_at(t, i), :] == cl
-                first = own_product(hit, products[:, k * LANES : (k + 1) * LANES])
-                first_ref[row_at(t, i), :] = first
-                weighted = slope_ref[row_at(t, i), :] * first
-                left_of[side][:, i * LANES : (i + 1) * LANES] = jnp.where(hit, weighted, 0.0).astype(jnp.bfloat16)
+        for i in range(TILE // LANES):
+            at = slice(i * LANES, (i + 1) * LANES)
+            hit = assign_ref[row_at(t, i), :] == cl
+            first = own_product(hit, products_of[side][:, at])
+            first_ref[row_at(t, i), :] = first
+            weighted = slope_ref[row_at(t, i), :] * first
+            left_of[side][:, at] = jnp.where(hit, weighted, 0.0).astype(jnp.bfloat16)
 
     def add_up(c, p):
         block = slots_ref[lax.rem(c, SLOTS), p * TILE : (p + 1) * TILE, :]
         sum_ref[...] += jnp.dot(left_of[p % 2][...], block, preferred_element_type=jnp.float32)
 
+    multiply(0, 0)
     select(0, 0)
+    multiply(1, 1)
 
     @pl.loop(0, copies - 1)
     def _(c):
         basis_copy(c).wait()
         for p in range(PER_COPY):
+            t = c * PER_COPY + p
             add_up(c, p)
-            select(c * PER_COPY + p + 1, (p + 1) % 2)
+            multiply(t + 2, p % 2)
+            select(t + 1, (p + 1) % 2)
 
         @pl.when(c + SLOTS < copies)
         def _():
@@ -231,10 +246,13 @@
 
     basis_copy(copies - 1).wait()
     for p in range(PER_COPY):
+        t = (copies - 1) * PER_COPY + p
         add_up(copies - 1, p)
+        if p + 2 < PER_COPY:
+            multiply(t + 2, p % 2)
         if p + 1 < PER_COPY:
-            select((copies - 1) * PER_COPY + p + 1, (p + 1) % 2)
-    spread_sums(devices, per_dev, sum_ref, out_ref)
+            select(t + 1, (p + 1) % 2)
+    put_sums(per_dev, sum_ref, out_ref)
 
 
 def last_kernel(
@@ -279,13 +297,12 @@
     coef_shape = jax.ShapeDtypeStruct((per_dev, NEAR * rank), bf16)
     params = pltpu.CompilerParams(vmem_limit_bytes=10 * 1024 * 1024)
 
-    coef1, turned_v, assign_v = pl.pallas_call(
+    coef1, assign_v = pl.pallas_call(
         functools.partial(coef_kernel, devices, per_dev),
         in_specs=[hbm] * 4,
-        out_specs=[vmem] * 3,
+        out_specs=[vmem] * 2,
         out_shape=[
             coef_shape,
-            pltpu.VMEM((rank, samples), bf16),
             pltpu.VMEM((high, LANES), jnp.int32),
         ],
         scratch_shapes=[
@@ -309,13 +326,6 @@
     def from_device(block, source):
         return lax.ppermute(block, "dev", [(source(i) % devices, i) for i in range(devices)])
 
-    def sum_over_devices(x):
-        distance = 1
-        while distance < devices:
-            x = x + from_device(x, lambda i: i ^ distance)
-            distance *= 2
-        return x
-
     def to_chips(mixed):
         own = jnp.concatenate([mixed, from_device(mixed, lambda i: i ^ 1)], axis=0)
         return from_device(own, lambda i: i - 2), own, from_device(own, lambda i: i + 2)
@@ -331,23 +341,40 @@
                 pltpu.VMEM((per_dev * n_links // 2, rank), f32),
                 pltpu.VMEM((8, rank), f32),
             ]
-            + [pltpu.SemaphoreType.DMA((per_dev * n_links // (2 * GROUP),))] * first_time,
+            + [pltpu.SemaphoreType.DMA((per_dev * n_links // LINKS,))] * first_time,
             compiler_params=params,
             name="link_product",
         )(slot_of, partners, coef, links)
         return out
 
     mixed1, links_v = mix(to_all(coef1), far(link_blocks), True)
+    chips1 = to_chips(mixed1)
+    turned_v = pl.pallas_call(
+        turn_kernel,
+        in_specs=[vmem, hbm],
+        out_specs=vmem,
+        out_shape=pltpu.VMEM((rank, samples), bf16),
+        scratch_shapes=[
+            pltpu.VMEM((SLOTS, COPY, rank), bf16),
+            pltpu.SemaphoreType.DMA((SLOTS,)),
+        ],
+        compiler_params=params,
+        cost_estimate=pl.CostEstimate(flops=0, bytes_accessed=4 * basis_rows.size, transcendentals=0),
+        name="turn_basis",
+    )(chips1[1], far(basis_rows))
+
     first, coef2 = pl.pallas_call(
         functools.partial(both_kernel, devices, per_dev),
         in_specs=[vmem] * 7 + [hbm],
         out_specs=[vmem, vmem],
-        out_shape=[pltpu.VMEM((high, LANES), f32), jax.ShapeDtypeStruct((devices, per_dev, rank), f32)],
+        out_shape=[pltpu.VMEM((high, LANES), f32), coef_shape],
         scratch_shapes=[
             pltpu.VMEM((ROWS, LANES), jnp.int32),
             pltpu.VMEM((ROWS, rank), f32),
             pltpu.VMEM((ROWS, rank), f32),
             pltpu.VMEM((high, LANES), f32),
+            pltpu.VMEM((ROWS, TILE), f32),
+            pltpu.VMEM((ROWS, TILE), f32),
             pltpu.VMEM((ROWS, TILE), bf16),
             pltpu.VMEM((ROWS, TILE), bf16),
             pltpu.VMEM((SLOTS, COPY, rank), bf16),
@@ -355,8 +382,8 @@
         ],
         compiler_params=params,
         name="first_and_coef_pass",
-    )(slot_row, *to_chips(mixed1), close(assign_v), scores, close(turned_v), far(basis_rows))
-    (mixed2,) = mix(sum_over_devices(coef2).reshape(clusters, rank), close(links_v), False)
+    )(slot_row, *chips1, close(assign_v), scores, close(turned_v), far(basis_rows))
+    (mixed2,) = mix(to_all(coef2), close(links_v), False)
 
     out = pl.pallas_call(
         functools.partial(last_kernel, devices, per_dev),

time: 72.9 us -> 70.6 us (0.968)
  waiting for transfers between devices: 25.3 us -> 7.23 us
  blocking collectives: 14.3 us -> 26.1 us
  Pallas kernels: 28.3 us -> 32.6 us
    ppermute x10 -> x6, waiting for transfers between devices: 25.3 us -> 7.23 us  [from_device(): lax.ppermute(block, 'dev', [(source(i) % devices, i) for i in range(devic...]
    all_to_all x1 -> x2, blocking collectives: 14.3 us -> 26.1 us  [to_all(): return lax.all_to_all(copies, 'dev', 0, 0, tiled=True)]
    pallas_call x0 -> x1, Pallas kernels: none -> 7.35 us  [shards(): pl.pallas_call(turn_kernel, in_specs=[vmem, hbm], out_specs=vmem, out_sha...]
    pallas_call x1, Pallas kernels: 9.58 us -> 7.69 us  [shards(): pl.pallas_call(functools.partial(both_kernel, devices, per_dev), in_specs...]
    ppermute x10 -> x6, starting transfers between devices: 4.58 us -> 4.3 us  [from_device(): lax.ppermute(block, 'dev', [(source(i) % devices, i) for i in range(devic...]
  transfers between devices with their start and end apart: 10 -> 6, of which waited for: 10 -> 4; matrix products, arithmetic and copies ran while one was open for 0% -> 0% of each run, Pallas kernels for 0% -> 10%
where the time goes in v11:
time: 70.6 us; the launch traced here: 70.4 us
  Pallas kernels  32.6 us (46%)
  blocking collectives  26.1 us (37%)
  waiting for transfers between devices  7.23 us (10%)
  starting transfers between devices  4.3 us (6%)
    all_to_all x2, blocking collectives, to_all(): return lax.all_to_all(copies, 'dev', 0, 0, tiled=True)  26.1 us
    pallas_call x1, Pallas kernels, shards(): pl.pallas_call(functools.partial(both_kernel, devices, per_dev), in_specs...  7.69 us
    pallas_call x1, Pallas kernels, shards(): pl.pallas_call(functools.partial(coef_kernel, devices, per_dev), in_specs...  7.61 us
    pallas_call x1, Pallas kernels, shards(): pl.pallas_call(turn_kernel, in_specs=[vmem, hbm], out_specs=vmem, out_sha...  7.35 us
    ppermute x6, waiting for transfers between devices, from_device(): lax.ppermute(block, 'dev', [(source(i) % devices, i) for i in range(devic...  7.23 us
    pallas_call x2, Pallas kernels, mix(): pl.pallas_call(functools.partial(link_kernel, norm, devices, per_dev, fir...  6.56 us
    ppermute x6, starting transfers between devices, from_device(): lax.ppermute(block, 'dev', [(source(i) % devices, i) for i in range(devic...  4.3 us
    pallas_call x1, Pallas kernels, shards(): pl.pallas_call(functools.partial(last_kernel, devices, per_dev), in_specs...  3.36 us
  transfers between devices with their start and end apart: 6, of which 4 were waited for; matrix products, arithmetic and copies ran while one was open for 0% of the time, Pallas kernels for 10%

profile of v11, /device:TPU:0, one launch (start us, length us, event | category | flops | bytes accessed | tf_op | source)
XLA Modules:
  0.0 70.4 jit_solution(11821708369731028809)
XLA Ops:
  0.0 7.6 %coef_pass.1 = (bf16[4,640]{1,0:T(4,128)(2,1)S(1)}, s32[512,128]{1,0:T(8,128)S(1)}) custom-call(s32[1,64]{1,0:T(1,128)} %bitcast.6, s32[512,128]{1,0:T(8,128)} %bitcast.9, bf16[512,128]{1,0:T(8,128)(2,1)} %bitcast.10, bf16[65536,128]{1,0:T(8,128)(2,1)} %basis_hbm.5), custom_call_target="tpu_custom_call" | custom-call | tf_op jit(solution)/shard_map/coef_pass/pallas_call | solution.py:300
  7.7 14.3 %all_to_all.10.parts_ref = bf16[16,4,640]{2,1,0:T(4,128)(2,1)S(1)} all-to-all(bf16[16,4,640]{2,1,0:T(4,128)(2,1)S(1)} %broadcast_in_dim.4), channel_id=1, replica_groups=mesh['groups'=2,'dev'=16] {'dev'}, dimensions={0} | all-to-all | bytes 163840 | tf_op jit(solution)/shard_map/all_to_all | solution.py:324
  22.0 0.0 copy-done.1
  22.0 0.0 copy-done.2
  22.0 4.3 %link_product.2 = (bf16[4,128]{1,0:T(4,128)(2,1)S(1)}, bf16[4,64,128,128]{3,2,1,0:T(8,128)(2,1)S(1)}) custom-call(s32[64]{0:T(128)S(1)} %copy-done.1, s32[4,64]{1,0:T(4,128)S(1)} %copy-done.2, bf16[16,4,640]{2,1,0:T(4,128)(2,1)S(1)} %all_to_all.10.parts_ref, bf16[4,64,128,128]{3,2,1,0:T(8,128)(2,1)} %refs_0_.1), custom_call_target="tpu_custom_call" | custom-call | tf_op jit(solution)/shard_map/link_product/pallas_call | solution.py:334
  26.3 0.1 collective-permute-start
  26.4 1.1 %collective-permute-done = bf16[4,128]{1,0:T(4,128)(2,1)S(1)} collective-permute-done((bf16[4,128]{1,0:T(4,128)(2,1)S(1)}, bf16[4,128]{1,0:T(4,128)(2,1)S(1)}, u32[]{:S(2)}, u32[]{:S(2)}) %collective-permute-start) | collective-permute-done | bytes 1056 | tf_op jit(solution)/shard_map/ppermute | solution.py:327
  27.6 0.0 copy-start
  27.6 0.8 %collective-permute-start.2 = (bf16[8,128]{1,0:T(8,128)(2,1)S(1)}, bf16[8,128]{1,0:T(8,128)(2,1)S(1)}, u32[]{:S(2)}, u32[]{:S(2)}) collective-permute-start(bf16[8,128]{1,0:T(8,128)(2,1)S(1)} %pad_maximum_fusion.after_ref.own_ref), channel_id=1, source_target_pairs={{2,0},{3,1},{4,2},{5,3},{6,4},{7,5},{8,6},{9,7},{10,8},{11,9},{12,... | collective-permute-start | bytes 6152 | tf_op jit(solution)/shard_map/ppermute | solution.py:327
  28.3 1.3 %collective-permute-start.1 = (bf16[8,128]{1,0:T(8,128)(2,1)S(1)}, bf16[8,128]{1,0:T(8,128)(2,1)S(1)}, u32[]{:S(2)}, u32[]{:S(2)}) collective-permute-start(bf16[8,128]{1,0:T(8,128)(2,1)S(1)} %pad_maximum_fusion.after_ref.own_ref), channel_id=1, source_target_pairs={{14,0},{15,1},{0,2},{1,3},{2,4},{3,5},{4,6},{5,7},{6,8},{7,9},{8,1... | collective-permute-start | bytes 6152 | tf_op jit(solution)/shard_map/ppermute | solution.py:327
  29.6 7.4 %turn_basis.1.turned_ref = bf16[128,65536]{1,0:T(8,128)(2,1)S(1)} custom-call(bf16[8,128]{1,0:T(8,128)(2,1)S(1)} %pad_maximum_fusion.after_ref.own_ref, bf16[65536,128]{1,0:T(8,128)(2,1)} %basis_hbm.5), custom_call_target="tpu_custom_call" | custom-call | bytes 33554432 | tf_op jit(solution)/shard_map/turn_basis/pallas_call | solution.py:352
  37.0 0.0 collective-permute-done.2.ahead_ref
  37.0 0.0 collective-permute-done.1.behind_ref
  37.0 0.0 copy-done
  37.0 7.7 %first_and_coef_pass.1 = (f32[512,128]{1,0:T(8,128)S(1)}, bf16[4,640]{1,0:T(4,128)(2,1)S(1)}) custom-call(s32[1,64]{1,0:T(1,128)S(1)} %bitcast.7, bf16[8,128]{1,0:T(8,128)(2,1)S(1)} %collective-permute-done.1.behind_ref, bf16[8,128]{1,0:T(8,128)(2,1)S(1)} %pad_maximum_fusion.after_ref.own_ref, bf16[8,128]{1,0:T(8,128)(2,1)S(1)} %collective-permute-done.2.ahead_ref, ...), custom_call_target="tpu_custom_call" | custom-call | tf_op jit(solution)/shard_map/first_and_coef_pass/pallas_call | solution.py:366
  44.8 11.7 %all_to_all.11.parts_ref = bf16[16,4,640]{2,1,0:T(4,128)(2,1)S(1)} all-to-all(bf16[16,4,640]{2,1,0:T(4,128)(2,1)S(1)} %broadcast_in_dim.5), channel_id=1, replica_groups=mesh['groups'=2,'dev'=16] {'dev'}, dimensions={0} | all-to-all | bytes 163840 | tf_op jit(solution)/shard_map/all_to_all | solution.py:324
  56.5 2.2 %link_product.3 = bf16[4,128]{1,0:T(4,128)(2,1)S(1)} custom-call(s32[64]{0:T(128)S(1)} %copy-done.1, s32[4,64]{1,0:T(4,128)S(1)} %copy-done.2, bf16[16,4,640]{2,1,0:T(4,128)(2,1)S(1)} %all_to_all.11.parts_ref, bf16[4,64,128,128]{3,2,1,0:T(8,128)(2,1)S(1)} %get-tuple-element.15.refs_0_), custom_call_target="tpu_custom_call" | custom-call | tf_op jit(solution)/shard_map/link_product/pallas_call | solution.py:334
  58.7 0.1 collective-permute-start.3
  58.8 1.1 %collective-permute-done.3 = bf16[4,128]{1,0:T(4,128)(2,1)S(1)} collective-permute-done((bf16[4,128]{1,0:T(4,128)(2,1)S(1)}, bf16[4,128]{1,0:T(4,128)(2,1)S(1)}, u32[]{:S(2)}, u32[]{:S(2)}) %collective-permute-start.3) | collective-permute-done | bytes 1056 | tf_op jit(solution)/shard_map/ppermute | solution.py:327
  59.9 0.8 %collective-permute-start.5 = (bf16[8,128]{1,0:T(8,128)(2,1)S(1)}, bf16[8,128]{1,0:T(8,128)(2,1)S(1)}, u32[]{:S(2)}, u32[]{:S(2)}) collective-permute-start(bf16[8,128]{1,0:T(8,128)(2,1)S(1)} %pad_maximum_fusion.1.own_ref), channel_id=1, source_target_pairs={{2,0},{3,1},{4,2},{5,3},{6,4},{7,5},{8,6},{9,7},{10,8},{11,9},{12,... | collective-permute-start | bytes 6152 | tf_op jit(solution)/shard_map/ppermute | solution.py:327
  60.7 1.3 %collective-permute-start.4 = (bf16[8,128]{1,0:T(8,128)(2,1)S(1)}, bf16[8,128]{1,0:T(8,128)(2,1)S(1)}, u32[]{:S(2)}, u32[]{:S(2)}) collective-permute-start(bf16[8,128]{1,0:T(8,128)(2,1)S(1)} %pad_maximum_fusion.1.own_ref), channel_id=1, source_target_pairs={{14,0},{15,1},{0,2},{1,3},{2,4},{3,5},{4,6},{5,7},{6,8},{7,9},{8,1... | collective-permute-start | bytes 6152 | tf_op jit(solution)/shard_map/ppermute | solution.py:327
  62.0 1.6 %collective-permute-done.5.ahead_ref = bf16[8,128]{1,0:T(8,128)(2,1)S(1)} collective-permute-done((bf16[8,128]{1,0:T(8,128)(2,1)S(1)}, bf16[8,128]{1,0:T(8,128)(2,1)S(1)}, u32[]{:S(2)}, u32[]{:S(2)}) %collective-permute-start.5) | collective-permute-done | bytes 2080 | tf_op jit(solution)/shard_map/ppermute | solution.py:327
  63.6 3.4 %collective-permute-done.4.behind_ref = bf16[8,128]{1,0:T(8,128)(2,1)S(1)} collective-permute-done((bf16[8,128]{1,0:T(8,128)(2,1)S(1)}, bf16[8,128]{1,0:T(8,128)(2,1)S(1)}, u32[]{:S(2)}, u32[]{:S(2)}) %collective-permute-start.4) | collective-permute-done | bytes 2080 | tf_op jit(solution)/shard_map/ppermute | solution.py:327
  67.0 3.4 %last_pass.1 = f32[512,128]{1,0:T(8,128)} custom-call(s32[1,64]{1,0:T(1,128)S(1)} %bitcast.8, bf16[8,128]{1,0:T(8,128)(2,1)S(1)} %collective-permute-done.4.behind_ref, bf16[8,128]{1,0:T(8,128)(2,1)S(1)} %pad_maximum_fusion.1.own_ref, bf16[8,128]{1,0:T(8,128)(2,1)S(1)} %collective-permute-done.5.ahead_ref, s32[512,128]{1,0:T(8,128)S(1)} %get-tuple-element.13.assign_ref, ...), custom_call_target="tpu_custom_call" | custom-call | tf_op jit(solution)/shard_map/last_pass/pallas_call | solution.py:388
  (6 shorter events, 0.1 us)
Async XLA Ops:
  0.0 22.0 %copy-start.1 = (s32[64]{0:T(128)S(1)}, s32[64]{0:T(128)}, u32[]{:S(2)}) copy-start(s32[64]{0:T(128)} %slot_of_ref.3) | copy-start | bytes 772
  0.0 22.0 %copy-start.2 = (s32[4,64]{1,0:T(4,128)S(1)}, s32[4,64]{1,0:T(4,128)}, u32[]{:S(2)}) copy-start(s32[4,64]{1,0:T(4,128)} %partners_ref.3) | copy-start | bytes 3076
  26.3 1.2 %collective-permute-start = (bf16[4,128]{1,0:T(4,128)(2,1)S(1)}, bf16[4,128]{1,0:T(4,128)(2,1)S(1)}, u32[]{:S(2)}, u32[]{:S(2)}) collective-permute-start(bf16[4,128]{1,0:T(4,128)(2,1)S(1)} %get-tuple-element.12), channel_id=1, source_target_pairs={{1,0},{0,1},{3,2},{2,3},{5,4},{4,5},{7,6},{6,7},{9,8},{8,9},{11,10... | collective-permute-start | bytes 3080 | tf_op jit(solution)/shard_map/ppermute | solution.py:327
  27.6 9.5 %copy-start = (f32[65536]{0:T(1024)S(1)}, f32[65536]{0:T(1024)}, u32[]{:S(2)}) copy-start(f32[65536]{0:T(1024)} %param.9) | copy-start | bytes 786436
  27.6 9.4 %collective-permute-start.2 = (bf16[8,128]{1,0:T(8,128)(2,1)S(1)}, bf16[8,128]{1,0:T(8,128)(2,1)S(1)}, u32[]{:S(2)}, u32[]{:S(2)}) collective-permute-start(bf16[8,128]{1,0:T(8,128)(2,1)S(1)} %pad_maximum_fusion.after_ref.own_ref), channel_id=1, source_target_pairs={{2,0},{3,1},{4,2},{5,3},{6,4},{7,5},{8,6},{9,7},{10,8},{11,9},{12,... | collective-permute-start | bytes 6152 | tf_op jit(solution)/shard_map/ppermute | solution.py:327
  28.3 8.7 %collective-permute-start.1 = (bf16[8,128]{1,0:T(8,128)(2,1)S(1)}, bf16[8,128]{1,0:T(8,128)(2,1)S(1)}, u32[]{:S(2)}, u32[]{:S(2)}) collective-permute-start(bf16[8,128]{1,0:T(8,128)(2,1)S(1)} %pad_maximum_fusion.after_ref.own_ref), channel_id=1, source_target_pairs={{14,0},{15,1},{0,2},{1,3},{2,4},{3,5},{4,6},{5,7},{6,8},{7,9},{8,1... | collective-permute-start | bytes 6152 | tf_op jit(solution)/shard_map/ppermute | solution.py:327
  58.7 1.2 %collective-permute-start.3 = (bf16[4,128]{1,0:T(4,128)(2,1)S(1)}, bf16[4,128]{1,0:T(4,128)(2,1)S(1)}, u32[]{:S(2)}, u32[]{:S(2)}) collective-permute-start(bf16[4,128]{1,0:T(4,128)(2,1)S(1)} %link_product.3), channel_id=1, source_target_pairs={{1,0},{0,1},{3,2},{2,3},{5,4},{4,5},{7,6},{6,7},{9,8},{8,9},{11,10... | collective-permute-start | bytes 3080 | tf_op jit(solution)/shard_map/ppermute | solution.py:327
  59.9 3.6 %collective-permute-start.5 = (bf16[8,128]{1,0:T(8,128)(2,1)S(1)}, bf16[8,128]{1,0:T(8,128)(2,1)S(1)}, u32[]{:S(2)}, u32[]{:S(2)}) collective-permute-start(bf16[8,128]{1,0:T(8,128)(2,1)S(1)} %pad_maximum_fusion.1.own_ref), channel_id=1, source_target_pairs={{2,0},{3,1},{4,2},{5,3},{6,4},{7,5},{8,6},{9,7},{10,8},{11,9},{12,... | collective-permute-start | bytes 6152 | tf_op jit(solution)/shard_map/ppermute | solution.py:327
  60.7 6.3 %collective-permute-start.4 = (bf16[8,128]{1,0:T(8,128)(2,1)S(1)}, bf16[8,128]{1,0:T(8,128)(2,1)S(1)}, u32[]{:S(2)}, u32[]{:S(2)}) collective-permute-start(bf16[8,128]{1,0:T(8,128)(2,1)S(1)} %pad_maximum_fusion.1.own_ref), channel_id=1, source_target_pairs={{14,0},{15,1},{0,2},{1,3},{2,4},{3,5},{4,6},{5,7},{6,8},{7,9},{8,1... | collective-permute-start | bytes 6152 | tf_op jit(solution)/shard_map/ppermute | solution.py:327

commit v12 on v11

--- a/solution.py
+++ b/solution.py
@@ -22,6 +22,7 @@
 BODY = 16
 PIECE = 512
 GROUP = 8
+BODY2 = 8
 LINKS = 32
 
 ridge = 0.5
@@ -72,7 +73,7 @@
 
 def coef_kernel(
     devices, per_dev, slot_of_hbm, assign_hbm, vector_hbm, basis_hbm,
-    out_ref, assign_ref,
+    out_ref, turned_ref, assign_ref,
     slot_of_ref, cl_ref, sum_ref, vector_ref, x_ref, slots_ref, small_sem, basis_sem,
 ):
     copies = basis_hbm.shape[0] // COPY
@@ -108,6 +109,7 @@
                 parts.append(jnp.where(hit, x_ref[row_at(t, i), :], 0.0).astype(jnp.bfloat16))
             left = jnp.concatenate(parts, axis=1)
             block = slots_ref[lax.rem(c, SLOTS), p * TILE : (p + 1) * TILE, :]
+            turned_ref[:, tile_at(t)] = block.T
             total += jnp.dot(left, block, preferred_element_type=jnp.float32)
         sum_ref[...] = total
 
@@ -116,26 +118,6 @@
             basis_copy(c + SLOTS).start()
 
     put_sums(per_dev, sum_ref, out_ref)
-
-
-def turn_kernel(after_ref, basis_hbm, turned_ref, slots_ref, basis_sem):
-    copies = basis_hbm.shape[0] // COPY
-
-    def basis_copy(c):
-        return slot_copy(basis_hbm, slots_ref, basis_sem, c)
-
-    for c in range(SLOTS):
-        basis_copy(c).start()
-
-    @pl.loop(0, copies)
-    def _(c):
-        basis_copy(c).wait()
-        for p in range(PER_COPY):
-            turned_ref[:, tile_at(c * PER_COPY + p)] = slots_ref[lax.rem(c, SLOTS), p * TILE : (p + 1) * TILE, :].T
-
-        @pl.when(c + SLOTS < copies)
-        def _():
-            basis_copy(c + SLOTS).start()
 
 
 def link_kernel(norm, devices, per_dev, first_time, slot_of_ref, partners_ref, parts_ref, *refs):
@@ -190,17 +172,10 @@
 
 
 def both_kernel(
-    devices, per_dev, slot_of_ref, behind_ref, own_ref, ahead_ref, assign_ref, scores_ref, turned_ref, basis_hbm,
-    first_ref, out_ref, cl_ref, rows_ref, sum_ref, slope_ref, even_ref, odd_ref, even_left, odd_left, slots_ref, basis_sem,
+    devices, per_dev, slot_of_ref, behind_ref, own_ref, ahead_ref, assign_ref, scores_ref, turned_ref,
+    first_ref, out_ref, cl_ref, rows_ref, sum_ref, tall_ref, slope_ref, even_ref, odd_ref, even_left, odd_left,
 ):
     tiles = turned_ref.shape[1] // TILE
-    copies = tiles // PER_COPY
-
-    def basis_copy(c):
-        return slot_copy(basis_hbm, slots_ref, basis_sem, c)
-
-    for c in range(SLOTS):
-        basis_copy(c).start()
     near_clusters(devices, per_dev, slot_of_ref, cl_ref)
     near_rows(per_dev, (behind_ref, own_ref, ahead_ref), rows_ref)
     sum_ref[...] = jnp.zeros_like(sum_ref)
@@ -223,35 +198,29 @@
             weighted = slope_ref[row_at(t, i), :] * first
             left_of[side][:, at] = jnp.where(hit, weighted, 0.0).astype(jnp.bfloat16)
 
-    def add_up(c, p):
-        block = slots_ref[lax.rem(c, SLOTS), p * TILE : (p + 1) * TILE, :]
-        sum_ref[...] += jnp.dot(left_of[p % 2][...], block, preferred_element_type=jnp.float32)
+    def add_up(t, side):
+        return lax.dot_general(
+            turned_ref[:, tile_at(t)], left_of[side][...], (((1,), (1,)), ((), ())), preferred_element_type=jnp.float32
+        )
 
     multiply(0, 0)
     select(0, 0)
     multiply(1, 1)
-
-    @pl.loop(0, copies - 1)
+    tall_ref[...] = jnp.zeros_like(tall_ref)
+
+    @pl.loop(0, tiles // BODY2)
     def _(c):
-        basis_copy(c).wait()
-        for p in range(PER_COPY):
-            t = c * PER_COPY + p
-            add_up(c, p)
-            multiply(t + 2, p % 2)
-            select(t + 1, (p + 1) % 2)
-
-        @pl.when(c + SLOTS < copies)
-        def _():
-            basis_copy(c + SLOTS).start()
-
-    basis_copy(copies - 1).wait()
-    for p in range(PER_COPY):
-        t = (copies - 1) * PER_COPY + p
-        add_up(copies - 1, p)
-        if p + 2 < PER_COPY:
-            multiply(t + 2, p % 2)
-        if p + 1 < PER_COPY:
-            select(t + 1, (p + 1) % 2)
+        total = tall_ref[...]
+        for p in range(BODY2):
+            t = c * BODY2 + p
+            total += add_up(t, p % 2)
+            multiply(lax.rem(t + 2, tiles), p % 2)
+            select(lax.rem(t + 1, tiles), (p + 1) % 2)
+        tall_ref[...] = total
+
+    rank = sum_ref.shape[1]
+    wide = jnp.concatenate([tall_ref[...], jnp.zeros((rank, rank - ROWS), jnp.float32)], axis=1)
+    sum_ref[...] = wide.T[:ROWS, :]
     put_sums(per_dev, sum_ref, out_ref)
 
 
@@ -297,12 +266,13 @@
     coef_shape = jax.ShapeDtypeStruct((per_dev, NEAR * rank), bf16)
     params = pltpu.CompilerParams(vmem_limit_bytes=10 * 1024 * 1024)
 
-    coef1, assign_v = pl.pallas_call(
+    coef1, turned_v, assign_v = pl.pallas_call(
         functools.partial(coef_kernel, devices, per_dev),
         in_specs=[hbm] * 4,
-        out_specs=[vmem] * 2,
+        out_specs=[vmem] * 3,
         out_shape=[
             coef_shape,
+            pltpu.VMEM((rank, samples), bf16),
             pltpu.VMEM((high, LANES), jnp.int32),
         ],
         scratch_shapes=[
@@ -348,41 +318,25 @@
         return out
 
     mixed1, links_v = mix(to_all(coef1), far(link_blocks), True)
-    chips1 = to_chips(mixed1)
-    turned_v = pl.pallas_call(
-        turn_kernel,
-        in_specs=[vmem, hbm],
-        out_specs=vmem,
-        out_shape=pltpu.VMEM((rank, samples), bf16),
-        scratch_shapes=[
-            pltpu.VMEM((SLOTS, COPY, rank), bf16),
-            pltpu.SemaphoreType.DMA((SLOTS,)),
-        ],
-        compiler_params=params,
-        cost_estimate=pl.CostEstimate(flops=0, bytes_accessed=4 * basis_rows.size, transcendentals=0),
-        name="turn_basis",
-    )(chips1[1], far(basis_rows))
-
     first, coef2 = pl.pallas_call(
         functools.partial(both_kernel, devices, per_dev),
-        in_specs=[vmem] * 7 + [hbm],
+        in_specs=[vmem] * 7,
         out_specs=[vmem, vmem],
         out_shape=[pltpu.VMEM((high, LANES), f32), coef_shape],
         scratch_shapes=[
             pltpu.VMEM((ROWS, LANES), jnp.int32),
             pltpu.VMEM((ROWS, rank), f32),
             pltpu.VMEM((ROWS, rank), f32),
+            pltpu.VMEM((rank, ROWS), f32),
             pltpu.VMEM((high, LANES), f32),
             pltpu.VMEM((ROWS, TILE), f32),
             pltpu.VMEM((ROWS, TILE), f32),
             pltpu.VMEM((ROWS, TILE), bf16),
             pltpu.VMEM((ROWS, TILE), bf16),
-            pltpu.VMEM((SLOTS, COPY, rank), bf16),
-            pltpu.SemaphoreType.DMA((SLOTS,)),
         ],
         compiler_params=params,
         name="first_and_coef_pass",
-    )(slot_row, *chips1, close(assign_v), scores, close(turned_v), far(basis_rows))
+    )(slot_row, *to_chips(mixed1), close(assign_v), scores, close(turned_v))
     (mixed2,) = mix(to_all(coef2), close(links_v), False)
 
     out = pl.pallas_call(

time: 70.6 us -> 68.8 us (0.975)
  waiting for transfers between devices: 7.23 us -> 12.1 us
  Pallas kernels: 32.6 us -> 27.9 us
  blocking collectives: 26.1 us -> 24.1 us
    pallas_call x1 -> x0, Pallas kernels: 7.35 us -> none  [shards(): pl.pallas_call(turn_kernel, in_specs=[vmem, hbm], out_specs=vmem, out_sha...]
    ppermute x6, waiting for transfers between devices: 7.23 us -> 12.1 us  [from_device(): lax.ppermute(block, 'dev', [(source(i) % devices, i) for i in range(devic...]
    pallas_call x1, Pallas kernels: 7.69 us -> 9.78 us  [shards(): pl.pallas_call(functools.partial(both_kernel, devices, per_dev), in_specs...]
    all_to_all x2, blocking collectives: 26.1 us -> 24.1 us  [to_all(): return lax.all_to_all(copies, 'dev', 0, 0, tiled=True)]
  transfers between devices with their start and end apart: 6 -> 6, of which waited for: 4 -> 6; matrix products, arithmetic and copies ran while one was open for 0% -> 0% of each run, Pallas kernels for 10% -> 0%
where the time goes in v12:
time: 68.8 us; the launch traced here: 68.6 us
  Pallas kernels  27.9 us (41%)
  blocking collectives  24.1 us (35%)
  waiting for transfers between devices  12.1 us (18%)
  starting transfers between devices  4.3 us (6%)
    all_to_all x2, blocking collectives, to_all(): return lax.all_to_all(copies, 'dev', 0, 0, tiled=True)  24.1 us
    ppermute x6, waiting for transfers between devices, from_device(): lax.ppermute(block, 'dev', [(source(i) % devices, i) for i in range(devic...  12.1 us
    pallas_call x1, Pallas kernels, shards(): pl.pallas_call(functools.partial(both_kernel, devices, per_dev), in_specs...  9.78 us
    pallas_call x1, Pallas kernels, shards(): pl.pallas_call(functools.partial(coef_kernel, devices, per_dev), in_specs...  8.21 us
    pallas_call x2, Pallas kernels, mix(): pl.pallas_call(functools.partial(link_kernel, norm, devices, per_dev, fir...  6.55 us
    ppermute x6, starting transfers between devices, from_device(): lax.ppermute(block, 'dev', [(source(i) % devices, i) for i in range(devic...  4.3 us
    pallas_call x1, Pallas kernels, shards(): pl.pallas_call(functools.partial(last_kernel, devices, per_dev), in_specs...  3.36 us
  transfers between devices with their start and end apart: 6, of which 6 were waited for; matrix products, arithmetic and copies ran while one was open for 0% of the time, Pallas kernels for 0%

profile of v12, /device:TPU:0, one launch (start us, length us, event | category | flops | bytes accessed | tf_op | source)
XLA Modules:
  0.0 68.6 jit_solution(2525403622911671435)
XLA Ops:
  0.0 0.0 copy-start.1
  0.0 0.0 copy-start.2
  0.0 8.2 %coef_pass.1 = (bf16[4,640]{1,0:T(4,128)(2,1)S(1)}, bf16[128,65536]{1,0:T(8,128)(2,1)S(1)}, s32[512,128]{1,0:T(8,128)S(1)}) custom-call(s32[1,64]{1,0:T(1,128)} %bitcast.6, s32[512,128]{1,0:T(8,128)} %bitcast.9, bf16[512,128]{1,0:T(8,128)(2,1)} %bitcast.10, bf16[65536,128]{1,0:T(8,128)(2,1)} %basis_hbm.1), custom_call_target="tpu_custom_call" | custom-call | tf_op jit(solution)/shard_map/coef_pass/pallas_call | solution.py:269
  8.3 14.3 %all_to_all.10.parts_ref = bf16[16,4,640]{2,1,0:T(4,128)(2,1)S(1)} all-to-all(bf16[16,4,640]{2,1,0:T(4,128)(2,1)S(1)} %broadcast_in_dim.4), channel_id=1, replica_groups=mesh['groups'=2,'dev'=16] {'dev'}, dimensions={0} | all-to-all | bytes 163840 | tf_op jit(solution)/shard_map/all_to_all | solution.py:294
  22.6 0.0 copy-done.1
  22.6 0.0 copy-done.2
  22.6 4.3 %link_product.2 = (bf16[4,128]{1,0:T(4,128)(2,1)S(1)}, bf16[4,64,128,128]{3,2,1,0:T(8,128)(2,1)S(1)}) custom-call(s32[64]{0:T(128)S(1)} %copy-done.1, s32[4,64]{1,0:T(4,128)S(1)} %copy-done.2, bf16[16,4,640]{2,1,0:T(4,128)(2,1)S(1)} %all_to_all.10.parts_ref, bf16[4,64,128,128]{3,2,1,0:T(8,128)(2,1)} %refs_0_.1), custom_call_target="tpu_custom_call" | custom-call | tf_op jit(solution)/shard_map/link_product/pallas_call | solution.py:304
  26.9 0.1 collective-permute-start
  27.0 1.1 %collective-permute-done = bf16[4,128]{1,0:T(4,128)(2,1)S(1)} collective-permute-done((bf16[4,128]{1,0:T(4,128)(2,1)S(1)}, bf16[4,128]{1,0:T(4,128)(2,1)S(1)}, u32[]{:S(2)}, u32[]{:S(2)}) %collective-permute-start) | collective-permute-done | bytes 1056 | tf_op jit(solution)/shard_map/ppermute | solution.py:297
  28.2 0.8 %collective-permute-start.2 = (bf16[8,128]{1,0:T(8,128)(2,1)S(1)}, bf16[8,128]{1,0:T(8,128)(2,1)S(1)}, u32[]{:S(2)}, u32[]{:S(2)}) collective-permute-start(bf16[8,128]{1,0:T(8,128)(2,1)S(1)} %pad_maximum_fusion.own_ref), channel_id=1, source_target_pairs={{2,0},{3,1},{4,2},{5,3},{6,4},{7,5},{8,6},{9,7},{10,8},{11,9},{12,... | collective-permute-start | bytes 6152 | tf_op jit(solution)/shard_map/ppermute | solution.py:297
  28.9 1.3 %collective-permute-start.1 = (bf16[8,128]{1,0:T(8,128)(2,1)S(1)}, bf16[8,128]{1,0:T(8,128)(2,1)S(1)}, u32[]{:S(2)}, u32[]{:S(2)}) collective-permute-start(bf16[8,128]{1,0:T(8,128)(2,1)S(1)} %pad_maximum_fusion.own_ref), channel_id=1, source_target_pairs={{14,0},{15,1},{0,2},{1,3},{2,4},{3,5},{4,6},{5,7},{6,8},{7,9},{8,1... | collective-permute-start | bytes 6152 | tf_op jit(solution)/shard_map/ppermute | solution.py:297
  30.2 1.6 %collective-permute-done.2.ahead_ref = bf16[8,128]{1,0:T(8,128)(2,1)S(1)} collective-permute-done((bf16[8,128]{1,0:T(8,128)(2,1)S(1)}, bf16[8,128]{1,0:T(8,128)(2,1)S(1)}, u32[]{:S(2)}, u32[]{:S(2)}) %collective-permute-start.2) | collective-permute-done | bytes 2080 | tf_op jit(solution)/shard_map/ppermute | solution.py:297
  31.8 3.4 %collective-permute-done.1.behind_ref = bf16[8,128]{1,0:T(8,128)(2,1)S(1)} collective-permute-done((bf16[8,128]{1,0:T(8,128)(2,1)S(1)}, bf16[8,128]{1,0:T(8,128)(2,1)S(1)}, u32[]{:S(2)}, u32[]{:S(2)}) %collective-permute-start.1) | collective-permute-done | bytes 2080 | tf_op jit(solution)/shard_map/ppermute | solution.py:297
  35.2 0.0 copy-done
  35.2 9.8 %first_and_coef_pass.1 = (f32[512,128]{1,0:T(8,128)S(1)}, bf16[4,640]{1,0:T(4,128)(2,1)S(1)}) custom-call(s32[1,64]{1,0:T(1,128)S(1)} %bitcast.7, bf16[8,128]{1,0:T(8,128)(2,1)S(1)} %collective-permute-done.1.behind_ref, bf16[8,128]{1,0:T(8,128)(2,1)S(1)} %pad_maximum_fusion.own_ref, bf16[8,128]{1,0:T(8,128)(2,1)S(1)} %collective-permute-done.2.ahead_ref, ...), custom_call_target="tpu_custom_call" | custom-call | tf_op jit(solution)/shard_map/first_and_coef_pass/pallas_call | solution.py:321
  45.0 9.7 %all_to_all.11.parts_ref = bf16[16,4,640]{2,1,0:T(4,128)(2,1)S(1)} all-to-all(bf16[16,4,640]{2,1,0:T(4,128)(2,1)S(1)} %broadcast_in_dim.5), channel_id=1, replica_groups=mesh['groups'=2,'dev'=16] {'dev'}, dimensions={0} | all-to-all | bytes 163840 | tf_op jit(solution)/shard_map/all_to_all | solution.py:294
  54.8 2.2 %link_product.3 = bf16[4,128]{1,0:T(4,128)(2,1)S(1)} custom-call(s32[64]{0:T(128)S(1)} %copy-done.1, s32[4,64]{1,0:T(4,128)S(1)} %copy-done.2, bf16[16,4,640]{2,1,0:T(4,128)(2,1)S(1)} %all_to_all.11.parts_ref, bf16[4,64,128,128]{3,2,1,0:T(8,128)(2,1)S(1)} %get-tuple-element.17.refs_0_), custom_call_target="tpu_custom_call" | custom-call | tf_op jit(solution)/shard_map/link_product/pallas_call | solution.py:304
  57.0 0.1 collective-permute-start.3
  57.1 1.1 %collective-permute-done.3 = bf16[4,128]{1,0:T(4,128)(2,1)S(1)} collective-permute-done((bf16[4,128]{1,0:T(4,128)(2,1)S(1)}, bf16[4,128]{1,0:T(4,128)(2,1)S(1)}, u32[]{:S(2)}, u32[]{:S(2)}) %collective-permute-start.3) | collective-permute-done | bytes 1056 | tf_op jit(solution)/shard_map/ppermute | solution.py:297
  58.2 0.7 %collective-permute-start.5 = (bf16[8,128]{1,0:T(8,128)(2,1)S(1)}, bf16[8,128]{1,0:T(8,128)(2,1)S(1)}, u32[]{:S(2)}, u32[]{:S(2)}) collective-permute-start(bf16[8,128]{1,0:T(8,128)(2,1)S(1)} %pad_maximum_fusion.1.own_ref), channel_id=1, source_target_pairs={{2,0},{3,1},{4,2},{5,3},{6,4},{7,5},{8,6},{9,7},{10,8},{11,9},{12,... | collective-permute-start | bytes 6152 | tf_op jit(solution)/shard_map/ppermute | solution.py:297
  58.9 1.4 %collective-permute-start.4 = (bf16[8,128]{1,0:T(8,128)(2,1)S(1)}, bf16[8,128]{1,0:T(8,128)(2,1)S(1)}, u32[]{:S(2)}, u32[]{:S(2)}) collective-permute-start(bf16[8,128]{1,0:T(8,128)(2,1)S(1)} %pad_maximum_fusion.1.own_ref), channel_id=1, source_target_pairs={{14,0},{15,1},{0,2},{1,3},{2,4},{3,5},{4,6},{5,7},{6,8},{7,9},{8,1... | collective-permute-start | bytes 6152 | tf_op jit(solution)/shard_map/ppermute | solution.py:297
  60.3 1.6 %collective-permute-done.5.ahead_ref = bf16[8,128]{1,0:T(8,128)(2,1)S(1)} collective-permute-done((bf16[8,128]{1,0:T(8,128)(2,1)S(1)}, bf16[8,128]{1,0:T(8,128)(2,1)S(1)}, u32[]{:S(2)}, u32[]{:S(2)}) %collective-permute-start.5) | collective-permute-done | bytes 2080 | tf_op jit(solution)/shard_map/ppermute | solution.py:297
  61.8 3.4 %collective-permute-done.4.behind_ref = bf16[8,128]{1,0:T(8,128)(2,1)S(1)} collective-permute-done((bf16[8,128]{1,0:T(8,128)(2,1)S(1)}, bf16[8,128]{1,0:T(8,128)(2,1)S(1)}, u32[]{:S(2)}, u32[]{:S(2)}) %collective-permute-start.4) | collective-permute-done | bytes 2080 | tf_op jit(solution)/shard_map/ppermute | solution.py:297
  65.2 3.4 %last_pass.1 = f32[512,128]{1,0:T(8,128)} custom-call(s32[1,64]{1,0:T(1,128)S(1)} %bitcast.8, bf16[8,128]{1,0:T(8,128)(2,1)S(1)} %collective-permute-done.4.behind_ref, bf16[8,128]{1,0:T(8,128)(2,1)S(1)} %pad_maximum_fusion.1.own_ref, bf16[8,128]{1,0:T(8,128)(2,1)S(1)} %collective-permute-done.5.ahead_ref, s32[512,128]{1,0:T(8,128)S(1)} %get-tuple-element.14.assign_ref, ...), custom_call_target="tpu_custom_call" | custom-call | tf_op jit(solution)/shard_map/last_pass/pallas_call | solution.py:342
  (5 shorter events, 0.1 us)
Async XLA Ops:
  0.0 22.6 %copy-start.1 = (s32[64]{0:T(128)S(1)}, s32[64]{0:T(128)}, u32[]{:S(2)}) copy-start(s32[64]{0:T(128)} %slot_of_ref.3) | copy-start | bytes 772
  0.0 22.6 %copy-start.2 = (s32[4,64]{1,0:T(4,128)S(1)}, s32[4,64]{1,0:T(4,128)}, u32[]{:S(2)}) copy-start(s32[4,64]{1,0:T(4,128)} %partners_ref.3) | copy-start | bytes 3076
  0.0 35.2 %copy-start = (f32[65536]{0:T(1024)S(1)}, f32[65536]{0:T(1024)}, u32[]{:S(2)}) copy-start(f32[65536]{0:T(1024)} %param.9) | copy-start | bytes 786436
  26.9 1.2 %collective-permute-start = (bf16[4,128]{1,0:T(4,128)(2,1)S(1)}, bf16[4,128]{1,0:T(4,128)(2,1)S(1)}, u32[]{:S(2)}, u32[]{:S(2)}) collective-permute-start(bf16[4,128]{1,0:T(4,128)(2,1)S(1)} %get-tuple-element.13), channel_id=1, source_target_pairs={{1,0},{0,1},{3,2},{2,3},{5,4},{4,5},{7,6},{6,7},{9,8},{8,9},{11,10... | collective-permute-start | bytes 3080 | tf_op jit(solution)/shard_map/ppermute | solution.py:297
  28.2 3.6 %collective-permute-start.2 = (bf16[8,128]{1,0:T(8,128)(2,1)S(1)}, bf16[8,128]{1,0:T(8,128)(2,1)S(1)}, u32[]{:S(2)}, u32[]{:S(2)}) collective-permute-start(bf16[8,128]{1,0:T(8,128)(2,1)S(1)} %pad_maximum_fusion.own_ref), channel_id=1, source_target_pairs={{2,0},{3,1},{4,2},{5,3},{6,4},{7,5},{8,6},{9,7},{10,8},{11,9},{12,... | collective-permute-start | bytes 6152 | tf_op jit(solution)/shard_map/ppermute | solution.py:297
  28.9 6.3 %collective-permute-start.1 = (bf16[8,128]{1,0:T(8,128)(2,1)S(1)}, bf16[8,128]{1,0:T(8,128)(2,1)S(1)}, u32[]{:S(2)}, u32[]{:S(2)}) collective-permute-start(bf16[8,128]{1,0:T(8,128)(2,1)S(1)} %pad_maximum_fusion.own_ref), channel_id=1, source_target_pairs={{14,0},{15,1},{0,2},{1,3},{2,4},{3,5},{4,6},{5,7},{6,8},{7,9},{8,1... | collective-permute-start | bytes 6152 | tf_op jit(solution)/shard_map/ppermute | solution.py:297
  57.0 1.2 %collective-permute-start.3 = (bf16[4,128]{1,0:T(4,128)(2,1)S(1)}, bf16[4,128]{1,0:T(4,128)(2,1)S(1)}, u32[]{:S(2)}, u32[]{:S(2)}) collective-permute-start(bf16[4,128]{1,0:T(4,128)(2,1)S(1)} %link_product.3), channel_id=1, source_target_pairs={{1,0},{0,1},{3,2},{2,3},{5,4},{4,5},{7,6},{6,7},{9,8},{8,9},{11,10... | collective-permute-start | bytes 3080 | tf_op jit(solution)/shard_map/ppermute | solution.py:297
  58.2 3.6 %collective-permute-start.5 = (bf16[8,128]{1,0:T(8,128)(2,1)S(1)}, bf16[8,128]{1,0:T(8,128)(2,1)S(1)}, u32[]{:S(2)}, u32[]{:S(2)}) collective-permute-start(bf16[8,128]{1,0:T(8,128)(2,1)S(1)} %pad_maximum_fusion.1.own_ref), channel_id=1, source_target_pairs={{2,0},{3,1},{4,2},{5,3},{6,4},{7,5},{8,6},{9,7},{10,8},{11,9},{12,... | collective-permute-start | bytes 6152 | tf_op jit(solution)/shard_map/ppermute | solution.py:297
  58.9 6.3 %collective-permute-start.4 = (bf16[8,128]{1,0:T(8,128)(2,1)S(1)}, bf16[8,128]{1,0:T(8,128)(2,1)S(1)}, u32[]{:S(2)}, u32[]{:S(2)}) collective-permute-start(bf16[8,128]{1,0:T(8,128)(2,1)S(1)} %pad_maximum_fusion.1.own_ref), channel_id=1, source_target_pairs={{14,0},{15,1},{0,2},{1,3},{2,4},{3,5},{4,6},{5,7},{6,8},{7,9},{8,1... | collective-permute-start | bytes 6152 | tf_op jit(solution)/shard_map/ppermute | solution.py:297

commit v13 on v11

--- a/solution.py
+++ b/solution.py
@@ -72,8 +72,8 @@
 
 def coef_kernel(
     devices, per_dev, slot_of_hbm, assign_hbm, vector_hbm, basis_hbm,
-    out_ref, assign_ref,
-    slot_of_ref, cl_ref, sum_ref, vector_ref, x_ref, slots_ref, small_sem, basis_sem,
+    out_ref, turned_ref, assign_ref, cl_ref,
+    slot_of_ref, sum_ref, vector_ref, x_ref, slots_ref, small_sem, basis_sem, last_sem,
 ):
     copies = basis_hbm.shape[0] // COPY
 
@@ -96,46 +96,48 @@
     x_ref[...] = vector_ref[...].astype(jnp.float32)
     cl = cl_ref[...]
 
-    @pl.loop(0, copies)
+    last = copies - 1
+
+    def last_copy(p):
+        rows = pl.ds(last * COPY + p * TILE, TILE)
+        return pltpu.make_async_copy(
+            basis_hbm.at[rows, :], slots_ref.at[last % SLOTS, pl.ds(p * TILE, TILE)], last_sem.at[p]
+        )
+
+    def add_up(c, p, total):
+        t = c * PER_COPY + p
+        parts = []
+        for i in range(TILE // LANES):
+            hit = assign_ref[row_at(t, i), :] == cl
+            parts.append(jnp.where(hit, x_ref[row_at(t, i), :], 0.0).astype(jnp.bfloat16))
+        left = jnp.concatenate(parts, axis=1)
+        block = slots_ref[lax.rem(c, SLOTS), p * TILE : (p + 1) * TILE, :]
+        turned_ref[:, tile_at(t)] = block.T
+        return total + jnp.dot(left, block, preferred_element_type=jnp.float32)
+
+    @pl.loop(0, last)
     def _(c):
         basis_copy(c).wait()
         total = sum_ref[...]
         for p in range(PER_COPY):
-            t = c * PER_COPY + p
-            parts = []
-            for i in range(TILE // LANES):
-                hit = assign_ref[row_at(t, i), :] == cl
-                parts.append(jnp.where(hit, x_ref[row_at(t, i), :], 0.0).astype(jnp.bfloat16))
-            left = jnp.concatenate(parts, axis=1)
-            block = slots_ref[lax.rem(c, SLOTS), p * TILE : (p + 1) * TILE, :]
-            total += jnp.dot(left, block, preferred_element_type=jnp.float32)
+            total = add_up(c, p, total)
         sum_ref[...] = total
 
-        @pl.when(c + SLOTS < copies)
+        @pl.when(c + SLOTS < last)
         def _():
             basis_copy(c + SLOTS).start()
 
+        @pl.when(c + SLOTS == last)
+        def _():
+            for p in range(PER_COPY):
+                last_copy(p).start()
+
+    total = sum_ref[...]
+    for p in range(PER_COPY):
+        last_copy(p).wait()
+        total = add_up(last, p, total)
+    sum_ref[...] = total
     put_sums(per_dev, sum_ref, out_ref)
-
-
-def turn_kernel(after_ref, basis_hbm, turned_ref, slots_ref, basis_sem):
-    copies = basis_hbm.shape[0] // COPY
-
-    def basis_copy(c):
-        return slot_copy(basis_hbm, slots_ref, basis_sem, c)
-
-    for c in range(SLOTS):
-        basis_copy(c).start()
-
-    @pl.loop(0, copies)
-    def _(c):
-        basis_copy(c).wait()
-        for p in range(PER_COPY):
-            turned_ref[:, tile_at(c * PER_COPY + p)] = slots_ref[lax.rem(c, SLOTS), p * TILE : (p + 1) * TILE, :].T
-
-        @pl.when(c + SLOTS < copies)
-        def _():
-            basis_copy(c + SLOTS).start()
 
 
 def link_kernel(norm, devices, per_dev, first_time, slot_of_ref, partners_ref, parts_ref, *refs):
@@ -190,8 +192,8 @@
 
 
 def both_kernel(
-    devices, per_dev, slot_of_ref, behind_ref, own_ref, ahead_ref, assign_ref, scores_ref, turned_ref, basis_hbm,
-    first_ref, out_ref, cl_ref, rows_ref, sum_ref, slope_ref, even_ref, odd_ref, even_left, odd_left, slots_ref, basis_sem,
+    per_dev, cl_ref, ahead_ref, own_ref, behind_ref, assign_ref, scores_ref, turned_ref, basis_hbm,
+    first_ref, out_ref, rows_ref, sum_ref, slope_ref, even_ref, odd_ref, even_left, odd_left, slots_ref, basis_sem,
 ):
     tiles = turned_ref.shape[1] // TILE
     copies = tiles // PER_COPY
@@ -201,7 +203,6 @@
 
     for c in range(SLOTS):
         basis_copy(c).start()
-    near_clusters(devices, per_dev, slot_of_ref, cl_ref)
     near_rows(per_dev, (behind_ref, own_ref, ahead_ref), rows_ref)
     sum_ref[...] = jnp.zeros_like(sum_ref)
     sig = jax.nn.sigmoid(scores_ref[...])
@@ -256,9 +257,8 @@
 
 
 def last_kernel(
-    devices, per_dev, slot_of_ref, behind_ref, own_ref, ahead_ref, assign_ref, first_ref, turned_ref, out_ref, cl_ref, rows_ref
+    per_dev, cl_ref, ahead_ref, own_ref, behind_ref, assign_ref, first_ref, turned_ref, out_ref, rows_ref
 ):
-    near_clusters(devices, per_dev, slot_of_ref, cl_ref)
     near_rows(per_dev, (behind_ref, own_ref, ahead_ref), rows_ref)
     cl = cl_ref[...]
     rows = rows_ref[...].astype(jnp.bfloat16)
@@ -297,23 +297,25 @@
     coef_shape = jax.ShapeDtypeStruct((per_dev, NEAR * rank), bf16)
     params = pltpu.CompilerParams(vmem_limit_bytes=10 * 1024 * 1024)
 
-    coef1, assign_v = pl.pallas_call(
+    coef1, turned_v, assign_v, cl_v = pl.pallas_call(
         functools.partial(coef_kernel, devices, per_dev),
         in_specs=[hbm] * 4,
-        out_specs=[vmem] * 2,
+        out_specs=[vmem] * 4,
         out_shape=[
             coef_shape,
+            pltpu.VMEM((rank, samples), bf16),
             pltpu.VMEM((high, LANES), jnp.int32),
+            pltpu.VMEM((ROWS, LANES), jnp.int32),
         ],
         scratch_shapes=[
             pltpu.VMEM((1, clusters), jnp.int32),
-            pltpu.VMEM((ROWS, LANES), jnp.int32),
             pltpu.VMEM((ROWS, rank), f32),
             pltpu.VMEM((high, LANES), bf16),
             pltpu.VMEM((high, LANES), f32),
             pltpu.VMEM((SLOTS, COPY, rank), bf16),
             pltpu.SemaphoreType.DMA((3,)),
             pltpu.SemaphoreType.DMA((SLOTS,)),
+            pltpu.SemaphoreType.DMA((PER_COPY,)),
         ],
         compiler_params=params,
         name="coef_pass",
@@ -328,7 +330,9 @@
 
     def to_chips(mixed):
         own = jnp.concatenate([mixed, from_device(mixed, lambda i: i ^ 1)], axis=0)
-        return from_device(own, lambda i: i - 2), own, from_device(own, lambda i: i + 2)
+        ahead = from_device(own, lambda i: i + 2)
+        behind = from_device(own, lambda i: i - 2)
+        return ahead, own, behind
 
     def mix(coef, links, first_time):
         out = pl.pallas_call(
@@ -348,28 +352,12 @@
         return out
 
     mixed1, links_v = mix(to_all(coef1), far(link_blocks), True)
-    chips1 = to_chips(mixed1)
-    turned_v = pl.pallas_call(
-        turn_kernel,
-        in_specs=[vmem, hbm],
-        out_specs=vmem,
-        out_shape=pltpu.VMEM((rank, samples), bf16),
-        scratch_shapes=[
-            pltpu.VMEM((SLOTS, COPY, rank), bf16),
-            pltpu.SemaphoreType.DMA((SLOTS,)),
-        ],
-        compiler_params=params,
-        cost_estimate=pl.CostEstimate(flops=0, bytes_accessed=4 * basis_rows.size, transcendentals=0),
-        name="turn_basis",
-    )(chips1[1], far(basis_rows))
-
     first, coef2 = pl.pallas_call(
-        functools.partial(both_kernel, devices, per_dev),
+        functools.partial(both_kernel, per_dev),
         in_specs=[vmem] * 7 + [hbm],
         out_specs=[vmem, vmem],
         out_shape=[pltpu.VMEM((high, LANES), f32), coef_shape],
         scratch_shapes=[
-            pltpu.VMEM((ROWS, LANES), jnp.int32),
             pltpu.VMEM((ROWS, rank), f32),
             pltpu.VMEM((ROWS, rank), f32),
             pltpu.VMEM((high, LANES), f32),
@@ -382,21 +370,20 @@
         ],
         compiler_params=params,
         name="first_and_coef_pass",
-    )(slot_row, *chips1, close(assign_v), scores, close(turned_v), far(basis_rows))
+    )(close(cl_v), *to_chips(mixed1), close(assign_v), scores, close(turned_v), far(basis_rows))
     (mixed2,) = mix(to_all(coef2), close(links_v), False)
 
     out = pl.pallas_call(
-        functools.partial(last_kernel, devices, per_dev),
+        functools.partial(last_kernel, per_dev),
         in_specs=[vmem] * 7,
         out_specs=vmem,
         out_shape=jax.ShapeDtypeStruct((high, LANES), f32),
         scratch_shapes=[
-            pltpu.VMEM((ROWS, LANES), jnp.int32),
             pltpu.VMEM((ROWS, rank), f32),
         ],
         compiler_params=params,
         name="last_pass",
-    )(slot_row, *to_chips(mixed2), close(assign_v), close(first), close(turned_v))
+    )(close(cl_v), *to_chips(mixed2), close(assign_v), close(first), close(turned_v))
     return out.reshape(samples)
 
 

time: 70.6 us -> 68.8 us (0.975)
  Pallas kernels: 32.6 us -> 26 us
  starting transfers between devices: 4.3 us -> 9.68 us
  waiting for transfers between devices: 7.23 us -> 5.37 us
  blocking collectives: 26.1 us -> 27.4 us
    pallas_call x3 -> x2, Pallas kernels: 18.4 us -> 11 us  [the longest x1 7.71 us: shards(): pl.pallas_call(functools.partial(both_kernel, per_dev), in_specs=[vmem] *...]
    ppermute x6, starting transfers between devices: 4.3 us -> 9.68 us  [from_device(): lax.ppermute(block, 'dev', [(source(i) % devices, i) for i in range(devic...]
    ppermute x6, waiting for transfers between devices: 7.23 us -> 5.37 us  [from_device(): lax.ppermute(block, 'dev', [(source(i) % devices, i) for i in range(devic...]
    all_to_all x2, blocking collectives: 26.1 us -> 27.4 us  [to_all(): return lax.all_to_all(copies, 'dev', 0, 0, tiled=True)]
    pallas_call x1, Pallas kernels: 7.61 us -> 8.48 us  [shards(): pl.pallas_call(functools.partial(coef_kernel, devices, per_dev), in_specs...]
  transfers between devices with their start and end apart: 6 -> 6, of which waited for: 4 -> 4; matrix products, arithmetic and copies ran while one was open for 0% -> 0% of each run, Pallas kernels for 10% -> 0%
where the time goes in v13:
time: 68.8 us; the launch traced here: 68.6 us
  blocking collectives  27.4 us (40%)
  Pallas kernels  26 us (38%)
  starting transfers between devices  9.68 us (14%)
  waiting for transfers between devices  5.37 us (8%)
    all_to_all x2, blocking collectives, to_all(): return lax.all_to_all(copies, 'dev', 0, 0, tiled=True)  27.4 us
    ppermute x6, starting transfers between devices, from_device(): lax.ppermute(block, 'dev', [(source(i) % devices, i) for i in range(devic...  9.68 us
    pallas_call x1, Pallas kernels, shards(): pl.pallas_call(functools.partial(coef_kernel, devices, per_dev), in_specs...  8.48 us
    pallas_call x1, Pallas kernels, shards(): pl.pallas_call(functools.partial(both_kernel, per_dev), in_specs=[vmem] *...  7.71 us
    pallas_call x2, Pallas kernels, mix(): pl.pallas_call(functools.partial(link_kernel, norm, devices, per_dev, fir...  6.5 us
    ppermute x6, waiting for transfers between devices, from_device(): lax.ppermute(block, 'dev', [(source(i) % devices, i) for i in range(devic...  5.37 us
    pallas_call x1, Pallas kernels, shards(): pl.pallas_call(functools.partial(last_kernel, per_dev), in_specs=[vmem] *...  3.28 us
  transfers between devices with their start and end apart: 6, of which 4 were waited for; matrix products, arithmetic and copies ran while one was open for 0% of the time, Pallas kernels for 0%

profile of v13, /device:TPU:0, one launch (start us, length us, event | category | flops | bytes accessed | tf_op | source)
XLA Modules:
  0.0 68.6 jit_solution(8929646842352280411)
XLA Ops:
  0.0 0.0 copy-start.2
  0.0 0.0 copy-start.1
  0.0 8.5 %coef_pass.1 = (bf16[4,640]{1,0:T(4,128)(2,1)S(1)}, bf16[128,65536]{1,0:T(8,128)(2,1)S(1)}, s32[512,128]{1,0:T(8,128)S(1)}, s32[24,128]{1,0:T(8,128)S(1)}) custom-call(s32[1,64]{1,0:T(1,128)} %bitcast.6, s32[512,128]{1,0:T(8,128)} %bitcast.7, bf16[512,128]{1,0:T(8,128)(2,1)} %bitcast.8, bf16[65536,128]{1,0:T(8,128)(2,1)} %basis_hbm.3), custom_call_target="tpu_custom_call" | custom-call | tf_op jit(solution)/shard_map/coef_pass/pallas_call | solution.py:300
  8.5 14.3 %all_to_all.10.parts_ref = bf16[16,4,640]{2,1,0:T(4,128)(2,1)S(1)} all-to-all(bf16[16,4,640]{2,1,0:T(4,128)(2,1)S(1)} %broadcast_in_dim.4), channel_id=1, replica_groups=mesh['groups'=2,'dev'=16] {'dev'}, dimensions={0} | all-to-all | bytes 163840 | tf_op jit(solution)/shard_map/all_to_all | solution.py:326
  22.9 0.0 copy-done.2
  22.9 0.0 copy-done.1
  22.9 4.3 %link_product.2 = (bf16[4,128]{1,0:T(4,128)(2,1)S(1)}, bf16[4,64,128,128]{3,2,1,0:T(8,128)(2,1)S(1)}) custom-call(s32[64]{0:T(128)S(1)} %copy-done.2, s32[4,64]{1,0:T(4,128)S(1)} %copy-done.1, bf16[16,4,640]{2,1,0:T(4,128)(2,1)S(1)} %all_to_all.10.parts_ref, bf16[4,64,128,128]{3,2,1,0:T(8,128)(2,1)} %refs_0_.1), custom_call_target="tpu_custom_call" | custom-call | tf_op jit(solution)/shard_map/link_product/pallas_call | solution.py:338
  27.2 0.1 collective-permute-start
  27.3 1.1 %collective-permute-done = bf16[4,128]{1,0:T(4,128)(2,1)S(1)} collective-permute-done((bf16[4,128]{1,0:T(4,128)(2,1)S(1)}, bf16[4,128]{1,0:T(4,128)(2,1)S(1)}, u32[]{:S(2)}, u32[]{:S(2)}) %collective-permute-start) | collective-permute-done | bytes 1056 | tf_op jit(solution)/shard_map/ppermute | solution.py:329
  28.4 0.1 collective-permute-start.2
  28.5 4.7 %collective-permute-start.1 = (bf16[8,128]{1,0:T(8,128)(2,1)S(1)}, bf16[8,128]{1,0:T(8,128)(2,1)S(1)}, u32[]{:S(2)}, u32[]{:S(2)}) collective-permute-start(bf16[8,128]{1,0:T(8,128)(2,1)S(1)} %pad_maximum_fusion.own_ref), channel_id=1, source_target_pairs={{2,0},{3,1},{4,2},{5,3},{6,4},{7,5},{8,6},{9,7},{10,8},{11,9},{12,... | collective-permute-start | bytes 6152 | tf_op jit(solution)/shard_map/ppermute | solution.py:329
  33.2 1.6 %collective-permute-done.2.behind_ref = bf16[8,128]{1,0:T(8,128)(2,1)S(1)} collective-permute-done((bf16[8,128]{1,0:T(8,128)(2,1)S(1)}, bf16[8,128]{1,0:T(8,128)(2,1)S(1)}, u32[]{:S(2)}, u32[]{:S(2)}) %collective-permute-start.2) | collective-permute-done | bytes 2080 | tf_op jit(solution)/shard_map/ppermute | solution.py:329
  34.8 0.0 collective-permute-done.1.ahead_ref
  34.8 0.0 copy-done
  34.8 7.7 %first_and_coef_pass.1 = (f32[512,128]{1,0:T(8,128)S(1)}, bf16[4,640]{1,0:T(4,128)(2,1)S(1)}) custom-call(s32[24,128]{1,0:T(8,128)S(1)} %get-tuple-element.13.cl_ref, bf16[8,128]{1,0:T(8,128)(2,1)S(1)} %collective-permute-done.1.ahead_ref, bf16[8,128]{1,0:T(8,128)(2,1)S(1)} %pad_maximum_fusion.own_ref, bf16[8,128]{1,0:T(8,128)(2,1)S(1)} %collective-permute-done.2.behind_ref, ...), custom_call_target="tpu_custom_call" | custom-call | tf_op jit(solution)/shard_map/first_and_coef_pass/pallas_call | solution.py:355
  42.5 13.0 %all_to_all.11.parts_ref = bf16[16,4,640]{2,1,0:T(4,128)(2,1)S(1)} all-to-all(bf16[16,4,640]{2,1,0:T(4,128)(2,1)S(1)} %broadcast_in_dim.5), channel_id=1, replica_groups=mesh['groups'=2,'dev'=16] {'dev'}, dimensions={0} | all-to-all | bytes 163840 | tf_op jit(solution)/shard_map/all_to_all | solution.py:326
  55.6 2.2 %link_product.3 = bf16[4,128]{1,0:T(4,128)(2,1)S(1)} custom-call(s32[64]{0:T(128)S(1)} %copy-done.2, s32[4,64]{1,0:T(4,128)S(1)} %copy-done.1, bf16[16,4,640]{2,1,0:T(4,128)(2,1)S(1)} %all_to_all.11.parts_ref, bf16[4,64,128,128]{3,2,1,0:T(8,128)(2,1)S(1)} %get-tuple-element.19.refs_0_), custom_call_target="tpu_custom_call" | custom-call | tf_op jit(solution)/shard_map/link_product/pallas_call | solution.py:338
  57.7 0.1 collective-permute-start.3
  57.8 1.1 %collective-permute-done.3 = bf16[4,128]{1,0:T(4,128)(2,1)S(1)} collective-permute-done((bf16[4,128]{1,0:T(4,128)(2,1)S(1)}, bf16[4,128]{1,0:T(4,128)(2,1)S(1)}, u32[]{:S(2)}, u32[]{:S(2)}) %collective-permute-start.3) | collective-permute-done | bytes 1056 | tf_op jit(solution)/shard_map/ppermute | solution.py:329
  58.9 0.1 collective-permute-start.5
  59.0 4.7 %collective-permute-start.4 = (bf16[8,128]{1,0:T(8,128)(2,1)S(1)}, bf16[8,128]{1,0:T(8,128)(2,1)S(1)}, u32[]{:S(2)}, u32[]{:S(2)}) collective-permute-start(bf16[8,128]{1,0:T(8,128)(2,1)S(1)} %pad_maximum_fusion.1.own_ref), channel_id=1, source_target_pairs={{2,0},{3,1},{4,2},{5,3},{6,4},{7,5},{8,6},{9,7},{10,8},{11,9},{12,... | collective-permute-start | bytes 6152 | tf_op jit(solution)/shard_map/ppermute | solution.py:329
  63.7 1.6 %collective-permute-done.5.behind_ref = bf16[8,128]{1,0:T(8,128)(2,1)S(1)} collective-permute-done((bf16[8,128]{1,0:T(8,128)(2,1)S(1)}, bf16[8,128]{1,0:T(8,128)(2,1)S(1)}, u32[]{:S(2)}, u32[]{:S(2)}) %collective-permute-start.5) | collective-permute-done | bytes 2080 | tf_op jit(solution)/shard_map/ppermute | solution.py:329
  65.3 0.0 collective-permute-done.4.ahead_ref
  65.3 3.3 %last_pass.1 = f32[512,128]{1,0:T(8,128)} custom-call(s32[24,128]{1,0:T(8,128)S(1)} %get-tuple-element.13.cl_ref, bf16[8,128]{1,0:T(8,128)(2,1)S(1)} %collective-permute-done.4.ahead_ref, bf16[8,128]{1,0:T(8,128)(2,1)S(1)} %pad_maximum_fusion.1.own_ref, bf16[8,128]{1,0:T(8,128)(2,1)S(1)} %collective-permute-done.5.behind_ref, ...), custom_call_target="tpu_custom_call" | custom-call | tf_op jit(solution)/shard_map/last_pass/pallas_call | solution.py:376
  (5 shorter events, 0.1 us)
Async XLA Ops:
  0.0 22.9 %copy-start.2 = (s32[64]{0:T(128)S(1)}, s32[64]{0:T(128)}, u32[]{:S(2)}) copy-start(s32[64]{0:T(128)} %slot_of_ref.3) | copy-start | bytes 772
  0.0 22.9 %copy-start.1 = (s32[4,64]{1,0:T(4,128)S(1)}, s32[4,64]{1,0:T(4,128)}, u32[]{:S(2)}) copy-start(s32[4,64]{1,0:T(4,128)} %partners_ref.3) | copy-start | bytes 3076
  0.0 34.8 %copy-start = (f32[65536]{0:T(1024)S(1)}, f32[65536]{0:T(1024)}, u32[]{:S(2)}) copy-start(f32[65536]{0:T(1024)} %param.9) | copy-start | bytes 786436
  27.2 1.2 %collective-permute-start = (bf16[4,128]{1,0:T(4,128)(2,1)S(1)}, bf16[4,128]{1,0:T(4,128)(2,1)S(1)}, u32[]{:S(2)}, u32[]{:S(2)}) collective-permute-start(bf16[4,128]{1,0:T(4,128)(2,1)S(1)} %get-tuple-element.15), channel_id=1, source_target_pairs={{1,0},{0,1},{3,2},{2,3},{5,4},{4,5},{7,6},{6,7},{9,8},{8,9},{11,10... | collective-permute-start | bytes 3080 | tf_op jit(solution)/shard_map/ppermute | solution.py:329
  28.4 6.3 %collective-permute-start.2 = (bf16[8,128]{1,0:T(8,128)(2,1)S(1)}, bf16[8,128]{1,0:T(8,128)(2,1)S(1)}, u32[]{:S(2)}, u32[]{:S(2)}) collective-permute-start(bf16[8,128]{1,0:T(8,128)(2,1)S(1)} %pad_maximum_fusion.own_ref), channel_id=1, source_target_pairs={{14,0},{15,1},{0,2},{1,3},{2,4},{3,5},{4,6},{5,7},{6,8},{7,9},{8,1... | collective-permute-start | bytes 6152 | tf_op jit(solution)/shard_map/ppermute | solution.py:329
  28.5 6.3 %collective-permute-start.1 = (bf16[8,128]{1,0:T(8,128)(2,1)S(1)}, bf16[8,128]{1,0:T(8,128)(2,1)S(1)}, u32[]{:S(2)}, u32[]{:S(2)}) collective-permute-start(bf16[8,128]{1,0:T(8,128)(2,1)S(1)} %pad_maximum_fusion.own_ref), channel_id=1, source_target_pairs={{2,0},{3,1},{4,2},{5,3},{6,4},{7,5},{8,6},{9,7},{10,8},{11,9},{12,... | collective-permute-start | bytes 6152 | tf_op jit(solution)/shard_map/ppermute | solution.py:329
  57.7 1.2 %collective-permute-start.3 = (bf16[4,128]{1,0:T(4,128)(2,1)S(1)}, bf16[4,128]{1,0:T(4,128)(2,1)S(1)}, u32[]{:S(2)}, u32[]{:S(2)}) collective-permute-start(bf16[4,128]{1,0:T(4,128)(2,1)S(1)} %link_product.3), channel_id=1, source_target_pairs={{1,0},{0,1},{3,2},{2,3},{5,4},{4,5},{7,6},{6,7},{9,8},{8,9},{11,10... | collective-permute-start | bytes 3080 | tf_op jit(solution)/shard_map/ppermute | solution.py:329
  58.9 6.3 %collective-permute-start.5 = (bf16[8,128]{1,0:T(8,128)(2,1)S(1)}, bf16[8,128]{1,0:T(8,128)(2,1)S(1)}, u32[]{:S(2)}, u32[]{:S(2)}) collective-permute-start(bf16[8,128]{1,0:T(8,128)(2,1)S(1)} %pad_maximum_fusion.1.own_ref), channel_id=1, source_target_pairs={{14,0},{15,1},{0,2},{1,3},{2,4},{3,5},{4,6},{5,7},{6,8},{7,9},{8,1... | collective-permute-start | bytes 6152 | tf_op jit(solution)/shard_map/ppermute | solution.py:329
  59.0 6.3 %collective-permute-start.4 = (bf16[8,128]{1,0:T(8,128)(2,1)S(1)}, bf16[8,128]{1,0:T(8,128)(2,1)S(1)}, u32[]{:S(2)}, u32[]{:S(2)}) collective-permute-start(bf16[8,128]{1,0:T(8,128)(2,1)S(1)} %pad_maximum_fusion.1.own_ref), channel_id=1, source_target_pairs={{2,0},{3,1},{4,2},{5,3},{6,4},{7,5},{8,6},{9,7},{10,8},{11,9},{12,... | collective-permute-start | bytes 6152 | tf_op jit(solution)/shard_map/ppermute | solution.py:329

commit v14 on v13

--- a/solution.py
+++ b/solution.py
@@ -39,9 +39,11 @@
     cl_ref[...] = jnp.broadcast_to(found, cl_ref.shape)
 
 
-def near_rows(per_dev, chips, rows_ref):
-    even_core = lax.rem(lax.axis_index("dev"), 2) == 0
-    chips = [chip[...].astype(jnp.float32) for chip in chips]
+def near_rows(devices, per_dev, chips, wrap_ref, rows_ref):
+    me = lax.axis_index("dev")
+    even_core = lax.rem(me, 2) == 0
+    behind, own, ahead, wrap = [chip[...].astype(jnp.float32) for chip in (*chips, wrap_ref)]
+    chips = [jnp.where(me < 2, wrap, behind), own, jnp.where(me >= devices - 2, wrap, ahead)]
     rows_ref[...] = jnp.zeros_like(rows_ref)
     for g in range(NEAR):
         if g % 2 == 0:
@@ -73,7 +75,7 @@
 def coef_kernel(
     devices, per_dev, slot_of_hbm, assign_hbm, vector_hbm, basis_hbm,
     out_ref, turned_ref, assign_ref, cl_ref,
-    slot_of_ref, sum_ref, vector_ref, x_ref, slots_ref, small_sem, basis_sem, last_sem,
+    slot_of_ref, sum_ref, vector_ref, x_ref, slots_ref, small_sem, basis_sem,
 ):
     copies = basis_hbm.shape[0] // COPY
 
@@ -96,47 +98,26 @@
     x_ref[...] = vector_ref[...].astype(jnp.float32)
     cl = cl_ref[...]
 
-    last = copies - 1
-
-    def last_copy(p):
-        rows = pl.ds(last * COPY + p * TILE, TILE)
-        return pltpu.make_async_copy(
-            basis_hbm.at[rows, :], slots_ref.at[last % SLOTS, pl.ds(p * TILE, TILE)], last_sem.at[p]
-        )
-
-    def add_up(c, p, total):
-        t = c * PER_COPY + p
-        parts = []
-        for i in range(TILE // LANES):
-            hit = assign_ref[row_at(t, i), :] == cl
-            parts.append(jnp.where(hit, x_ref[row_at(t, i), :], 0.0).astype(jnp.bfloat16))
-        left = jnp.concatenate(parts, axis=1)
-        block = slots_ref[lax.rem(c, SLOTS), p * TILE : (p + 1) * TILE, :]
-        turned_ref[:, tile_at(t)] = block.T
-        return total + jnp.dot(left, block, preferred_element_type=jnp.float32)
-
-    @pl.loop(0, last)
+    @pl.loop(0, copies)
     def _(c):
         basis_copy(c).wait()
         total = sum_ref[...]
         for p in range(PER_COPY):
-            total = add_up(c, p, total)
+            t = c * PER_COPY + p
+            parts = []
+            for i in range(TILE // LANES):
+                hit = assign_ref[row_at(t, i), :] == cl
+                parts.append(jnp.where(hit, x_ref[row_at(t, i), :], 0.0).astype(jnp.bfloat16))
+            left = jnp.concatenate(parts, axis=1)
+            block = slots_ref[lax.rem(c, SLOTS), p * TILE : (p + 1) * TILE, :]
+            turned_ref[:, tile_at(t)] = block.T
+            total += jnp.dot(left, block, preferred_element_type=jnp.float32)
         sum_ref[...] = total
 
-        @pl.when(c + SLOTS < last)
+        @pl.when(c + SLOTS < copies)
         def _():
             basis_copy(c + SLOTS).start()
 
-        @pl.when(c + SLOTS == last)
-        def _():
-            for p in range(PER_COPY):
-                last_copy(p).start()
-
-    total = sum_ref[...]
-    for p in range(PER_COPY):
-        last_copy(p).wait()
-        total = add_up(last, p, total)
-    sum_ref[...] = total
     put_sums(per_dev, sum_ref, out_ref)
 
 
@@ -192,7 +173,7 @@
 
 
 def both_kernel(
-    per_dev, cl_ref, ahead_ref, own_ref, behind_ref, assign_ref, scores_ref, turned_ref, basis_hbm,
+    devices, per_dev, cl_ref, behind_ref, own_ref, ahead_ref, wrap_ref, assign_ref, scores_ref, turned_ref, basis_hbm,
     first_ref, out_ref, rows_ref, sum_ref, slope_ref, even_ref, odd_ref, even_left, odd_left, slots_ref, basis_sem,
 ):
     tiles = turned_ref.shape[1] // TILE
@@ -203,7 +184,7 @@
 
     for c in range(SLOTS):
         basis_copy(c).start()
-    near_rows(per_dev, (behind_ref, own_ref, ahead_ref), rows_ref)
+    near_rows(devices, per_dev, (behind_ref, own_ref, ahead_ref), wrap_ref, rows_ref)
     sum_ref[...] = jnp.zeros_like(sum_ref)
     sig = jax.nn.sigmoid(scores_ref[...])
     slope_ref[...] = sig * (1.0 - sig)
@@ -257,9 +238,9 @@
 
 
 def last_kernel(
-    per_dev, cl_ref, ahead_ref, own_ref, behind_ref, assign_ref, first_ref, turned_ref, out_ref, rows_ref
+    devices, per_dev, cl_ref, behind_ref, own_ref, ahead_ref, wrap_ref, assign_ref, first_ref, turned_ref, out_ref, rows_ref
 ):
-    near_rows(per_dev, (behind_ref, own_ref, ahead_ref), rows_ref)
+    near_rows(devices, per_dev, (behind_ref, own_ref, ahead_ref), wrap_ref, rows_ref)
     cl = cl_ref[...]
     rows = rows_ref[...].astype(jnp.bfloat16)
 
@@ -315,7 +296,6 @@
             pltpu.VMEM((SLOTS, COPY, rank), bf16),
             pltpu.SemaphoreType.DMA((3,)),
             pltpu.SemaphoreType.DMA((SLOTS,)),
-            pltpu.SemaphoreType.DMA((PER_COPY,)),
         ],
         compiler_params=params,
         name="coef_pass",
@@ -325,14 +305,17 @@
         copies = jnp.broadcast_to(block[None], (devices,) + block.shape)
         return lax.all_to_all(copies, "dev", 0, 0, tiled=True)
 
-    def from_device(block, source):
-        return lax.ppermute(block, "dev", [(source(i) % devices, i) for i in range(devices)])
+    def permute(block, pairs):
+        return lax.ppermute(block, "dev", pairs)
 
     def to_chips(mixed):
-        own = jnp.concatenate([mixed, from_device(mixed, lambda i: i ^ 1)], axis=0)
-        ahead = from_device(own, lambda i: i + 2)
-        behind = from_device(own, lambda i: i - 2)
-        return ahead, own, behind
+        sibling = permute(mixed, [(i ^ 1, i) for i in range(devices)])
+        own = jnp.concatenate([mixed, sibling], axis=0)
+        behind = permute(own, [(i - 2, i) for i in range(2, devices)])
+        ahead = permute(own, [(i + 2, i) for i in range(devices - 2)])
+        ends = [(i, devices - 2 + i) for i in range(2)]
+        wrap = permute(own, ends + [(j, i) for i, j in ends])
+        return behind, own, ahead, wrap
 
     def mix(coef, links, first_time):
         out = pl.pallas_call(
@@ -353,8 +336,8 @@
 
     mixed1, links_v = mix(to_all(coef1), far(link_blocks), True)
     first, coef2 = pl.pallas_call(
-        functools.partial(both_kernel, per_dev),
-        in_specs=[vmem] * 7 + [hbm],
+        functools.partial(both_kernel, devices, per_dev),
+        in_specs=[vmem] * 8 + [hbm],
         out_specs=[vmem, vmem],
         out_shape=[pltpu.VMEM((high, LANES), f32), coef_shape],
         scratch_shapes=[
@@ -374,8 +357,8 @@
     (mixed2,) = mix(to_all(coef2), close(links_v), False)
 
     out = pl.pallas_call(
-        functools.partial(last_kernel, per_dev),
-        in_specs=[vmem] * 7,
+        functools.partial(last_kernel, devices, per_dev),
+        in_specs=[vmem] * 8,
         out_specs=vmem,
         out_shape=jax.ShapeDtypeStruct((high, LANES), f32),
         scratch_shapes=[

time: 68.8 us -> 74.4 us (1.081)
  starting transfers between devices: 9.68 us -> 17.1 us
  blocking collectives: 27.4 us -> 26.3 us
    ppermute x6 -> x8, starting transfers between devices: 9.68 us -> 17.1 us  [permute(): return lax.ppermute(block, 'dev', pairs)]
    all_to_all x2, blocking collectives: 27.4 us -> 26.3 us  [to_all(): return lax.all_to_all(copies, 'dev', 0, 0, tiled=True)]
    ppermute x6 -> x8, waiting for transfers between devices: 5.37 us -> 4.8 us  [permute(): return lax.ppermute(block, 'dev', pairs)]
  transfers between devices with their start and end apart: 6 -> 8, of which waited for: 4 -> 4; matrix products, arithmetic and copies ran while one was open for 0% -> 0% of each run, Pallas kernels for 0% -> 0%
where the time goes in v14:
time: 74.4 us; the launch traced here: 74.1 us
  blocking collectives  26.3 us (35%)
  Pallas kernels  25.7 us (35%)
  starting transfers between devices  17.1 us (23%)
  waiting for transfers between devices  4.8 us (6%)
    all_to_all x2, blocking collectives, to_all(): return lax.all_to_all(copies, 'dev', 0, 0, tiled=True)  26.3 us
    ppermute x8, starting transfers between devices, permute(): return lax.ppermute(block, 'dev', pairs)  17.1 us
    pallas_call x1, Pallas kernels, shards(): pl.pallas_call(functools.partial(coef_kernel, devices, per_dev), in_specs...  8.2 us
    pallas_call x1, Pallas kernels, shards(): pl.pallas_call(functools.partial(both_kernel, devices, per_dev), in_specs...  7.69 us
    pallas_call x2, Pallas kernels, mix(): pl.pallas_call(functools.partial(link_kernel, norm, devices, per_dev, fir...  6.55 us
    ppermute x8, waiting for transfers between devices, permute(): return lax.ppermute(block, 'dev', pairs)  4.8 us
    pallas_call x1, Pallas kernels, shards(): pl.pallas_call(functools.partial(last_kernel, devices, per_dev), in_specs...  3.25 us
  transfers between devices with their start and end apart: 8, of which 4 were waited for; matrix products, arithmetic and copies ran while one was open for 0% of the time, Pallas kernels for 0%

profile of v14, /device:TPU:0, one launch (start us, length us, event | category | flops | bytes accessed | tf_op | source)
XLA Modules:
  0.0 74.1 jit_solution(15184632489688312533)
XLA Ops:
  0.0 8.2 %coef_pass.1 = (bf16[4,640]{1,0:T(4,128)(2,1)S(1)}, bf16[128,65536]{1,0:T(8,128)(2,1)S(1)}, s32[512,128]{1,0:T(8,128)S(1)}, s32[24,128]{1,0:T(8,128)S(1)}) custom-call(s32[1,64]{1,0:T(1,128)} %bitcast.6, s32[512,128]{1,0:T(8,128)} %bitcast.7, bf16[512,128]{1,0:T(8,128)(2,1)} %bitcast.8, bf16[65536,128]{1,0:T(8,128)(2,1)} %basis_hbm.3), custom_call_target="tpu_custom_call" | custom-call | tf_op jit(solution)/shard_map/coef_pass/pallas_call | solution.py:281
  8.2 14.3 %all_to_all.10.parts_ref = bf16[16,4,640]{2,1,0:T(4,128)(2,1)S(1)} all-to-all(bf16[16,4,640]{2,1,0:T(4,128)(2,1)S(1)} %broadcast_in_dim.4), channel_id=1, replica_groups=mesh['groups'=2,'dev'=16] {'dev'}, dimensions={0} | all-to-all | bytes 163840 | tf_op jit(solution)/shard_map/all_to_all | solution.py:306
  22.6 0.0 copy-done.2
  22.6 4.3 %link_product.2 = (bf16[4,128]{1,0:T(4,128)(2,1)S(1)}, bf16[4,64,128,128]{3,2,1,0:T(8,128)(2,1)S(1)}) custom-call(s32[64]{0:T(128)S(1)} %copy-done.2, s32[4,64]{1,0:T(4,128)S(1)} %copy-done.1, bf16[16,4,640]{2,1,0:T(4,128)(2,1)S(1)} %all_to_all.10.parts_ref, bf16[4,64,128,128]{3,2,1,0:T(8,128)(2,1)} %refs_0_.1), custom_call_target="tpu_custom_call" | custom-call | tf_op jit(solution)/shard_map/link_product/pallas_call | solution.py:321
  26.9 0.1 collective-permute-start
  27.0 1.1 %collective-permute-done = bf16[4,128]{1,0:T(4,128)(2,1)S(1)} collective-permute-done((bf16[4,128]{1,0:T(4,128)(2,1)S(1)}, bf16[4,128]{1,0:T(4,128)(2,1)S(1)}, u32[]{:S(2)}, u32[]{:S(2)}) %collective-permute-start) | collective-permute-done | bytes 1056 | tf_op jit(solution)/shard_map/ppermute | solution.py:309
  28.2 2.6 %collective-permute-start.3 = (bf16[8,128]{1,0:T(8,128)(2,1)S(1)}, bf16[8,128]{1,0:T(8,128)(2,1)S(1)}, u32[]{:S(2)}, u32[]{:S(2)}) collective-permute-start(bf16[8,128]{1,0:T(8,128)(2,1)S(1)} %pad_maximum_fusion.own_ref), channel_id=1, source_target_pairs={{0,14},{1,15},{14,0},{15,1},{16,30},{17,31},{30,16},{31,17}} | collective-permute-start | bytes 6152 | tf_op jit(solution)/shard_map/ppermute | solution.py:309
  30.8 1.3 %collective-permute-start.2 = (bf16[8,128]{1,0:T(8,128)(2,1)S(1)}, bf16[8,128]{1,0:T(8,128)(2,1)S(1)}, u32[]{:S(2)}, u32[]{:S(2)}) collective-permute-start(bf16[8,128]{1,0:T(8,128)(2,1)S(1)} %pad_maximum_fusion.own_ref), channel_id=1, source_target_pairs={{2,0},{3,1},{4,2},{5,3},{6,4},{7,5},{8,6},{9,7},{10,8},{11,9},{12,... | collective-permute-start | bytes 6152 | tf_op jit(solution)/shard_map/ppermute | solution.py:309
  32.1 4.5 %collective-permute-start.1 = (bf16[8,128]{1,0:T(8,128)(2,1)S(1)}, bf16[8,128]{1,0:T(8,128)(2,1)S(1)}, u32[]{:S(2)}, u32[]{:S(2)}) collective-permute-start(bf16[8,128]{1,0:T(8,128)(2,1)S(1)} %pad_maximum_fusion.own_ref), channel_id=1, source_target_pairs={{0,2},{1,3},{2,4},{3,5},{4,6},{5,7},{6,8},{7,9},{8,10},{9,11},{10,... | collective-permute-start | bytes 6152 | tf_op jit(solution)/shard_map/ppermute | solution.py:309
  36.7 0.0 collective-permute-done.3.wrap_ref
  36.7 0.0 collective-permute-done.2.ahead_ref
  36.7 1.3 %collective-permute-done.1.behind_ref = bf16[8,128]{1,0:T(8,128)(2,1)S(1)} collective-permute-done((bf16[8,128]{1,0:T(8,128)(2,1)S(1)}, bf16[8,128]{1,0:T(8,128)(2,1)S(1)}, u32[]{:S(2)}, u32[]{:S(2)}) %collective-permute-start.1) | collective-permute-done | bytes 2080 | tf_op jit(solution)/shard_map/ppermute | solution.py:309
  37.9 7.7 %first_and_coef_pass.1 = (f32[512,128]{1,0:T(8,128)S(1)}, bf16[4,640]{1,0:T(4,128)(2,1)S(1)}) custom-call(s32[24,128]{1,0:T(8,128)S(1)} %get-tuple-element.13.cl_ref, bf16[8,128]{1,0:T(8,128)(2,1)S(1)} %collective-permute-done.1.behind_ref, bf16[8,128]{1,0:T(8,128)(2,1)S(1)} %pad_maximum_fusion.own_ref, bf16[8,128]{1,0:T(8,128)(2,1)S(1)} %collective-permute-done.2.ahead_ref, ...), custom_call_target="tpu_custom_call" | custom-call | tf_op jit(solution)/shard_map/first_and_coef_pass/pallas_call | solution.py:338
  45.7 12.0 %all_to_all.11.parts_ref = bf16[16,4,640]{2,1,0:T(4,128)(2,1)S(1)} all-to-all(bf16[16,4,640]{2,1,0:T(4,128)(2,1)S(1)} %broadcast_in_dim.5), channel_id=1, replica_groups=mesh['groups'=2,'dev'=16] {'dev'}, dimensions={0} | all-to-all | bytes 163840 | tf_op jit(solution)/shard_map/all_to_all | solution.py:306
  57.6 2.2 %link_product.3 = bf16[4,128]{1,0:T(4,128)(2,1)S(1)} custom-call(s32[64]{0:T(128)S(1)} %copy-done.2, s32[4,64]{1,0:T(4,128)S(1)} %copy-done.1, bf16[16,4,640]{2,1,0:T(4,128)(2,1)S(1)} %all_to_all.11.parts_ref, bf16[4,64,128,128]{3,2,1,0:T(8,128)(2,1)S(1)} %get-tuple-element.19.refs_0_), custom_call_target="tpu_custom_call" | custom-call | tf_op jit(solution)/shard_map/link_product/pallas_call | solution.py:321
  59.8 0.1 collective-permute-start.4
  59.9 1.1 %collective-permute-done.4 = bf16[4,128]{1,0:T(4,128)(2,1)S(1)} collective-permute-done((bf16[4,128]{1,0:T(4,128)(2,1)S(1)}, bf16[4,128]{1,0:T(4,128)(2,1)S(1)}, u32[]{:S(2)}, u32[]{:S(2)}) %collective-permute-start.4) | collective-permute-done | bytes 1056 | tf_op jit(solution)/shard_map/ppermute | solution.py:309
  61.1 2.6 %collective-permute-start.7 = (bf16[8,128]{1,0:T(8,128)(2,1)S(1)}, bf16[8,128]{1,0:T(8,128)(2,1)S(1)}, u32[]{:S(2)}, u32[]{:S(2)}) collective-permute-start(bf16[8,128]{1,0:T(8,128)(2,1)S(1)} %pad_maximum_fusion.1.own_ref), channel_id=1, source_target_pairs={{0,14},{1,15},{14,0},{15,1},{16,30},{17,31},{30,16},{31,17}} | collective-permute-start | bytes 6152 | tf_op jit(solution)/shard_map/ppermute | solution.py:309
  63.7 1.3 %collective-permute-start.6 = (bf16[8,128]{1,0:T(8,128)(2,1)S(1)}, bf16[8,128]{1,0:T(8,128)(2,1)S(1)}, u32[]{:S(2)}, u32[]{:S(2)}) collective-permute-start(bf16[8,128]{1,0:T(8,128)(2,1)S(1)} %pad_maximum_fusion.1.own_ref), channel_id=1, source_target_pairs={{2,0},{3,1},{4,2},{5,3},{6,4},{7,5},{8,6},{9,7},{10,8},{11,9},{12,... | collective-permute-start | bytes 6152 | tf_op jit(solution)/shard_map/ppermute | solution.py:309
  65.0 4.5 %collective-permute-start.5 = (bf16[8,128]{1,0:T(8,128)(2,1)S(1)}, bf16[8,128]{1,0:T(8,128)(2,1)S(1)}, u32[]{:S(2)}, u32[]{:S(2)}) collective-permute-start(bf16[8,128]{1,0:T(8,128)(2,1)S(1)} %pad_maximum_fusion.1.own_ref), channel_id=1, source_target_pairs={{0,2},{1,3},{2,4},{3,5},{4,6},{5,7},{6,8},{7,9},{8,10},{9,11},{10,... | collective-permute-start | bytes 6152 | tf_op jit(solution)/shard_map/ppermute | solution.py:309
  69.6 0.0 collective-permute-done.7.wrap_ref
  69.6 0.0 collective-permute-done.6.ahead_ref
  69.6 1.3 %collective-permute-done.5.behind_ref = bf16[8,128]{1,0:T(8,128)(2,1)S(1)} collective-permute-done((bf16[8,128]{1,0:T(8,128)(2,1)S(1)}, bf16[8,128]{1,0:T(8,128)(2,1)S(1)}, u32[]{:S(2)}, u32[]{:S(2)}) %collective-permute-start.5) | collective-permute-done | bytes 2080 | tf_op jit(solution)/shard_map/ppermute | solution.py:309
  70.8 3.2 %last_pass.1 = f32[512,128]{1,0:T(8,128)} custom-call(s32[24,128]{1,0:T(8,128)S(1)} %get-tuple-element.13.cl_ref, bf16[8,128]{1,0:T(8,128)(2,1)S(1)} %collective-permute-done.5.behind_ref, bf16[8,128]{1,0:T(8,128)(2,1)S(1)} %pad_maximum_fusion.1.own_ref, bf16[8,128]{1,0:T(8,128)(2,1)S(1)} %collective-permute-done.6.ahead_ref, ...), custom_call_target="tpu_custom_call" | custom-call | tf_op jit(solution)/shard_map/last_pass/pallas_call | solution.py:359
  (9 shorter events, 0.1 us)
Async XLA Ops:
  0.0 22.6 %copy-start.2 = (s32[64]{0:T(128)S(1)}, s32[64]{0:T(128)}, u32[]{:S(2)}) copy-start(s32[64]{0:T(128)} %slot_of_ref.3) | copy-start | bytes 772
  0.0 22.6 %copy-start.1 = (s32[4,64]{1,0:T(4,128)S(1)}, s32[4,64]{1,0:T(4,128)}, u32[]{:S(2)}) copy-start(s32[4,64]{1,0:T(4,128)} %partners_ref.3) | copy-start | bytes 3076
  0.0 37.9 %copy-start = (f32[65536]{0:T(1024)S(1)}, f32[65536]{0:T(1024)}, u32[]{:S(2)}) copy-start(f32[65536]{0:T(1024)} %param.9) | copy-start | bytes 786436
  26.9 1.2 %collective-permute-start = (bf16[4,128]{1,0:T(4,128)(2,1)S(1)}, bf16[4,128]{1,0:T(4,128)(2,1)S(1)}, u32[]{:S(2)}, u32[]{:S(2)}) collective-permute-start(bf16[4,128]{1,0:T(4,128)(2,1)S(1)} %get-tuple-element.15), channel_id=1, source_target_pairs={{1,0},{0,1},{3,2},{2,3},{5,4},{4,5},{7,6},{6,7},{9,8},{8,9},{11,10... | collective-permute-start | bytes 3080 | tf_op jit(solution)/shard_map/ppermute | solution.py:309
  28.2 8.5 %collective-permute-start.3 = (bf16[8,128]{1,0:T(8,128)(2,1)S(1)}, bf16[8,128]{1,0:T(8,128)(2,1)S(1)}, u32[]{:S(2)}, u32[]{:S(2)}) collective-permute-start(bf16[8,128]{1,0:T(8,128)(2,1)S(1)} %pad_maximum_fusion.own_ref), channel_id=1, source_target_pairs={{0,14},{1,15},{14,0},{15,1},{16,30},{17,31},{30,16},{31,17}} | collective-permute-start | bytes 6152 | tf_op jit(solution)/shard_map/ppermute | solution.py:309
  30.8 5.9 %collective-permute-start.2 = (bf16[8,128]{1,0:T(8,128)(2,1)S(1)}, bf16[8,128]{1,0:T(8,128)(2,1)S(1)}, u32[]{:S(2)}, u32[]{:S(2)}) collective-permute-start(bf16[8,128]{1,0:T(8,128)(2,1)S(1)} %pad_maximum_fusion.own_ref), channel_id=1, source_target_pairs={{2,0},{3,1},{4,2},{5,3},{6,4},{7,5},{8,6},{9,7},{10,8},{11,9},{12,... | collective-permute-start | bytes 6152 | tf_op jit(solution)/shard_map/ppermute | solution.py:309
  32.1 5.8 %collective-permute-start.1 = (bf16[8,128]{1,0:T(8,128)(2,1)S(1)}, bf16[8,128]{1,0:T(8,128)(2,1)S(1)}, u32[]{:S(2)}, u32[]{:S(2)}) collective-permute-start(bf16[8,128]{1,0:T(8,128)(2,1)S(1)} %pad_maximum_fusion.own_ref), channel_id=1, source_target_pairs={{0,2},{1,3},{2,4},{3,5},{4,6},{5,7},{6,8},{7,9},{8,10},{9,11},{10,... | collective-permute-start | bytes 6152 | tf_op jit(solution)/shard_map/ppermute | solution.py:309
  59.8 1.2 %collective-permute-start.4 = (bf16[4,128]{1,0:T(4,128)(2,1)S(1)}, bf16[4,128]{1,0:T(4,128)(2,1)S(1)}, u32[]{:S(2)}, u32[]{:S(2)}) collective-permute-start(bf16[4,128]{1,0:T(4,128)(2,1)S(1)} %link_product.3), channel_id=1, source_target_pairs={{1,0},{0,1},{3,2},{2,3},{5,4},{4,5},{7,6},{6,7},{9,8},{8,9},{11,10... | collective-permute-start | bytes 3080 | tf_op jit(solution)/shard_map/ppermute | solution.py:309
  61.1 8.5 %collective-permute-start.7 = (bf16[8,128]{1,0:T(8,128)(2,1)S(1)}, bf16[8,128]{1,0:T(8,128)(2,1)S(1)}, u32[]{:S(2)}, u32[]{:S(2)}) collective-permute-start(bf16[8,128]{1,0:T(8,128)(2,1)S(1)} %pad_maximum_fusion.1.own_ref), channel_id=1, source_target_pairs={{0,14},{1,15},{14,0},{15,1},{16,30},{17,31},{30,16},{31,17}} | collective-permute-start | bytes 6152 | tf_op jit(solution)/shard_map/ppermute | solution.py:309
  63.7 5.9 %collective-permute-start.6 = (bf16[8,128]{1,0:T(8,128)(2,1)S(1)}, bf16[8,128]{1,0:T(8,128)(2,1)S(1)}, u32[]{:S(2)}, u32[]{:S(2)}) collective-permute-start(bf16[8,128]{1,0:T(8,128)(2,1)S(1)} %pad_maximum_fusion.1.own_ref), channel_id=1, source_target_pairs={{2,0},{3,1},{4,2},{5,3},{6,4},{7,5},{8,6},{9,7},{10,8},{11,9},{12,... | collective-permute-start | bytes 6152 | tf_op jit(solution)/shard_map/ppermute | solution.py:309
  65.0 5.8 %collective-permute-start.5 = (bf16[8,128]{1,0:T(8,128)(2,1)S(1)}, bf16[8,128]{1,0:T(8,128)(2,1)S(1)}, u32[]{:S(2)}, u32[]{:S(2)}) collective-permute-start(bf16[8,128]{1,0:T(8,128)(2,1)S(1)} %pad_maximum_fusion.1.own_ref), channel_id=1, source_target_pairs={{0,2},{1,3},{2,4},{3,5},{4,6},{5,7},{6,8},{7,9},{8,10},{9,11},{10,... | collective-permute-start | bytes 6152 | tf_op jit(solution)/shard_map/ppermute | solution.py:309

commit v15 on v14

--- a/solution.py
+++ b/solution.py
@@ -22,7 +22,6 @@
 BODY = 16
 PIECE = 512
 GROUP = 8
-LINKS = 32
 
 ridge = 0.5
 
@@ -39,11 +38,9 @@
     cl_ref[...] = jnp.broadcast_to(found, cl_ref.shape)
 
 
-def near_rows(devices, per_dev, chips, wrap_ref, rows_ref):
-    me = lax.axis_index("dev")
-    even_core = lax.rem(me, 2) == 0
-    behind, own, ahead, wrap = [chip[...].astype(jnp.float32) for chip in (*chips, wrap_ref)]
-    chips = [jnp.where(me < 2, wrap, behind), own, jnp.where(me >= devices - 2, wrap, ahead)]
+def near_rows(per_dev, chips, rows_ref):
+    even_core = lax.rem(lax.axis_index("dev"), 2) == 0
+    chips = [chip[...].astype(jnp.float32) for chip in chips]
     rows_ref[...] = jnp.zeros_like(rows_ref)
     for g in range(NEAR):
         if g % 2 == 0:
@@ -73,14 +70,17 @@
 
 
 def coef_kernel(
-    devices, per_dev, slot_of_hbm, assign_hbm, vector_hbm, basis_hbm,
-    out_ref, turned_ref, assign_ref, cl_ref,
-    slot_of_ref, sum_ref, vector_ref, x_ref, slots_ref, small_sem, basis_sem,
+    devices, per_dev, slot_of_hbm, assign_hbm, vector_hbm, basis_hbm, links_hbm,
+    out_ref, turned_ref, assign_ref, cl_ref, links_ref,
+    slot_of_ref, sum_ref, vector_ref, x_ref, slots_ref, small_sem, basis_sem, links_sem,
 ):
     copies = basis_hbm.shape[0] // COPY
 
     def basis_copy(c):
         return slot_copy(basis_hbm, slots_ref, basis_sem, c)
+
+    def links_copy(j):
+        return pltpu.make_async_copy(links_hbm.at[j], links_ref.at[j], links_sem.at[j])
 
     slot_of_copy = pltpu.make_async_copy(slot_of_hbm, slot_of_ref, small_sem.at[2])
     assign_copy = pltpu.make_async_copy(assign_hbm, assign_ref, small_sem.at[0])
@@ -101,6 +101,11 @@
     @pl.loop(0, copies)
     def _(c):
         basis_copy(c).wait()
+
+        @pl.when(c < per_dev)
+        def _():
+            links_copy(c).start()
+
         total = sum_ref[...]
         for p in range(PER_COPY):
             t = c * PER_COPY + p
@@ -119,24 +124,15 @@
             basis_copy(c + SLOTS).start()
 
     put_sums(per_dev, sum_ref, out_ref)
-
-
-def link_kernel(norm, devices, per_dev, first_time, slot_of_ref, partners_ref, parts_ref, *refs):
-    if first_time:
-        links_hbm, out_ref, links_ref, scaled_ref, picked_ref, mixed_ref, links_sem = refs
-    else:
-        links_ref, out_ref, scaled_ref, picked_ref, mixed_ref = refs
+    for j in range(per_dev):
+        links_copy(j).wait()
+
+
+def link_kernel(
+    norm, devices, per_dev, slot_of_ref, partners_ref, parts_ref, links_ref, out_ref, scaled_ref, picked_ref, mixed_ref
+):
     n_links, rank = links_ref.shape[1:3]
     step = 2 * GROUP
-
-    def piece_copy(j, k):
-        ks = pl.ds(k, LINKS)
-        return pltpu.make_async_copy(links_hbm.at[j, ks], links_ref.at[j, ks], links_sem.at[(j * n_links + k) // LINKS])
-
-    if first_time:
-        for j in range(per_dev):
-            for k in range(0, n_links, LINKS):
-                piece_copy(j, k).start()
     for owner in range(devices):
         coef = parts_ref[(owner + REACH) % devices, :, :LANES].astype(jnp.float32)
         for g in range(1, NEAR):
@@ -152,8 +148,6 @@
         acc = jnp.zeros((rank, rank), jnp.float32)
         few = jnp.zeros((GROUP, rank), jnp.float32)
         for k in range(0, n_links, step):
-            if first_time and k % LINKS == 0:
-                piece_copy(j, k).wait()
             at = (j * n_links + k) // 2
             for u in range(GROUP):
                 picked_ref[at + u : at + u + 1, :] = partner(j, k + GROUP + u)
@@ -173,7 +167,7 @@
 
 
 def both_kernel(
-    devices, per_dev, cl_ref, behind_ref, own_ref, ahead_ref, wrap_ref, assign_ref, scores_ref, turned_ref, basis_hbm,
+    per_dev, cl_ref, behind_ref, own_ref, ahead_ref, assign_ref, scores_ref, turned_ref, basis_hbm,
     first_ref, out_ref, rows_ref, sum_ref, slope_ref, even_ref, odd_ref, even_left, odd_left, slots_ref, basis_sem,
 ):
     tiles = turned_ref.shape[1] // TILE
@@ -184,7 +178,7 @@
 
     for c in range(SLOTS):
         basis_copy(c).start()
-    near_rows(devices, per_dev, (behind_ref, own_ref, ahead_ref), wrap_ref, rows_ref)
+    near_rows(per_dev, (behind_ref, own_ref, ahead_ref), rows_ref)
     sum_ref[...] = jnp.zeros_like(sum_ref)
     sig = jax.nn.sigmoid(scores_ref[...])
     slope_ref[...] = sig * (1.0 - sig)
@@ -238,9 +232,9 @@
 
 
 def last_kernel(
-    devices, per_dev, cl_ref, behind_ref, own_ref, ahead_ref, wrap_ref, assign_ref, first_ref, turned_ref, out_ref, rows_ref
+    per_dev, cl_ref, behind_ref, own_ref, ahead_ref, assign_ref, first_ref, turned_ref, out_ref, rows_ref
 ):
-    near_rows(devices, per_dev, (behind_ref, own_ref, ahead_ref), wrap_ref, rows_ref)
+    near_rows(per_dev, (behind_ref, own_ref, ahead_ref), rows_ref)
     cl = cl_ref[...]
     rows = rows_ref[...].astype(jnp.bfloat16)
 
@@ -278,15 +272,16 @@
     coef_shape = jax.ShapeDtypeStruct((per_dev, NEAR * rank), bf16)
     params = pltpu.CompilerParams(vmem_limit_bytes=10 * 1024 * 1024)
 
-    coef1, turned_v, assign_v, cl_v = pl.pallas_call(
+    coef1, turned_v, assign_v, cl_v, links_v = pl.pallas_call(
         functools.partial(coef_kernel, devices, per_dev),
-        in_specs=[hbm] * 4,
-        out_specs=[vmem] * 4,
+        in_specs=[hbm] * 5,
+        out_specs=[vmem] * 5,
         out_shape=[
             coef_shape,
             pltpu.VMEM((rank, samples), bf16),
             pltpu.VMEM((high, LANES), jnp.int32),
             pltpu.VMEM((ROWS, LANES), jnp.int32),
+            pltpu.VMEM(link_blocks.shape, bf16),
         ],
         scratch_shapes=[
             pltpu.VMEM((1, clusters), jnp.int32),
@@ -296,10 +291,11 @@
             pltpu.VMEM((SLOTS, COPY, rank), bf16),
             pltpu.SemaphoreType.DMA((3,)),
             pltpu.SemaphoreType.DMA((SLOTS,)),
+            pltpu.SemaphoreType.DMA((per_dev,)),
         ],
         compiler_params=params,
         name="coef_pass",
-    )(far(slot_row), far(assign), far(vector), far(basis_rows))
+    )(far(slot_row), far(assign), far(vector), far(basis_rows), far(link_blocks))
 
     def to_all(block):
         copies = jnp.broadcast_to(block[None], (devices,) + block.shape)
@@ -311,33 +307,28 @@
     def to_chips(mixed):
         sibling = permute(mixed, [(i ^ 1, i) for i in range(devices)])
         own = jnp.concatenate([mixed, sibling], axis=0)
-        behind = permute(own, [(i - 2, i) for i in range(2, devices)])
-        ahead = permute(own, [(i + 2, i) for i in range(devices - 2)])
-        ends = [(i, devices - 2 + i) for i in range(2)]
-        wrap = permute(own, ends + [(j, i) for i, j in ends])
-        return behind, own, ahead, wrap
-
-    def mix(coef, links, first_time):
-        out = pl.pallas_call(
-            functools.partial(link_kernel, norm, devices, per_dev, first_time),
-            in_specs=[smem, smem, vmem, hbm if first_time else vmem],
-            out_specs=[vmem, vmem] if first_time else [vmem],
-            out_shape=[jax.ShapeDtypeStruct((per_dev, rank), bf16)] + [pltpu.VMEM(links.shape, bf16)] * first_time,
+        behind = permute(own, [((i - 2) % devices, i) for i in range(devices)])
+        ahead = permute(own, [((i + 2) % devices, i) for i in range(devices)])
+        return behind, own, ahead
+
+    def mix(coef):
+        return pl.pallas_call(
+            functools.partial(link_kernel, norm, devices, per_dev),
+            in_specs=[smem, smem, vmem, vmem],
+            out_specs=vmem,
+            out_shape=jax.ShapeDtypeStruct((per_dev, rank), bf16),
             scratch_shapes=[
                 pltpu.VMEM((clusters, rank), f32),
                 pltpu.VMEM((per_dev * n_links // 2, rank), f32),
                 pltpu.VMEM((8, rank), f32),
-            ]
-            + [pltpu.SemaphoreType.DMA((per_dev * n_links // LINKS,))] * first_time,
+            ],
             compiler_params=params,
             name="link_product",
-        )(slot_of, partners, coef, links)
-        return out
-
-    mixed1, links_v = mix(to_all(coef1), far(link_blocks), True)
+        )(slot_of, partners, to_all(coef), close(links_v))
+
     first, coef2 = pl.pallas_call(
-        functools.partial(both_kernel, devices, per_dev),
-        in_specs=[vmem] * 8 + [hbm],
+        functools.partial(both_kernel, per_dev),
+        in_specs=[vmem] * 7 + [hbm],
         out_specs=[vmem, vmem],
         out_shape=[pltpu.VMEM((high, LANES), f32), coef_shape],
         scratch_shapes=[
@@ -353,12 +344,11 @@
         ],
         compiler_params=params,
         name="first_and_coef_pass",
-    )(close(cl_v), *to_chips(mixed1), close(assign_v), scores, close(turned_v), far(basis_rows))
-    (mixed2,) = mix(to_all(coef2), close(links_v), False)
+    )(close(cl_v), *to_chips(mix(coef1)), close(assign_v), scores, close(turned_v), far(basis_rows))
 
     out = pl.pallas_call(
-        functools.partial(last_kernel, devices, per_dev),
-        in_specs=[vmem] * 8,
+        functools.partial(last_kernel, per_dev),
+        in_specs=[vmem] * 7,
         out_specs=vmem,
         out_shape=jax.ShapeDtypeStruct((high, LANES), f32),
         scratch_shapes=[
@@ -366,7 +356,7 @@
         ],
         compiler_params=params,
         name="last_pass",
-    )(close(cl_v), *to_chips(mixed2), close(assign_v), close(first), close(turned_v))
+    )(close(cl_v), *to_chips(mix(coef2)), close(assign_v), close(first), close(turned_v))
     return out.reshape(samples)
 
 

time: 74.4 us -> 65.9 us (0.89)
  starting transfers between devices: 17.1 us -> 4.29 us
  waiting for transfers between devices: 4.8 us -> 12.2 us
  blocking collectives: 26.3 us -> 24.1 us
    ppermute x8 -> x6, starting transfers between devices: 17.1 us -> 4.29 us  [permute(): return lax.ppermute(block, 'dev', pairs)]
    ppermute x8 -> x6, waiting for transfers between devices: 4.8 us -> 12.2 us  [permute(): return lax.ppermute(block, 'dev', pairs)]
    all_to_all x2, blocking collectives: 26.3 us -> 24.1 us  [to_all(): return lax.all_to_all(copies, 'dev', 0, 0, tiled=True)]
    pallas_call x4, Pallas kernels: 17.5 us -> 15.4 us  [the longest x1 7.69 us: shards(): pl.pallas_call(functools.partial(both_kernel, per_dev), in_specs=[vmem] *...]
    pallas_call x1, Pallas kernels: 8.2 us -> 9.68 us  [shards(): pl.pallas_call(functools.partial(coef_kernel, devices, per_dev), in_specs...]
  transfers between devices with their start and end apart: 8 -> 6, of which waited for: 4 -> 6; matrix products, arithmetic and copies ran while one was open for 0% -> 0% of each run, Pallas kernels for 0% -> 0%
where the time goes in v15:
time: 65.9 us; the launch traced here: 65.7 us
  Pallas kernels  25.1 us (38%)
  blocking collectives  24.1 us (37%)
  waiting for transfers between devices  12.2 us (19%)
  starting transfers between devices  4.29 us (7%)
    all_to_all x2, blocking collectives, to_all(): return lax.all_to_all(copies, 'dev', 0, 0, tiled=True)  24.1 us
    ppermute x6, waiting for transfers between devices, permute(): return lax.ppermute(block, 'dev', pairs)  12.2 us
    pallas_call x1, Pallas kernels, shards(): pl.pallas_call(functools.partial(coef_kernel, devices, per_dev), in_specs...  9.68 us
    pallas_call x1, Pallas kernels, shards(): pl.pallas_call(functools.partial(both_kernel, per_dev), in_specs=[vmem] *...  7.69 us
    pallas_call x2, Pallas kernels, mix(): pl.pallas_call(functools.partial(link_kernel, norm, devices, per_dev), in...  4.43 us
    ppermute x6, starting transfers between devices, permute(): return lax.ppermute(block, 'dev', pairs)  4.29 us
    pallas_call x1, Pallas kernels, shards(): pl.pallas_call(functools.partial(last_kernel, per_dev), in_specs=[vmem] *...  3.27 us
  transfers between devices with their start and end apart: 6, of which 6 were waited for; matrix products, arithmetic and copies ran while one was open for 0% of the time, Pallas kernels for 0%

profile of v15, /device:TPU:0, one launch (start us, length us, event | category | flops | bytes accessed | tf_op | source)
XLA Modules:
  0.0 65.7 jit_solution(8684875470769199780)
XLA Ops:
  0.0 0.0 copy-start.2
  0.0 0.0 copy-start.1
  0.0 9.7 %coef_pass.1 = (bf16[4,640]{1,0:T(4,128)(2,1)S(1)}, bf16[128,65536]{1,0:T(8,128)(2,1)S(1)}, s32[512,128]{1,0:T(8,128)S(1)}, s32[24,128]{1,0:T(8,128)S(1)}, bf16[4,64,128,128]{3,2,1,0:T(8,128)(2,1)S(1)}) custom-call(s32[1,64]{1,0:T(1,128)} %bitcast.6, s32[512,128]{1,0:T(8,128)} %bitcast.7, bf16[512,128]{1,0:T(8,128)(2,1)} %bitcast.8, ...), custom_call_target="tpu_custom_call" | custom-call | tf_op jit(solution)/shard_map/coef_pass/pallas_call | solution.py:275
  9.7 14.3 %all_to_all.10.parts_ref = bf16[16,4,640]{2,1,0:T(4,128)(2,1)S(1)} all-to-all(bf16[16,4,640]{2,1,0:T(4,128)(2,1)S(1)} %broadcast_in_dim.4), channel_id=1, replica_groups=mesh['groups'=2,'dev'=16] {'dev'}, dimensions={0} | all-to-all | bytes 163840 | tf_op jit(solution)/shard_map/all_to_all | solution.py:302
  24.1 0.0 copy-done.2
  24.1 0.0 copy-done.1
  24.1 2.2 %link_product.2 = bf16[4,128]{1,0:T(4,128)(2,1)S(1)} custom-call(s32[64]{0:T(128)S(1)} %copy-done.2, s32[4,64]{1,0:T(4,128)S(1)} %copy-done.1, bf16[16,4,640]{2,1,0:T(4,128)(2,1)S(1)} %all_to_all.10.parts_ref, bf16[4,64,128,128]{3,2,1,0:T(8,128)(2,1)S(1)} %get-tuple-element.14.links_ref), custom_call_target="tpu_custom_call" | custom-call | tf_op jit(solution)/shard_map/link_product/pallas_call | solution.py:315
  26.3 0.1 collective-permute-start
  26.4 1.1 %collective-permute-done = bf16[4,128]{1,0:T(4,128)(2,1)S(1)} collective-permute-done((bf16[4,128]{1,0:T(4,128)(2,1)S(1)}, bf16[4,128]{1,0:T(4,128)(2,1)S(1)}, u32[]{:S(2)}, u32[]{:S(2)}) %collective-permute-start) | collective-permute-done | bytes 1056 | tf_op jit(solution)/shard_map/ppermute | solution.py:305
  27.5 0.8 %collective-permute-start.2 = (bf16[8,128]{1,0:T(8,128)(2,1)S(1)}, bf16[8,128]{1,0:T(8,128)(2,1)S(1)}, u32[]{:S(2)}, u32[]{:S(2)}) collective-permute-start(bf16[8,128]{1,0:T(8,128)(2,1)S(1)} %pad_maximum_fusion.own_ref), channel_id=1, source_target_pairs={{2,0},{3,1},{4,2},{5,3},{6,4},{7,5},{8,6},{9,7},{10,8},{11,9},{12,... | collective-permute-start | bytes 6152 | tf_op jit(solution)/shard_map/ppermute | solution.py:305
  28.3 1.3 %collective-permute-start.1 = (bf16[8,128]{1,0:T(8,128)(2,1)S(1)}, bf16[8,128]{1,0:T(8,128)(2,1)S(1)}, u32[]{:S(2)}, u32[]{:S(2)}) collective-permute-start(bf16[8,128]{1,0:T(8,128)(2,1)S(1)} %pad_maximum_fusion.own_ref), channel_id=1, source_target_pairs={{14,0},{15,1},{0,2},{1,3},{2,4},{3,5},{4,6},{5,7},{6,8},{7,9},{8,1... | collective-permute-start | bytes 6152 | tf_op jit(solution)/shard_map/ppermute | solution.py:305
  29.6 1.6 %collective-permute-done.2.ahead_ref = bf16[8,128]{1,0:T(8,128)(2,1)S(1)} collective-permute-done((bf16[8,128]{1,0:T(8,128)(2,1)S(1)}, bf16[8,128]{1,0:T(8,128)(2,1)S(1)}, u32[]{:S(2)}, u32[]{:S(2)}) %collective-permute-start.2) | collective-permute-done | bytes 2080 | tf_op jit(solution)/shard_map/ppermute | solution.py:305
  31.1 3.4 %collective-permute-done.1.behind_ref = bf16[8,128]{1,0:T(8,128)(2,1)S(1)} collective-permute-done((bf16[8,128]{1,0:T(8,128)(2,1)S(1)}, bf16[8,128]{1,0:T(8,128)(2,1)S(1)}, u32[]{:S(2)}, u32[]{:S(2)}) %collective-permute-start.1) | collective-permute-done | bytes 2080 | tf_op jit(solution)/shard_map/ppermute | solution.py:305
  34.6 0.0 copy-done
  34.6 7.7 %first_and_coef_pass.1 = (f32[512,128]{1,0:T(8,128)S(1)}, bf16[4,640]{1,0:T(4,128)(2,1)S(1)}) custom-call(s32[24,128]{1,0:T(8,128)S(1)} %get-tuple-element.12.cl_ref, bf16[8,128]{1,0:T(8,128)(2,1)S(1)} %collective-permute-done.1.behind_ref, bf16[8,128]{1,0:T(8,128)(2,1)S(1)} %pad_maximum_fusion.own_ref, bf16[8,128]{1,0:T(8,128)(2,1)S(1)} %collective-permute-done.2.ahead_ref, ...), custom_call_target="tpu_custom_call" | custom-call | tf_op jit(solution)/shard_map/first_and_coef_pass/pallas_call | solution.py:329
  42.3 9.7 %all_to_all.11.parts_ref = bf16[16,4,640]{2,1,0:T(4,128)(2,1)S(1)} all-to-all(bf16[16,4,640]{2,1,0:T(4,128)(2,1)S(1)} %broadcast_in_dim.5), channel_id=1, replica_groups=mesh['groups'=2,'dev'=16] {'dev'}, dimensions={0} | all-to-all | bytes 163840 | tf_op jit(solution)/shard_map/all_to_all | solution.py:302
  52.0 2.2 %link_product.3 = bf16[4,128]{1,0:T(4,128)(2,1)S(1)} custom-call(s32[64]{0:T(128)S(1)} %copy-done.2, s32[4,64]{1,0:T(4,128)S(1)} %copy-done.1, bf16[16,4,640]{2,1,0:T(4,128)(2,1)S(1)} %all_to_all.11.parts_ref, bf16[4,64,128,128]{3,2,1,0:T(8,128)(2,1)S(1)} %get-tuple-element.14.links_ref), custom_call_target="tpu_custom_call" | custom-call | tf_op jit(solution)/shard_map/link_product/pallas_call | solution.py:315
  54.2 0.1 collective-permute-start.3
  54.3 1.1 %collective-permute-done.3 = bf16[4,128]{1,0:T(4,128)(2,1)S(1)} collective-permute-done((bf16[4,128]{1,0:T(4,128)(2,1)S(1)}, bf16[4,128]{1,0:T(4,128)(2,1)S(1)}, u32[]{:S(2)}, u32[]{:S(2)}) %collective-permute-start.3) | collective-permute-done | bytes 1056 | tf_op jit(solution)/shard_map/ppermute | solution.py:305
  55.4 0.7 %collective-permute-start.5 = (bf16[8,128]{1,0:T(8,128)(2,1)S(1)}, bf16[8,128]{1,0:T(8,128)(2,1)S(1)}, u32[]{:S(2)}, u32[]{:S(2)}) collective-permute-start(bf16[8,128]{1,0:T(8,128)(2,1)S(1)} %pad_maximum_fusion.1.own_ref), channel_id=1, source_target_pairs={{2,0},{3,1},{4,2},{5,3},{6,4},{7,5},{8,6},{9,7},{10,8},{11,9},{12,... | collective-permute-start | bytes 6152 | tf_op jit(solution)/shard_map/ppermute | solution.py:305
  56.2 1.4 %collective-permute-start.4 = (bf16[8,128]{1,0:T(8,128)(2,1)S(1)}, bf16[8,128]{1,0:T(8,128)(2,1)S(1)}, u32[]{:S(2)}, u32[]{:S(2)}) collective-permute-start(bf16[8,128]{1,0:T(8,128)(2,1)S(1)} %pad_maximum_fusion.1.own_ref), channel_id=1, source_target_pairs={{14,0},{15,1},{0,2},{1,3},{2,4},{3,5},{4,6},{5,7},{6,8},{7,9},{8,1... | collective-permute-start | bytes 6152 | tf_op jit(solution)/shard_map/ppermute | solution.py:305
  57.5 1.6 %collective-permute-done.5.ahead_ref = bf16[8,128]{1,0:T(8,128)(2,1)S(1)} collective-permute-done((bf16[8,128]{1,0:T(8,128)(2,1)S(1)}, bf16[8,128]{1,0:T(8,128)(2,1)S(1)}, u32[]{:S(2)}, u32[]{:S(2)}) %collective-permute-start.5) | collective-permute-done | bytes 2080 | tf_op jit(solution)/shard_map/ppermute | solution.py:305
  59.1 3.4 %collective-permute-done.4.behind_ref = bf16[8,128]{1,0:T(8,128)(2,1)S(1)} collective-permute-done((bf16[8,128]{1,0:T(8,128)(2,1)S(1)}, bf16[8,128]{1,0:T(8,128)(2,1)S(1)}, u32[]{:S(2)}, u32[]{:S(2)}) %collective-permute-start.4) | collective-permute-done | bytes 2080 | tf_op jit(solution)/shard_map/ppermute | solution.py:305
  62.5 3.3 %last_pass.1 = f32[512,128]{1,0:T(8,128)} custom-call(s32[24,128]{1,0:T(8,128)S(1)} %get-tuple-element.12.cl_ref, bf16[8,128]{1,0:T(8,128)(2,1)S(1)} %collective-permute-done.4.behind_ref, bf16[8,128]{1,0:T(8,128)(2,1)S(1)} %pad_maximum_fusion.1.own_ref, bf16[8,128]{1,0:T(8,128)(2,1)S(1)} %collective-permute-done.5.ahead_ref, ...), custom_call_target="tpu_custom_call" | custom-call | tf_op jit(solution)/shard_map/last_pass/pallas_call | solution.py:349
  (5 shorter events, 0.1 us)
Async XLA Ops:
  0.0 24.1 %copy-start.2 = (s32[64]{0:T(128)S(1)}, s32[64]{0:T(128)}, u32[]{:S(2)}) copy-start(s32[64]{0:T(128)} %slot_of_ref.3) | copy-start | bytes 772
  0.0 24.1 %copy-start.1 = (s32[4,64]{1,0:T(4,128)S(1)}, s32[4,64]{1,0:T(4,128)}, u32[]{:S(2)}) copy-start(s32[4,64]{1,0:T(4,128)} %partners_ref.3) | copy-start | bytes 3076
  0.0 34.6 %copy-start = (f32[65536]{0:T(1024)S(1)}, f32[65536]{0:T(1024)}, u32[]{:S(2)}) copy-start(f32[65536]{0:T(1024)} %param.9) | copy-start | bytes 786436
  26.3 1.2 %collective-permute-start = (bf16[4,128]{1,0:T(4,128)(2,1)S(1)}, bf16[4,128]{1,0:T(4,128)(2,1)S(1)}, u32[]{:S(2)}, u32[]{:S(2)}) collective-permute-start(bf16[4,128]{1,0:T(4,128)(2,1)S(1)} %link_product.2), channel_id=1, source_target_pairs={{1,0},{0,1},{3,2},{2,3},{5,4},{4,5},{7,6},{6,7},{9,8},{8,9},{11,10... | collective-permute-start | bytes 3080 | tf_op jit(solution)/shard_map/ppermute | solution.py:305
  27.5 3.6 %collective-permute-start.2 = (bf16[8,128]{1,0:T(8,128)(2,1)S(1)}, bf16[8,128]{1,0:T(8,128)(2,1)S(1)}, u32[]{:S(2)}, u32[]{:S(2)}) collective-permute-start(bf16[8,128]{1,0:T(8,128)(2,1)S(1)} %pad_maximum_fusion.own_ref), channel_id=1, source_target_pairs={{2,0},{3,1},{4,2},{5,3},{6,4},{7,5},{8,6},{9,7},{10,8},{11,9},{12,... | collective-permute-start | bytes 6152 | tf_op jit(solution)/shard_map/ppermute | solution.py:305
  28.3 6.3 %collective-permute-start.1 = (bf16[8,128]{1,0:T(8,128)(2,1)S(1)}, bf16[8,128]{1,0:T(8,128)(2,1)S(1)}, u32[]{:S(2)}, u32[]{:S(2)}) collective-permute-start(bf16[8,128]{1,0:T(8,128)(2,1)S(1)} %pad_maximum_fusion.own_ref), channel_id=1, source_target_pairs={{14,0},{15,1},{0,2},{1,3},{2,4},{3,5},{4,6},{5,7},{6,8},{7,9},{8,1... | collective-permute-start | bytes 6152 | tf_op jit(solution)/shard_map/ppermute | solution.py:305
  54.2 1.2 %collective-permute-start.3 = (bf16[4,128]{1,0:T(4,128)(2,1)S(1)}, bf16[4,128]{1,0:T(4,128)(2,1)S(1)}, u32[]{:S(2)}, u32[]{:S(2)}) collective-permute-start(bf16[4,128]{1,0:T(4,128)(2,1)S(1)} %link_product.3), channel_id=1, source_target_pairs={{1,0},{0,1},{3,2},{2,3},{5,4},{4,5},{7,6},{6,7},{9,8},{8,9},{11,10... | collective-permute-start | bytes 3080 | tf_op jit(solution)/shard_map/ppermute | solution.py:305
  55.4 3.6 %collective-permute-start.5 = (bf16[8,128]{1,0:T(8,128)(2,1)S(1)}, bf16[8,128]{1,0:T(8,128)(2,1)S(1)}, u32[]{:S(2)}, u32[]{:S(2)}) collective-permute-start(bf16[8,128]{1,0:T(8,128)(2,1)S(1)} %pad_maximum_fusion.1.own_ref), channel_id=1, source_target_pairs={{2,0},{3,1},{4,2},{5,3},{6,4},{7,5},{8,6},{9,7},{10,8},{11,9},{12,... | collective-permute-start | bytes 6152 | tf_op jit(solution)/shard_map/ppermute | solution.py:305
  56.2 6.3 %collective-permute-start.4 = (bf16[8,128]{1,0:T(8,128)(2,1)S(1)}, bf16[8,128]{1,0:T(8,128)(2,1)S(1)}, u32[]{:S(2)}, u32[]{:S(2)}) collective-permute-start(bf16[8,128]{1,0:T(8,128)(2,1)S(1)} %pad_maximum_fusion.1.own_ref), channel_id=1, source_target_pairs={{14,0},{15,1},{0,2},{1,3},{2,4},{3,5},{4,6},{5,7},{6,8},{7,9},{8,1... | collective-permute-start | bytes 6152 | tf_op jit(solution)/shard_map/ppermute | solution.py:305

commit v16 on v15

--- a/solution.py
+++ b/solution.py
@@ -18,7 +18,7 @@
 COPY = 8192
 TILE = 2048
 PER_COPY = COPY // TILE
-SLOTS = 3
+SLOTS = 4
 BODY = 16
 PIECE = 512
 GROUP = 8
@@ -166,9 +166,20 @@
     return jnp.sum(jnp.where(hit, products, 0.0), axis=0, keepdims=True)
 
 
+def prepare_kernel(after_ref, scores_hbm, basis_hbm, slope_ref, head_ref, scores_ref, sems):
+    scores_copy = pltpu.make_async_copy(scores_hbm, scores_ref, sems.at[0])
+    head_copy = pltpu.make_async_copy(basis_hbm.at[pl.ds(0, COPY), :], head_ref, sems.at[1])
+    scores_copy.start()
+    head_copy.start()
+    scores_copy.wait()
+    sig = jax.nn.sigmoid(scores_ref[...])
+    slope_ref[...] = sig * (1.0 - sig)
+    head_copy.wait()
+
+
 def both_kernel(
-    per_dev, cl_ref, behind_ref, own_ref, ahead_ref, assign_ref, scores_ref, turned_ref, basis_hbm,
-    first_ref, out_ref, rows_ref, sum_ref, slope_ref, even_ref, odd_ref, even_left, odd_left, slots_ref, basis_sem,
+    per_dev, cl_ref, behind_ref, own_ref, ahead_ref, assign_ref, slope_ref, head_ref, turned_ref, basis_hbm,
+    first_ref, out_ref, rows_ref, sum_ref, even_ref, odd_ref, even_left, odd_left, slots_ref, basis_sem,
 ):
     tiles = turned_ref.shape[1] // TILE
     copies = tiles // PER_COPY
@@ -176,12 +187,10 @@
     def basis_copy(c):
         return slot_copy(basis_hbm, slots_ref, basis_sem, c)
 
-    for c in range(SLOTS):
+    for c in range(1, SLOTS + 1):
         basis_copy(c).start()
     near_rows(per_dev, (behind_ref, own_ref, ahead_ref), rows_ref)
     sum_ref[...] = jnp.zeros_like(sum_ref)
-    sig = jax.nn.sigmoid(scores_ref[...])
-    slope_ref[...] = sig * (1.0 - sig)
     cl = cl_ref[...]
     rows = rows_ref[...].astype(jnp.bfloat16)
     products_of = (even_ref, odd_ref)
@@ -200,21 +209,26 @@
             left_of[side][:, at] = jnp.where(hit, weighted, 0.0).astype(jnp.bfloat16)
 
     def add_up(c, p):
-        block = slots_ref[lax.rem(c, SLOTS), p * TILE : (p + 1) * TILE, :]
+        at = slice(p * TILE, (p + 1) * TILE)
+        block = head_ref[at, :] if isinstance(c, int) and c == 0 else slots_ref[lax.rem(c, SLOTS), at, :]
         sum_ref[...] += jnp.dot(left_of[p % 2][...], block, preferred_element_type=jnp.float32)
 
-    multiply(0, 0)
-    select(0, 0)
-    multiply(1, 1)
-
-    @pl.loop(0, copies - 1)
-    def _(c):
-        basis_copy(c).wait()
+    def body(c):
         for p in range(PER_COPY):
             t = c * PER_COPY + p
             add_up(c, p)
             multiply(t + 2, p % 2)
             select(t + 1, (p + 1) % 2)
+
+    multiply(0, 0)
+    select(0, 0)
+    multiply(1, 1)
+    body(0)
+
+    @pl.loop(1, copies - 1)
+    def _(c):
+        basis_copy(c).wait()
+        body(c)
 
         @pl.when(c + SLOTS < copies)
         def _():
@@ -270,7 +284,7 @@
     smem = pl.BlockSpec(memory_space=pltpu.SMEM)
     hbm = pl.BlockSpec(memory_space=pltpu.HBM)
     coef_shape = jax.ShapeDtypeStruct((per_dev, NEAR * rank), bf16)
-    params = pltpu.CompilerParams(vmem_limit_bytes=10 * 1024 * 1024)
+    params = pltpu.CompilerParams(vmem_limit_bytes=12 * 1024 * 1024)
 
     coef1, turned_v, assign_v, cl_v, links_v = pl.pallas_call(
         functools.partial(coef_kernel, devices, per_dev),
@@ -326,15 +340,26 @@
             name="link_product",
         )(slot_of, partners, to_all(coef), close(links_v))
 
+    chips1 = to_chips(mix(coef1))
+    slope_v, head_v = pl.pallas_call(
+        prepare_kernel,
+        in_specs=[vmem, hbm, hbm],
+        out_specs=[vmem, vmem],
+        out_shape=[pltpu.VMEM((high, LANES), f32), pltpu.VMEM((COPY, rank), bf16)],
+        scratch_shapes=[pltpu.VMEM((high, LANES), f32), pltpu.SemaphoreType.DMA((2,))],
+        compiler_params=params,
+        cost_estimate=pl.CostEstimate(flops=0, bytes_accessed=4 * COPY * rank, transcendentals=samples),
+        name="prepare",
+    )(chips1[1], far(scores), far(basis_rows))
+
     first, coef2 = pl.pallas_call(
         functools.partial(both_kernel, per_dev),
-        in_specs=[vmem] * 7 + [hbm],
+        in_specs=[vmem] * 8 + [hbm],
         out_specs=[vmem, vmem],
         out_shape=[pltpu.VMEM((high, LANES), f32), coef_shape],
         scratch_shapes=[
             pltpu.VMEM((ROWS, rank), f32),
             pltpu.VMEM((ROWS, rank), f32),
-            pltpu.VMEM((high, LANES), f32),
             pltpu.VMEM((ROWS, TILE), f32),
             pltpu.VMEM((ROWS, TILE), f32),
             pltpu.VMEM((ROWS, TILE), bf16),
@@ -344,7 +369,7 @@
         ],
         compiler_params=params,
         name="first_and_coef_pass",
-    )(close(cl_v), *to_chips(mix(coef1)), close(assign_v), scores, close(turned_v), far(basis_rows))
+    )(close(cl_v), *chips1, close(assign_v), close(slope_v), close(head_v), close(turned_v), far(basis_rows))
 
     out = pl.pallas_call(
         functools.partial(last_kernel, per_dev),

time: 65.9 us -> 64.8 us (0.983)
  waiting for transfers between devices: 12.2 us -> 10.4 us
    ppermute x6, waiting for transfers between devices: 12.2 us -> 10.4 us  [permute(): return lax.ppermute(block, 'dev', pairs)]
    pallas_call x0 -> x1, Pallas kernels: none -> 1.71 us  [shards(): pl.pallas_call(prepare_kernel, in_specs=[vmem, hbm, hbm], out_specs=[vmem...]
    pallas_call x1, Pallas kernels: 7.69 us -> 6.62 us  [shards(): pl.pallas_call(functools.partial(both_kernel, per_dev), in_specs=[vmem] *...]
  transfers between devices with their start and end apart: 6 -> 6, of which waited for: 6 -> 5; matrix products, arithmetic and copies ran while one was open for 0% -> 0% of each run, Pallas kernels for 0% -> 3%
where the time goes in v16:
time: 64.8 us; the launch traced here: 64.6 us
  Pallas kernels  25.7 us (40%)
  blocking collectives  24.1 us (37%)
  waiting for transfers between devices  10.4 us (16%)
  starting transfers between devices  4.29 us (7%)
    all_to_all x2, blocking collectives, to_all(): return lax.all_to_all(copies, 'dev', 0, 0, tiled=True)  24.1 us
    ppermute x6, waiting for transfers between devices, permute(): return lax.ppermute(block, 'dev', pairs)  10.4 us
    pallas_call x1, Pallas kernels, shards(): pl.pallas_call(functools.partial(coef_kernel, devices, per_dev), in_specs...  9.63 us
    pallas_call x1, Pallas kernels, shards(): pl.pallas_call(functools.partial(both_kernel, per_dev), in_specs=[vmem] *...  6.62 us
    pallas_call x2, Pallas kernels, mix(): pl.pallas_call(functools.partial(link_kernel, norm, devices, per_dev), in...  4.43 us
    ppermute x6, starting transfers between devices, permute(): return lax.ppermute(block, 'dev', pairs)  4.29 us
    pallas_call x1, Pallas kernels, shards(): pl.pallas_call(functools.partial(last_kernel, per_dev), in_specs=[vmem] *...  3.29 us
    pallas_call x1, Pallas kernels, shards(): pl.pallas_call(prepare_kernel, in_specs=[vmem, hbm, hbm], out_specs=[vmem...  1.71 us
  transfers between devices with their start and end apart: 6, of which 5 were waited for; matrix products, arithmetic and copies ran while one was open for 0% of the time, Pallas kernels for 3%

profile of v16, /device:TPU:0, one launch (start us, length us, event | category | flops | bytes accessed | tf_op | source)
XLA Modules:
  0.0 64.6 jit_solution(17761429715751096803)
XLA Ops:
  0.0 0.0 copy-start
  0.0 0.0 copy-start.1
  0.0 9.6 %coef_pass.1 = (bf16[4,640]{1,0:T(4,128)(2,1)S(1)}, bf16[128,65536]{1,0:T(8,128)(2,1)S(1)}, s32[512,128]{1,0:T(8,128)S(1)}, s32[24,128]{1,0:T(8,128)S(1)}, bf16[4,64,128,128]{3,2,1,0:T(8,128)(2,1)S(1)}) custom-call(s32[1,64]{1,0:T(1,128)} %bitcast.5, s32[512,128]{1,0:T(8,128)} %bitcast.6, bf16[512,128]{1,0:T(8,128)(2,1)} %bitcast.8, ...), custom_call_target="tpu_custom_call" | custom-call | tf_op jit(solution)/shard_map/coef_pass/pallas_call | solution.py:289
  9.7 14.3 %all_to_all.10.parts_ref = bf16[16,4,640]{2,1,0:T(4,128)(2,1)S(1)} all-to-all(bf16[16,4,640]{2,1,0:T(4,128)(2,1)S(1)} %broadcast_in_dim.4), channel_id=1, replica_groups=mesh['groups'=2,'dev'=16] {'dev'}, dimensions={0} | all-to-all | bytes 163840 | tf_op jit(solution)/shard_map/all_to_all | solution.py:316
  24.0 0.0 copy-done
  24.0 0.0 copy-done.1
  24.0 2.2 %link_product.2 = bf16[4,128]{1,0:T(4,128)(2,1)S(1)} custom-call(s32[64]{0:T(128)S(1)} %copy-done.1, s32[4,64]{1,0:T(4,128)S(1)} %copy-done, bf16[16,4,640]{2,1,0:T(4,128)(2,1)S(1)} %all_to_all.10.parts_ref, bf16[4,64,128,128]{3,2,1,0:T(8,128)(2,1)S(1)} %get-tuple-element.16.links_ref), custom_call_target="tpu_custom_call" | custom-call | tf_op jit(solution)/shard_map/link_product/pallas_call | solution.py:329
  26.2 0.1 collective-permute-start
  26.3 1.1 %collective-permute-done = bf16[4,128]{1,0:T(4,128)(2,1)S(1)} collective-permute-done((bf16[4,128]{1,0:T(4,128)(2,1)S(1)}, bf16[4,128]{1,0:T(4,128)(2,1)S(1)}, u32[]{:S(2)}, u32[]{:S(2)}) %collective-permute-start) | collective-permute-done | bytes 1056 | tf_op jit(solution)/shard_map/ppermute | solution.py:319
  27.4 0.8 %collective-permute-start.2 = (bf16[8,128]{1,0:T(8,128)(2,1)S(1)}, bf16[8,128]{1,0:T(8,128)(2,1)S(1)}, u32[]{:S(2)}, u32[]{:S(2)}) collective-permute-start(bf16[8,128]{1,0:T(8,128)(2,1)S(1)} %pad_maximum_fusion.after_ref.own_ref), channel_id=1, source_target_pairs={{2,0},{3,1},{4,2},{5,3},{6,4},{7,5},{8,6},{9,7},{10,8},{11,9},{12,... | collective-permute-start | bytes 6152 | tf_op jit(solution)/shard_map/ppermute | solution.py:319
  28.2 1.3 %collective-permute-start.1 = (bf16[8,128]{1,0:T(8,128)(2,1)S(1)}, bf16[8,128]{1,0:T(8,128)(2,1)S(1)}, u32[]{:S(2)}, u32[]{:S(2)}) collective-permute-start(bf16[8,128]{1,0:T(8,128)(2,1)S(1)} %pad_maximum_fusion.after_ref.own_ref), channel_id=1, source_target_pairs={{14,0},{15,1},{0,2},{1,3},{2,4},{3,5},{4,6},{5,7},{6,8},{7,9},{8,1... | collective-permute-start | bytes 6152 | tf_op jit(solution)/shard_map/ppermute | solution.py:319
  29.5 1.7 %prepare.1 = (f32[512,128]{1,0:T(8,128)S(1)}, bf16[8192,128]{1,0:T(8,128)(2,1)S(1)}) custom-call(bf16[8,128]{1,0:T(8,128)(2,1)S(1)} %pad_maximum_fusion.after_ref.own_ref, f32[512,128]{1,0:T(8,128)} %bitcast.7, bf16[65536,128]{1,0:T(8,128)(2,1)} %basis_hbm.5), custom_call_target="tpu_custom_call" | custom-call | bytes 4194304 | tf_op jit(solution)/shard_map/prepare/pallas_call | solution.py:344
  31.2 0.0 collective-permute-done.2.ahead_ref
  31.2 3.3 %collective-permute-done.1.behind_ref = bf16[8,128]{1,0:T(8,128)(2,1)S(1)} collective-permute-done((bf16[8,128]{1,0:T(8,128)(2,1)S(1)}, bf16[8,128]{1,0:T(8,128)(2,1)S(1)}, u32[]{:S(2)}, u32[]{:S(2)}) %collective-permute-start.1) | collective-permute-done | bytes 2080 | tf_op jit(solution)/shard_map/ppermute | solution.py:319
  34.5 6.6 %first_and_coef_pass.1 = (f32[512,128]{1,0:T(8,128)S(1)}, bf16[4,640]{1,0:T(4,128)(2,1)S(1)}) custom-call(s32[24,128]{1,0:T(8,128)S(1)} %get-tuple-element.14.cl_ref, bf16[8,128]{1,0:T(8,128)(2,1)S(1)} %collective-permute-done.1.behind_ref, bf16[8,128]{1,0:T(8,128)(2,1)S(1)} %pad_maximum_fusion.after_ref.own_ref, ...), custom_call_target="tpu_custom_call" | custom-call | tf_op jit(solution)/shard_map/first_and_coef_pass/pallas_call | solution.py:355
  41.2 9.7 %all_to_all.11.parts_ref = bf16[16,4,640]{2,1,0:T(4,128)(2,1)S(1)} all-to-all(bf16[16,4,640]{2,1,0:T(4,128)(2,1)S(1)} %broadcast_in_dim.5), channel_id=1, replica_groups=mesh['groups'=2,'dev'=16] {'dev'}, dimensions={0} | all-to-all | bytes 163840 | tf_op jit(solution)/shard_map/all_to_all | solution.py:316
  50.9 2.2 %link_product.3 = bf16[4,128]{1,0:T(4,128)(2,1)S(1)} custom-call(s32[64]{0:T(128)S(1)} %copy-done.1, s32[4,64]{1,0:T(4,128)S(1)} %copy-done, bf16[16,4,640]{2,1,0:T(4,128)(2,1)S(1)} %all_to_all.11.parts_ref, bf16[4,64,128,128]{3,2,1,0:T(8,128)(2,1)S(1)} %get-tuple-element.16.links_ref), custom_call_target="tpu_custom_call" | custom-call | tf_op jit(solution)/shard_map/link_product/pallas_call | solution.py:329
  53.1 0.1 collective-permute-start.3
  53.2 1.1 %collective-permute-done.3 = bf16[4,128]{1,0:T(4,128)(2,1)S(1)} collective-permute-done((bf16[4,128]{1,0:T(4,128)(2,1)S(1)}, bf16[4,128]{1,0:T(4,128)(2,1)S(1)}, u32[]{:S(2)}, u32[]{:S(2)}) %collective-permute-start.3) | collective-permute-done | bytes 1056 | tf_op jit(solution)/shard_map/ppermute | solution.py:319
  54.3 0.7 %collective-permute-start.5 = (bf16[8,128]{1,0:T(8,128)(2,1)S(1)}, bf16[8,128]{1,0:T(8,128)(2,1)S(1)}, u32[]{:S(2)}, u32[]{:S(2)}) collective-permute-start(bf16[8,128]{1,0:T(8,128)(2,1)S(1)} %pad_maximum_fusion.1.own_ref), channel_id=1, source_target_pairs={{2,0},{3,1},{4,2},{5,3},{6,4},{7,5},{8,6},{9,7},{10,8},{11,9},{12,... | collective-permute-start | bytes 6152 | tf_op jit(solution)/shard_map/ppermute | solution.py:319
  55.0 1.4 %collective-permute-start.4 = (bf16[8,128]{1,0:T(8,128)(2,1)S(1)}, bf16[8,128]{1,0:T(8,128)(2,1)S(1)}, u32[]{:S(2)}, u32[]{:S(2)}) collective-permute-start(bf16[8,128]{1,0:T(8,128)(2,1)S(1)} %pad_maximum_fusion.1.own_ref), channel_id=1, source_target_pairs={{14,0},{15,1},{0,2},{1,3},{2,4},{3,5},{4,6},{5,7},{6,8},{7,9},{8,1... | collective-permute-start | bytes 6152 | tf_op jit(solution)/shard_map/ppermute | solution.py:319
  56.4 1.6 %collective-permute-done.5.ahead_ref = bf16[8,128]{1,0:T(8,128)(2,1)S(1)} collective-permute-done((bf16[8,128]{1,0:T(8,128)(2,1)S(1)}, bf16[8,128]{1,0:T(8,128)(2,1)S(1)}, u32[]{:S(2)}, u32[]{:S(2)}) %collective-permute-start.5) | collective-permute-done | bytes 2080 | tf_op jit(solution)/shard_map/ppermute | solution.py:319
  58.0 3.4 %collective-permute-done.4.behind_ref = bf16[8,128]{1,0:T(8,128)(2,1)S(1)} collective-permute-done((bf16[8,128]{1,0:T(8,128)(2,1)S(1)}, bf16[8,128]{1,0:T(8,128)(2,1)S(1)}, u32[]{:S(2)}, u32[]{:S(2)}) %collective-permute-start.4) | collective-permute-done | bytes 2080 | tf_op jit(solution)/shard_map/ppermute | solution.py:319
  61.3 3.3 %last_pass.1 = f32[512,128]{1,0:T(8,128)} custom-call(s32[24,128]{1,0:T(8,128)S(1)} %get-tuple-element.14.cl_ref, bf16[8,128]{1,0:T(8,128)(2,1)S(1)} %collective-permute-done.4.behind_ref, bf16[8,128]{1,0:T(8,128)(2,1)S(1)} %pad_maximum_fusion.1.own_ref, bf16[8,128]{1,0:T(8,128)(2,1)S(1)} %collective-permute-done.5.ahead_ref, ...), custom_call_target="tpu_custom_call" | custom-call | tf_op jit(solution)/shard_map/last_pass/pallas_call | solution.py:374
  (4 shorter events, 0.1 us)
Async XLA Ops:
  0.0 24.0 %copy-start = (s32[4,64]{1,0:T(4,128)S(1)}, s32[4,64]{1,0:T(4,128)}, u32[]{:S(2)}) copy-start(s32[4,64]{1,0:T(4,128)} %partners_ref.3) | copy-start | bytes 3076
  0.0 24.0 %copy-start.1 = (s32[64]{0:T(128)S(1)}, s32[64]{0:T(128)}, u32[]{:S(2)}) copy-start(s32[64]{0:T(128)} %slot_of_ref.3) | copy-start | bytes 772
  26.2 1.2 %collective-permute-start = (bf16[4,128]{1,0:T(4,128)(2,1)S(1)}, bf16[4,128]{1,0:T(4,128)(2,1)S(1)}, u32[]{:S(2)}, u32[]{:S(2)}) collective-permute-start(bf16[4,128]{1,0:T(4,128)(2,1)S(1)} %link_product.2), channel_id=1, source_target_pairs={{1,0},{0,1},{3,2},{2,3},{5,4},{4,5},{7,6},{6,7},{9,8},{8,9},{11,10... | collective-permute-start | bytes 3080 | tf_op jit(solution)/shard_map/ppermute | solution.py:319
  27.4 3.8 %collective-permute-start.2 = (bf16[8,128]{1,0:T(8,128)(2,1)S(1)}, bf16[8,128]{1,0:T(8,128)(2,1)S(1)}, u32[]{:S(2)}, u32[]{:S(2)}) collective-permute-start(bf16[8,128]{1,0:T(8,128)(2,1)S(1)} %pad_maximum_fusion.after_ref.own_ref), channel_id=1, source_target_pairs={{2,0},{3,1},{4,2},{5,3},{6,4},{7,5},{8,6},{9,7},{10,8},{11,9},{12,... | collective-permute-start | bytes 6152 | tf_op jit(solution)/shard_map/ppermute | solution.py:319
  28.2 6.3 %collective-permute-start.1 = (bf16[8,128]{1,0:T(8,128)(2,1)S(1)}, bf16[8,128]{1,0:T(8,128)(2,1)S(1)}, u32[]{:S(2)}, u32[]{:S(2)}) collective-permute-start(bf16[8,128]{1,0:T(8,128)(2,1)S(1)} %pad_maximum_fusion.after_ref.own_ref), channel_id=1, source_target_pairs={{14,0},{15,1},{0,2},{1,3},{2,4},{3,5},{4,6},{5,7},{6,8},{7,9},{8,1... | collective-permute-start | bytes 6152 | tf_op jit(solution)/shard_map/ppermute | solution.py:319
  53.1 1.2 %collective-permute-start.3 = (bf16[4,128]{1,0:T(4,128)(2,1)S(1)}, bf16[4,128]{1,0:T(4,128)(2,1)S(1)}, u32[]{:S(2)}, u32[]{:S(2)}) collective-permute-start(bf16[4,128]{1,0:T(4,128)(2,1)S(1)} %link_product.3), channel_id=1, source_target_pairs={{1,0},{0,1},{3,2},{2,3},{5,4},{4,5},{7,6},{6,7},{9,8},{8,9},{11,10... | collective-permute-start | bytes 3080 | tf_op jit(solution)/shard_map/ppermute | solution.py:319
  54.3 3.6 %collective-permute-start.5 = (bf16[8,128]{1,0:T(8,128)(2,1)S(1)}, bf16[8,128]{1,0:T(8,128)(2,1)S(1)}, u32[]{:S(2)}, u32[]{:S(2)}) collective-permute-start(bf16[8,128]{1,0:T(8,128)(2,1)S(1)} %pad_maximum_fusion.1.own_ref), channel_id=1, source_target_pairs={{2,0},{3,1},{4,2},{5,3},{6,4},{7,5},{8,6},{9,7},{10,8},{11,9},{12,... | collective-permute-start | bytes 6152 | tf_op jit(solution)/shard_map/ppermute | solution.py:319
  55.0 6.3 %collective-permute-start.4 = (bf16[8,128]{1,0:T(8,128)(2,1)S(1)}, bf16[8,128]{1,0:T(8,128)(2,1)S(1)}, u32[]{:S(2)}, u32[]{:S(2)}) collective-permute-start(bf16[8,128]{1,0:T(8,128)(2,1)S(1)} %pad_maximum_fusion.1.own_ref), channel_id=1, source_target_pairs={{14,0},{15,1},{0,2},{1,3},{2,4},{3,5},{4,6},{5,7},{6,8},{7,9},{8,1... | collective-permute-start | bytes 6152 | tf_op jit(solution)/shard_map/ppermute | solution.py:319

commit v17 on v16

--- a/solution.py
+++ b/solution.py
@@ -22,6 +22,7 @@
 BODY = 16
 PIECE = 512
 GROUP = 8
+LINKS = 32
 
 ridge = 0.5
 
@@ -102,7 +103,7 @@
     def _(c):
         basis_copy(c).wait()
 
-        @pl.when(c < per_dev)
+        @pl.when(c < links_ref.shape[0])
         def _():
             links_copy(c).start()
 
@@ -124,15 +125,28 @@
             basis_copy(c + SLOTS).start()
 
     put_sums(per_dev, sum_ref, out_ref)
-    for j in range(per_dev):
+    for j in range(links_ref.shape[0]):
         links_copy(j).wait()
 
 
-def link_kernel(
-    norm, devices, per_dev, slot_of_ref, partners_ref, parts_ref, links_ref, out_ref, scaled_ref, picked_ref, mixed_ref
-):
-    n_links, rank = links_ref.shape[1:3]
+def link_kernel(norm, devices, per_dev, first_time, slot_of_ref, partners_ref, parts_ref, links1_ref, *refs):
+    if first_time:
+        links_hbm, out_ref, links2_ref, scaled_ref, picked_ref, mixed_ref, links_sem = refs
+    else:
+        links2_ref, out_ref, scaled_ref, picked_ref, mixed_ref = refs
+    n_links, rank = links1_ref.shape[1:3]
     step = 2 * GROUP
+    half = per_dev // 2
+
+    def piece_copy(j, k):
+        ks = pl.ds(k, LINKS)
+        sem = links_sem.at[((j - half) * n_links + k) // LINKS]
+        return pltpu.make_async_copy(links_hbm.at[j, ks], links2_ref.at[j - half, ks], sem)
+
+    if first_time:
+        for j in range(half, per_dev):
+            for k in range(0, n_links, LINKS):
+                piece_copy(j, k).start()
     for owner in range(devices):
         coef = parts_ref[(owner + REACH) % devices, :, :LANES].astype(jnp.float32)
         for g in range(1, NEAR):
@@ -147,15 +161,18 @@
     for j in range(per_dev):
         acc = jnp.zeros((rank, rank), jnp.float32)
         few = jnp.zeros((GROUP, rank), jnp.float32)
+        links_ref = links1_ref.at[j] if j < half else links2_ref.at[j - half]
         for k in range(0, n_links, step):
+            if first_time and j >= half and k % LINKS == 0:
+                piece_copy(j, k).wait()
             at = (j * n_links + k) // 2
             for u in range(GROUP):
                 picked_ref[at + u : at + u + 1, :] = partner(j, k + GROUP + u)
-            blocks = links_ref[j, k + GROUP : k + step].reshape(GROUP * rank, rank)
+            blocks = links_ref[k + GROUP : k + step].reshape(GROUP * rank, rank)
             picked = picked_ref[at : at + GROUP, :].astype(jnp.bfloat16)
             products = lax.dot_general(picked, blocks, (((1,), (1,)), ((), ())), preferred_element_type=jnp.float32)
             for u in range(GROUP):
-                acc += links_ref[j, k + u].astype(jnp.float32) * partner(j, k + u)
+                acc += links_ref[k + u].astype(jnp.float32) * partner(j, k + u)
             for u in range(GROUP):
                 few += jnp.where(row == u, products[:, u * rank : (u + 1) * rank], 0.0)
         mixed_ref[j : j + 1, :] = jnp.sum(acc.T, axis=0, keepdims=True) + jnp.sum(few, axis=0, keepdims=True)
@@ -283,10 +300,11 @@
     vmem = pl.BlockSpec(memory_space=pltpu.VMEM)
     smem = pl.BlockSpec(memory_space=pltpu.SMEM)
     hbm = pl.BlockSpec(memory_space=pltpu.HBM)
+    half_shape = (per_dev // 2,) + link_blocks.shape[1:]
     coef_shape = jax.ShapeDtypeStruct((per_dev, NEAR * rank), bf16)
     params = pltpu.CompilerParams(vmem_limit_bytes=12 * 1024 * 1024)
 
-    coef1, turned_v, assign_v, cl_v, links_v = pl.pallas_call(
+    coef1, turned_v, assign_v, cl_v, links1_v = pl.pallas_call(
         functools.partial(coef_kernel, devices, per_dev),
         in_specs=[hbm] * 5,
         out_specs=[vmem] * 5,
@@ -295,7 +313,7 @@
             pltpu.VMEM((rank, samples), bf16),
             pltpu.VMEM((high, LANES), jnp.int32),
             pltpu.VMEM((ROWS, LANES), jnp.int32),
-            pltpu.VMEM(link_blocks.shape, bf16),
+            pltpu.VMEM(half_shape, bf16),
         ],
         scratch_shapes=[
             pltpu.VMEM((1, clusters), jnp.int32),
@@ -305,7 +323,7 @@
             pltpu.VMEM((SLOTS, COPY, rank), bf16),
             pltpu.SemaphoreType.DMA((3,)),
             pltpu.SemaphoreType.DMA((SLOTS,)),
-            pltpu.SemaphoreType.DMA((per_dev,)),
+            pltpu.SemaphoreType.DMA((per_dev // 2,)),
         ],
         compiler_params=params,
         name="coef_pass",
@@ -325,22 +343,24 @@
         ahead = permute(own, [((i + 2) % devices, i) for i in range(devices)])
         return behind, own, ahead
 
-    def mix(coef):
+    def mix(coef, links2, first_time):
         return pl.pallas_call(
-            functools.partial(link_kernel, norm, devices, per_dev),
-            in_specs=[smem, smem, vmem, vmem],
-            out_specs=vmem,
-            out_shape=jax.ShapeDtypeStruct((per_dev, rank), bf16),
+            functools.partial(link_kernel, norm, devices, per_dev, first_time),
+            in_specs=[smem, smem, vmem, vmem, hbm if first_time else vmem],
+            out_specs=[vmem, vmem] if first_time else [vmem],
+            out_shape=[jax.ShapeDtypeStruct((per_dev, rank), bf16)] + [pltpu.VMEM(half_shape, bf16)] * first_time,
             scratch_shapes=[
                 pltpu.VMEM((clusters, rank), f32),
                 pltpu.VMEM((per_dev * n_links // 2, rank), f32),
                 pltpu.VMEM((8, rank), f32),
-            ],
+            ]
+            + [pltpu.SemaphoreType.DMA(((per_dev - per_dev // 2) * n_links // LINKS,))] * first_time,
             compiler_params=params,
             name="link_product",
-        )(slot_of, partners, to_all(coef), close(links_v))
-
-    chips1 = to_chips(mix(coef1))
+        )(slot_of, partners, to_all(coef), close(links1_v), links2)
+
+    mixed1, links2_v = mix(coef1, far(link_blocks), True)
+    chips1 = to_chips(mixed1)
     slope_v, head_v = pl.pallas_call(
         prepare_kernel,
         in_specs=[vmem, hbm, hbm],
@@ -371,6 +391,7 @@
         name="first_and_coef_pass",
     )(close(cl_v), *chips1, close(assign_v), close(slope_v), close(head_v), close(turned_v), far(basis_rows))
 
+    (mixed2,) = mix(coef2, close(links2_v), False)
     out = pl.pallas_call(
         functools.partial(last_kernel, per_dev),
         in_specs=[vmem] * 7,
@@ -381,7 +402,7 @@
         ],
         compiler_params=params,
         name="last_pass",
-    )(close(cl_v), *to_chips(mix(coef2)), close(assign_v), close(first), close(turned_v))
+    )(close(cl_v), *to_chips(mixed2), close(assign_v), close(first), close(turned_v))
     return out.reshape(samples)
 
 

time: 64.8 us -> 65.4 us (level)
    pallas_call x2, Pallas kernels: 4.43 us -> 6.09 us  [mix(): pl.pallas_call(functools.partial(link_kernel, norm, devices, per_dev, fir...]
    pallas_call x1, Pallas kernels: 9.63 us -> 8.49 us  [shards(): pl.pallas_call(functools.partial(coef_kernel, devices, per_dev), in_specs...]
where the time goes in v17:
time: 65.4 us; the launch traced here: 65.2 us
  Pallas kernels  26.2 us (40%)
  blocking collectives  24.1 us (37%)
  waiting for transfers between devices  10.4 us (16%)
  starting transfers between devices  4.3 us (7%)
    all_to_all x2, blocking collectives, to_all(): return lax.all_to_all(copies, 'dev', 0, 0, tiled=True)  24.1 us
    ppermute x6, waiting for transfers between devices, permute(): return lax.ppermute(block, 'dev', pairs)  10.4 us
    pallas_call x1, Pallas kernels, shards(): pl.pallas_call(functools.partial(coef_kernel, devices, per_dev), in_specs...  8.49 us
    pallas_call x1, Pallas kernels, shards(): pl.pallas_call(functools.partial(both_kernel, per_dev), in_specs=[vmem] *...  6.63 us
    pallas_call x2, Pallas kernels, mix(): pl.pallas_call(functools.partial(link_kernel, norm, devices, per_dev, fir...  6.09 us
    ppermute x6, starting transfers between devices, permute(): return lax.ppermute(block, 'dev', pairs)  4.3 us
    pallas_call x1, Pallas kernels, shards(): pl.pallas_call(functools.partial(last_kernel, per_dev), in_specs=[vmem] *...  3.29 us
    pallas_call x1, Pallas kernels, shards(): pl.pallas_call(prepare_kernel, in_specs=[vmem, hbm, hbm], out_specs=[vmem...  1.71 us
  transfers between devices with their start and end apart: 6, of which 5 were waited for; matrix products, arithmetic and copies ran while one was open for 0% of the time, Pallas kernels for 3%

profile of v17, /device:TPU:0, one launch (start us, length us, event | category | flops | bytes accessed | tf_op | source)
XLA Modules:
  0.0 65.2 jit_solution(4571721984209747322)
XLA Ops:
  0.0 0.0 copy-start
  0.0 0.0 copy-start.1
  0.0 8.5 %coef_pass.1 = (bf16[4,640]{1,0:T(4,128)(2,1)S(1)}, bf16[128,65536]{1,0:T(8,128)(2,1)S(1)}, s32[512,128]{1,0:T(8,128)S(1)}, s32[24,128]{1,0:T(8,128)S(1)}, bf16[2,64,128,128]{3,2,1,0:T(8,128)(2,1)S(1)}) custom-call(s32[1,64]{1,0:T(1,128)} %bitcast.5, s32[512,128]{1,0:T(8,128)} %bitcast.6, bf16[512,128]{1,0:T(8,128)(2,1)} %bitcast.8, ...), custom_call_target="tpu_custom_call" | custom-call | tf_op jit(solution)/shard_map/coef_pass/pallas_call | solution.py:307
  8.5 14.3 %all_to_all.10.parts_ref = bf16[16,4,640]{2,1,0:T(4,128)(2,1)S(1)} all-to-all(bf16[16,4,640]{2,1,0:T(4,128)(2,1)S(1)} %broadcast_in_dim.4), channel_id=1, replica_groups=mesh['groups'=2,'dev'=16] {'dev'}, dimensions={0} | all-to-all | bytes 163840 | tf_op jit(solution)/shard_map/all_to_all | solution.py:334
  22.9 0.0 copy-done
  22.9 0.0 copy-done.1
  22.9 3.9 %link_product.2 = (bf16[4,128]{1,0:T(4,128)(2,1)S(1)}, bf16[2,64,128,128]{3,2,1,0:T(8,128)(2,1)S(1)}) custom-call(s32[64]{0:T(128)S(1)} %copy-done.1, s32[4,64]{1,0:T(4,128)S(1)} %copy-done, bf16[16,4,640]{2,1,0:T(4,128)(2,1)S(1)} %all_to_all.10.parts_ref, bf16[2,64,128,128]{3,2,1,0:T(8,128)(2,1)S(1)} %get-tuple-element.18.links1_ref, ...), custom_call_target="tpu_custom_call" | custom-call | tf_op jit(solution)/shard_map/link_product/pallas_call | solution.py:347
  26.8 0.1 collective-permute-start
  26.8 1.1 %collective-permute-done = bf16[4,128]{1,0:T(4,128)(2,1)S(1)} collective-permute-done((bf16[4,128]{1,0:T(4,128)(2,1)S(1)}, bf16[4,128]{1,0:T(4,128)(2,1)S(1)}, u32[]{:S(2)}, u32[]{:S(2)}) %collective-permute-start) | collective-permute-done | bytes 1056 | tf_op jit(solution)/shard_map/ppermute | solution.py:337
  28.0 0.8 %collective-permute-start.2 = (bf16[8,128]{1,0:T(8,128)(2,1)S(1)}, bf16[8,128]{1,0:T(8,128)(2,1)S(1)}, u32[]{:S(2)}, u32[]{:S(2)}) collective-permute-start(bf16[8,128]{1,0:T(8,128)(2,1)S(1)} %pad_maximum_fusion.after_ref.own_ref), channel_id=1, source_target_pairs={{2,0},{3,1},{4,2},{5,3},{6,4},{7,5},{8,6},{9,7},{10,8},{11,9},{12,... | collective-permute-start | bytes 6152 | tf_op jit(solution)/shard_map/ppermute | solution.py:337
  28.8 1.3 %collective-permute-start.1 = (bf16[8,128]{1,0:T(8,128)(2,1)S(1)}, bf16[8,128]{1,0:T(8,128)(2,1)S(1)}, u32[]{:S(2)}, u32[]{:S(2)}) collective-permute-start(bf16[8,128]{1,0:T(8,128)(2,1)S(1)} %pad_maximum_fusion.after_ref.own_ref), channel_id=1, source_target_pairs={{14,0},{15,1},{0,2},{1,3},{2,4},{3,5},{4,6},{5,7},{6,8},{7,9},{8,1... | collective-permute-start | bytes 6152 | tf_op jit(solution)/shard_map/ppermute | solution.py:337
  30.1 1.7 %prepare.1 = (f32[512,128]{1,0:T(8,128)S(1)}, bf16[8192,128]{1,0:T(8,128)(2,1)S(1)}) custom-call(bf16[8,128]{1,0:T(8,128)(2,1)S(1)} %pad_maximum_fusion.after_ref.own_ref, f32[512,128]{1,0:T(8,128)} %bitcast.7, bf16[65536,128]{1,0:T(8,128)(2,1)} %basis_hbm.5), custom_call_target="tpu_custom_call" | custom-call | bytes 4194304 | tf_op jit(solution)/shard_map/prepare/pallas_call | solution.py:364
  31.8 0.0 collective-permute-done.2.ahead_ref
  31.8 3.3 %collective-permute-done.1.behind_ref = bf16[8,128]{1,0:T(8,128)(2,1)S(1)} collective-permute-done((bf16[8,128]{1,0:T(8,128)(2,1)S(1)}, bf16[8,128]{1,0:T(8,128)(2,1)S(1)}, u32[]{:S(2)}, u32[]{:S(2)}) %collective-permute-start.1) | collective-permute-done | bytes 2080 | tf_op jit(solution)/shard_map/ppermute | solution.py:337
  35.0 6.6 %first_and_coef_pass.1 = (f32[512,128]{1,0:T(8,128)S(1)}, bf16[4,640]{1,0:T(4,128)(2,1)S(1)}) custom-call(s32[24,128]{1,0:T(8,128)S(1)} %get-tuple-element.16.cl_ref, bf16[8,128]{1,0:T(8,128)(2,1)S(1)} %collective-permute-done.1.behind_ref, bf16[8,128]{1,0:T(8,128)(2,1)S(1)} %pad_maximum_fusion.after_ref.own_ref, ...), custom_call_target="tpu_custom_call" | custom-call | tf_op jit(solution)/shard_map/first_and_coef_pass/pallas_call | solution.py:375
  41.7 9.7 %all_to_all.11.parts_ref = bf16[16,4,640]{2,1,0:T(4,128)(2,1)S(1)} all-to-all(bf16[16,4,640]{2,1,0:T(4,128)(2,1)S(1)} %broadcast_in_dim.5), channel_id=1, replica_groups=mesh['groups'=2,'dev'=16] {'dev'}, dimensions={0} | all-to-all | bytes 163840 | tf_op jit(solution)/shard_map/all_to_all | solution.py:334
  51.4 2.2 %link_product.3 = bf16[4,128]{1,0:T(4,128)(2,1)S(1)} custom-call(s32[64]{0:T(128)S(1)} %copy-done.1, s32[4,64]{1,0:T(4,128)S(1)} %copy-done, bf16[16,4,640]{2,1,0:T(4,128)(2,1)S(1)} %all_to_all.11.parts_ref, bf16[2,64,128,128]{3,2,1,0:T(8,128)(2,1)S(1)} %get-tuple-element.18.links1_ref, bf16[2,64,128,128]{3,2,1,0:T(8,128)(2,1)S(1)} %get-tuple-element.25.refs_0_), custom_call_target="tpu_custom_call" | custom-call | tf_op jit(solution)/shard_map/link_product/pallas_call | solution.py:347
  53.7 0.1 collective-permute-start.3
  53.7 1.1 %collective-permute-done.3 = bf16[4,128]{1,0:T(4,128)(2,1)S(1)} collective-permute-done((bf16[4,128]{1,0:T(4,128)(2,1)S(1)}, bf16[4,128]{1,0:T(4,128)(2,1)S(1)}, u32[]{:S(2)}, u32[]{:S(2)}) %collective-permute-start.3) | collective-permute-done | bytes 1056 | tf_op jit(solution)/shard_map/ppermute | solution.py:337
  54.9 0.7 %collective-permute-start.5 = (bf16[8,128]{1,0:T(8,128)(2,1)S(1)}, bf16[8,128]{1,0:T(8,128)(2,1)S(1)}, u32[]{:S(2)}, u32[]{:S(2)}) collective-permute-start(bf16[8,128]{1,0:T(8,128)(2,1)S(1)} %pad_maximum_fusion.1.own_ref), channel_id=1, source_target_pairs={{2,0},{3,1},{4,2},{5,3},{6,4},{7,5},{8,6},{9,7},{10,8},{11,9},{12,... | collective-permute-start | bytes 6152 | tf_op jit(solution)/shard_map/ppermute | solution.py:337
  55.6 1.4 %collective-permute-start.4 = (bf16[8,128]{1,0:T(8,128)(2,1)S(1)}, bf16[8,128]{1,0:T(8,128)(2,1)S(1)}, u32[]{:S(2)}, u32[]{:S(2)}) collective-permute-start(bf16[8,128]{1,0:T(8,128)(2,1)S(1)} %pad_maximum_fusion.1.own_ref), channel_id=1, source_target_pairs={{14,0},{15,1},{0,2},{1,3},{2,4},{3,5},{4,6},{5,7},{6,8},{7,9},{8,1... | collective-permute-start | bytes 6152 | tf_op jit(solution)/shard_map/ppermute | solution.py:337
  56.9 1.6 %collective-permute-done.5.ahead_ref = bf16[8,128]{1,0:T(8,128)(2,1)S(1)} collective-permute-done((bf16[8,128]{1,0:T(8,128)(2,1)S(1)}, bf16[8,128]{1,0:T(8,128)(2,1)S(1)}, u32[]{:S(2)}, u32[]{:S(2)}) %collective-permute-start.5) | collective-permute-done | bytes 2080 | tf_op jit(solution)/shard_map/ppermute | solution.py:337
  58.5 3.4 %collective-permute-done.4.behind_ref = bf16[8,128]{1,0:T(8,128)(2,1)S(1)} collective-permute-done((bf16[8,128]{1,0:T(8,128)(2,1)S(1)}, bf16[8,128]{1,0:T(8,128)(2,1)S(1)}, u32[]{:S(2)}, u32[]{:S(2)}) %collective-permute-start.4) | collective-permute-done | bytes 2080 | tf_op jit(solution)/shard_map/ppermute | solution.py:337
  61.9 3.3 %last_pass.1 = f32[512,128]{1,0:T(8,128)} custom-call(s32[24,128]{1,0:T(8,128)S(1)} %get-tuple-element.16.cl_ref, bf16[8,128]{1,0:T(8,128)(2,1)S(1)} %collective-permute-done.4.behind_ref, bf16[8,128]{1,0:T(8,128)(2,1)S(1)} %pad_maximum_fusion.1.own_ref, bf16[8,128]{1,0:T(8,128)(2,1)S(1)} %collective-permute-done.5.ahead_ref, ...), custom_call_target="tpu_custom_call" | custom-call | tf_op jit(solution)/shard_map/last_pass/pallas_call | solution.py:395
  (4 shorter events, 0.1 us)
Async XLA Ops:
  0.0 22.9 %copy-start = (s32[4,64]{1,0:T(4,128)S(1)}, s32[4,64]{1,0:T(4,128)}, u32[]{:S(2)}) copy-start(s32[4,64]{1,0:T(4,128)} %partners_ref.3) | copy-start | bytes 3076
  0.0 22.9 %copy-start.1 = (s32[64]{0:T(128)S(1)}, s32[64]{0:T(128)}, u32[]{:S(2)}) copy-start(s32[64]{0:T(128)} %slot_of_ref.3) | copy-start | bytes 772
  26.8 1.2 %collective-permute-start = (bf16[4,128]{1,0:T(4,128)(2,1)S(1)}, bf16[4,128]{1,0:T(4,128)(2,1)S(1)}, u32[]{:S(2)}, u32[]{:S(2)}) collective-permute-start(bf16[4,128]{1,0:T(4,128)(2,1)S(1)} %get-tuple-element.19), channel_id=1, source_target_pairs={{1,0},{0,1},{3,2},{2,3},{5,4},{4,5},{7,6},{6,7},{9,8},{8,9},{11,10... | collective-permute-start | bytes 3080 | tf_op jit(solution)/shard_map/ppermute | solution.py:337
  28.0 3.8 %collective-permute-start.2 = (bf16[8,128]{1,0:T(8,128)(2,1)S(1)}, bf16[8,128]{1,0:T(8,128)(2,1)S(1)}, u32[]{:S(2)}, u32[]{:S(2)}) collective-permute-start(bf16[8,128]{1,0:T(8,128)(2,1)S(1)} %pad_maximum_fusion.after_ref.own_ref), channel_id=1, source_target_pairs={{2,0},{3,1},{4,2},{5,3},{6,4},{7,5},{8,6},{9,7},{10,8},{11,9},{12,... | collective-permute-start | bytes 6152 | tf_op jit(solution)/shard_map/ppermute | solution.py:337
  28.8 6.3 %collective-permute-start.1 = (bf16[8,128]{1,0:T(8,128)(2,1)S(1)}, bf16[8,128]{1,0:T(8,128)(2,1)S(1)}, u32[]{:S(2)}, u32[]{:S(2)}) collective-permute-start(bf16[8,128]{1,0:T(8,128)(2,1)S(1)} %pad_maximum_fusion.after_ref.own_ref), channel_id=1, source_target_pairs={{14,0},{15,1},{0,2},{1,3},{2,4},{3,5},{4,6},{5,7},{6,8},{7,9},{8,1... | collective-permute-start | bytes 6152 | tf_op jit(solution)/shard_map/ppermute | solution.py:337
  53.7 1.2 %collective-permute-start.3 = (bf16[4,128]{1,0:T(4,128)(2,1)S(1)}, bf16[4,128]{1,0:T(4,128)(2,1)S(1)}, u32[]{:S(2)}, u32[]{:S(2)}) collective-permute-start(bf16[4,128]{1,0:T(4,128)(2,1)S(1)} %link_product.3), channel_id=1, source_target_pairs={{1,0},{0,1},{3,2},{2,3},{5,4},{4,5},{7,6},{6,7},{9,8},{8,9},{11,10... | collective-permute-start | bytes 3080 | tf_op jit(solution)/shard_map/ppermute | solution.py:337
  54.9 3.6 %collective-permute-start.5 = (bf16[8,128]{1,0:T(8,128)(2,1)S(1)}, bf16[8,128]{1,0:T(8,128)(2,1)S(1)}, u32[]{:S(2)}, u32[]{:S(2)}) collective-permute-start(bf16[8,128]{1,0:T(8,128)(2,1)S(1)} %pad_maximum_fusion.1.own_ref), channel_id=1, source_target_pairs={{2,0},{3,1},{4,2},{5,3},{6,4},{7,5},{8,6},{9,7},{10,8},{11,9},{12,... | collective-permute-start | bytes 6152 | tf_op jit(solution)/shard_map/ppermute | solution.py:337
  55.6 6.3 %collective-permute-start.4 = (bf16[8,128]{1,0:T(8,128)(2,1)S(1)}, bf16[8,128]{1,0:T(8,128)(2,1)S(1)}, u32[]{:S(2)}, u32[]{:S(2)}) collective-permute-start(bf16[8,128]{1,0:T(8,128)(2,1)S(1)} %pad_maximum_fusion.1.own_ref), channel_id=1, source_target_pairs={{14,0},{15,1},{0,2},{1,3},{2,4},{3,5},{4,6},{5,7},{6,8},{7,9},{8,1... | collective-permute-start | bytes 6152 | tf_op jit(solution)/shard_map/ppermute | solution.py:337

commit v18 on v16

--- a/solution.py
+++ b/solution.py
@@ -20,7 +20,7 @@
 PER_COPY = COPY // TILE
 SLOTS = 4
 BODY = 16
-PIECE = 512
+PIECE = 1024
 GROUP = 8
 
 ridge = 0.5
@@ -78,6 +78,8 @@
 
     def basis_copy(c):
         return slot_copy(basis_hbm, slots_ref, basis_sem, c)
+
+    links_from = copies - per_dev - 1
 
     def links_copy(j):
         return pltpu.make_async_copy(links_hbm.at[j], links_ref.at[j], links_sem.at[j])
@@ -102,9 +104,9 @@
     def _(c):
         basis_copy(c).wait()
 
-        @pl.when(c < per_dev)
+        @pl.when((c >= links_from) & (c < links_from + per_dev))
         def _():
-            links_copy(c).start()
+            links_copy(c - links_from).start()
 
         total = sum_ref[...]
         for p in range(PER_COPY):

time: 64.8 us -> 64.8 us (level)
  no operation moved by 1% of the time
where the time goes in v18:
time: 64.8 us; the launch traced here: 64.6 us
  Pallas kernels  25.7 us (40%)
  blocking collectives  24.1 us (37%)
  waiting for transfers between devices  10.5 us (16%)
  starting transfers between devices  4.29 us (7%)
    all_to_all x2, blocking collectives, to_all(): return lax.all_to_all(copies, 'dev', 0, 0, tiled=True)  24.1 us
    ppermute x6, waiting for transfers between devices, permute(): return lax.ppermute(block, 'dev', pairs)  10.5 us
    pallas_call x1, Pallas kernels, shards(): pl.pallas_call(functools.partial(coef_kernel, devices, per_dev), in_specs...  9.62 us
    pallas_call x1, Pallas kernels, shards(): pl.pallas_call(functools.partial(both_kernel, per_dev), in_specs=[vmem] *...  6.62 us
    pallas_call x2, Pallas kernels, mix(): pl.pallas_call(functools.partial(link_kernel, norm, devices, per_dev), in...  4.41 us
    ppermute x6, starting transfers between devices, permute(): return lax.ppermute(block, 'dev', pairs)  4.29 us
    pallas_call x1, Pallas kernels, shards(): pl.pallas_call(functools.partial(last_kernel, per_dev), in_specs=[vmem] *...  3.3 us
    pallas_call x1, Pallas kernels, shards(): pl.pallas_call(prepare_kernel, in_specs=[vmem, hbm, hbm], out_specs=[vmem...  1.71 us
  transfers between devices with their start and end apart: 6, of which 5 were waited for; matrix products, arithmetic and copies ran while one was open for 0% of the time, Pallas kernels for 3%

profile of v18, /device:TPU:0, one launch (start us, length us, event | category | flops | bytes accessed | tf_op | source)
XLA Modules:
  0.0 64.6 jit_solution(14451573621220585762)
XLA Ops:
  0.0 0.0 copy-start
  0.0 0.0 copy-start.1
  0.0 9.6 %coef_pass.1 = (bf16[4,640]{1,0:T(4,128)(2,1)S(1)}, bf16[128,65536]{1,0:T(8,128)(2,1)S(1)}, s32[512,128]{1,0:T(8,128)S(1)}, s32[24,128]{1,0:T(8,128)S(1)}, bf16[4,64,128,128]{3,2,1,0:T(8,128)(2,1)S(1)}) custom-call(s32[1,64]{1,0:T(1,128)} %bitcast.5, s32[512,128]{1,0:T(8,128)} %bitcast.6, bf16[512,128]{1,0:T(8,128)(2,1)} %bitcast.8, ...), custom_call_target="tpu_custom_call" | custom-call | tf_op jit(solution)/shard_map/coef_pass/pallas_call | solution.py:291
  9.7 14.3 %all_to_all.10.parts_ref = bf16[16,4,640]{2,1,0:T(4,128)(2,1)S(1)} all-to-all(bf16[16,4,640]{2,1,0:T(4,128)(2,1)S(1)} %broadcast_in_dim.4), channel_id=1, replica_groups=mesh['groups'=2,'dev'=16] {'dev'}, dimensions={0} | all-to-all | bytes 163840 | tf_op jit(solution)/shard_map/all_to_all | solution.py:318
  24.0 0.0 copy-done
  24.0 0.0 copy-done.1
  24.0 2.2 %link_product.2 = bf16[4,128]{1,0:T(4,128)(2,1)S(1)} custom-call(s32[64]{0:T(128)S(1)} %copy-done.1, s32[4,64]{1,0:T(4,128)S(1)} %copy-done, bf16[16,4,640]{2,1,0:T(4,128)(2,1)S(1)} %all_to_all.10.parts_ref, bf16[4,64,128,128]{3,2,1,0:T(8,128)(2,1)S(1)} %get-tuple-element.16.links_ref), custom_call_target="tpu_custom_call" | custom-call | tf_op jit(solution)/shard_map/link_product/pallas_call | solution.py:331
  26.2 0.1 collective-permute-start
  26.3 1.1 %collective-permute-done = bf16[4,128]{1,0:T(4,128)(2,1)S(1)} collective-permute-done((bf16[4,128]{1,0:T(4,128)(2,1)S(1)}, bf16[4,128]{1,0:T(4,128)(2,1)S(1)}, u32[]{:S(2)}, u32[]{:S(2)}) %collective-permute-start) | collective-permute-done | bytes 1056 | tf_op jit(solution)/shard_map/ppermute | solution.py:321
  27.4 0.8 %collective-permute-start.2 = (bf16[8,128]{1,0:T(8,128)(2,1)S(1)}, bf16[8,128]{1,0:T(8,128)(2,1)S(1)}, u32[]{:S(2)}, u32[]{:S(2)}) collective-permute-start(bf16[8,128]{1,0:T(8,128)(2,1)S(1)} %pad_maximum_fusion.after_ref.own_ref), channel_id=1, source_target_pairs={{2,0},{3,1},{4,2},{5,3},{6,4},{7,5},{8,6},{9,7},{10,8},{11,9},{12,... | collective-permute-start | bytes 6152 | tf_op jit(solution)/shard_map/ppermute | solution.py:321
  28.2 1.3 %collective-permute-start.1 = (bf16[8,128]{1,0:T(8,128)(2,1)S(1)}, bf16[8,128]{1,0:T(8,128)(2,1)S(1)}, u32[]{:S(2)}, u32[]{:S(2)}) collective-permute-start(bf16[8,128]{1,0:T(8,128)(2,1)S(1)} %pad_maximum_fusion.after_ref.own_ref), channel_id=1, source_target_pairs={{14,0},{15,1},{0,2},{1,3},{2,4},{3,5},{4,6},{5,7},{6,8},{7,9},{8,1... | collective-permute-start | bytes 6152 | tf_op jit(solution)/shard_map/ppermute | solution.py:321
  29.5 1.7 %prepare.1 = (f32[512,128]{1,0:T(8,128)S(1)}, bf16[8192,128]{1,0:T(8,128)(2,1)S(1)}) custom-call(bf16[8,128]{1,0:T(8,128)(2,1)S(1)} %pad_maximum_fusion.after_ref.own_ref, f32[512,128]{1,0:T(8,128)} %bitcast.7, bf16[65536,128]{1,0:T(8,128)(2,1)} %basis_hbm.5), custom_call_target="tpu_custom_call" | custom-call | bytes 4194304 | tf_op jit(solution)/shard_map/prepare/pallas_call | solution.py:346
  31.2 0.0 collective-permute-done.2.ahead_ref
  31.2 3.3 %collective-permute-done.1.behind_ref = bf16[8,128]{1,0:T(8,128)(2,1)S(1)} collective-permute-done((bf16[8,128]{1,0:T(8,128)(2,1)S(1)}, bf16[8,128]{1,0:T(8,128)(2,1)S(1)}, u32[]{:S(2)}, u32[]{:S(2)}) %collective-permute-start.1) | collective-permute-done | bytes 2080 | tf_op jit(solution)/shard_map/ppermute | solution.py:321
  34.5 6.6 %first_and_coef_pass.1 = (f32[512,128]{1,0:T(8,128)S(1)}, bf16[4,640]{1,0:T(4,128)(2,1)S(1)}) custom-call(s32[24,128]{1,0:T(8,128)S(1)} %get-tuple-element.14.cl_ref, bf16[8,128]{1,0:T(8,128)(2,1)S(1)} %collective-permute-done.1.behind_ref, bf16[8,128]{1,0:T(8,128)(2,1)S(1)} %pad_maximum_fusion.after_ref.own_ref, ...), custom_call_target="tpu_custom_call" | custom-call | tf_op jit(solution)/shard_map/first_and_coef_pass/pallas_call | solution.py:357
  41.2 9.7 %all_to_all.11.parts_ref = bf16[16,4,640]{2,1,0:T(4,128)(2,1)S(1)} all-to-all(bf16[16,4,640]{2,1,0:T(4,128)(2,1)S(1)} %broadcast_in_dim.5), channel_id=1, replica_groups=mesh['groups'=2,'dev'=16] {'dev'}, dimensions={0} | all-to-all | bytes 163840 | tf_op jit(solution)/shard_map/all_to_all | solution.py:318
  50.9 2.2 %link_product.3 = bf16[4,128]{1,0:T(4,128)(2,1)S(1)} custom-call(s32[64]{0:T(128)S(1)} %copy-done.1, s32[4,64]{1,0:T(4,128)S(1)} %copy-done, bf16[16,4,640]{2,1,0:T(4,128)(2,1)S(1)} %all_to_all.11.parts_ref, bf16[4,64,128,128]{3,2,1,0:T(8,128)(2,1)S(1)} %get-tuple-element.16.links_ref), custom_call_target="tpu_custom_call" | custom-call | tf_op jit(solution)/shard_map/link_product/pallas_call | solution.py:331
  53.1 0.1 collective-permute-start.3
  53.2 1.1 %collective-permute-done.3 = bf16[4,128]{1,0:T(4,128)(2,1)S(1)} collective-permute-done((bf16[4,128]{1,0:T(4,128)(2,1)S(1)}, bf16[4,128]{1,0:T(4,128)(2,1)S(1)}, u32[]{:S(2)}, u32[]{:S(2)}) %collective-permute-start.3) | collective-permute-done | bytes 1056 | tf_op jit(solution)/shard_map/ppermute | solution.py:321
  54.3 0.7 %collective-permute-start.5 = (bf16[8,128]{1,0:T(8,128)(2,1)S(1)}, bf16[8,128]{1,0:T(8,128)(2,1)S(1)}, u32[]{:S(2)}, u32[]{:S(2)}) collective-permute-start(bf16[8,128]{1,0:T(8,128)(2,1)S(1)} %pad_maximum_fusion.1.own_ref), channel_id=1, source_target_pairs={{2,0},{3,1},{4,2},{5,3},{6,4},{7,5},{8,6},{9,7},{10,8},{11,9},{12,... | collective-permute-start | bytes 6152 | tf_op jit(solution)/shard_map/ppermute | solution.py:321
  55.0 1.3 %collective-permute-start.4 = (bf16[8,128]{1,0:T(8,128)(2,1)S(1)}, bf16[8,128]{1,0:T(8,128)(2,1)S(1)}, u32[]{:S(2)}, u32[]{:S(2)}) collective-permute-start(bf16[8,128]{1,0:T(8,128)(2,1)S(1)} %pad_maximum_fusion.1.own_ref), channel_id=1, source_target_pairs={{14,0},{15,1},{0,2},{1,3},{2,4},{3,5},{4,6},{5,7},{6,8},{7,9},{8,1... | collective-permute-start | bytes 6152 | tf_op jit(solution)/shard_map/ppermute | solution.py:321
  56.4 1.6 %collective-permute-done.5.ahead_ref = bf16[8,128]{1,0:T(8,128)(2,1)S(1)} collective-permute-done((bf16[8,128]{1,0:T(8,128)(2,1)S(1)}, bf16[8,128]{1,0:T(8,128)(2,1)S(1)}, u32[]{:S(2)}, u32[]{:S(2)}) %collective-permute-start.5) | collective-permute-done | bytes 2080 | tf_op jit(solution)/shard_map/ppermute | solution.py:321
  57.9 3.4 %collective-permute-done.4.behind_ref = bf16[8,128]{1,0:T(8,128)(2,1)S(1)} collective-permute-done((bf16[8,128]{1,0:T(8,128)(2,1)S(1)}, bf16[8,128]{1,0:T(8,128)(2,1)S(1)}, u32[]{:S(2)}, u32[]{:S(2)}) %collective-permute-start.4) | collective-permute-done | bytes 2080 | tf_op jit(solution)/shard_map/ppermute | solution.py:321
  61.3 3.3 %last_pass.1 = f32[512,128]{1,0:T(8,128)} custom-call(s32[24,128]{1,0:T(8,128)S(1)} %get-tuple-element.14.cl_ref, bf16[8,128]{1,0:T(8,128)(2,1)S(1)} %collective-permute-done.4.behind_ref, bf16[8,128]{1,0:T(8,128)(2,1)S(1)} %pad_maximum_fusion.1.own_ref, bf16[8,128]{1,0:T(8,128)(2,1)S(1)} %collective-permute-done.5.ahead_ref, ...), custom_call_target="tpu_custom_call" | custom-call | tf_op jit(solution)/shard_map/last_pass/pallas_call | solution.py:376
  (4 shorter events, 0.1 us)
Async XLA Ops:
  0.0 24.0 %copy-start = (s32[4,64]{1,0:T(4,128)S(1)}, s32[4,64]{1,0:T(4,128)}, u32[]{:S(2)}) copy-start(s32[4,64]{1,0:T(4,128)} %partners_ref.3) | copy-start | bytes 3076
  0.0 24.0 %copy-start.1 = (s32[64]{0:T(128)S(1)}, s32[64]{0:T(128)}, u32[]{:S(2)}) copy-start(s32[64]{0:T(128)} %slot_of_ref.3) | copy-start | bytes 772
  26.2 1.2 %collective-permute-start = (bf16[4,128]{1,0:T(4,128)(2,1)S(1)}, bf16[4,128]{1,0:T(4,128)(2,1)S(1)}, u32[]{:S(2)}, u32[]{:S(2)}) collective-permute-start(bf16[4,128]{1,0:T(4,128)(2,1)S(1)} %link_product.2), channel_id=1, source_target_pairs={{1,0},{0,1},{3,2},{2,3},{5,4},{4,5},{7,6},{6,7},{9,8},{8,9},{11,10... | collective-permute-start | bytes 3080 | tf_op jit(solution)/shard_map/ppermute | solution.py:321
  27.4 3.8 %collective-permute-start.2 = (bf16[8,128]{1,0:T(8,128)(2,1)S(1)}, bf16[8,128]{1,0:T(8,128)(2,1)S(1)}, u32[]{:S(2)}, u32[]{:S(2)}) collective-permute-start(bf16[8,128]{1,0:T(8,128)(2,1)S(1)} %pad_maximum_fusion.after_ref.own_ref), channel_id=1, source_target_pairs={{2,0},{3,1},{4,2},{5,3},{6,4},{7,5},{8,6},{9,7},{10,8},{11,9},{12,... | collective-permute-start | bytes 6152 | tf_op jit(solution)/shard_map/ppermute | solution.py:321
  28.2 6.3 %collective-permute-start.1 = (bf16[8,128]{1,0:T(8,128)(2,1)S(1)}, bf16[8,128]{1,0:T(8,128)(2,1)S(1)}, u32[]{:S(2)}, u32[]{:S(2)}) collective-permute-start(bf16[8,128]{1,0:T(8,128)(2,1)S(1)} %pad_maximum_fusion.after_ref.own_ref), channel_id=1, source_target_pairs={{14,0},{15,1},{0,2},{1,3},{2,4},{3,5},{4,6},{5,7},{6,8},{7,9},{8,1... | collective-permute-start | bytes 6152 | tf_op jit(solution)/shard_map/ppermute | solution.py:321
  53.1 1.2 %collective-permute-start.3 = (bf16[4,128]{1,0:T(4,128)(2,1)S(1)}, bf16[4,128]{1,0:T(4,128)(2,1)S(1)}, u32[]{:S(2)}, u32[]{:S(2)}) collective-permute-start(bf16[4,128]{1,0:T(4,128)(2,1)S(1)} %link_product.3), channel_id=1, source_target_pairs={{1,0},{0,1},{3,2},{2,3},{5,4},{4,5},{7,6},{6,7},{9,8},{8,9},{11,10... | collective-permute-start | bytes 3080 | tf_op jit(solution)/shard_map/ppermute | solution.py:321
  54.3 3.6 %collective-permute-start.5 = (bf16[8,128]{1,0:T(8,128)(2,1)S(1)}, bf16[8,128]{1,0:T(8,128)(2,1)S(1)}, u32[]{:S(2)}, u32[]{:S(2)}) collective-permute-start(bf16[8,128]{1,0:T(8,128)(2,1)S(1)} %pad_maximum_fusion.1.own_ref), channel_id=1, source_target_pairs={{2,0},{3,1},{4,2},{5,3},{6,4},{7,5},{8,6},{9,7},{10,8},{11,9},{12,... | collective-permute-start | bytes 6152 | tf_op jit(solution)/shard_map/ppermute | solution.py:321
  55.0 6.3 %collective-permute-start.4 = (bf16[8,128]{1,0:T(8,128)(2,1)S(1)}, bf16[8,128]{1,0:T(8,128)(2,1)S(1)}, u32[]{:S(2)}, u32[]{:S(2)}) collective-permute-start(bf16[8,128]{1,0:T(8,128)(2,1)S(1)} %pad_maximum_fusion.1.own_ref), channel_id=1, source_target_pairs={{14,0},{15,1},{0,2},{1,3},{2,4},{3,5},{4,6},{5,7},{6,8},{7,9},{8,1... | collective-permute-start | bytes 6152 | tf_op jit(solution)/shard_map/ppermute | solution.py:321

commit v19 on v18

--- a/solution.py
+++ b/solution.py
@@ -16,10 +16,10 @@
 ROWS = 24
 
 COPY = 8192
-TILE = 2048
+TILE = 4096
 PER_COPY = COPY // TILE
 SLOTS = 4
-BODY = 16
+BODY = 8
 PIECE = 1024
 GROUP = 8
 

time: 64.8 us -> 65.9 us (1.017)
  Pallas kernels: 25.7 us -> 26.7 us
    pallas_call x1, Pallas kernels: 6.62 us -> 7.64 us  [shards(): pl.pallas_call(functools.partial(both_kernel, per_dev), in_specs=[vmem] *...]
where the time goes in v19:
time: 65.9 us; the launch traced here: 65.7 us
  Pallas kernels  26.7 us (41%)
  blocking collectives  24.1 us (37%)
  waiting for transfers between devices  10.4 us (16%)
  starting transfers between devices  4.29 us (7%)
    all_to_all x2, blocking collectives, to_all(): return lax.all_to_all(copies, 'dev', 0, 0, tiled=True)  24.1 us
    ppermute x6, waiting for transfers between devices, permute(): return lax.ppermute(block, 'dev', pairs)  10.4 us
    pallas_call x1, Pallas kernels, shards(): pl.pallas_call(functools.partial(coef_kernel, devices, per_dev), in_specs...  9.63 us
    pallas_call x1, Pallas kernels, shards(): pl.pallas_call(functools.partial(both_kernel, per_dev), in_specs=[vmem] *...  7.64 us
    pallas_call x2, Pallas kernels, mix(): pl.pallas_call(functools.partial(link_kernel, norm, devices, per_dev), in...  4.43 us
    ppermute x6, starting transfers between devices, permute(): return lax.ppermute(block, 'dev', pairs)  4.29 us
    pallas_call x1, Pallas kernels, shards(): pl.pallas_call(functools.partial(last_kernel, per_dev), in_specs=[vmem] *...  3.3 us
    pallas_call x1, Pallas kernels, shards(): pl.pallas_call(prepare_kernel, in_specs=[vmem, hbm, hbm], out_specs=[vmem...  1.71 us
  transfers between devices with their start and end apart: 6, of which 5 were waited for; matrix products, arithmetic and copies ran while one was open for 0% of the time, Pallas kernels for 3%

profile of v19, /device:TPU:0, one launch (start us, length us, event | category | flops | bytes accessed | tf_op | source)
XLA Modules:
  0.0 65.7 jit_solution(1125947004130067631)
XLA Ops:
  0.0 0.0 copy-start
  0.0 0.0 copy-start.1
  0.0 9.6 %coef_pass.1 = (bf16[4,640]{1,0:T(4,128)(2,1)S(1)}, bf16[128,65536]{1,0:T(8,128)(2,1)S(1)}, s32[512,128]{1,0:T(8,128)S(1)}, s32[24,128]{1,0:T(8,128)S(1)}, bf16[4,64,128,128]{3,2,1,0:T(8,128)(2,1)S(1)}) custom-call(s32[1,64]{1,0:T(1,128)} %bitcast.5, s32[512,128]{1,0:T(8,128)} %bitcast.6, bf16[512,128]{1,0:T(8,128)(2,1)} %bitcast.8, ...), custom_call_target="tpu_custom_call" | custom-call | tf_op jit(solution)/shard_map/coef_pass/pallas_call | solution.py:291
  9.7 14.3 %all_to_all.10.parts_ref = bf16[16,4,640]{2,1,0:T(4,128)(2,1)S(1)} all-to-all(bf16[16,4,640]{2,1,0:T(4,128)(2,1)S(1)} %broadcast_in_dim.4), channel_id=1, replica_groups=mesh['groups'=2,'dev'=16] {'dev'}, dimensions={0} | all-to-all | bytes 163840 | tf_op jit(solution)/shard_map/all_to_all | solution.py:318
  24.0 0.0 copy-done
  24.0 0.0 copy-done.1
  24.0 2.2 %link_product.2 = bf16[4,128]{1,0:T(4,128)(2,1)S(1)} custom-call(s32[64]{0:T(128)S(1)} %copy-done.1, s32[4,64]{1,0:T(4,128)S(1)} %copy-done, bf16[16,4,640]{2,1,0:T(4,128)(2,1)S(1)} %all_to_all.10.parts_ref, bf16[4,64,128,128]{3,2,1,0:T(8,128)(2,1)S(1)} %get-tuple-element.16.links_ref), custom_call_target="tpu_custom_call" | custom-call | tf_op jit(solution)/shard_map/link_product/pallas_call | solution.py:331
  26.2 0.1 collective-permute-start
  26.3 1.1 %collective-permute-done = bf16[4,128]{1,0:T(4,128)(2,1)S(1)} collective-permute-done((bf16[4,128]{1,0:T(4,128)(2,1)S(1)}, bf16[4,128]{1,0:T(4,128)(2,1)S(1)}, u32[]{:S(2)}, u32[]{:S(2)}) %collective-permute-start) | collective-permute-done | bytes 1056 | tf_op jit(solution)/shard_map/ppermute | solution.py:321
  27.4 0.8 %collective-permute-start.2 = (bf16[8,128]{1,0:T(8,128)(2,1)S(1)}, bf16[8,128]{1,0:T(8,128)(2,1)S(1)}, u32[]{:S(2)}, u32[]{:S(2)}) collective-permute-start(bf16[8,128]{1,0:T(8,128)(2,1)S(1)} %pad_maximum_fusion.after_ref.own_ref), channel_id=1, source_target_pairs={{2,0},{3,1},{4,2},{5,3},{6,4},{7,5},{8,6},{9,7},{10,8},{11,9},{12,... | collective-permute-start | bytes 6152 | tf_op jit(solution)/shard_map/ppermute | solution.py:321
  28.2 1.3 %collective-permute-start.1 = (bf16[8,128]{1,0:T(8,128)(2,1)S(1)}, bf16[8,128]{1,0:T(8,128)(2,1)S(1)}, u32[]{:S(2)}, u32[]{:S(2)}) collective-permute-start(bf16[8,128]{1,0:T(8,128)(2,1)S(1)} %pad_maximum_fusion.after_ref.own_ref), channel_id=1, source_target_pairs={{14,0},{15,1},{0,2},{1,3},{2,4},{3,5},{4,6},{5,7},{6,8},{7,9},{8,1... | collective-permute-start | bytes 6152 | tf_op jit(solution)/shard_map/ppermute | solution.py:321
  29.5 1.7 %prepare.1 = (f32[512,128]{1,0:T(8,128)S(1)}, bf16[8192,128]{1,0:T(8,128)(2,1)S(1)}) custom-call(bf16[8,128]{1,0:T(8,128)(2,1)S(1)} %pad_maximum_fusion.after_ref.own_ref, f32[512,128]{1,0:T(8,128)} %bitcast.7, bf16[65536,128]{1,0:T(8,128)(2,1)} %basis_hbm.5), custom_call_target="tpu_custom_call" | custom-call | bytes 4194304 | tf_op jit(solution)/shard_map/prepare/pallas_call | solution.py:346
  31.2 0.0 collective-permute-done.2.ahead_ref
  31.2 3.3 %collective-permute-done.1.behind_ref = bf16[8,128]{1,0:T(8,128)(2,1)S(1)} collective-permute-done((bf16[8,128]{1,0:T(8,128)(2,1)S(1)}, bf16[8,128]{1,0:T(8,128)(2,1)S(1)}, u32[]{:S(2)}, u32[]{:S(2)}) %collective-permute-start.1) | collective-permute-done | bytes 2080 | tf_op jit(solution)/shard_map/ppermute | solution.py:321
  34.5 7.6 %first_and_coef_pass.1 = (f32[512,128]{1,0:T(8,128)S(1)}, bf16[4,640]{1,0:T(4,128)(2,1)S(1)}) custom-call(s32[24,128]{1,0:T(8,128)S(1)} %get-tuple-element.14.cl_ref, bf16[8,128]{1,0:T(8,128)(2,1)S(1)} %collective-permute-done.1.behind_ref, bf16[8,128]{1,0:T(8,128)(2,1)S(1)} %pad_maximum_fusion.after_ref.own_ref, ...), custom_call_target="tpu_custom_call" | custom-call | tf_op jit(solution)/shard_map/first_and_coef_pass/pallas_call | solution.py:357
  42.2 9.7 %all_to_all.11.parts_ref = bf16[16,4,640]{2,1,0:T(4,128)(2,1)S(1)} all-to-all(bf16[16,4,640]{2,1,0:T(4,128)(2,1)S(1)} %broadcast_in_dim.5), channel_id=1, replica_groups=mesh['groups'=2,'dev'=16] {'dev'}, dimensions={0} | all-to-all | bytes 163840 | tf_op jit(solution)/shard_map/all_to_all | solution.py:318
  51.9 2.2 %link_product.3 = bf16[4,128]{1,0:T(4,128)(2,1)S(1)} custom-call(s32[64]{0:T(128)S(1)} %copy-done.1, s32[4,64]{1,0:T(4,128)S(1)} %copy-done, bf16[16,4,640]{2,1,0:T(4,128)(2,1)S(1)} %all_to_all.11.parts_ref, bf16[4,64,128,128]{3,2,1,0:T(8,128)(2,1)S(1)} %get-tuple-element.16.links_ref), custom_call_target="tpu_custom_call" | custom-call | tf_op jit(solution)/shard_map/link_product/pallas_call | solution.py:331
  54.1 0.1 collective-permute-start.3
  54.2 1.1 %collective-permute-done.3 = bf16[4,128]{1,0:T(4,128)(2,1)S(1)} collective-permute-done((bf16[4,128]{1,0:T(4,128)(2,1)S(1)}, bf16[4,128]{1,0:T(4,128)(2,1)S(1)}, u32[]{:S(2)}, u32[]{:S(2)}) %collective-permute-start.3) | collective-permute-done | bytes 1056 | tf_op jit(solution)/shard_map/ppermute | solution.py:321
  55.3 0.7 %collective-permute-start.5 = (bf16[8,128]{1,0:T(8,128)(2,1)S(1)}, bf16[8,128]{1,0:T(8,128)(2,1)S(1)}, u32[]{:S(2)}, u32[]{:S(2)}) collective-permute-start(bf16[8,128]{1,0:T(8,128)(2,1)S(1)} %pad_maximum_fusion.1.own_ref), channel_id=1, source_target_pairs={{2,0},{3,1},{4,2},{5,3},{6,4},{7,5},{8,6},{9,7},{10,8},{11,9},{12,... | collective-permute-start | bytes 6152 | tf_op jit(solution)/shard_map/ppermute | solution.py:321
  56.1 1.4 %collective-permute-start.4 = (bf16[8,128]{1,0:T(8,128)(2,1)S(1)}, bf16[8,128]{1,0:T(8,128)(2,1)S(1)}, u32[]{:S(2)}, u32[]{:S(2)}) collective-permute-start(bf16[8,128]{1,0:T(8,128)(2,1)S(1)} %pad_maximum_fusion.1.own_ref), channel_id=1, source_target_pairs={{14,0},{15,1},{0,2},{1,3},{2,4},{3,5},{4,6},{5,7},{6,8},{7,9},{8,1... | collective-permute-start | bytes 6152 | tf_op jit(solution)/shard_map/ppermute | solution.py:321
  57.4 1.6 %collective-permute-done.5.ahead_ref = bf16[8,128]{1,0:T(8,128)(2,1)S(1)} collective-permute-done((bf16[8,128]{1,0:T(8,128)(2,1)S(1)}, bf16[8,128]{1,0:T(8,128)(2,1)S(1)}, u32[]{:S(2)}, u32[]{:S(2)}) %collective-permute-start.5) | collective-permute-done | bytes 2080 | tf_op jit(solution)/shard_map/ppermute | solution.py:321
  59.0 3.4 %collective-permute-done.4.behind_ref = bf16[8,128]{1,0:T(8,128)(2,1)S(1)} collective-permute-done((bf16[8,128]{1,0:T(8,128)(2,1)S(1)}, bf16[8,128]{1,0:T(8,128)(2,1)S(1)}, u32[]{:S(2)}, u32[]{:S(2)}) %collective-permute-start.4) | collective-permute-done | bytes 2080 | tf_op jit(solution)/shard_map/ppermute | solution.py:321
  62.3 3.3 %last_pass.1 = f32[512,128]{1,0:T(8,128)} custom-call(s32[24,128]{1,0:T(8,128)S(1)} %get-tuple-element.14.cl_ref, bf16[8,128]{1,0:T(8,128)(2,1)S(1)} %collective-permute-done.4.behind_ref, bf16[8,128]{1,0:T(8,128)(2,1)S(1)} %pad_maximum_fusion.1.own_ref, bf16[8,128]{1,0:T(8,128)(2,1)S(1)} %collective-permute-done.5.ahead_ref, ...), custom_call_target="tpu_custom_call" | custom-call | tf_op jit(solution)/shard_map/last_pass/pallas_call | solution.py:376
  (4 shorter events, 0.1 us)
Async XLA Ops:
  0.0 24.0 %copy-start = (s32[4,64]{1,0:T(4,128)S(1)}, s32[4,64]{1,0:T(4,128)}, u32[]{:S(2)}) copy-start(s32[4,64]{1,0:T(4,128)} %partners_ref.3) | copy-start | bytes 3076
  0.0 24.0 %copy-start.1 = (s32[64]{0:T(128)S(1)}, s32[64]{0:T(128)}, u32[]{:S(2)}) copy-start(s32[64]{0:T(128)} %slot_of_ref.3) | copy-start | bytes 772
  26.2 1.2 %collective-permute-start = (bf16[4,128]{1,0:T(4,128)(2,1)S(1)}, bf16[4,128]{1,0:T(4,128)(2,1)S(1)}, u32[]{:S(2)}, u32[]{:S(2)}) collective-permute-start(bf16[4,128]{1,0:T(4,128)(2,1)S(1)} %link_product.2), channel_id=1, source_target_pairs={{1,0},{0,1},{3,2},{2,3},{5,4},{4,5},{7,6},{6,7},{9,8},{8,9},{11,10... | collective-permute-start | bytes 3080 | tf_op jit(solution)/shard_map/ppermute | solution.py:321
  27.4 3.8 %collective-permute-start.2 = (bf16[8,128]{1,0:T(8,128)(2,1)S(1)}, bf16[8,128]{1,0:T(8,128)(2,1)S(1)}, u32[]{:S(2)}, u32[]{:S(2)}) collective-permute-start(bf16[8,128]{1,0:T(8,128)(2,1)S(1)} %pad_maximum_fusion.after_ref.own_ref), channel_id=1, source_target_pairs={{2,0},{3,1},{4,2},{5,3},{6,4},{7,5},{8,6},{9,7},{10,8},{11,9},{12,... | collective-permute-start | bytes 6152 | tf_op jit(solution)/shard_map/ppermute | solution.py:321
  28.2 6.3 %collective-permute-start.1 = (bf16[8,128]{1,0:T(8,128)(2,1)S(1)}, bf16[8,128]{1,0:T(8,128)(2,1)S(1)}, u32[]{:S(2)}, u32[]{:S(2)}) collective-permute-start(bf16[8,128]{1,0:T(8,128)(2,1)S(1)} %pad_maximum_fusion.after_ref.own_ref), channel_id=1, source_target_pairs={{14,0},{15,1},{0,2},{1,3},{2,4},{3,5},{4,6},{5,7},{6,8},{7,9},{8,1... | collective-permute-start | bytes 6152 | tf_op jit(solution)/shard_map/ppermute | solution.py:321
  54.1 1.2 %collective-permute-start.3 = (bf16[4,128]{1,0:T(4,128)(2,1)S(1)}, bf16[4,128]{1,0:T(4,128)(2,1)S(1)}, u32[]{:S(2)}, u32[]{:S(2)}) collective-permute-start(bf16[4,128]{1,0:T(4,128)(2,1)S(1)} %link_product.3), channel_id=1, source_target_pairs={{1,0},{0,1},{3,2},{2,3},{5,4},{4,5},{7,6},{6,7},{9,8},{8,9},{11,10... | collective-permute-start | bytes 3080 | tf_op jit(solution)/shard_map/ppermute | solution.py:321
  55.3 3.6 %collective-permute-start.5 = (bf16[8,128]{1,0:T(8,128)(2,1)S(1)}, bf16[8,128]{1,0:T(8,128)(2,1)S(1)}, u32[]{:S(2)}, u32[]{:S(2)}) collective-permute-start(bf16[8,128]{1,0:T(8,128)(2,1)S(1)} %pad_maximum_fusion.1.own_ref), channel_id=1, source_target_pairs={{2,0},{3,1},{4,2},{5,3},{6,4},{7,5},{8,6},{9,7},{10,8},{11,9},{12,... | collective-permute-start | bytes 6152 | tf_op jit(solution)/shard_map/ppermute | solution.py:321
  56.1 6.3 %collective-permute-start.4 = (bf16[8,128]{1,0:T(8,128)(2,1)S(1)}, bf16[8,128]{1,0:T(8,128)(2,1)S(1)}, u32[]{:S(2)}, u32[]{:S(2)}) collective-permute-start(bf16[8,128]{1,0:T(8,128)(2,1)S(1)} %pad_maximum_fusion.1.own_ref), channel_id=1, source_target_pairs={{14,0},{15,1},{0,2},{1,3},{2,4},{3,5},{4,6},{5,7},{6,8},{7,9},{8,1... | collective-permute-start | bytes 6152 | tf_op jit(solution)/shard_map/ppermute | solution.py:321
